TPU v7x, 128 devices: a whole 4x4x4 slice. The times are simulated.
128 devices in a mesh: seq: 32 (over z, x, core), head: 4 (over y).
Axes of the slice: x: 4, y: 4, z: 4, core: 2. Of those that a mesh axis runs over, the one named last changes fastest.
Arguments:
- queries: bfloat16 [16384, 4096], P('seq', 'head'), may hold values from -6 to 6
- keys: bfloat16 [16384, 4096], P('seq', 'head'), may hold values from -0.625 to 0.625
- values: bfloat16 [16384, 4096], P('seq', 'head'), may hold values from -6 to 6
- logdecay: float32 [16384, 32], P('seq', 'head'), may hold values from -1 to 0
- out_weight: bfloat16 [4096, 6144], P('head'), may hold values from -0.09375 to 0.09375
- output_gradient: bfloat16 [16384, 6144], P('seq', 'head'), may hold values from -6 to 6
Outputs:
- attn_out: bfloat16 [16384, 6144], P('seq', 'head')
- grad_queries: bfloat16 [16384, 4096], P('seq', 'head')
- grad_keys: bfloat16 [16384, 4096], P('seq', 'head')
- grad_values: bfloat16 [16384, 4096], P('seq', 'head')
All inputs are finite; a program needn't handle non-finite values.
Results may differ from a plain program's by a relative error of at most 0.018.
Values may be sent and summed in bfloat16 or wider, within the bound.
No kernel may reach another device: no remote copies, remote signals or barrier semaphores. Data moves between devices by JAX's collectives and lax.ppermute only.
A program may use at most 192 MiB of HBM per device.

v0:
```python
import jax
import jax.numpy as jnp
from jax import lax
from jax.sharding import PartitionSpec as P

EPS = 1e-05


def decay_lookup_grid(cum_decay):
    along = cum_decay.T
    diff = along[:, :, None] - along[:, None, :]
    rows = cum_decay.shape[0]
    later = lax.broadcasted_iota(jnp.int32, (rows, rows), 0) >= lax.broadcasted_iota(
        jnp.int32, (rows, rows), 1
    )
    return jnp.exp(jnp.where(later[None], diff, -1e30))


def head_norm(attention):
    return attention * lax.rsqrt(jnp.mean(attention * attention, axis=-1, keepdims=True) + EPS)


def exact(form, left, right):
    return jnp.einsum(form, left, right, precision=lax.Precision.HIGHEST)


def narrow(form, left, right):
    return jnp.einsum(form, left, right, preferred_element_type=jnp.float32)


def earlier_weights(totals_all, position):
    running = jnp.cumsum(totals_all, axis=0)
    before = running - totals_all
    index_col = lax.broadcasted_iota(jnp.int32, totals_all.shape, 0)
    mine_before = jnp.sum(jnp.where(index_col == position, before, 0.0), axis=0)
    return jnp.exp(jnp.where(index_col < position, mine_before[None, :] - running, -1e30))


def later_weights(totals_all, position):
    running = jnp.cumsum(totals_all, axis=0)
    before = running - totals_all
    index_col = lax.broadcasted_iota(jnp.int32, totals_all.shape, 0)
    mine_running = jnp.sum(jnp.where(index_col == position, running, 0.0), axis=0)
    return jnp.exp(jnp.where(index_col > position, before - mine_running[None, :], -1e30))


def body(queries, keys, values, logdecay, out_weight, output_gradient):
    rows = queries.shape[0]
    heads = logdecay.shape[1]
    width = queries.shape[1] // heads
    head_query = queries.reshape(rows, heads, width)
    head_key = keys.reshape(rows, heads, width)
    head_value = values.reshape(rows, heads, width)
    position = lax.axis_index("seq")
    cum_decay = jnp.cumsum(logdecay, axis=0)
    block_decay = cum_decay[-1]
    table = decay_lookup_grid(cum_decay)
    rise = jnp.exp(cum_decay)[:, :, None]
    fall = jnp.exp(block_decay[None, :] - cum_decay)[:, :, None]
    value_wide = head_value.astype(jnp.float32)
    key_wide = head_key.astype(jnp.float32)
    scaled_query = head_query.astype(jnp.float32) * rise
    own_state = exact("thd,the->hde", key_wide * fall, value_wide)
    totals_all, states_all = (
        lax.all_gather(block_decay[None].astype(jnp.bfloat16), "seq", axis=0, tiled=True).astype(
            jnp.float32
        ),
        lax.all_gather(own_state[None].astype(jnp.bfloat16), "seq", axis=0, tiled=True).astype(
            jnp.float32
        ),
    )
    incoming = exact("ch,chde->hde", earlier_weights(totals_all, position), states_all)
    probs = (narrow("thd,shd->hts", head_query, head_key) * table).astype(jnp.bfloat16)
    attention = narrow("hts,she->the", probs, head_value) + exact(
        "thd,hde->the", scaled_query, incoming
    )
    normed = head_norm(attention).astype(jnp.bfloat16).reshape(rows, heads * width)
    term = jnp.dot(normed, out_weight, preferred_element_type=jnp.float32)
    attn_out = lax.psum_scatter(term.astype(jnp.bfloat16), "head", scatter_dimension=1, tiled=True)
    grad_normed = lax.dot_general(
        lax.all_gather(output_gradient, "head", axis=1, tiled=True),
        out_weight,
        (((1,), (1,)), ((), ())),
        preferred_element_type=jnp.float32,
    )
    _, pullback = jax.vjp(head_norm, attention)
    grad_head = pullback(grad_normed.reshape(rows, heads, width))[0].astype(jnp.bfloat16)
    grad_wide = grad_head.astype(jnp.float32)
    own_grad = exact("thd,the->hde", scaled_query, grad_wide)
    grads_all = lax.all_gather(
        own_grad[None].astype(jnp.bfloat16), "seq", axis=0, tiled=True
    ).astype(jnp.float32)
    outgoing = exact("ch,chde->hde", later_weights(totals_all, position), grads_all)
    grad_scores = (narrow("the,she->hts", grad_head, head_value) * table).astype(jnp.bfloat16)
    query_gradient_rows = narrow("hts,shd->thd", grad_scores, head_key) + rise * exact(
        "the,hde->thd", grad_wide, incoming
    )
    grad_key = narrow("hts,thd->shd", grad_scores, head_query) + fall * exact(
        "the,hde->thd", value_wide, outgoing
    )
    grad_value = narrow("hts,the->she", probs, grad_head) + fall * exact(
        "thd,hde->the", key_wide, outgoing
    )
    flat = (rows, heads * width)
    return (
        attn_out,
        query_gradient_rows.astype(jnp.bfloat16).reshape(flat),
        grad_key.astype(jnp.bfloat16).reshape(flat),
        grad_value.astype(jnp.bfloat16).reshape(flat),
    )


def solution(mesh):
    return jax.shard_map(
        body,
        mesh=mesh,
        in_specs=(
            P("seq", "head"),
            P("seq", "head"),
            P("seq", "head"),
            P("seq", "head"),
            P("head", None),
            P("seq", "head"),
        ),
        out_specs=(P("seq", "head"), P("seq", "head"), P("seq", "head"), P("seq", "head")),
        check_vma=False,
    )
```

profile of v0, /device:TPU:0, one launch (start us, length us, event | category | flops | bytes accessed | tf_op | source)
XLA Modules:
  0.0 277.8 jit_solution(8615897591845083256)
XLA Ops:
  7.2 0.0 all-gather.7.cloned.1.call-start
  7.2 0.7 all-gather.7.cloned.1.call-update
  7.9 0.0 all-gather.9.cloned.1.call-start
  8.0 2.2 reduce-window.6
  10.2 0.2 slice_reduce_fusion
  10.4 0.5 copy.75
  10.9 0.1 fusion.32
  11.0 0.2 slice_reduce_fusion.1
  11.2 0.1 subtract_exponential_fusion
  11.3 2.0 fusion.14
  13.3 0.0 all-gather.9.cloned.1.call-update
  13.3 0.0 all-gather.11.cloned.1.call-start
  13.4 0.2 fusion.31
  13.5 22.8 %all-gather.2 = bf16[32,1,8]{2,1,0:T(2,128)(2,1)S(1)} all-gather(bf16[1,1,8]{2,1,0:T(2,128)(2,1)S(1)} %bitcast.125), channel_id=1, replica_groups=mesh['seq'=32,'head'=4] {'seq'}, dimensions={0}, use_global_device_ids=true | all-gather | bytes 528 | tf_op jit(solution)/shard_map/all_gather | solution.py:65
  36.4 0.1 reduce_window_sum.37
  36.4 0.1 select_reduce_fusion
  36.5 0.1 exponential_bitcast_fusion
  36.6 0.1 copy.96
  36.7 1.5 copy.74
  38.2 0.1 iota_compare_fusion
  38.3 0.1 add_bitcast_fusion.1
  38.4 2.5 multiply_convert_fusion.1
  40.8 2.0 copy-done.1
  42.8 2.8 %fusion.18 = f32[8,512,128]{1,2,0:T(8,128)} fusion(bf16[8,512,512]{2,1,0:T(8,128)(2,1)S(1)} %multiply_convert_fusion.1, bf16[512,1024]{1,0:T(8,128)(2,1)S(1)} %copy-done), kind=kOutput, calls=%fused_computation.30 | convolution fusion | flops 536870912 | bytes 7340032 | tf_op jit(solution)/shard_map/hts,she->the/dot_general | solution.py:28
  45.6 32.2 %all-gather.7.cloned.1.call-done = bf16[512,6144]{1,0:T(8,128)(2,1)} async-done(((bf16[512,1536]{1,0:T(8,128)(2,1)}), bf16[512,6144]{1,0:T(8,128)(2,1)}) %all-gather.7.cloned.1.call-update) | async-done | bytes 6291472 | tf_op jit(solution)/shard_map/all_gather | solution.py:81
  77.9 12.5 %fusion.33 = f32[512,1024]{0,1:T(8,128)} fusion(bf16[512,6144]{1,0:T(8,128)(2,1)} %all-gather.7.cloned.1.call-done, bf16[1024,6144]{1,0:T(8,128)(2,1)} %param.10), kind=kOutput, calls=%fused_computation.62 | convolution fusion | flops 6442450944 | bytes 20971520 | tf_op jit(solution)/shard_map/dot_general | solution.py:80
  90.4 44.1 %all-gather.9.cloned.1.call-done = bf16[256,128,128]{2,1,0:T(8,128)(2,1)} async-done(((bf16[8,128,128]{2,1,0:T(8,128)(2,1)}), bf16[256,128,128]{2,1,0:T(8,128)(2,1)}) %all-gather.9.cloned.1.call-update) | async-done | bytes 8388624 | tf_op jit(solution)/shard_map/all_gather | solution.py:68
  134.4 11.8 %fusion = f32[8,1,128,128]{3,1,2,0:T(1,128)S(1)} fusion(f32[32,8,1,1]{0,2,3,1:T(1,128)S(1)} %copy.96, bf16[32,8,128,128]{3,2,1,0:T(8,128)(2,1)} %bitcast.107), kind=kOutput, calls=%fused_computation.2 | convolution fusion | flops 50331648 | bytes 8913920 | tf_op jit(solution)/shard_map/ch,chde->hde/dot_general | solution.py:24
  146.2 2.4 multiply_reduce_fusion.1
  148.7 1.7 fusion.2
  150.3 1.9 fusion.17
  152.2 0.0 all-gather.11.cloned.1.call-update
  152.3 0.0 reduce-scatter.2.cloned.1.call-start
  152.3 11.8 %convolution_convert_fusion = bf16[512,6144]{1,0:T(8,128)(2,1)} fusion(bf16[512,1024]{0,1:T(8,128)(2,1)} %bitcast.123, bf16[1024,6144]{1,0:T(8,128)(2,1)} %param.10), kind=kOutput, calls=%fused_computation.1 | convolution fusion | flops 6445596672 | bytes 19922944 | tf_op jit(solution)/shard_map/dot_general | solution.py:78
  164.1 2.9 %multiply_convert_fusion = bf16[8,512,512]{2,1,0:T(8,128)(2,1)S(1)} fusion(f32[8,512]{1,0:T(8,128)S(1)} %add_bitcast_fusion.1, pred[512,512]{1,0:T(8,128)(4,1)S(1)} %iota_compare_fusion, bf16[512,8,128]{0,2,1:T(8,128)(2,1)S(1)} %get-tuple-element.26, bf16[512,1024]{1,0:T(8,128)(2,1)S(1)} %copy-done), kind=kOutput, calls=%fused_computation.4 | convolution fusion | flops 545259520 | bytes 6569984 | tf_op jit(solution)/shard_map/the,she->hts/dot_general | solution.py:28
  167.1 1.5 fusion.34
  168.6 0.5 copy-done.2
  169.1 2.1 fusion.8
  171.2 2.3 copy.91
  173.5 4.4 %fusion.35 = f32[8,128,512]{2,1,0:T(8,128)} fusion(bf16[512,8,128]{0,2,1:T(8,128)(2,1)S(1)} %get-tuple-element.26, bf16[8,512,512]{2,1,0:T(8,128)(2,1)} %copy-done.1), kind=kOutput, calls=%fused_computation.64 | convolution fusion | flops 536870912 | bytes 7340032 | tf_op jit(solution)/shard_map/hts,the->she/dot_general | solution.py:28
  177.9 2.0 fusion.36
  180.0 25.0 %all-gather.11.cloned.1.call-done = bf16[256,128,128]{2,1,0:T(8,128)(2,1)} async-done(((bf16[8,128,128]{2,1,0:T(8,128)(2,1)}), bf16[256,128,128]{2,1,0:T(8,128)(2,1)}) %all-gather.11.cloned.1.call-update) | async-done | bytes 8388624 | tf_op jit(solution)/shard_map/all_gather | solution.py:90
  205.0 5.2 %multiply_reduce_fusion = f32[8,128,128]{2,1,0:T(8,128)S(1)} fusion(bf16[8,32,128,128]{3,2,0,1:T(8,128)(2,1)} %bitcast.116, f32[8,32]{0,1:T(8,128)S(1)} %get-tuple-element.28), kind=kLoop, calls=%fused_computation | loop fusion | flops 12451840 | bytes 8913920 | tf_op jit(solution)/shard_map/ch,chde->hde/dot_general | solution.py:24
  210.2 2.2 fusion.4
  212.4 2.4 copy.93
  214.8 3.1 %fusion.6 = bf16[512,8,128]{0,2,1:T(8,128)(2,1)} fusion(f32[8,512,128]{1,2,0:T(8,128)S(1)} %copy-done.7, f32[8,128,128]{2,1,0:T(8,128)} %copy-done.13, f32[512,8]{0,1:T(8,128)S(1)} %subtract_exponential_fusion, bf16[512,1024]{1,0:T(8,128)(2,1)S(1)} %copy-done), kind=kOutput, calls=%fused_computation.14 | convolution fusion | flops 806879232 | bytes 4734976 | tf_op jit(solution)/shard_map/the,hde->thd/dot_general | solution.py:24
  217.9 2.3 copy.92
  220.2 51.1 %reduce-scatter.2.cloned.1.call-done = bf16[512,1536]{1,0:T(8,128)(2,1)} async-done(((bf16[512,6144]{1,0:T(8,128)(2,1)}), bf16[512,1536]{1,0:T(8,128)(2,1)}) %reduce-scatter.2.cloned.1.call-update) | async-done | bytes 1572880 | tf_op jit(solution)/shard_map/reduce_scatter | solution.py:79
  (35 shorter events, 0.2 us)
Async XLA Ops:
  7.2 4.1 %copy-start = (bf16[512,1024]{1,0:T(8,128)(2,1)S(1)}, bf16[512,1024]{1,0:T(8,128)(2,1)}, u32[]{:S(2)}) copy-start(bf16[512,1024]{1,0:T(8,128)(2,1)} %param.8) | copy-start | bytes 3145732
  7.2 3.2 %copy-start.14 = (bf16[512,1024]{1,0:T(8,128)(2,1)S(1)}, bf16[512,1024]{1,0:T(8,128)(2,1)}, u32[]{:S(2)}) copy-start(bf16[512,1024]{1,0:T(8,128)(2,1)} %param.7) | copy-start | bytes 3145732
  7.2 70.7 %all-gather.7.cloned.1.call-start = ((), (), s32[]{:S(2)}) async-start(), calls=%async_computation.2 | async-start | bytes 7864320 | tf_op jit(solution)/shard_map/all_gather | solution.py:81
  7.9 126.5 %all-gather.9.cloned.1.call-start = ((), (), s32[]{:S(2)}) async-start(), calls=%async_computation.3 | async-start | bytes 8650752 | tf_op jit(solution)/shard_map/all_gather | solution.py:68
  10.9 27.4 %copy-start.4 = (bf16[512,1024]{0,1:T(8,128)(2,1)}, bf16[512,1024]{0,1:T(8,128)(2,1)S(1)}, u32[]{:S(2)}) copy-start(bf16[512,1024]{0,1:T(8,128)(2,1)S(1)} %copy.75) | copy-start | bytes 3145732
  13.3 191.6 %all-gather.11.cloned.1.call-start = ((), (), s32[]{:S(2)}) async-start(), calls=%async_computation.4 | async-start | bytes 8650752 | tf_op jit(solution)/shard_map/all_gather | solution.py:90
  40.8 2.0 copy-start.1
  134.4 11.8 %copy-start.9 = (f32[512,1024]{0,1:T(8,128)S(1)}, f32[512,1024]{0,1:T(8,128)}, u32[]{:S(2)}) copy-start(f32[512,1024]{0,1:T(8,128)} %fusion.33) | copy-start | bytes 6291460
  134.4 11.8 %copy-start.10 = (f32[8,512,128]{1,2,0:T(8,128)S(1)}, f32[8,512,128]{1,2,0:T(8,128)}, u32[]{:S(2)}) copy-start(f32[8,512,128]{1,2,0:T(8,128)} %fusion.18) | copy-start | bytes 6291460
  146.2 2.4 copy-start.11
  152.3 119.0 %reduce-scatter.2.cloned.1.call-start = ((), (), s32[]{:S(2)}) async-start(), calls=%async_computation.1 | async-start | bytes 7864320 | tf_op jit(solution)/shard_map/reduce_scatter | solution.py:79
  164.1 3.0 %copy-start.5 = (bf16[512,1024]{0,1:T(8,128)(2,1)S(1)}, bf16[512,1024]{0,1:T(8,128)(2,1)}, u32[]{:S(2)}) copy-start(bf16[512,1024]{0,1:T(8,128)(2,1)} %copy-done.4) | copy-start | bytes 3145732
  167.1 2.0 copy-start.2
  167.1 2.0 copy-start.12
  173.5 4.4 %copy-start.3 = (bf16[8,512,512]{2,1,0:T(8,128)(2,1)S(1)}, bf16[8,512,512]{2,1,0:T(8,128)(2,1)}, u32[]{:S(2)}) copy-start(bf16[8,512,512]{2,1,0:T(8,128)(2,1)} %copy-done.2) | copy-start | bytes 12582916
  204.9 5.3 %copy-start.6 = (bf16[512,1024]{0,1:T(8,128)(2,1)S(1)}, bf16[512,1024]{0,1:T(8,128)(2,1)}, u32[]{:S(2)}) copy-start(bf16[512,1024]{0,1:T(8,128)(2,1)} %copy-done.4) | copy-start | bytes 3145732
  205.0 5.3 %copy-start.8 = (f32[8,128,512]{2,1,0:T(8,128)S(1)}, f32[8,128,512]{2,1,0:T(8,128)}, u32[]{:S(2)}) copy-start(f32[8,128,512]{2,1,0:T(8,128)} %fusion.35) | copy-start | bytes 6291460
  210.2 2.2 copy-start.13
  212.4 2.4 copy-start.7
Sparse Core Ops, SparseCore 0:
  9.7 68.1 all-gather.6
  80.7 53.6 all-gather.8
  152.4 52.5 all-gather.10
  207.8 63.4 reduce-scatter.1
where the time goes:
time: 279 us; the launch traced here: 278 us
  waiting for transfers between devices  153 us (55%)
  matrix products  65.9 us (24%)
  blocking collectives  22.8 us (8%)
  between operations  14 us (5%)
  local copies, waits for them, and re-layouts  12.1 us (4%)
  other arithmetic  9.75 us (3%)
    reduce_scatter x1, waiting for transfers between devices, body(): lax.psum_scatter(term.astype(jnp.bfloat16), 'head', scatter_dimension=1,...  51.1 us
    all_gather x1, waiting for transfers between devices, body(): lax.all_gather(own_state[None].astype(jnp.bfloat16), 'seq', axis=0, tiled...  44.1 us
    all_gather x1, waiting for transfers between devices, body(): lax.all_gather(output_gradient, 'head', axis=1, tiled=True)  32.2 us
    dot_general x7, matrix products, exact(): return jnp.einsum(form, left, right, precision=lax.Precision.HIGHEST)  25.4 us
    all_gather x1, waiting for transfers between devices, body(): lax.all_gather(own_grad[None].astype(jnp.bfloat16), 'seq', axis=0, tiled=...  25 us
    all_gather x1, blocking collectives, body(): lax.all_gather(block_decay[None].astype(jnp.bfloat16), 'seq', axis=0, til...  22.8 us
    dot_general x6, matrix products, narrow(): return jnp.einsum(form, left, right, preferred_element_type=jnp.float32)  16.1 us
    dot_general x1, matrix products, body(): lax.dot_general(lax.all_gather(output_gradient, 'head', axis=1, tiled=Tru...  12.5 us
  transfers between devices with their start and end apart: 4, of which 4 were waited for; matrix products, arithmetic and copies ran while one was open for 24% of the time, Pallas kernels for 0%

commit v1 on v0

v1 whole, which is shorter than its diff:
```python
import functools

import jax
import jax.numpy as jnp
from jax import lax
from jax.experimental import pallas as pl
from jax.experimental.pallas import tpu as pltpu
from jax.sharding import PartitionSpec as P

EPS = 1e-05
F32 = jnp.float32
BF16 = jnp.bfloat16
MIB = 1024 * 1024

NN = (((1,), (0,)), ((), ()))
NT = (((1,), (1,)), ((), ()))
TN = (((0,), (0,)), ((), ()))


def dot(left, right, form=NN):
    return lax.dot_general(left, right, form, preferred_element_type=F32)


def call(kernel, grid, in_specs, out_specs, out_shape, scratch=(), flops=0, moved=0, name=None):
    return pl.pallas_call(
        kernel,
        out_shape=out_shape,
        grid_spec=pltpu.PrefetchScalarGridSpec(
            num_scalar_prefetch=1,
            grid=grid,
            in_specs=in_specs,
            out_specs=out_specs,
            scratch_shapes=list(scratch),
        ),
        compiler_params=pltpu.CompilerParams(vmem_limit_bytes=40 * MIB),
        cost_estimate=pl.CostEstimate(flops=flops, bytes_accessed=moved, transcendentals=0),
        name=name,
    )


def whole(shape):
    return pl.BlockSpec(shape, lambda *_: (0,) * len(shape))


def three_terms(x):
    high = x.astype(BF16)
    rest = x - high.astype(F32)
    middle = rest.astype(BF16)
    low = (rest - middle.astype(F32)).astype(BF16)
    return high, middle, low


def column(table, head):
    lane = lax.broadcasted_iota(jnp.int32, table.shape, 1)
    return jnp.sum(jnp.where(lane == head, table, 0.0), axis=1, keepdims=True)


def pack_decays(decays):
    high, middle, low = three_terms(decays)
    rows = [t.astype(F32) for t in (high, middle, low)]
    return jnp.concatenate(rows + [jnp.zeros_like(decays)], axis=0).astype(BF16)


def message_decays(ref):
    rows = ref[512:528, :].astype(F32)
    return rows[0:4] + rows[4:8] + rows[8:12]


def state_kernel(s_ref, ld_ref, km_ref, vm_ref, kp_ref, vp_ref, cum_ref, cumt_ref, mine_ref, send_ref):
    j = pl.program_id(0)
    core = s_ref[0]

    @pl.when(j == 0)
    def _():
        rows = lax.broadcasted_iota(jnp.int32, (512, 512), 0)
        cols = lax.broadcasted_iota(jnp.int32, (512, 512), 1)
        tri = jnp.where(rows >= cols, 1.0, 0.0).astype(BF16)
        total = jnp.zeros((512, 8), F32)
        total_t = jnp.zeros((8, 512), F32)
        for term in three_terms(ld_ref[...])[::-1]:
            total = total + dot(tri, term)
            total_t = total_t + lax.dot_general(
                term, tri, (((0,), (1,)), ((), ())), preferred_element_type=F32
            )
        cum_ref[...] = total
        cumt_ref[...] = total_t

    cum = cum_ref[...]
    for group, k_ref, v_ref, out_ref in ((core, km_ref, vm_ref, mine_ref), (1 - core, kp_ref, vp_ref, send_ref)):
        along = column(cum, group * 4 + j)
        last = along[511:512, :]
        faded = (k_ref[...].astype(F32) * jnp.exp(last - along)).astype(BF16)
        out_ref[pl.ds(pl.multiple_of(j * 128, 128), 128), :] = dot(faded, v_ref[...], TN).astype(BF16)

        @pl.when(j == 0)
        def _():
            decays = jnp.concatenate(
                [jnp.broadcast_to(column(cum[504:512, :], group * 4 + i)[7:8, :], (1, 128)) for i in range(4)],
                axis=0,
            )
            out_ref[512:528, :] = pack_decays(decays)


def own_states(scalars, logdecay, keys, values):
    mine = pl.BlockSpec((512, 128), lambda j, s: (0, s[0] * 4 + j))
    other = pl.BlockSpec((512, 128), lambda j, s: (0, (1 - s[0]) * 4 + j))
    return call(
        state_kernel,
        (4,),
        [whole((512, 8)), mine, mine, other, other],
        [whole((512, 8)), whole((8, 512)), whole((528, 128)), whole((528, 128))],
        [
            jax.ShapeDtypeStruct((512, 8), F32),
            jax.ShapeDtypeStruct((8, 512), F32),
            jax.ShapeDtypeStruct((528, 128), BF16),
            jax.ShapeDtypeStruct((528, 128), BF16),
        ],
        flops=2 * 8 * 512 * 128 * 128,
        moved=3 * MIB,
        name="own_states",
    )(scalars, logdecay, keys, values, keys, values)


def chip_kernel(s_ref, mine_ref, got_ref, out_ref):
    first = s_ref[0] == 0
    d_mine, d_got = message_decays(mine_ref), message_decays(got_ref)
    w_mine = jnp.where(first, jnp.exp(d_got), 1.0)
    w_got = jnp.where(first, 1.0, jnp.exp(d_mine))
    for i in range(4):
        rows = slice(i * 128, i * 128 + 128)
        out_ref[rows, :] = (
            w_mine[i : i + 1] * mine_ref[rows, :].astype(F32) + w_got[i : i + 1] * got_ref[rows, :].astype(F32)
        ).astype(BF16)
    out_ref[512:528, :] = pack_decays(d_mine + d_got)


def chip_total(scalars, mine, got):
    return call(
        chip_kernel,
        (1,),
        [whole((528, 128))] * 2,
        whole((528, 128)),
        jax.ShapeDtypeStruct((528, 128), BF16),
        flops=MIB,
        moved=400 * 1024,
        name="chip_total",
    )(scalars, mine, got)


def prefix_weights(place, decays):
    weights, between = [], jnp.zeros_like(decays[0])
    before = jnp.zeros_like(decays[0])
    for k in range(1, 4):
        weights.append(jnp.where(place >= k, jnp.exp(between), 0.0))
        between = between + decays[k]
        before = before + jnp.where(place >= k, decays[k], 0.0)
    return weights, before


def row_kernel(s_ref, m0, m1, m2, m3, total_ref, prefix_ref, before_ref):
    place = s_ref[1]
    refs = (m0, m1, m2, m3)
    decays = [message_decays(r) for r in refs]
    weights, before = prefix_weights(place, decays)
    places = [lax.rem(place - k + 4, 4) for k in range(4)]
    totals = []
    for k in range(4):
        after = jnp.zeros_like(before)
        for m in range(4):
            if m != k:
                after = after + jnp.where(places[m] > places[k], decays[m], 0.0)
        totals.append(jnp.exp(after))
    for i in range(4):
        rows = slice(i * 128, i * 128 + 128)
        values = [r[rows, :].astype(F32) for r in refs]
        prefix_ref[rows, :] = sum(weights[k - 1][i : i + 1] * values[k] for k in range(1, 4))
        total_ref[rows, :] = sum(totals[k][i : i + 1] * values[k] for k in range(4)).astype(BF16)
    total_ref[512:528, :] = pack_decays(decays[0] + decays[1] + decays[2] + decays[3])
    before_ref[...] = jnp.concatenate([before, before], axis=0)


def row_total(scalars, messages):
    return call(
        row_kernel,
        (1,),
        [whole((528, 128))] * 4,
        [whole((528, 128)), whole((512, 128)), whole((8, 128))],
        [
            jax.ShapeDtypeStruct((528, 128), BF16),
            jax.ShapeDtypeStruct((512, 128), F32),
            jax.ShapeDtypeStruct((8, 128), F32),
        ],
        flops=MIB,
        moved=900 * 1024,
        name="row_total",
    )(scalars, *messages)


def arrive_kernel(s_ref, m1, m2, m3, prefix_ref, before_ref, mine_ref, got_ref, keep_ref, send_ref):
    place = s_ref[2]
    first = s_ref[0] == 0
    refs = (None, m1, m2, m3)
    decays = [None] + [message_decays(r) for r in refs[1:]]
    decays[0] = jnp.zeros_like(decays[1])
    weights, _ = prefix_weights(place, decays)
    fade = jnp.exp(before_ref[0:4, :])
    d_first = jnp.where(first, message_decays(mine_ref), message_decays(got_ref))
    w_first = jnp.exp(d_first)
    for i in range(4):
        rows = slice(i * 128, i * 128 + 128)
        earlier = sum(weights[k - 1][i : i + 1] * refs[k][rows, :].astype(F32) for k in range(1, 4))
        at_first = fade[i : i + 1] * earlier + prefix_ref[rows, :]
        state_first = jnp.where(first, mine_ref[rows, :].astype(F32), got_ref[rows, :].astype(F32))
        at_second = w_first[i : i + 1] * at_first + state_first
        keep_ref[rows, :] = jnp.where(first, at_first, at_second).astype(BF16)
        send_ref[rows, :] = jnp.where(first, at_second, at_first).astype(BF16)


def arrive(scalars, messages, prefix, before, mine, got):
    return call(
        arrive_kernel,
        (1,),
        [whole((528, 128))] * 3 + [whole((512, 128)), whole((8, 128)), whole((528, 128)), whole((528, 128))],
        [whole((512, 128))] * 2,
        [jax.ShapeDtypeStruct((512, 128), BF16)] * 2,
        flops=MIB,
        moved=1100 * 1024,
        name="arrive",
    )(scalars, *messages, prefix, before, mine, got)


SWAP = [(i, i ^ 1) for i in range(32)]


def shifts_x(k):
    return [(i, i // 8 * 8 + (i // 2 + k) % 4 * 2 + i % 2) for i in range(32)]


def shifts_z(k):
    return [(i, i + 8 * k) for i in range(32) if 0 <= i + 8 * k < 32]


def scan_blocks(scalars, mine, send, sign):
    got = lax.ppermute(send, "seq", SWAP)
    chip = chip_total(scalars, mine, got)
    row = [chip] + [lax.ppermute(chip, "seq", shifts_x(sign * k)) for k in (1, 2, 3)]
    total, prefix, before = row_total(scalars, row)
    planes = [lax.ppermute(total, "seq", shifts_z(sign * k)) for k in (1, 2, 3)]
    keep, send_back = arrive(scalars, planes, prefix, before, mine, got)
    return keep, lax.ppermute(send_back, "seq", SWAP)


def decay_block(along, along_t, low, high, cols):
    diff = along[low:high, :] - along_t[:, :cols]
    rows_at = lax.broadcasted_iota(jnp.int32, diff.shape, 0) + low
    cols_at = lax.broadcasted_iota(jnp.int32, diff.shape, 1)
    return jnp.exp(jnp.where(rows_at >= cols_at, diff, -1e30))


def head_of(s_ref):
    return lax.rem(pl.program_id(0) + 4 * s_ref[0], 8)


def forward_kernel(s_ref, cum_ref, cumt_ref, q_ref, k_ref, v_ref, keep_ref, got_ref, normed_ref, att_ref):
    head = head_of(s_ref)
    along = column(cum_ref[...], head)
    along_t = cumt_ref[pl.ds(head, 1), :]
    incoming = jnp.where(pl.program_id(0) < 4, keep_ref[...], got_ref[...])
    for low in (0, 256):
        high = low + 256
        q = q_ref[low:high, :]
        table = decay_block(along, along_t, low, high, high)
        probs = (dot(q, k_ref[:high, :], NT) * table).astype(BF16)
        att = dot(probs, v_ref[:high, :]) + jnp.exp(along[low:high, :]) * dot(q, incoming)
        att_ref[low:high, :] = att
        scale = lax.rsqrt(jnp.mean(att * att, axis=1, keepdims=True) + EPS)
        normed_ref[low:high, :] = (att * scale).astype(BF16)


def head_spec(rows=512):
    return pl.BlockSpec((rows, 128), lambda i, s: (0, lax.rem(i + 4 * s[0], 8)))


def state_specs():
    return [
        pl.BlockSpec((128, 128), lambda i, s: (jnp.minimum(i, 3), 0)),
        pl.BlockSpec((128, 128), lambda i, s: (jnp.maximum(i - 4, 0), 0)),
    ]


def forward(scalars, cum, cum_t, q, k, v, keep, got):
    return call(
        forward_kernel,
        (8,),
        [whole((512, 8)), whole((8, 512))] + [head_spec()] * 3 + state_specs(),
        [head_spec()] * 2,
        [jax.ShapeDtypeStruct((512, 1024), BF16), jax.ShapeDtypeStruct((512, 1024), F32)],
        flops=8 * 6 * 512 * 512 * 128,
        moved=6 * MIB,
        name="forward",
    )(scalars, cum, cum_t, q, k, v, keep, got)


def project_kernel(s_ref, x_ref, w_ref, *refs):
    out_ref = refs[-1]
    total = dot(x_ref[...], w_ref[...])
    for r in refs[:-1]:
        total = total + r[...].astype(F32)
    out_ref[...] = total.astype(BF16)


def project(scalars, slot, normed, half, weight, adds=()):
    rows = 512 if half is None else 256
    start = half or 0
    tile = 512
    part = pl.BlockSpec((rows, tile), lambda n, s: (0, n))
    return call(
        project_kernel,
        (1536 // tile,),
        [
            pl.BlockSpec((rows, 1024), lambda n, s: (start, 0)),
            pl.BlockSpec((1024, tile), lambda n, s: (0, s[slot] * (1536 // tile) + n)),
        ]
        + [part] * len(adds),
        part,
        jax.ShapeDtypeStruct((rows, 1536), BF16),
        flops=2 * rows * 1024 * 1536,
        moved=5 * MIB,
        name="project",
    )(scalars, normed, weight, *adds)


def grad_own_kernel(s_ref, x_ref, w_ref, out_ref):
    out_ref[...] = dot(x_ref[...], w_ref[...], NT)


def grad_own(scalars, x, weight):
    return call(
        grad_own_kernel,
        (4,),
        [whole((512, 1536)), pl.BlockSpec((256, 1536), lambda n, s: (n, s[3]))],
        pl.BlockSpec((512, 256), lambda n, s: (0, n)),
        jax.ShapeDtypeStruct((512, 1024), F32),
        flops=2 * 512 * 1024 * 1536,
        moved=7 * MIB,
        name="grad_own",
    )(scalars, x, weight)


def grad_near_kernel(s_ref, alo, ahi, blo, bhi, wa_ref, wb_ref, acc_ref, out_ref):
    wa, wb = wa_ref[...], wb_ref[...]
    out_ref[:256, :] = acc_ref[:256, :] + dot(alo[...], wa, NT) + dot(blo[...], wb, NT)
    out_ref[256:, :] = acc_ref[256:, :] + dot(ahi[...], wa, NT) + dot(bhi[...], wb, NT)


def grad_near(scalars, pieces, weight, acc):
    tile = pl.BlockSpec((512, 256), lambda n, s: (0, n))
    return call(
        grad_near_kernel,
        (4,),
        [whole((256, 1536))] * 4
        + [
            pl.BlockSpec((256, 1536), lambda n, s: (n, s[4])),
            pl.BlockSpec((256, 1536), lambda n, s: (n, s[5])),
            tile,
        ],
        tile,
        jax.ShapeDtypeStruct((512, 1024), F32),
        flops=4 * 512 * 1024 * 1536,
        moved=12 * MIB,
        name="grad_near",
    )(scalars, *pieces, weight, weight, acc)


def grad_far_kernel(s_ref, c_ref, d_ref, w_ref, acc_ref, att_ref, q_ref, cum_ref, grad_ref, mine_ref, send_ref):
    n = pl.program_id(0)
    w = w_ref[...]
    core = s_ref[6]
    acc = jnp.concatenate([acc_ref[:256, :] + dot(c_ref[...], w, NT), acc_ref[256:, :] + dot(d_ref[...], w, NT)], axis=0)
    cum = cum_ref[...]
    for i in range(2):
        cols = slice(i * 128, i * 128 + 128)
        head = n * 2 + i
        att, grad = att_ref[:, cols], acc[:, cols]
        scale = lax.rsqrt(jnp.mean(att * att, axis=1, keepdims=True) + EPS)
        unit = att * scale
        out = (scale * (grad - unit * jnp.mean(grad * unit, axis=1, keepdims=True))).astype(BF16)
        grad_ref[:, cols] = out
        along = column(cum, head)
        scaled = (q_ref[:, cols].astype(F32) * jnp.exp(along)).astype(BF16)
        state = dot(scaled, out, TN).astype(BF16)
        decay = pl.ds(pl.multiple_of(lax.rem(head, 4) * 128, 128), 128)
        here = lax.div(head, 4) == core

        @pl.when(here)
        def _():
            mine_ref[decay, :] = state

        @pl.when(jnp.logical_not(here))
        def _():
            send_ref[decay, :] = state

    @pl.when(n == 0)
    def _():
        for group, out_ref in ((core, mine_ref), (1 - core, send_ref)):
            decays = jnp.concatenate(
                [jnp.broadcast_to(column(cum[504:512, :], group * 4 + i)[7:8, :], (1, 128)) for i in range(4)],
                axis=0,
            )
            out_ref[512:528, :] = pack_decays(decays)


def grad_far(scalars, c, d, weight, acc, att, q, cum):
    tile = pl.BlockSpec((512, 256), lambda n, s: (0, n))
    return call(
        grad_far_kernel,
        (4,),
        [whole((256, 1536))] * 2
        + [pl.BlockSpec((256, 1536), lambda n, s: (n, s[7])), tile, tile, tile, whole((512, 8))],
        [tile, whole((528, 128)), whole((528, 128))],
        [
            jax.ShapeDtypeStruct((512, 1024), BF16),
            jax.ShapeDtypeStruct((528, 128), BF16),
            jax.ShapeDtypeStruct((528, 128), BF16),
        ],
        flops=2 * 512 * 1024 * 1536,
        moved=11 * MIB,
        name="grad_far",
    )(scalars, c, d, weight, acc, att, q, cum)


def inside_kernel(s_ref, cum_ref, cumt_ref, q_ref, k_ref, v_ref, g_ref, keep_ref, got_ref, gq_ref, gk_ref, gv_ref):
    head = head_of(s_ref)
    along = column(cum_ref[...], head)
    along_t = cumt_ref[pl.ds(head, 1), :]
    incoming = jnp.where(pl.program_id(0) < 4, keep_ref[...], got_ref[...])
    gk, gv = [None, None], [None, None]
    for low in (0, 256):
        high = low + 256
        q, g = q_ref[low:high, :], g_ref[low:high, :]
        k, v = k_ref[:high, :], v_ref[:high, :]
        table = decay_block(along, along_t, low, high, high)
        probs = (dot(q, k, NT) * table).astype(BF16)
        scores = (dot(g, v, NT) * table).astype(BF16)
        gq = dot(scores, k) + jnp.exp(along[low:high, :]) * dot(g, incoming, NT)
        gq_ref[low:high, :] = gq.astype(BF16)
        if low == 0:
            gk[0], gv[0] = dot(scores, q, TN), dot(probs, g, TN)
        else:
            more_k, more_v = dot(scores, q, TN), dot(probs, g, TN)
            gk_ref[:256, :] = gk[0] + more_k[:256]
            gk_ref[256:, :] = more_k[256:]
            gv_ref[:256, :] = gv[0] + more_v[:256]
            gv_ref[256:, :] = more_v[256:]


def inside(scalars, cum, cum_t, q, k, v, grad, keep, got):
    return call(
        inside_kernel,
        (8,),
        [whole((512, 8)), whole((8, 512))] + [head_spec()] * 4 + state_specs(),
        [head_spec()] * 3,
        [
            jax.ShapeDtypeStruct((512, 1024), BF16),
            jax.ShapeDtypeStruct((512, 1024), F32),
            jax.ShapeDtypeStruct((512, 1024), F32),
        ],
        flops=8 * 12 * 512 * 512 * 128,
        moved=10 * MIB,
        name="inside",
    )(scalars, cum, cum_t, q, k, v, grad, keep, got)


def finish_kernel(s_ref, cum_ref, k_ref, v_ref, gk_ref, gv_ref, keep_ref, got_ref, gk_out, gv_out):
    along = column(cum_ref[...], head_of(s_ref))
    fall = jnp.exp(along[511:512, :] - along)
    outgoing = jnp.where(pl.program_id(0) < 4, keep_ref[...], got_ref[...])
    gk_out[...] = (gk_ref[...] + fall * dot(v_ref[...], outgoing, NT)).astype(BF16)
    gv_out[...] = (gv_ref[...] + fall * dot(k_ref[...], outgoing)).astype(BF16)


def finish(scalars, cum, k, v, gk, gv, keep, got):
    return call(
        finish_kernel,
        (8,),
        [whole((512, 8))] + [head_spec()] * 4 + state_specs(),
        [head_spec()] * 2,
        [jax.ShapeDtypeStruct((512, 1024), BF16)] * 2,
        flops=8 * 4 * 512 * 128 * 128,
        moved=8 * MIB,
        name="finish",
    )(scalars, cum, k, v, gk, gv, keep, got)


RIGHT = [(i, (i + 1) % 4) for i in range(4)]
LEFT = [(i, (i + 3) % 4) for i in range(4)]


def body(queries, keys, values, logdecay, out_weight, output_gradient):
    at = lax.axis_index("seq").astype(jnp.int32)
    h = lax.axis_index("head").astype(jnp.int32)
    core, x, z = at % 2, at // 2 % 4, at // 8
    blocks = [h, (h + 3) % 4, (h + 1) % 4]
    scalars = jnp.stack([core, x, z] + blocks + [core, (h + 2) % 4]).astype(jnp.int32)
    back = jnp.stack([1 - core, 3 - x, 3 - z] + blocks + [core, (h + 2) % 4]).astype(jnp.int32)

    right = lambda a: lax.ppermute(a, "head", RIGHT)
    left = lambda a: lax.ppermute(a, "head", LEFT)

    lo, hi = output_gradient[:256], output_gradient[256:]
    a_lo, b_hi = right(lo), left(hi)
    a_hi, b_lo = right(hi), left(lo)
    c_lo, d_hi = right(a_lo), left(b_hi)

    cum, cum_t, mine, send = own_states(scalars, logdecay, keys, values)
    acc = grad_own(scalars, output_gradient, out_weight)
    keep, got = scan_blocks(scalars, mine, send, 1)
    normed, att = forward(scalars, cum, cum_t, queries, keys, values, keep, got)

    acc = grad_near(scalars, (a_lo, a_hi, b_lo, b_hi), out_weight, acc)
    grad, mine_g, send_g = grad_far(scalars, c_lo, d_hi, out_weight, acc, att, queries, cum)
    keep_g, got_g = scan_blocks(back, mine_g, send_g, -1)
    gq, gk, gv = inside(scalars, cum, cum_t, queries, keys, values, grad, keep, got)
    gk, gv = finish(scalars, cum, keys, values, gk, gv, keep_g, got_g)

    from_left = right(project(scalars, 7, normed, 0, out_weight))
    from_right = left(project(scalars, 7, normed, 1, out_weight))
    direct_r = right(project(scalars, 5, normed, 1, out_weight))
    direct_l = left(project(scalars, 4, normed, 0, out_weight))
    joined_r = right(project(scalars, 5, normed, 0, out_weight, (from_left,)))
    joined_l = left(project(scalars, 4, normed, 1, out_weight, (from_right,)))
    top = project(scalars, 3, normed, 0, out_weight, (joined_r, direct_l))
    bottom = project(scalars, 3, normed, 1, out_weight, (direct_r, joined_l))
    return jnp.concatenate([top, bottom], axis=0), gq, gk, gv


def solution(mesh):
    return jax.shard_map(
        body,
        mesh=mesh,
        in_specs=(
            P("seq", "head"),
            P("seq", "head"),
            P("seq", "head"),
            P("seq", "head"),
            P("head", None),
            P("seq", "head"),
        ),
        out_specs=(P("seq", "head"), P("seq", "head"), P("seq", "head"), P("seq", "head")),
        check_vma=False,
    )
```

time: 279 us -> 175 us (0.63)
  waiting for transfers between devices: 153 us -> 27.5 us
  Pallas kernels: 0 us -> 81.4 us
  matrix products: 65.9 us -> 0 us
  starting transfers between devices: 0.16 us -> 44.8 us
  blocking collectives: 22.8 us -> 0 us
  between operations: 14 us -> 1.03 us
  other arithmetic: 9.75 us -> 1.25 us
  local copies, waits for them, and re-layouts: 12.1 us -> 16.9 us
    all_gather x3 -> x0, waiting for transfers between devices: 101 us -> none  [the longest x1 44.1 us: body(): lax.all_gather(own_state[None].astype(jnp.bfloat16), 'seq', axis=0, tiled...]
    pallas_call x0 -> x21, Pallas kernels: none -> 81.4 us  [the longest x8 27.2 us: project(): call(project_kernel, (1536 // tile,), [pl.BlockSpec((rows, 1024), lambda...]
    dot_general x15 -> x0, matrix products: 65.9 us -> none  [the longest x7 25.4 us: exact(): return jnp.einsum(form, left, right, precision=lax.Precision.HIGHEST)]
    reduce_scatter x1 -> x0, waiting for transfers between devices: 51.1 us -> none  [body(): lax.psum_scatter(term.astype(jnp.bfloat16), 'head', scatter_dimension=1,...]
    ppermute x0 -> x28, starting transfers between devices: none -> 44.8 us  [the longest x6 17 us: scan_blocks(): planes = [lax.ppermute(total, 'seq', shifts_z(sign * k)) for k in (1, 2, 3)]]
    ppermute x0 -> x28, waiting for transfers between devices: none -> 27.5 us  [the longest x6 15.9 us: scan_blocks(): planes = [lax.ppermute(total, 'seq', shifts_z(sign * k)) for k in (1, 2, 3)]]
    all_gather x1 -> x0, blocking collectives: 22.8 us -> none  [body(): lax.all_gather(block_decay[None].astype(jnp.bfloat16), 'seq', axis=0, til...]
    dot_general x1 -> x0, other arithmetic: 5.25 us -> none  [exact(): return jnp.einsum(form, left, right, precision=lax.Precision.HIGHEST)]
  transfers between devices with their start and end apart: 4 -> 28, of which waited for: 4 -> 8; matrix products, arithmetic and copies ran while one was open for 24% -> 1% of each run, Pallas kernels for 0% -> 44%
where the time goes in v1:
time: 175 us; the launch traced here: 173 us
  Pallas kernels  81.4 us (47%)
  starting transfers between devices  44.8 us (26%)
  waiting for transfers between devices  27.5 us (16%)
  local copies, waits for them, and re-layouts  16.9 us (10%)
    pallas_call x8, Pallas kernels, project(): call(project_kernel, (1536 // tile,), [pl.BlockSpec((rows, 1024), lambda...  27.2 us
    ppermute x6, starting transfers between devices, scan_blocks(): planes = [lax.ppermute(total, 'seq', shifts_z(sign * k)) for k in (1, 2, 3)]  17 us
    ppermute x6, waiting for transfers between devices, scan_blocks(): planes = [lax.ppermute(total, 'seq', shifts_z(sign * k)) for k in (1, 2, 3)]  15.9 us
    unnamed x31, local copies, waits for them, and re-layouts  14 us
    ppermute x6, starting transfers between devices, body(): left = lambda a: lax.ppermute(a, 'head', LEFT)  12.8 us
    pallas_call x1, Pallas kernels, inside(): call(inside_kernel, (8,), [whole((512, 8)), whole((8, 512))] + [head_spec...  10.4 us
    ppermute x6, waiting for transfers between devices, scan_blocks(): lax.ppermute(chip, 'seq', shifts_x(sign * k))  10.2 us
    ppermute x6, starting transfers between devices, scan_blocks(): lax.ppermute(chip, 'seq', shifts_x(sign * k))  9.95 us
  transfers between devices with their start and end apart: 28, of which 8 were waited for; matrix products, arithmetic and copies ran while one was open for 1% of the time, Pallas kernels for 44%

profile of v1, /device:TPU:0, one launch (start us, length us, event | category | flops | bytes accessed | tf_op | source)
XLA Modules:
  0.0 172.8 jit_solution(10513147206504673815)
XLA Ops:
  0.7 2.8 %fusion = (bf16[256,1536]{1,0:T(8,128)(2,1)}, bf16[256,1536]{1,0:T(8,128)(2,1)}) fusion(bf16[512,1536]{1,0:T(8,128)(2,1)} %x_ref.1), kind=kLoop, calls=%fused_computation.1 | loop fusion | bytes 3145728 | tf_op jit(solution)/shard_map/slice | solution.py:510
  3.4 1.7 collective-permute-start.14
  5.1 1.6 collective-permute-start.16
  7.6 0.9 copy-done.8
  8.5 5.2 %own_states.1 = (f32[512,8]{1,0:T(8,128)S(1)}, f32[8,512]{1,0:T(8,128)S(1)}, bf16[528,128]{1,0:T(8,128)(2,1)S(1)}, bf16[528,128]{1,0:T(8,128)(2,1)S(1)}) custom-call(s32[8]{0:T(128)S(1)} %stack.49.s_ref, f32[512,8]{1,0:T(8,128)S(1)} %copy-done.8, bf16[512,1024]{1,0:T(8,128)(2,1)S(1)} %copy-done.2, bf16[512,1024]{1,0:T(8,128)(2,1)S(1)} %copy-done.3, ...), custom_call_target="tpu_custom_call" | custom-call | flops 134217728 | bytes 3145728 | tf_op jit(solution)/shard_map/own_states/pallas_call | solution.py:107
  13.9 1.3 collective-permute-done.got_ref
  15.8 1.6 collective-permute-start.1
  17.5 2.7 %collective-permute-start.2 = (bf16[528,128]{1,0:T(8,128)(2,1)S(1)}, bf16[528,128]{1,0:T(8,128)(2,1)S(1)}, u32[]{:S(2)}, u32[]{:S(2)}) collective-permute-start(bf16[528,128]{1,0:T(8,128)(2,1)S(1)} %chip_total.2.m0), channel_id=1, source_target_pairs={{0,16},{4,20},{8,24},{12,28},{16,0},{20,4},{24,8},{28,12},{32,48},... | collective-permute-start | bytes 405512 | tf_op jit(solution)/shard_map/ppermute | solution.py:246
  20.2 1.4 collective-permute-start.3
  21.7 1.1 collective-permute-done.1.m1
  23.2 3.5 %collective-permute-done.2.m2 = bf16[528,128]{1,0:T(8,128)(2,1)S(1)} collective-permute-done((bf16[528,128]{1,0:T(8,128)(2,1)S(1)}, bf16[528,128]{1,0:T(8,128)(2,1)S(1)}, u32[]{:S(2)}, u32[]{:S(2)}) %collective-permute-start.2) | collective-permute-done | bytes 135200 | tf_op jit(solution)/shard_map/ppermute | solution.py:246
  27.5 3.8 %collective-permute-start.4 = (bf16[528,128]{1,0:T(8,128)(2,1)S(1)}, bf16[528,128]{1,0:T(8,128)(2,1)S(1)}, u32[]{:S(2)}, u32[]{:S(2)}) collective-permute-start(bf16[528,128]{1,0:T(8,128)(2,1)S(1)} %get-tuple-element.32), channel_id=1, source_target_pairs={{0,32},{4,36},{8,40},{12,44},{16,48},{20,52},{24,56},{28,60},{32,6... | collective-permute-start | bytes 405512 | tf_op jit(solution)/shard_map/ppermute | solution.py:248
  31.3 5.5 %collective-permute-start.5 = (bf16[528,128]{1,0:T(8,128)(2,1)S(1)}, bf16[528,128]{1,0:T(8,128)(2,1)S(1)}, u32[]{:S(2)}, u32[]{:S(2)}) collective-permute-start(bf16[528,128]{1,0:T(8,128)(2,1)S(1)} %get-tuple-element.32), channel_id=1, source_target_pairs={{0,64},{4,68},{8,72},{12,76},{16,80},{20,84},{24,88},{28,92},{32,9... | collective-permute-start | bytes 405512 | tf_op jit(solution)/shard_map/ppermute | solution.py:248
  36.8 1.9 %collective-permute-start.19 = (bf16[256,1536]{1,0:T(8,128)(2,1)}, bf16[256,1536]{1,0:T(8,128)(2,1)}, u32[]{:S(2)}, u32[]{:S(2)}) collective-permute-start(bf16[256,1536]{1,0:T(8,128)(2,1)} %get-tuple-element.53), channel_id=1, source_target_pairs={{0,3},{1,0},{2,1},{3,2},{4,7},{5,4},{6,5},{7,6},{8,11},{9,8},{10,9... | collective-permute-start | bytes 2359304 | tf_op jit(solution)/shard_map/ppermute | solution.py:508
  39.3 3.8 %collective-permute-start.6 = (bf16[528,128]{1,0:T(8,128)(2,1)S(1)}, bf16[528,128]{1,0:T(8,128)(2,1)S(1)}, u32[]{:S(2)}, u32[]{:S(2)}) collective-permute-start(bf16[528,128]{1,0:T(8,128)(2,1)S(1)} %get-tuple-element.32), channel_id=1, source_target_pairs={{0,96},{4,100},{8,104},{12,108},{16,112},{20,116},{24,120},{28,124... | collective-permute-start | bytes 405512 | tf_op jit(solution)/shard_map/ppermute | solution.py:248
  43.1 2.5 %collective-permute-done.6.m3 = bf16[528,128]{1,0:T(8,128)(2,1)S(1)} collective-permute-done((bf16[528,128]{1,0:T(8,128)(2,1)S(1)}, bf16[528,128]{1,0:T(8,128)(2,1)S(1)}, u32[]{:S(2)}, u32[]{:S(2)}) %collective-permute-start.6) | collective-permute-done | bytes 135200 | tf_op jit(solution)/shard_map/ppermute | solution.py:248
  45.7 1.4 arrive.2
  47.4 2.9 %collective-permute-start.17 = (bf16[256,1536]{1,0:T(8,128)(2,1)}, bf16[256,1536]{1,0:T(8,128)(2,1)}, u32[]{:S(2)}, u32[]{:S(2)}) collective-permute-start(bf16[256,1536]{1,0:T(8,128)(2,1)} %collective-permute-done.16.bhi), channel_id=1, source_target_pairs={{0,3},{1,0},{2,1},{3,2},{4,7},{5,4},{6,5},{7,6},{8,11},{9,8},{10,9... | collective-permute-start | bytes 2359304 | tf_op jit(solution)/shard_map/ppermute | solution.py:508
  51.1 8.1 %forward.1 = (bf16[512,1024]{1,0:T(8,128)(2,1)S(1)}, f32[512,1024]{1,0:T(8,128)S(1)}) custom-call(s32[8]{0:T(128)S(1)} %stack.49.s_ref, f32[512,8]{1,0:T(8,128)S(1)} %get-tuple-element.28.cum_ref, f32[8,512]{1,0:T(8,128)S(1)} %copy-done.12, bf16[512,1024]{1,0:T(8,128)(2,1)S(1)} %copy-done.7, bf16[512,1024]{1,0:T(8,128)(2,1)S(1)} %copy-done.2, ...), custom_call_target="tpu_custom_call" | custom-call | flops 1610612736 | bytes 6291456 | tf_op jit(solution)/shard_map/forward/pallas_call | solution.py:292
  59.2 1.3 copy-done.5
  60.5 4.6 %copy-done = bf16[1024,6144]{1,0:T(8,128)(2,1)S(1)} copy-done((bf16[1024,6144]{1,0:T(8,128)(2,1)S(1)}, bf16[1024,6144]{1,0:T(8,128)(2,1)}, u32[]{:S(2)}) %copy-start) | copy-done | bytes 12582936
  65.1 3.0 %project.8 = bf16[256,1536]{1,0:T(8,128)(2,1)} custom-call(s32[8]{0:T(128)S(1)} %stack.49.s_ref, bf16[512,1024]{1,0:T(8,128)(2,1)S(1)} %get-tuple-element.37.x_ref, bf16[1024,6144]{1,0:T(8,128)(2,1)S(1)} %copy-done), custom_call_target="tpu_custom_call" | custom-call | flops 805306368 | bytes 5242880 | tf_op jit(solution)/shard_map/project/pallas_call | solution.py:317
  68.1 3.0 %project.13 = bf16[256,1536]{1,0:T(8,128)(2,1)} custom-call(s32[8]{0:T(128)S(1)} %stack.49.s_ref, bf16[512,1024]{1,0:T(8,128)(2,1)S(1)} %get-tuple-element.37.x_ref, bf16[1024,6144]{1,0:T(8,128)(2,1)S(1)} %copy-done), custom_call_target="tpu_custom_call" | custom-call | flops 805306368 | bytes 5242880 | tf_op jit(solution)/shard_map/project/pallas_call | solution.py:317
  71.1 3.2 %collective-permute-start.12 = (bf16[256,1536]{1,0:T(8,128)(2,1)}, bf16[256,1536]{1,0:T(8,128)(2,1)S(1)}, u32[]{:S(2)}, u32[]{:S(2)}) collective-permute-start(bf16[256,1536]{1,0:T(8,128)(2,1)} %project.13), channel_id=1, source_target_pairs={{0,3},{1,0},{2,1},{3,2},{4,7},{5,4},{6,5},{7,6},{8,11},{9,8},{10,9... | collective-permute-start | bytes 2359304 | tf_op jit(solution)/shard_map/ppermute | solution.py:508
  74.4 4.8 %grad_own.1.acc_ref = f32[512,1024]{1,0:T(8,128)S(1)} custom-call(s32[8]{0:T(128)S(1)} %stack.49.s_ref, bf16[512,1536]{1,0:T(8,128)(2,1)S(1)} %copy-done.4, bf16[1024,6144]{1,0:T(8,128)(2,1)} %w_ref.19), custom_call_target="tpu_custom_call" | custom-call | flops 1610612736 | bytes 7340032 | tf_op jit(solution)/shard_map/grad_own/pallas_call | solution.py:338
  79.2 7.6 %grad_near.1.acc_ref = f32[512,1024]{1,0:T(8,128)S(1)} custom-call(s32[8]{0:T(128)S(1)} %stack.49.s_ref, bf16[256,1536]{1,0:T(8,128)(2,1)} %collective-permute-done.14.alo, bf16[256,1536]{1,0:T(8,128)(2,1)} %collective-permute-done.18.ahi, bf16[256,1536]{1,0:T(8,128)(2,1)} %collective-permute-done.19.blo, bf16[256,1536]{1,0:T(8,128)(2,1)} %collective-permute-done.16.bhi, ...), custom_call_target="tpu_custom_call" | custom-call | flops 3221225472 | bytes 12582912 | tf_op jit(solution)/shard_map/grad_near/pallas_call | solution.py:358
  86.9 8.0 %grad_far.1 = (bf16[512,1024]{1,0:T(8,128)(2,1)S(1)}, bf16[528,128]{1,0:T(8,128)(2,1)S(1)}, bf16[528,128]{1,0:T(8,128)(2,1)S(1)}) custom-call(s32[8]{0:T(128)S(1)} %stack.49.s_ref, bf16[256,1536]{1,0:T(8,128)(2,1)} %collective-permute-done.15.c_ref, bf16[256,1536]{1,0:T(8,128)(2,1)} %collective-permute-done.17.d_ref, bf16[1024,6144]{1,0:T(8,128)(2,1)} %w_ref.19, ...), custom_call_target="tpu_custom_call" | custom-call | flops 1610612736 | bytes 11534336 | tf_op jit(solution)/shard_map/grad_far/pallas_call | solution.py:415
  94.9 1.0 copy-done.9
  95.9 4.6 %copy-done.1 = bf16[1024,6144]{1,0:T(8,128)(2,1)S(1)} copy-done((bf16[1024,6144]{1,0:T(8,128)(2,1)S(1)}, bf16[1024,6144]{1,0:T(8,128)(2,1)}, u32[]{:S(2)}) %copy-start.1) | copy-done | bytes 12582936
  100.4 3.1 %project.10 = bf16[256,1536]{1,0:T(8,128)(2,1)} custom-call(s32[8]{0:T(128)S(1)} %stack.49.s_ref, bf16[512,1024]{1,0:T(8,128)(2,1)S(1)} %get-tuple-element.37.x_ref, bf16[1024,6144]{1,0:T(8,128)(2,1)S(1)} %copy-done.1), custom_call_target="tpu_custom_call" | custom-call | flops 805306368 | bytes 5242880 | tf_op jit(solution)/shard_map/project/pallas_call | solution.py:317
  103.5 2.2 %project.12 = bf16[256,1536]{1,0:T(8,128)(2,1)S(1)} custom-call(s32[8]{0:T(128)S(1)} %stack.49.s_ref, bf16[512,1024]{1,0:T(8,128)(2,1)S(1)} %get-tuple-element.37.x_ref, bf16[1024,6144]{1,0:T(8,128)(2,1)S(1)} %copy-done.1), custom_call_target="tpu_custom_call" | custom-call | flops 805306368 | bytes 5242880 | tf_op jit(solution)/shard_map/project/pallas_call | solution.py:317
  105.7 2.3 %collective-permute-start.11 = (bf16[256,1536]{1,0:T(8,128)(2,1)S(1)}, bf16[256,1536]{1,0:T(8,128)(2,1)S(1)}, u32[]{:S(2)}, u32[]{:S(2)}) collective-permute-start(bf16[256,1536]{1,0:T(8,128)(2,1)S(1)} %project.12), channel_id=1, source_target_pairs={{0,1},{1,2},{2,3},{3,0},{4,5},{5,6},{6,7},{7,4},{8,9},{9,10},{10,1... | collective-permute-start | bytes 2359304 | tf_op jit(solution)/shard_map/ppermute | solution.py:507
  108.6 2.3 %collective-permute-start.21 = (bf16[528,128]{1,0:T(8,128)(2,1)S(1)}, bf16[528,128]{1,0:T(8,128)(2,1)S(1)}, u32[]{:S(2)}, u32[]{:S(2)}) collective-permute-start(bf16[528,128]{1,0:T(8,128)(2,1)S(1)} %chip_total.3.m0), channel_id=1, source_target_pairs={{0,24},{4,28},{8,0},{12,4},{16,8},{20,12},{24,16},{28,20},{32,56},... | collective-permute-start | bytes 405512 | tf_op jit(solution)/shard_map/ppermute | solution.py:246
  110.9 1.2 collective-permute-start.22
  112.1 3.9 %project.9 = bf16[256,1536]{1,0:T(8,128)(2,1)S(1)} custom-call(s32[8]{0:T(128)S(1)} %stack.49.s_ref, bf16[512,1024]{1,0:T(8,128)(2,1)S(1)} %get-tuple-element.37.x_ref, bf16[1024,6144]{1,0:T(8,128)(2,1)} %w_ref.19, bf16[256,1536]{1,0:T(8,128)(2,1)S(1)} %collective-permute-done.8.refs_0_), custom_call_target="tpu_custom_call" | custom-call | flops 805306368 | bytes 5242880 | tf_op jit(solution)/shard_map/project/pallas_call | solution.py:317
  116.2 3.9 %project.14 = bf16[256,1536]{1,0:T(8,128)(2,1)S(1)} custom-call(s32[8]{0:T(128)S(1)} %stack.49.s_ref, bf16[512,1024]{1,0:T(8,128)(2,1)S(1)} %get-tuple-element.37.x_ref, bf16[1024,6144]{1,0:T(8,128)(2,1)} %w_ref.19, bf16[256,1536]{1,0:T(8,128)(2,1)S(1)} %collective-permute-done.12.refs_0_), custom_call_target="tpu_custom_call" | custom-call | flops 805306368 | bytes 5242880 | tf_op jit(solution)/shard_map/project/pallas_call | solution.py:317
  120.1 3.3 %collective-permute-start.13 = (bf16[256,1536]{1,0:T(8,128)(2,1)S(1)}, bf16[256,1536]{1,0:T(8,128)(2,1)S(1)}, u32[]{:S(2)}, u32[]{:S(2)}) collective-permute-start(bf16[256,1536]{1,0:T(8,128)(2,1)S(1)} %project.14), channel_id=1, source_target_pairs={{0,3},{1,0},{2,1},{3,2},{4,7},{5,4},{6,5},{7,6},{8,11},{9,8},{10,9... | collective-permute-start | bytes 2359304 | tf_op jit(solution)/shard_map/ppermute | solution.py:508
  124.1 5.5 %collective-permute-done.23.m3 = bf16[528,128]{1,0:T(8,128)(2,1)S(1)} collective-permute-done((bf16[528,128]{1,0:T(8,128)(2,1)S(1)}, bf16[528,128]{1,0:T(8,128)(2,1)S(1)}, u32[]{:S(2)}, u32[]{:S(2)}) %collective-permute-start.23) | collective-permute-done | bytes 135200 | tf_op jit(solution)/shard_map/ppermute | solution.py:246
  130.4 1.3 collective-permute-start.24
  131.7 5.6 %collective-permute-done.24.m1 = bf16[528,128]{1,0:T(8,128)(2,1)S(1)} collective-permute-done((bf16[528,128]{1,0:T(8,128)(2,1)S(1)}, bf16[528,128]{1,0:T(8,128)(2,1)S(1)}, u32[]{:S(2)}, u32[]{:S(2)}) %collective-permute-start.24) | collective-permute-done | bytes 135200 | tf_op jit(solution)/shard_map/ppermute | solution.py:248
  137.3 1.3 collective-permute-start.25
  138.6 7.1 %collective-permute-done.25.m2 = bf16[528,128]{1,0:T(8,128)(2,1)S(1)} collective-permute-done((bf16[528,128]{1,0:T(8,128)(2,1)S(1)}, bf16[528,128]{1,0:T(8,128)(2,1)S(1)}, u32[]{:S(2)}, u32[]{:S(2)}) %collective-permute-start.25) | collective-permute-done | bytes 135200 | tf_op jit(solution)/shard_map/ppermute | solution.py:248
  145.7 1.3 collective-permute-start.26
  147.0 10.4 %inside.1 = (bf16[512,1024]{1,0:T(8,128)(2,1)}, f32[512,1024]{1,0:T(8,128)S(1)}, f32[512,1024]{1,0:T(8,128)S(1)}) custom-call(s32[8]{0:T(128)S(1)} %stack.49.s_ref, f32[512,8]{1,0:T(8,128)S(1)} %get-tuple-element.28.cum_ref, f32[8,512]{1,0:T(8,128)S(1)} %copy-done.13, bf16[512,1024]{1,0:T(8,128)(2,1)S(1)} %copy-done.7, bf16[512,1024]{1,0:T(8,128)(2,1)S(1)} %copy-done.2, ...), custom_call_target="tpu_custom_call" | custom-call | flops 3221225472 | bytes 10485760 | tf_op jit(solution)/shard_map/inside/pallas_call | solution.py:458
  158.2 4.0 %project.11 = bf16[256,1536]{1,0:T(8,128)(2,1)S(1)} custom-call(s32[8]{0:T(128)S(1)} %stack.49.s_ref, bf16[512,1024]{1,0:T(8,128)(2,1)S(1)} %get-tuple-element.37.x_ref, bf16[1024,6144]{1,0:T(8,128)(2,1)} %w_ref.19, bf16[256,1536]{1,0:T(8,128)(2,1)S(1)} %collective-permute-done.9.refs_0_, bf16[256,1536]{1,0:T(8,128)(2,1)S(1)} %collective-permute-done.10.refs_1_), custom_call_target="tpu_custom_call" | custom-call | flops 805306368 | bytes 5242880 | tf_op jit(solution)/shard_map/project/pallas_call | solution.py:317
  162.2 4.0 %project.15 = bf16[256,1536]{1,0:T(8,128)(2,1)S(1)} custom-call(s32[8]{0:T(128)S(1)} %stack.49.s_ref, bf16[512,1024]{1,0:T(8,128)(2,1)S(1)} %get-tuple-element.37.x_ref, bf16[1024,6144]{1,0:T(8,128)(2,1)} %w_ref.19, bf16[256,1536]{1,0:T(8,128)(2,1)S(1)} %collective-permute-done.11.refs_0_, bf16[256,1536]{1,0:T(8,128)(2,1)S(1)} %collective-permute-done.13.refs_1_), custom_call_target="tpu_custom_call" | custom-call | flops 805306368 | bytes 5242880 | tf_op jit(solution)/shard_map/project/pallas_call | solution.py:317
  166.2 1.2 pad_maximum_fusion
  167.5 5.4 %finish.1 = (bf16[512,1024]{1,0:T(8,128)(2,1)}, bf16[512,1024]{1,0:T(8,128)(2,1)}) custom-call(s32[8]{0:T(128)S(1)} %stack.49.s_ref, f32[512,8]{1,0:T(8,128)S(1)} %get-tuple-element.28.cum_ref, bf16[512,1024]{1,0:T(8,128)(2,1)S(1)} %copy-done.2, bf16[512,1024]{1,0:T(8,128)(2,1)S(1)} %copy-done.3, f32[512,1024]{1,0:T(8,128)S(1)} %get-tuple-element.41.gk_ref, ...), custom_call_target="tpu_custom_call" | custom-call | flops 268435456 | bytes 8388608 | tf_op jit(solution)/shard_map/finish/pallas_call | solution.py:483
  (64 shorter events, 7.6 us)
Async XLA Ops:
  0.6 6.0 %copy-start.14 = (f32[512,8]{0,1:T(8,128)S(1)}, f32[512,8]{0,1:T(8,128)}, u32[]{:S(2)}) copy-start(f32[512,8]{0,1:T(8,128)} %param.9) | copy-start | bytes 49156
  0.6 6.9 %copy-start.2 = (bf16[512,1024]{1,0:T(8,128)(2,1)S(1)}, bf16[512,1024]{1,0:T(8,128)(2,1)}, u32[]{:S(2)}) copy-start(bf16[512,1024]{1,0:T(8,128)(2,1)} %k_ref.5) | copy-start | bytes 3145732
  0.7 6.9 %copy-start.3 = (bf16[512,1024]{1,0:T(8,128)(2,1)S(1)}, bf16[512,1024]{1,0:T(8,128)(2,1)}, u32[]{:S(2)}) copy-start(bf16[512,1024]{1,0:T(8,128)(2,1)} %v_ref.5) | copy-start | bytes 3145732
  3.4 43.6 %collective-permute-start.14 = (bf16[256,1536]{1,0:T(8,128)(2,1)}, bf16[256,1536]{1,0:T(8,128)(2,1)}, u32[]{:S(2)}, u32[]{:S(2)}) collective-permute-start(bf16[256,1536]{1,0:T(8,128)(2,1)} %get-tuple-element.53), channel_id=1, source_target_pairs={{0,1},{1,2},{2,3},{3,0},{4,5},{5,6},{6,7},{7,4},{8,9},{9,10},{10,1... | collective-permute-start | bytes 2359304 | tf_op jit(solution)/shard_map/ppermute | solution.py:507
  5.1 42.3 %collective-permute-start.16 = (bf16[256,1536]{1,0:T(8,128)(2,1)}, bf16[256,1536]{1,0:T(8,128)(2,1)}, u32[]{:S(2)}, u32[]{:S(2)}) collective-permute-start(bf16[256,1536]{1,0:T(8,128)(2,1)} %get-tuple-element.52), channel_id=1, source_target_pairs={{0,3},{1,0},{2,1},{3,2},{4,7},{5,4},{6,5},{7,6},{8,11},{9,8},{10,9... | collective-permute-start | bytes 2359304 | tf_op jit(solution)/shard_map/ppermute | solution.py:508
  7.6 1.0 copy-start.8
  8.5 41.8 %copy-start.7 = (bf16[512,1024]{1,0:T(8,128)(2,1)S(1)}, bf16[512,1024]{1,0:T(8,128)(2,1)}, u32[]{:S(2)}) copy-start(bf16[512,1024]{1,0:T(8,128)(2,1)} %q_ref.5) | copy-start | bytes 3145732
  13.8 3.7 %copy-start.11 = (f32[8,512]{1,0:T(8,128)}, f32[8,512]{1,0:T(8,128)S(1)}, u32[]{:S(2)}) copy-start(f32[8,512]{1,0:T(8,128)S(1)} %get-tuple-element.29.cumt_ref) | copy-start | bytes 49156
  13.8 1.4 collective-permute-start
  15.8 6.9 %collective-permute-start.1 = (bf16[528,128]{1,0:T(8,128)(2,1)S(1)}, bf16[528,128]{1,0:T(8,128)(2,1)S(1)}, u32[]{:S(2)}, u32[]{:S(2)}) collective-permute-start(bf16[528,128]{1,0:T(8,128)(2,1)S(1)} %chip_total.2.m0), channel_id=1, source_target_pairs={{0,8},{4,12},{8,16},{12,20},{16,24},{20,28},{24,0},{28,4},{32,40},... | collective-permute-start | bytes 405512 | tf_op jit(solution)/shard_map/ppermute | solution.py:246
  17.5 9.2 %collective-permute-start.2 = (bf16[528,128]{1,0:T(8,128)(2,1)S(1)}, bf16[528,128]{1,0:T(8,128)(2,1)S(1)}, u32[]{:S(2)}, u32[]{:S(2)}) collective-permute-start(bf16[528,128]{1,0:T(8,128)(2,1)S(1)} %chip_total.2.m0), channel_id=1, source_target_pairs={{0,16},{4,20},{8,24},{12,28},{16,0},{20,4},{24,8},{28,12},{32,48},... | collective-permute-start | bytes 405512 | tf_op jit(solution)/shard_map/ppermute | solution.py:246
  20.2 6.5 %collective-permute-start.3 = (bf16[528,128]{1,0:T(8,128)(2,1)S(1)}, bf16[528,128]{1,0:T(8,128)(2,1)S(1)}, u32[]{:S(2)}, u32[]{:S(2)}) collective-permute-start(bf16[528,128]{1,0:T(8,128)(2,1)S(1)} %chip_total.2.m0), channel_id=1, source_target_pairs={{0,24},{4,28},{8,0},{12,4},{16,8},{20,12},{24,16},{28,20},{32,56},... | collective-permute-start | bytes 405512 | tf_op jit(solution)/shard_map/ppermute | solution.py:246
  22.8 48.4 %collective-permute-start.18 = (bf16[256,1536]{1,0:T(8,128)(2,1)}, bf16[256,1536]{1,0:T(8,128)(2,1)}, u32[]{:S(2)}, u32[]{:S(2)}) collective-permute-start(bf16[256,1536]{1,0:T(8,128)(2,1)} %get-tuple-element.52), channel_id=1, source_target_pairs={{0,1},{1,2},{2,3},{3,0},{4,5},{5,6},{6,7},{7,4},{8,9},{9,10},{10,1... | collective-permute-start | bytes 2359304 | tf_op jit(solution)/shard_map/ppermute | solution.py:507
  27.5 9.3 %collective-permute-start.4 = (bf16[528,128]{1,0:T(8,128)(2,1)S(1)}, bf16[528,128]{1,0:T(8,128)(2,1)S(1)}, u32[]{:S(2)}, u32[]{:S(2)}) collective-permute-start(bf16[528,128]{1,0:T(8,128)(2,1)S(1)} %get-tuple-element.32), channel_id=1, source_target_pairs={{0,32},{4,36},{8,40},{12,44},{16,48},{20,52},{24,56},{28,60},{32,6... | collective-permute-start | bytes 405512 | tf_op jit(solution)/shard_map/ppermute | solution.py:248
  31.3 8.0 %collective-permute-start.5 = (bf16[528,128]{1,0:T(8,128)(2,1)S(1)}, bf16[528,128]{1,0:T(8,128)(2,1)S(1)}, u32[]{:S(2)}, u32[]{:S(2)}) collective-permute-start(bf16[528,128]{1,0:T(8,128)(2,1)S(1)} %get-tuple-element.32), channel_id=1, source_target_pairs={{0,64},{4,68},{8,72},{12,76},{16,80},{20,84},{24,88},{28,92},{32,9... | collective-permute-start | bytes 405512 | tf_op jit(solution)/shard_map/ppermute | solution.py:248
  36.8 42.4 %collective-permute-start.19 = (bf16[256,1536]{1,0:T(8,128)(2,1)}, bf16[256,1536]{1,0:T(8,128)(2,1)}, u32[]{:S(2)}, u32[]{:S(2)}) collective-permute-start(bf16[256,1536]{1,0:T(8,128)(2,1)} %get-tuple-element.53), channel_id=1, source_target_pairs={{0,3},{1,0},{2,1},{3,2},{4,7},{5,4},{6,5},{7,6},{8,11},{9,8},{10,9... | collective-permute-start | bytes 2359304 | tf_op jit(solution)/shard_map/ppermute | solution.py:508
  39.3 6.3 %collective-permute-start.6 = (bf16[528,128]{1,0:T(8,128)(2,1)S(1)}, bf16[528,128]{1,0:T(8,128)(2,1)S(1)}, u32[]{:S(2)}, u32[]{:S(2)}) collective-permute-start(bf16[528,128]{1,0:T(8,128)(2,1)S(1)} %get-tuple-element.32), channel_id=1, source_target_pairs={{0,96},{4,100},{8,104},{12,108},{16,112},{20,116},{24,120},{28,124... | collective-permute-start | bytes 405512 | tf_op jit(solution)/shard_map/ppermute | solution.py:248
  47.0 3.3 %collective-permute-start.7 = (bf16[512,128]{1,0:T(8,128)(2,1)}, bf16[512,128]{1,0:T(8,128)(2,1)}, u32[]{:S(2)}, u32[]{:S(2)}) collective-permute-start(bf16[512,128]{1,0:T(8,128)(2,1)} %get-tuple-element.36), channel_id=1, source_target_pairs={{0,4},{4,0},{8,12},{12,8},{16,20},{20,16},{24,28},{28,24},{32,36},... | collective-permute-start | bytes 393224 | tf_op jit(solution)/shard_map/ppermute | solution.py:250
  47.0 39.8 %collective-permute-start.15 = (bf16[256,1536]{1,0:T(8,128)(2,1)}, bf16[256,1536]{1,0:T(8,128)(2,1)}, u32[]{:S(2)}, u32[]{:S(2)}) collective-permute-start(bf16[256,1536]{1,0:T(8,128)(2,1)} %collective-permute-done.14.alo), channel_id=1, source_target_pairs={{0,1},{1,2},{2,3},{3,0},{4,5},{5,6},{6,7},{7,4},{8,9},{9,10},{10,1... | collective-permute-start | bytes 2359304 | tf_op jit(solution)/shard_map/ppermute | solution.py:507
  47.4 39.5 %collective-permute-start.17 = (bf16[256,1536]{1,0:T(8,128)(2,1)}, bf16[256,1536]{1,0:T(8,128)(2,1)}, u32[]{:S(2)}, u32[]{:S(2)}) collective-permute-start(bf16[256,1536]{1,0:T(8,128)(2,1)} %collective-permute-done.16.bhi), channel_id=1, source_target_pairs={{0,3},{1,0},{2,1},{3,2},{4,7},{5,4},{6,5},{7,6},{8,11},{9,8},{10,9... | collective-permute-start | bytes 2359304 | tf_op jit(solution)/shard_map/ppermute | solution.py:508
  50.4 0.7 copy-start.12
  59.1 1.3 copy-start.5
  60.5 4.6 %copy-start = (bf16[1024,6144]{1,0:T(8,128)(2,1)S(1)}, bf16[1024,6144]{1,0:T(8,128)(2,1)}, u32[]{:S(2)}) copy-start(bf16[1024,6144]{1,0:T(8,128)(2,1)} %w_ref.19) | copy-start | bytes 37748740
  68.1 6.3 %copy-start.4 = (bf16[512,1536]{1,0:T(8,128)(2,1)S(1)}, bf16[512,1536]{1,0:T(8,128)(2,1)}, u32[]{:S(2)}) copy-start(bf16[512,1536]{1,0:T(8,128)(2,1)} %x_ref.1) | copy-start | bytes 4718596
  68.1 42.8 %collective-permute-start.8 = (bf16[256,1536]{1,0:T(8,128)(2,1)}, bf16[256,1536]{1,0:T(8,128)(2,1)S(1)}, u32[]{:S(2)}, u32[]{:S(2)}) collective-permute-start(bf16[256,1536]{1,0:T(8,128)(2,1)} %project.8), channel_id=1, source_target_pairs={{0,1},{1,2},{2,3},{3,0},{4,5},{5,6},{6,7},{7,4},{8,9},{9,10},{10,1... | collective-permute-start | bytes 2359304 | tf_op jit(solution)/shard_map/ppermute | solution.py:507
  71.1 44.9 %collective-permute-start.12 = (bf16[256,1536]{1,0:T(8,128)(2,1)}, bf16[256,1536]{1,0:T(8,128)(2,1)S(1)}, u32[]{:S(2)}, u32[]{:S(2)}) collective-permute-start(bf16[256,1536]{1,0:T(8,128)(2,1)} %project.13), channel_id=1, source_target_pairs={{0,3},{1,0},{2,1},{3,2},{4,7},{5,4},{6,5},{7,6},{8,11},{9,8},{10,9... | collective-permute-start | bytes 2359304 | tf_op jit(solution)/shard_map/ppermute | solution.py:508
  79.2 7.7 %copy-start.6 = (f32[512,1024]{1,0:T(8,128)S(1)}, f32[512,1024]{1,0:T(8,128)}, u32[]{:S(2)}) copy-start(f32[512,1024]{1,0:T(8,128)} %copy-done.5) | copy-start | bytes 6291460
  94.9 1.0 copy-start.9
  95.8 12.2 %collective-permute-start.20 = (bf16[528,128]{1,0:T(8,128)(2,1)S(1)}, bf16[528,128]{1,0:T(8,128)(2,1)S(1)}, u32[]{:S(2)}, u32[]{:S(2)}) collective-permute-start(bf16[528,128]{1,0:T(8,128)(2,1)S(1)} %get-tuple-element.44), channel_id=1, source_target_pairs={{0,4},{4,0},{8,12},{12,8},{16,20},{20,16},{24,28},{28,24},{32,36},... | collective-permute-start | bytes 405512 | tf_op jit(solution)/shard_map/ppermute | solution.py:244
  95.9 4.6 %copy-start.1 = (bf16[1024,6144]{1,0:T(8,128)(2,1)S(1)}, bf16[1024,6144]{1,0:T(8,128)(2,1)}, u32[]{:S(2)}) copy-start(bf16[1024,6144]{1,0:T(8,128)(2,1)} %w_ref.19) | copy-start | bytes 37748740
  103.5 54.7 %collective-permute-start.10 = (bf16[256,1536]{1,0:T(8,128)(2,1)}, bf16[256,1536]{1,0:T(8,128)(2,1)S(1)}, u32[]{:S(2)}, u32[]{:S(2)}) collective-permute-start(bf16[256,1536]{1,0:T(8,128)(2,1)} %project.10), channel_id=1, source_target_pairs={{0,3},{1,0},{2,1},{3,2},{4,7},{5,4},{6,5},{7,6},{8,11},{9,8},{10,9... | collective-permute-start | bytes 2359304 | tf_op jit(solution)/shard_map/ppermute | solution.py:508
  105.7 56.5 %collective-permute-start.11 = (bf16[256,1536]{1,0:T(8,128)(2,1)S(1)}, bf16[256,1536]{1,0:T(8,128)(2,1)S(1)}, u32[]{:S(2)}, u32[]{:S(2)}) collective-permute-start(bf16[256,1536]{1,0:T(8,128)(2,1)S(1)} %project.12), channel_id=1, source_target_pairs={{0,1},{1,2},{2,3},{3,0},{4,5},{5,6},{6,7},{7,4},{8,9},{9,10},{10,1... | collective-permute-start | bytes 2359304 | tf_op jit(solution)/shard_map/ppermute | solution.py:507
  108.6 11.5 %collective-permute-start.21 = (bf16[528,128]{1,0:T(8,128)(2,1)S(1)}, bf16[528,128]{1,0:T(8,128)(2,1)S(1)}, u32[]{:S(2)}, u32[]{:S(2)}) collective-permute-start(bf16[528,128]{1,0:T(8,128)(2,1)S(1)} %chip_total.3.m0), channel_id=1, source_target_pairs={{0,24},{4,28},{8,0},{12,4},{16,8},{20,12},{24,16},{28,20},{32,56},... | collective-permute-start | bytes 405512 | tf_op jit(solution)/shard_map/ppermute | solution.py:246
  110.9 12.5 %collective-permute-start.22 = (bf16[528,128]{1,0:T(8,128)(2,1)S(1)}, bf16[528,128]{1,0:T(8,128)(2,1)S(1)}, u32[]{:S(2)}, u32[]{:S(2)}) collective-permute-start(bf16[528,128]{1,0:T(8,128)(2,1)S(1)} %chip_total.3.m0), channel_id=1, source_target_pairs={{0,16},{4,20},{8,24},{12,28},{16,0},{20,4},{24,8},{28,12},{32,48},... | collective-permute-start | bytes 405512 | tf_op jit(solution)/shard_map/ppermute | solution.py:246
  116.0 30.9 %copy-start.10 = (bf16[512,1024]{1,0:T(8,128)(2,1)S(1)}, bf16[512,1024]{1,0:T(8,128)(2,1)}, u32[]{:S(2)}) copy-start(bf16[512,1024]{1,0:T(8,128)(2,1)} %copy-done.9) | copy-start | bytes 3145732
  116.1 30.9 %copy-start.13 = (f32[8,512]{1,0:T(8,128)S(1)}, f32[8,512]{1,0:T(8,128)}, u32[]{:S(2)}) copy-start(f32[8,512]{1,0:T(8,128)} %copy-done.11) | copy-start | bytes 49156
  116.1 42.1 %collective-permute-start.9 = (bf16[256,1536]{1,0:T(8,128)(2,1)S(1)}, bf16[256,1536]{1,0:T(8,128)(2,1)S(1)}, u32[]{:S(2)}, u32[]{:S(2)}) collective-permute-start(bf16[256,1536]{1,0:T(8,128)(2,1)S(1)} %project.9), channel_id=1, source_target_pairs={{0,1},{1,2},{2,3},{3,0},{4,5},{5,6},{6,7},{7,4},{8,9},{9,10},{10,1... | collective-permute-start | bytes 2359304 | tf_op jit(solution)/shard_map/ppermute | solution.py:507
  120.1 42.1 %collective-permute-start.13 = (bf16[256,1536]{1,0:T(8,128)(2,1)S(1)}, bf16[256,1536]{1,0:T(8,128)(2,1)S(1)}, u32[]{:S(2)}, u32[]{:S(2)}) collective-permute-start(bf16[256,1536]{1,0:T(8,128)(2,1)S(1)} %project.14), channel_id=1, source_target_pairs={{0,3},{1,0},{2,1},{3,2},{4,7},{5,4},{6,5},{7,6},{8,11},{9,8},{10,9... | collective-permute-start | bytes 2359304 | tf_op jit(solution)/shard_map/ppermute | solution.py:508
  123.4 6.2 %collective-permute-start.23 = (bf16[528,128]{1,0:T(8,128)(2,1)S(1)}, bf16[528,128]{1,0:T(8,128)(2,1)S(1)}, u32[]{:S(2)}, u32[]{:S(2)}) collective-permute-start(bf16[528,128]{1,0:T(8,128)(2,1)S(1)} %chip_total.3.m0), channel_id=1, source_target_pairs={{0,8},{4,12},{8,16},{12,20},{16,24},{20,28},{24,0},{28,4},{32,40},... | collective-permute-start | bytes 405512 | tf_op jit(solution)/shard_map/ppermute | solution.py:246
  130.4 6.9 %collective-permute-start.24 = (bf16[528,128]{1,0:T(8,128)(2,1)S(1)}, bf16[528,128]{1,0:T(8,128)(2,1)S(1)}, u32[]{:S(2)}, u32[]{:S(2)}) collective-permute-start(bf16[528,128]{1,0:T(8,128)(2,1)S(1)} %get-tuple-element.45), channel_id=1, source_target_pairs={{32,0},{36,4},{40,8},{44,12},{48,16},{52,20},{56,24},{60,28},{64,3... | collective-permute-start | bytes 405512 | tf_op jit(solution)/shard_map/ppermute | solution.py:248
  137.3 8.4 %collective-permute-start.25 = (bf16[528,128]{1,0:T(8,128)(2,1)S(1)}, bf16[528,128]{1,0:T(8,128)(2,1)S(1)}, u32[]{:S(2)}, u32[]{:S(2)}) collective-permute-start(bf16[528,128]{1,0:T(8,128)(2,1)S(1)} %get-tuple-element.45), channel_id=1, source_target_pairs={{64,0},{68,4},{72,8},{76,12},{80,16},{84,20},{88,24},{92,28},{96,3... | collective-permute-start | bytes 405512 | tf_op jit(solution)/shard_map/ppermute | solution.py:248
  145.7 11.7 %collective-permute-start.26 = (bf16[528,128]{1,0:T(8,128)(2,1)S(1)}, bf16[528,128]{1,0:T(8,128)(2,1)S(1)}, u32[]{:S(2)}, u32[]{:S(2)}) collective-permute-start(bf16[528,128]{1,0:T(8,128)(2,1)S(1)} %get-tuple-element.45), channel_id=1, source_target_pairs={{96,0},{100,4},{104,8},{108,12},{112,16},{116,20},{120,24},{124,28... | collective-permute-start | bytes 405512 | tf_op jit(solution)/shard_map/ppermute | solution.py:248
  158.1 9.3 %collective-permute-start.27 = (bf16[512,128]{1,0:T(8,128)(2,1)S(1)}, bf16[512,128]{1,0:T(8,128)(2,1)S(1)}, u32[]{:S(2)}, u32[]{:S(2)}) collective-permute-start(bf16[512,128]{1,0:T(8,128)(2,1)S(1)} %get-tuple-element.49), channel_id=1, source_target_pairs={{0,4},{4,0},{8,12},{12,8},{16,20},{20,16},{24,28},{28,24},{32,36},... | collective-permute-start | bytes 393224 | tf_op jit(solution)/shard_map/ppermute | solution.py:250

commit v2 on v0

v2 whole, which is shorter than its diff:
```python
import functools

import jax
import jax.numpy as jnp
from jax import lax
from jax.experimental import pallas as pl
from jax.experimental.pallas import tpu as pltpu
from jax.sharding import PartitionSpec as P

EPS = 1e-05
F32 = jnp.float32
BF16 = jnp.bfloat16
MIB = 1024 * 1024

NN = (((1,), (0,)), ((), ()))
NT = (((1,), (1,)), ((), ()))
TN = (((0,), (0,)), ((), ()))


def dot(left, right, form=NN):
    return lax.dot_general(left, right, form, preferred_element_type=F32)


VMEM = pl.BlockSpec(memory_space=pltpu.VMEM)
SMEM = pl.BlockSpec(memory_space=pltpu.SMEM)
ANY = pl.BlockSpec(memory_space=pl.ANY)


def call(kernel, name, scalars, args, outs, after=(), flops=0):
    count, waits = len(args), len(after)

    def run(*refs):
        kernel(*refs[: 1 + count], *refs[1 + count + waits :])

    return pl.pallas_call(
        run,
        out_shape=[jax.ShapeDtypeStruct(shape, dtype) for shape, dtype in outs],
        in_specs=[SMEM] + [VMEM] * count + [ANY] * waits,
        out_specs=[VMEM] * len(outs),
        compiler_params=pltpu.CompilerParams(vmem_limit_bytes=12 * MIB),
        cost_estimate=pl.CostEstimate(flops=flops, bytes_accessed=0, transcendentals=0),
        name=name,
    )(scalars, *args, *after)


def three_terms(x):
    high = x.astype(BF16)
    rest = x - high.astype(F32)
    middle = rest.astype(BF16)
    low = (rest - middle.astype(F32)).astype(BF16)
    return high, middle, low


def head_columns(head):
    return slice(head * 128, head * 128 + 128)


def pack_decays(decays):
    high, middle, low = three_terms(decays)
    rows = [t.astype(F32) for t in (high, middle, low)]
    return jnp.concatenate(rows + [jnp.zeros_like(decays)], axis=0).astype(BF16)


def message_decays(ref):
    rows = ref[512:528, :].astype(F32)
    return rows[0:4] + rows[4:8] + rows[8:12]


MESSAGE = ((528, 128), BF16)
STATES = ((512, 128), BF16)


def put_state(core, head, state, mine_ref, send_ref):
    rows = slice(head % 4 * 128, head % 4 * 128 + 128)
    here = core == head // 4

    @pl.when(here)
    def _():
        mine_ref[rows, :] = state

    @pl.when(jnp.logical_not(here))
    def _():
        send_ref[rows, :] = state


def put_decays(core, cum_t, mine_ref, send_ref):
    last = jnp.broadcast_to(cum_t[:, 511:512], (8, 128))
    swap = core == 1
    mine_ref[512:528, :] = pack_decays(jnp.where(swap, last[4:8], last[0:4]))
    send_ref[512:528, :] = pack_decays(jnp.where(swap, last[0:4], last[4:8]))


def state_kernel(s_ref, ld_ref, k_ref, v_ref, cum_ref, cumt_ref, mine_ref, send_ref):
    core = s_ref[6]
    rows = lax.broadcasted_iota(jnp.int32, (512, 512), 0)
    cols = lax.broadcasted_iota(jnp.int32, (512, 512), 1)
    upper = jnp.where(rows <= cols, 1.0, 0.0).astype(BF16)
    lower = jnp.where(rows >= cols, 1.0, 0.0).astype(BF16)
    cum = jnp.zeros((512, 8), F32)
    cum_t = jnp.zeros((8, 512), F32)
    for term in three_terms(ld_ref[...])[::-1]:
        cum = cum + dot(lower, term, NT)
        cum_t = cum_t + dot(term, upper)
    cum_ref[...] = cum
    cumt_ref[...] = cum_t
    fall = jnp.exp(cum[511:512, :] - cum)
    for head in range(8):
        at = head_columns(head)
        faded = (k_ref[:, at].astype(F32) * fall[:, head : head + 1]).astype(BF16)
        put_state(core, head, dot(faded, v_ref[:, at], TN).astype(BF16), mine_ref, send_ref)
    put_decays(core, cum_t, mine_ref, send_ref)


def own_states(scalars, logdecay_t, keys, values):
    return call(
        state_kernel,
        "own_states",
        scalars,
        (logdecay_t, keys, values),
        [((512, 8), F32), ((8, 512), F32), MESSAGE, MESSAGE],
    )


def chip_kernel(base, s_ref, mine_ref, got_ref, out_ref):
    first = s_ref[base] == 0
    d_mine, d_got = message_decays(mine_ref), message_decays(got_ref)
    w_mine = jnp.where(first, jnp.exp(d_got), 1.0)
    w_got = jnp.where(first, 1.0, jnp.exp(d_mine))
    for i in range(4):
        rows = slice(i * 128, i * 128 + 128)
        out_ref[rows, :] = (
            w_mine[i : i + 1] * mine_ref[rows, :].astype(F32) + w_got[i : i + 1] * got_ref[rows, :].astype(F32)
        ).astype(BF16)
    out_ref[512:528, :] = pack_decays(d_mine + d_got)


def prefix_weights(place, decays):
    weights, between = [], jnp.zeros_like(decays[0])
    before = jnp.zeros_like(decays[0])
    for k in range(1, 4):
        weights.append(jnp.where(place >= k, jnp.exp(between), 0.0))
        between = between + decays[k]
        before = before + jnp.where(place >= k, decays[k], 0.0)
    return weights, before


def row_kernel(base, s_ref, m0, m1, m2, m3, total_ref, prefix_ref, before_ref):
    place = s_ref[base + 1]
    refs = (m0, m1, m2, m3)
    decays = [message_decays(r) for r in refs]
    weights, before = prefix_weights(place, decays)
    places = [lax.rem(place - k + 4, 4) for k in range(4)]
    totals = []
    for k in range(4):
        after = jnp.zeros_like(before)
        for m in range(4):
            if m != k:
                after = after + jnp.where(places[m] > places[k], decays[m], 0.0)
        totals.append(jnp.exp(after))
    for i in range(4):
        rows = slice(i * 128, i * 128 + 128)
        values = [r[rows, :].astype(F32) for r in refs]
        prefix_ref[rows, :] = sum(weights[k - 1][i : i + 1] * values[k] for k in range(1, 4))
        total_ref[rows, :] = sum(totals[k][i : i + 1] * values[k] for k in range(4)).astype(BF16)
    total_ref[512:528, :] = pack_decays(decays[0] + decays[1] + decays[2] + decays[3])
    before_ref[...] = jnp.concatenate([before, before], axis=0)


def arrive_kernel(base, s_ref, m1, m2, m3, prefix_ref, before_ref, mine_ref, got_ref, keep_ref, send_ref):
    place = s_ref[base + 2]
    first = s_ref[base] == 0
    refs = (None, m1, m2, m3)
    decays = [None] + [message_decays(r) for r in refs[1:]]
    decays[0] = jnp.zeros_like(decays[1])
    weights, _ = prefix_weights(place, decays)
    fade = jnp.exp(before_ref[0:4, :])
    d_first = jnp.where(first, message_decays(mine_ref), message_decays(got_ref))
    w_first = jnp.exp(d_first)
    for i in range(4):
        rows = slice(i * 128, i * 128 + 128)
        earlier = sum(weights[k - 1][i : i + 1] * refs[k][rows, :].astype(F32) for k in range(1, 4))
        at_first = fade[i : i + 1] * earlier + prefix_ref[rows, :]
        state_first = jnp.where(first, mine_ref[rows, :].astype(F32), got_ref[rows, :].astype(F32))
        at_second = w_first[i : i + 1] * at_first + state_first
        keep_ref[rows, :] = jnp.where(first, at_first, at_second).astype(BF16)
        send_ref[rows, :] = jnp.where(first, at_second, at_first).astype(BF16)


SWAP = [(i, i ^ 1) for i in range(32)]


def shifts_x(k):
    return [(i, i // 8 * 8 + (i // 2 + k) % 4 * 2 + i % 2) for i in range(32)]


def shifts_z(k):
    return [(i, i + 8 * k) for i in range(32) if 0 <= i + 8 * k < 32]


def scan_blocks(scalars, mine, send, sign, beside):
    base = 0 if sign > 0 else 8
    got = lax.ppermute(send, "seq", SWAP)
    (chip,) = call(functools.partial(chip_kernel, base), "chip_total", scalars, (mine, got), [MESSAGE])
    row = [chip] + [lax.ppermute(chip, "seq", shifts_x(sign * k)) for k in (1, 2, 3)]
    first = beside[0]((chip,))
    total, prefix, before = call(
        functools.partial(row_kernel, base),
        "row_total",
        scalars,
        row,
        [MESSAGE, ((512, 128), F32), ((8, 128), F32)],
        first[-1:],
    )
    planes = [lax.ppermute(total, "seq", shifts_z(sign * k)) for k in (1, 2, 3)]
    second = beside[1]((before,), first)
    keep, send_back = call(
        functools.partial(arrive_kernel, base),
        "arrive",
        scalars,
        (*planes, prefix, before, mine, got),
        [STATES, STATES],
        second[-1:],
    )
    return keep, lax.ppermute(send_back, "seq", SWAP), first, second


def decay_block(cum, cum_t, head, low, high):
    diff = cum[low:high, head : head + 1] - cum_t[head : head + 1, :high]
    rows = lax.broadcasted_iota(jnp.int32, diff.shape, 0) + low
    cols = lax.broadcasted_iota(jnp.int32, diff.shape, 1)
    return jnp.exp(jnp.where(rows >= cols, diff, -1e30))


def local_kernel(s_ref, cum_ref, cumt_ref, q_ref, k_ref, v_ref, out_ref):
    cum, cum_t = cum_ref[...], cumt_ref[...]
    for head in range(8):
        at = head_columns(head)
        for low in (0, 256):
            high = low + 256
            table = decay_block(cum, cum_t, head, low, high)
            probs = (dot(q_ref[low:high, at], k_ref[:high, at], NT) * table).astype(BF16)
            out_ref[low:high, at] = dot(probs, v_ref[:high, at])


def local(scalars, cum, cum_t, q, k, v, after):
    return call(local_kernel, "local", scalars, (cum, cum_t, q, k, v), [((512, 1024), F32)], after)


def arrived(s_ref, head, keep_ref, got_ref):
    rows = slice(head % 4 * 128, head % 4 * 128 + 128)
    return jnp.where(s_ref[6] == head // 4, keep_ref[rows, :], got_ref[rows, :])


def attend_kernel(s_ref, local_ref, cum_ref, q_ref, keep_ref, got_ref, normed_ref, att_ref):
    rise = jnp.exp(cum_ref[...])
    for head in range(8):
        at = head_columns(head)
        past = dot(q_ref[:, at], arrived(s_ref, head, keep_ref, got_ref))
        att = local_ref[:, at] + rise[:, head : head + 1] * past
        att_ref[:, at] = att
        scale = lax.rsqrt(jnp.mean(att * att, axis=1, keepdims=True) + EPS)
        normed_ref[:, at] = (att * scale).astype(BF16)


def attend(scalars, local_part, cum, q, keep, got, after):
    return call(
        attend_kernel,
        "attend",
        scalars,
        (local_part, cum, q, keep, got),
        [((512, 1024), BF16), ((512, 1024), F32)],
        after,
    )


HALF = ((256, 1536), BF16)
WIDE_HALF = ((256, 1536), F32)


def block_columns(s_ref, slot, offset=0, size=1536):
    return pl.ds(pl.multiple_of(s_ref[slot] * 1536 + offset, 128), size)


def products(s_ref, x_ref, w_ref, slot, top_ref, bottom_ref):
    for offset in (0, 512, 1024):
        out = dot(x_ref[...], w_ref[:, block_columns(s_ref, slot, offset, 512)])
        at = slice(offset, offset + 512)
        top_ref[:, at] = out[:256].astype(top_ref.dtype)
        bottom_ref[:, at] = out[256:].astype(bottom_ref.dtype)


def project_near_kernel(s_ref, x_ref, w_ref, right_top, right_bottom, left_top, left_bottom):
    products(s_ref, x_ref, w_ref, 5, right_top, right_bottom)
    products(s_ref, x_ref, w_ref, 4, left_top, left_bottom)


def project_one_kernel(slot, s_ref, x_ref, w_ref, top_ref, bottom_ref):
    products(s_ref, x_ref, w_ref, slot, top_ref, bottom_ref)


def split_kernel(s_ref, a_ref, b_ref, top_ref, bottom_ref):
    top_ref[...] = a_ref[:256, :]
    bottom_ref[...] = b_ref[256:, :]


def round_kernel(s_ref, a_ref, b_ref, a_out, b_out):
    a_out[...] = a_ref[...].astype(BF16)
    b_out[...] = b_ref[...].astype(BF16)


def join_kernel(s_ref, right_ref, from_left, left_ref, from_right, out_right, out_left):
    out_right[...] = (right_ref[...] + from_left[...].astype(F32)).astype(BF16)
    out_left[...] = (left_ref[...] + from_right[...].astype(F32)).astype(BF16)


def total_kernel(s_ref, top_ref, bottom_ref, top_a, top_b, bottom_a, bottom_b, out_ref):
    out_ref[:256, :] = (top_ref[...] + top_a[...].astype(F32) + top_b[...].astype(F32)).astype(BF16)
    out_ref[256:, :] = (bottom_ref[...] + bottom_a[...].astype(F32) + bottom_b[...].astype(F32)).astype(BF16)


def grad_own_kernel(s_ref, x_ref, w_ref, out_ref):
    for low in range(0, 1024, 256):
        rows = slice(low, low + 256)
        out_ref[:, rows] = dot(x_ref[...], w_ref[rows, block_columns(s_ref, 3)], NT)


def grad_near_kernel(s_ref, a_ref, b_ref, w_ref, acc_ref, out_ref):
    for low in range(0, 1024, 256):
        rows = slice(low, low + 256)
        out_ref[:, rows] = (
            acc_ref[:, rows]
            + dot(a_ref[...], w_ref[rows, block_columns(s_ref, 4)], NT)
            + dot(b_ref[...], w_ref[rows, block_columns(s_ref, 5)], NT)
        )


def grad_far_kernel(s_ref, c_ref, d_ref, w_ref, acc_ref, att_ref, q_ref, cum_ref, cumt_ref, grad_ref, mine_ref, send_ref):
    core = s_ref[6]
    rise = jnp.exp(cum_ref[...])
    x = jnp.concatenate([c_ref[...], d_ref[...]], axis=0)
    for low in range(0, 1024, 256):
        rows = slice(low, low + 256)
        acc = acc_ref[:, rows] + dot(x, w_ref[rows, block_columns(s_ref, 7)], NT)
        for i in range(2):
            head = low // 128 + i
            at = head_columns(head)
            att, grad = att_ref[:, at], acc[:, i * 128 : i * 128 + 128]
            scale = lax.rsqrt(jnp.mean(att * att, axis=1, keepdims=True) + EPS)
            unit = att * scale
            out = (scale * (grad - unit * jnp.mean(grad * unit, axis=1, keepdims=True))).astype(BF16)
            grad_ref[:, at] = out
            scaled = (q_ref[:, at].astype(F32) * rise[:, head : head + 1]).astype(BF16)
            put_state(core, head, dot(scaled, out, TN).astype(BF16), mine_ref, send_ref)
    put_decays(core, cumt_ref[...], mine_ref, send_ref)


def inside_kernel(heads, s_ref, cum_ref, cumt_ref, q_ref, k_ref, v_ref, g_ref, keep_ref, got_ref, *refs):
    gq_ref, gk_ref, gv_ref = refs[-3:]
    cum, cum_t = cum_ref[...], cumt_ref[...]
    rise = jnp.exp(cum)
    if len(refs) > 3:
        gq_ref[:, :512] = refs[0][...]
    for head in heads:
        at = head_columns(head)
        to = head_columns(head - heads[0])
        to_q = at if len(refs) > 3 else to
        incoming = arrived(s_ref, head, keep_ref, got_ref)
        early_k = early_v = None
        for low in (0, 256):
            high = low + 256
            q, g = q_ref[low:high, at], g_ref[low:high, at]
            k, v = k_ref[:high, at], v_ref[:high, at]
            table = decay_block(cum, cum_t, head, low, high)
            probs = (dot(q, k, NT) * table).astype(BF16)
            scores = (dot(g, v, NT) * table).astype(BF16)
            gq = dot(scores, k) + rise[low:high, head : head + 1] * dot(g, incoming, NT)
            gq_ref[low:high, to_q] = gq.astype(BF16)
            part_k, part_v = dot(scores, q, TN), dot(probs, g, TN)
            if low == 0:
                early_k, early_v = part_k, part_v
            else:
                gk_ref[:256, to] = early_k + part_k[:256]
                gk_ref[256:, to] = part_k[256:]
                gv_ref[:256, to] = early_v + part_v[:256]
                gv_ref[256:, to] = part_v[256:]


def finish_kernel(s_ref, cum_ref, k_ref, v_ref, gk_a, gv_a, gk_b, gv_b, keep_ref, got_ref, gk_out, gv_out):
    cum = cum_ref[...]
    fall = jnp.exp(cum[511:512, :] - cum)
    for head in range(8):
        at, part = head_columns(head), head_columns(head % 4)
        gk_ref, gv_ref = ((gk_a, gv_a), (gk_b, gv_b))[head // 4]
        outgoing = arrived(s_ref, head, keep_ref, got_ref)
        factor = fall[:, head : head + 1]
        gk_out[:, at] = (gk_ref[:, part] + factor * dot(v_ref[:, at], outgoing, NT)).astype(BF16)
        gv_out[:, at] = (gv_ref[:, part] + factor * dot(k_ref[:, at], outgoing)).astype(BF16)


RIGHT = [(i, (i + 1) % 4) for i in range(4)]
LEFT = [(i, (i + 3) % 4) for i in range(4)]


def body(queries, keys, values, logdecay, weight, output_gradient):
    at = lax.axis_index("seq").astype(jnp.int32)
    h = lax.axis_index("head").astype(jnp.int32)
    core, x, z = at % 2, at // 2 % 4, at // 8
    blocks = [h, (h + 3) % 4, (h + 1) % 4]
    scalars = jnp.stack([core, x, z] + blocks + [core, (h + 2) % 4, 1 - core, 3 - x, 3 - z]).astype(jnp.int32)

    right = lambda a: lax.ppermute(a, "head", RIGHT)
    left = lambda a: lax.ppermute(a, "head", LEFT)
    wide, narrow = ((512, 1024), F32), ((512, 1024), BF16)
    wide_part, narrow_part = ((512, 512), F32), ((512, 512), BF16)

    a, b = right(output_gradient), left(output_gradient)

    cum, cum_t, mine, send = own_states(scalars, logdecay.T, keys, values)
    keep, got, (local_part,), (acc,) = scan_blocks(
        scalars,
        mine,
        send,
        1,
        (
            lambda after: local(scalars, cum, cum_t, queries, keys, values, after),
            lambda after, _: call(grad_own_kernel, "grad_own", scalars, (output_gradient, weight), [wide], after),
        ),
    )
    a_top, b_bottom = call(split_kernel, "split", scalars, (a, b), [HALF, HALF], (keep,))
    c, d = right(a_top), left(b_bottom)
    normed, att = attend(scalars, local_part, cum, queries, keep, got, (a_top,))

    (acc,) = call(grad_near_kernel, "grad_near", scalars, (a, b, weight, acc), [wide], (att,))
    near = call(project_near_kernel, "project_near", scalars, (normed, weight), [WIDE_HALF] * 4, (acc,))
    right_top, right_bottom, left_top, left_bottom = near
    own = call(
        functools.partial(project_one_kernel, 3), "project_own", scalars, (normed, weight), [WIDE_HALF] * 2, near[:1]
    )
    far = call(functools.partial(project_one_kernel, 7), "project_far", scalars, (normed, weight), [HALF] * 2, own[:1])
    from_left, from_right = right(far[0]), left(far[1])
    grad, mine_g, send_g = call(
        grad_far_kernel,
        "grad_far",
        scalars,
        (c, d, weight, acc, att, queries, cum, cum_t),
        [narrow, MESSAGE, MESSAGE],
        far[:1],
    )
    inputs = (cum, cum_t, queries, keys, values, grad, keep, got)
    direct, joined = [], []

    def first(after):
        direct.extend(call(round_kernel, "direct", scalars, (right_bottom, left_top), [HALF, HALF], after))
        return call(
            functools.partial(inside_kernel, range(0, 4)),
            "inside_a",
            scalars,
            inputs,
            [narrow_part, wide_part, wide_part],
            direct[:1],
        )

    def second(after, one):
        joined.extend(
            call(join_kernel, "join", scalars, (right_top, from_left, left_bottom, from_right), [HALF, HALF], after)
        )
        return call(
            functools.partial(inside_kernel, range(4, 8)),
            "inside_b",
            scalars,
            inputs + (one[0],),
            [narrow, wide_part, wide_part],
            joined[:1],
        )

    keep_g, got_g, (_, gk_a, gv_a), (gq, gk_b, gv_b) = scan_blocks(scalars, mine_g, send_g, -1, (first, second))
    direct_r, direct_l = right(direct[0]), left(direct[1])
    joined_r, joined_l = right(joined[0]), left(joined[1])
    gk, gv = call(
        finish_kernel,
        "finish",
        scalars,
        (cum, keys, values, gk_a, gv_a, gk_b, gv_b, keep_g, got_g),
        [narrow, narrow],
    )
    (out,) = call(
        total_kernel,
        "total",
        scalars,
        (*own, joined_r, direct_l, direct_r, joined_l),
        [((512, 1536), BF16)],
        (gk,),
    )
    return out, gq, gk, gv


def solution(mesh):
    return jax.shard_map(
        body,
        mesh=mesh,
        in_specs=(
            P("seq", "head"),
            P("seq", "head"),
            P("seq", "head"),
            P("seq", "head"),
            P("head", None),
            P("seq", "head"),
        ),
        out_specs=(P("seq", "head"), P("seq", "head"), P("seq", "head"), P("seq", "head")),
        check_vma=False,
    )
```

time: 279 us -> 131 us (0.47)
  waiting for transfers between devices: 153 us -> 27.4 us
  matrix products: 65.9 us -> 0 us
  Pallas kernels: 0 us -> 54.3 us
  starting transfers between devices: 0.16 us -> 37.1 us
  blocking collectives: 22.8 us -> 0 us
  between operations: 14 us -> 0.96 us
  other arithmetic: 9.75 us -> 0.01 us
    all_gather x3 -> x0, waiting for transfers between devices: 101 us -> none  [the longest x1 44.1 us: body(): lax.all_gather(own_state[None].astype(jnp.bfloat16), 'seq', axis=0, tiled...]
    dot_general x15 -> x0, matrix products: 65.9 us -> none  [the longest x7 25.4 us: exact(): return jnp.einsum(form, left, right, precision=lax.Precision.HIGHEST)]
    pallas_call x0 -> x22, Pallas kernels: none -> 54.3 us  [call(): pl.pallas_call(run, out_shape=[jax.ShapeDtypeStruct(shape, dtype) for sha...]
    reduce_scatter x1 -> x0, waiting for transfers between devices: 51.1 us -> none  [body(): lax.psum_scatter(term.astype(jnp.bfloat16), 'head', scatter_dimension=1,...]
    ppermute x0 -> x26, starting transfers between devices: none -> 37.1 us  [the longest x5 15.1 us: body(): left = lambda a: lax.ppermute(a, 'head', LEFT)]
    ppermute x0 -> x26, waiting for transfers between devices: none -> 27.4 us  [the longest x6 15.1 us: scan_blocks(): planes = [lax.ppermute(total, 'seq', shifts_z(sign * k)) for k in (1, 2, 3)]]
    all_gather x1 -> x0, blocking collectives: 22.8 us -> none  [body(): lax.all_gather(block_decay[None].astype(jnp.bfloat16), 'seq', axis=0, til...]
    dot_general x1 -> x0, other arithmetic: 5.25 us -> none  [exact(): return jnp.einsum(form, left, right, precision=lax.Precision.HIGHEST)]
  transfers between devices with their start and end apart: 4 -> 26, of which waited for: 4 -> 13; matrix products, arithmetic and copies ran while one was open for 24% -> 0% of each run, Pallas kernels for 0% -> 39%
where the time goes in v2:
time: 131 us
  Pallas kernels  54.3 us (41%)
  starting transfers between devices  37.1 us (28%)
  waiting for transfers between devices  27.4 us (21%)
  local copies, waits for them, and re-layouts  10.8 us (8%)
    pallas_call x22, Pallas kernels, call(): pl.pallas_call(run, out_shape=[jax.ShapeDtypeStruct(shape, dtype) for sha...  54.3 us
    ppermute x6, waiting for transfers between devices, scan_blocks(): planes = [lax.ppermute(total, 'seq', shifts_z(sign * k)) for k in (1, 2, 3)]  15.1 us
    ppermute x5, starting transfers between devices, body(): left = lambda a: lax.ppermute(a, 'head', LEFT)  15.1 us
    ppermute x6, starting transfers between devices, scan_blocks(): planes = [lax.ppermute(total, 'seq', shifts_z(sign * k)) for k in (1, 2, 3)]  13.9 us
    unnamed x26, local copies, waits for them, and re-layouts  10.7 us
    ppermute x6, starting transfers between devices, scan_blocks(): lax.ppermute(chip, 'seq', shifts_x(sign * k))  8.01 us
    ppermute x6, waiting for transfers between devices, scan_blocks(): lax.ppermute(chip, 'seq', shifts_x(sign * k))  5.45 us
    ppermute x2, waiting for transfers between devices, scan_blocks(): got = lax.ppermute(send, 'seq', SWAP)  2.68 us
  transfers between devices with their start and end apart: 26, of which 13 were waited for; matrix products, arithmetic and copies ran while one was open for 0% of the time, Pallas kernels for 39%

profile of v2, /device:TPU:0, one launch (start us, length us, event | category | flops | bytes accessed | tf_op | source)
XLA Modules:
  0.0 130.6 jit_solution(3089200352864722367)
XLA Ops:
  0.6 3.2 %collective-permute-start.9 = (bf16[512,1536]{1,0:T(8,128)(2,1)}, bf16[512,1536]{1,0:T(8,128)(2,1)S(1)}, u32[]{:S(2)}, u32[]{:S(2)}) collective-permute-start(bf16[512,1536]{1,0:T(8,128)(2,1)} %refs_1_.1), channel_id=1, source_target_pairs={{0,3},{1,0},{2,1},{3,2},{4,7},{5,4},{6,5},{7,6},{8,11},{9,8},{10,9... | collective-permute-start | bytes 4718600 | tf_op jit(solution)/shard_map/ppermute | solution.py:412
  3.9 1.2 copy-done.2
  5.1 1.2 copy-done.4
  7.1 4.2 %own_states.1 = (f32[512,8]{1,0:T(8,128)S(1)}, f32[8,512]{1,0:T(8,128)S(1)}, bf16[528,128]{1,0:T(8,128)(2,1)S(1)}, bf16[528,128]{1,0:T(8,128)(2,1)S(1)}) custom-call(s32[11]{0:T(128)S(1)} %stack.44.refs_0_, f32[8,512]{1,0:T(8,128)S(1)} %bitcast.13, bf16[512,1024]{1,0:T(8,128)(2,1)S(1)} %copy-done.2, bf16[512,1024]{1,0:T(8,128)(2,1)S(1)} %copy-done.4), custom_call_target="tpu_custom_call" | custom-call | tf_op jit(solution)/shard_map/own_states/pallas_call | solution.py:35
  11.3 1.3 %collective-permute-done.refs_2_.refs_7_ = bf16[528,128]{1,0:T(8,128)(2,1)S(1)} collective-permute-done((bf16[528,128]{1,0:T(8,128)(2,1)S(1)}, bf16[528,128]{1,0:T(8,128)(2,1)S(1)}, u32[]{:S(2)}, u32[]{:S(2)}) %collective-permute-start) | collective-permute-done | bytes 135200 | tf_op jit(solution)/shard_map/ppermute | solution.py:202
  13.2 2.8 %collective-permute-start.3 = (bf16[528,128]{1,0:T(8,128)(2,1)S(1)}, bf16[528,128]{1,0:T(8,128)(2,1)S(1)}, u32[]{:S(2)}, u32[]{:S(2)}) collective-permute-start(bf16[528,128]{1,0:T(8,128)(2,1)S(1)} %chip_total.2.refs_6_.refs_1_), channel_id=1, source_target_pairs={{0,24},{4,28},{8,0},{12,4},{16,8},{20,12},{24,16},{28,20},{32,56},... | collective-permute-start | bytes 405512 | tf_op jit(solution)/shard_map/ppermute | solution.py:204
  16.1 0.8 collective-permute-start.2
  16.9 0.9 collective-permute-start.1
  17.8 1.2 copy-done.5
  19.0 3.0 %local.1.refs_5_.refs_1_ = f32[512,1024]{1,0:T(8,128)S(1)} custom-call(s32[11]{0:T(128)S(1)} %stack.44.refs_0_, f32[512,8]{1,0:T(8,128)S(1)} %get-tuple-element.45.refs_1_.refs_2_.refs_7_, f32[8,512]{1,0:T(8,128)S(1)} %get-tuple-element.46.refs_2_.refs_8_, bf16[512,1024]{1,0:T(8,128)(2,1)S(1)} %copy-done.1, bf16[512,1024]{1,0:T(8,128)(2,1)S(1)} %copy-done.3, ...), custom_call_target="tpu_custom_call" | custom-call | tf_op jit(solution)/shard_map/local/pallas_call | solution.py:35
  22.1 1.9 %collective-permute-done.2.refs_3_ = bf16[528,128]{1,0:T(8,128)(2,1)S(1)} collective-permute-done((bf16[528,128]{1,0:T(8,128)(2,1)S(1)}, bf16[528,128]{1,0:T(8,128)(2,1)S(1)}, u32[]{:S(2)}, u32[]{:S(2)}) %collective-permute-start.2) | collective-permute-done | bytes 135200 | tf_op jit(solution)/shard_map/ppermute | solution.py:204
  24.0 1.8 %collective-permute-done.1.refs_2_ = bf16[528,128]{1,0:T(8,128)(2,1)S(1)} collective-permute-done((bf16[528,128]{1,0:T(8,128)(2,1)S(1)}, bf16[528,128]{1,0:T(8,128)(2,1)S(1)}, u32[]{:S(2)}, u32[]{:S(2)}) %collective-permute-start.1) | collective-permute-done | bytes 135200 | tf_op jit(solution)/shard_map/ppermute | solution.py:204
  26.5 6.0 %collective-permute-start.6 = (bf16[528,128]{1,0:T(8,128)(2,1)S(1)}, bf16[528,128]{1,0:T(8,128)(2,1)S(1)}, u32[]{:S(2)}, u32[]{:S(2)}) collective-permute-start(bf16[528,128]{1,0:T(8,128)(2,1)S(1)} %get-tuple-element.49), channel_id=1, source_target_pairs={{0,96},{4,100},{8,104},{12,108},{16,112},{20,116},{24,120},{28,124... | collective-permute-start | bytes 405512 | tf_op jit(solution)/shard_map/ppermute | solution.py:214
  32.5 1.3 collective-permute-start.5
  33.8 2.8 %collective-permute-start.4 = (bf16[528,128]{1,0:T(8,128)(2,1)S(1)}, bf16[528,128]{1,0:T(8,128)(2,1)S(1)}, u32[]{:S(2)}, u32[]{:S(2)}) collective-permute-start(bf16[528,128]{1,0:T(8,128)(2,1)S(1)} %get-tuple-element.49), channel_id=1, source_target_pairs={{0,32},{4,36},{8,40},{12,44},{16,48},{20,52},{24,56},{28,60},{32,6... | collective-permute-start | bytes 405512 | tf_op jit(solution)/shard_map/ppermute | solution.py:214
  36.6 4.6 %copy-done = bf16[1024,6144]{1,0:T(8,128)(2,1)S(1)} copy-done((bf16[1024,6144]{1,0:T(8,128)(2,1)S(1)}, bf16[1024,6144]{1,0:T(8,128)(2,1)}, u32[]{:S(2)}) %copy-start) | copy-done | bytes 12582936
  41.2 2.4 %grad_own.1.refs_8_.refs_4_ = f32[512,1024]{1,0:T(8,128)S(1)} custom-call(s32[11]{0:T(128)S(1)} %stack.44.refs_0_, bf16[512,1536]{1,0:T(8,128)(2,1)S(1)} %copy-done.7, bf16[1024,6144]{1,0:T(8,128)(2,1)S(1)} %copy-done, f32[8,128]{1,0:T(8,128)S(1)} %get-tuple-element.51.refs_3_.refs_5_), custom_call_target="tpu_custom_call" | custom-call | tf_op jit(solution)/shard_map/grad_own/pallas_call | solution.py:35
  44.3 1.9 %split.1 = (bf16[256,1536]{1,0:T(8,128)(2,1)S(1)}, bf16[256,1536]{1,0:T(8,128)(2,1)S(1)}) custom-call(s32[11]{0:T(128)S(1)} %stack.44.refs_0_, bf16[512,1536]{1,0:T(8,128)(2,1)} %collective-permute-done.8.refs_1_, bf16[512,1536]{1,0:T(8,128)(2,1)S(1)} %collective-permute-done.9.refs_2_, bf16[512,128]{1,0:T(8,128)(2,1)S(1)} %get-tuple-element.52.refs_3_.refs_4_.refs_7_), custom_call_target="tpu_custom_call" | custom-call | tf_op jit(solution)/shard_map/split/pallas_call | solution.py:35
  46.2 3.3 %collective-permute-start.13 = (bf16[256,1536]{1,0:T(8,128)(2,1)S(1)}, bf16[256,1536]{1,0:T(8,128)(2,1)S(1)}, u32[]{:S(2)}, u32[]{:S(2)}) collective-permute-start(bf16[256,1536]{1,0:T(8,128)(2,1)S(1)} %get-tuple-element.63), channel_id=1, source_target_pairs={{0,3},{1,0},{2,1},{3,2},{4,7},{5,4},{6,5},{7,6},{8,11},{9,8},{10,9... | collective-permute-start | bytes 2359304 | tf_op jit(solution)/shard_map/ppermute | solution.py:412
  49.5 1.3 %collective-permute-done.7.refs_5_.refs_8_ = bf16[512,128]{1,0:T(8,128)(2,1)S(1)} collective-permute-done((bf16[512,128]{1,0:T(8,128)(2,1)S(1)}, bf16[512,128]{1,0:T(8,128)(2,1)S(1)}, u32[]{:S(2)}, u32[]{:S(2)}) %collective-permute-start.7) | collective-permute-done | bytes 131104 | tf_op jit(solution)/shard_map/ppermute | solution.py:224
  50.9 2.2 %attend.1 = (bf16[512,1024]{1,0:T(8,128)(2,1)S(1)}, f32[512,1024]{1,0:T(8,128)S(1)}) custom-call(s32[11]{0:T(128)S(1)} %stack.44.refs_0_, f32[512,1024]{1,0:T(8,128)S(1)} %local.1.refs_5_.refs_1_, f32[512,8]{1,0:T(8,128)S(1)} %get-tuple-element.45.refs_1_.refs_2_.refs_7_, bf16[512,1024]{1,0:T(8,128)(2,1)S(1)} %copy-done.1, ...), custom_call_target="tpu_custom_call" | custom-call | tf_op jit(solution)/shard_map/attend/pallas_call | solution.py:35
  53.1 4.9 %grad_near.1.refs_3_.refs_4_ = f32[512,1024]{1,0:T(8,128)S(1)} custom-call(s32[11]{0:T(128)S(1)} %stack.44.refs_0_, bf16[512,1536]{1,0:T(8,128)(2,1)} %collective-permute-done.8.refs_1_, bf16[512,1536]{1,0:T(8,128)(2,1)S(1)} %collective-permute-done.9.refs_2_, bf16[1024,6144]{1,0:T(8,128)(2,1)S(1)} %bitcast.12, f32[512,1024]{1,0:T(8,128)S(1)} %grad_own.1.refs_8_.refs_4_, ...), custom_call_target="tpu_custom_call" | custom-call | tf_op jit(solution)/shard_map/grad_near/pallas_call | solution.py:35
  58.0 4.0 %project_near.1 = (f32[256,1536]{1,0:T(8,128)S(1)}, f32[256,1536]{1,0:T(8,128)S(1)}, f32[256,1536]{1,0:T(8,128)S(1)}, f32[256,1536]{1,0:T(8,128)S(1)}) custom-call(s32[11]{0:T(128)S(1)} %stack.44.refs_0_, bf16[512,1024]{1,0:T(8,128)(2,1)S(1)} %get-tuple-element.55.refs_1_, bf16[1024,6144]{1,0:T(8,128)(2,1)S(1)} %bitcast.12, ...), custom_call_target="tpu_custom_call" | custom-call | tf_op jit(solution)/shard_map/project_near/pallas_call | solution.py:35
  62.0 2.3 %project_own.1 = (f32[256,1536]{1,0:T(8,128)S(1)}, f32[256,1536]{1,0:T(8,128)S(1)}) custom-call(s32[11]{0:T(128)S(1)} %stack.44.refs_0_, bf16[512,1024]{1,0:T(8,128)(2,1)S(1)} %get-tuple-element.55.refs_1_, bf16[1024,6144]{1,0:T(8,128)(2,1)S(1)} %bitcast.12, f32[256,1536]{1,0:T(8,128)S(1)} %get-tuple-element.57.refs_3_.refs_1_), custom_call_target="tpu_custom_call" | custom-call | tf_op jit(solution)/shard_map/project_own/pallas_call | solution.py:35
  64.4 2.3 %project_far.1 = (bf16[256,1536]{1,0:T(8,128)(2,1)S(1)}, bf16[256,1536]{1,0:T(8,128)(2,1)S(1)}) custom-call(s32[11]{0:T(128)S(1)} %stack.44.refs_0_, bf16[512,1024]{1,0:T(8,128)(2,1)S(1)} %get-tuple-element.55.refs_1_, bf16[1024,6144]{1,0:T(8,128)(2,1)S(1)} %bitcast.12, f32[256,1536]{1,0:T(8,128)S(1)} %get-tuple-element.58.refs_3_.refs_1_), custom_call_target="tpu_custom_call" | custom-call | tf_op jit(solution)/shard_map/project_far/pallas_call | solution.py:35
  66.7 3.3 %collective-permute-start.11 = (bf16[256,1536]{1,0:T(8,128)(2,1)S(1)}, bf16[256,1536]{1,0:T(8,128)(2,1)S(1)}, u32[]{:S(2)}, u32[]{:S(2)}) collective-permute-start(bf16[256,1536]{1,0:T(8,128)(2,1)S(1)} %get-tuple-element.62), channel_id=1, source_target_pairs={{0,3},{1,0},{2,1},{3,2},{4,7},{5,4},{6,5},{7,6},{8,11},{9,8},{10,9... | collective-permute-start | bytes 2359304 | tf_op jit(solution)/shard_map/ppermute | solution.py:412
  70.0 8.3 %grad_far.1 = (bf16[512,1024]{1,0:T(8,128)(2,1)S(1)}, bf16[528,128]{1,0:T(8,128)(2,1)S(1)}, bf16[528,128]{1,0:T(8,128)(2,1)S(1)}) custom-call(s32[11]{0:T(128)S(1)} %stack.44.refs_0_, bf16[256,1536]{1,0:T(8,128)(2,1)S(1)} %collective-permute-done.12.refs_1_, bf16[256,1536]{1,0:T(8,128)(2,1)S(1)} %collective-permute-done.13.refs_2_, ...), custom_call_target="tpu_custom_call" | custom-call | tf_op jit(solution)/shard_map/grad_far/pallas_call | solution.py:35
  78.4 1.3 %collective-permute-done.14.refs_2_.refs_7_ = bf16[528,128]{1,0:T(8,128)(2,1)S(1)} collective-permute-done((bf16[528,128]{1,0:T(8,128)(2,1)S(1)}, bf16[528,128]{1,0:T(8,128)(2,1)S(1)}, u32[]{:S(2)}, u32[]{:S(2)}) %collective-permute-start.14) | collective-permute-done | bytes 135200 | tf_op jit(solution)/shard_map/ppermute | solution.py:202
  80.4 2.0 %collective-permute-start.16 = (bf16[528,128]{1,0:T(8,128)(2,1)S(1)}, bf16[528,128]{1,0:T(8,128)(2,1)S(1)}, u32[]{:S(2)}, u32[]{:S(2)}) collective-permute-start(bf16[528,128]{1,0:T(8,128)(2,1)S(1)} %chip_total.3.refs_3_.refs_1_), channel_id=1, source_target_pairs={{0,16},{4,20},{8,24},{12,28},{16,0},{20,4},{24,8},{28,12},{32,48},... | collective-permute-start | bytes 405512 | tf_op jit(solution)/shard_map/ppermute | solution.py:204
  82.5 1.4 %collective-permute-start.15 = (bf16[528,128]{1,0:T(8,128)(2,1)S(1)}, bf16[528,128]{1,0:T(8,128)(2,1)S(1)}, u32[]{:S(2)}, u32[]{:S(2)}) collective-permute-start(bf16[528,128]{1,0:T(8,128)(2,1)S(1)} %chip_total.3.refs_3_.refs_1_), channel_id=1, source_target_pairs={{0,24},{4,28},{8,0},{12,4},{16,8},{20,12},{24,16},{28,20},{32,56},... | collective-permute-start | bytes 405512 | tf_op jit(solution)/shard_map/ppermute | solution.py:204
  85.1 3.4 %inside_a.1 = (bf16[512,512]{1,0:T(8,128)(2,1)S(1)}, f32[512,512]{1,0:T(8,128)S(1)}, f32[512,512]{1,0:T(8,128)S(1)}) custom-call(s32[11]{0:T(128)S(1)} %stack.44.refs_0_, f32[512,8]{1,0:T(8,128)S(1)} %get-tuple-element.45.refs_1_.refs_2_.refs_7_, f32[8,512]{1,0:T(8,128)S(1)} %get-tuple-element.46.refs_2_.refs_8_, bf16[512,1024]{1,0:T(8,128)(2,1)S(1)} %copy-done.1, ...), custom_call_target="tpu_custom_call" | custom-call | tf_op jit(solution)/shard_map/inside_a/pallas_call | solution.py:35
  88.5 1.7 %collective-permute-done.17.refs_4_ = bf16[528,128]{1,0:T(8,128)(2,1)S(1)} collective-permute-done((bf16[528,128]{1,0:T(8,128)(2,1)S(1)}, bf16[528,128]{1,0:T(8,128)(2,1)S(1)}, u32[]{:S(2)}, u32[]{:S(2)}) %collective-permute-start.17) | collective-permute-done | bytes 135200 | tf_op jit(solution)/shard_map/ppermute | solution.py:204
  90.2 3.2 %collective-permute-start.19 = (bf16[256,1536]{1,0:T(8,128)(2,1)S(1)}, bf16[256,1536]{1,0:T(8,128)(2,1)S(1)}, u32[]{:S(2)}, u32[]{:S(2)}) collective-permute-start(bf16[256,1536]{1,0:T(8,128)(2,1)S(1)} %get-tuple-element.73), channel_id=1, source_target_pairs={{0,3},{1,0},{2,1},{3,2},{4,7},{5,4},{6,5},{7,6},{8,11},{9,8},{10,9... | collective-permute-start | bytes 2359304 | tf_op jit(solution)/shard_map/ppermute | solution.py:412
  93.4 0.7 row_total.3
  94.2 0.9 join.1
  95.1 2.1 %collective-permute-start.21 = (bf16[256,1536]{1,0:T(8,128)(2,1)S(1)}, bf16[256,1536]{1,0:T(8,128)(2,1)S(1)}, u32[]{:S(2)}, u32[]{:S(2)}) collective-permute-start(bf16[256,1536]{1,0:T(8,128)(2,1)S(1)} %get-tuple-element.74), channel_id=1, source_target_pairs={{0,3},{1,0},{2,1},{3,2},{4,7},{5,4},{6,5},{7,6},{8,11},{9,8},{10,9... | collective-permute-start | bytes 2359304 | tf_op jit(solution)/shard_map/ppermute | solution.py:412
  97.2 1.3 collective-permute-start.24
  98.5 6.8 %collective-permute-done.24.refs_3_ = bf16[528,128]{1,0:T(8,128)(2,1)S(1)} collective-permute-done((bf16[528,128]{1,0:T(8,128)(2,1)S(1)}, bf16[528,128]{1,0:T(8,128)(2,1)S(1)}, u32[]{:S(2)}, u32[]{:S(2)}) %collective-permute-start.24) | collective-permute-done | bytes 135200 | tf_op jit(solution)/shard_map/ppermute | solution.py:214
  105.3 1.3 collective-permute-start.23
  106.6 7.1 %collective-permute-done.23.refs_2_ = bf16[528,128]{1,0:T(8,128)(2,1)S(1)} collective-permute-done((bf16[528,128]{1,0:T(8,128)(2,1)S(1)}, bf16[528,128]{1,0:T(8,128)(2,1)S(1)}, u32[]{:S(2)}, u32[]{:S(2)}) %collective-permute-start.23) | collective-permute-done | bytes 135200 | tf_op jit(solution)/shard_map/ppermute | solution.py:214
  113.7 1.3 collective-permute-start.22
  115.0 4.4 %inside_b.1 = (bf16[512,1024]{1,0:T(8,128)(2,1)}, f32[512,512]{1,0:T(8,128)S(1)}, f32[512,512]{1,0:T(8,128)S(1)}) custom-call(s32[11]{0:T(128)S(1)} %stack.44.refs_0_, f32[512,8]{1,0:T(8,128)S(1)} %get-tuple-element.45.refs_1_.refs_2_.refs_7_, f32[8,512]{1,0:T(8,128)S(1)} %get-tuple-element.46.refs_2_.refs_8_, bf16[512,1024]{1,0:T(8,128)(2,1)S(1)} %copy-done.1, ...), custom_call_target="tpu_custom_call" | custom-call | tf_op jit(solution)/shard_map/inside_b/pallas_call | solution.py:35
  119.4 1.2 collective-permute-done.22.refs_1_
  121.4 1.3 %collective-permute-done.25.refs_9_ = bf16[512,128]{1,0:T(8,128)(2,1)S(1)} collective-permute-done((bf16[512,128]{1,0:T(8,128)(2,1)S(1)}, bf16[512,128]{1,0:T(8,128)(2,1)S(1)}, u32[]{:S(2)}, u32[]{:S(2)}) %collective-permute-start.25) | collective-permute-done | bytes 131104 | tf_op jit(solution)/shard_map/ppermute | solution.py:224
  122.7 3.1 %finish.1 = (bf16[512,1024]{1,0:T(8,128)(2,1)}, bf16[512,1024]{1,0:T(8,128)(2,1)}) custom-call(s32[11]{0:T(128)S(1)} %stack.44.refs_0_, f32[512,8]{1,0:T(8,128)S(1)} %get-tuple-element.45.refs_1_.refs_2_.refs_7_, bf16[512,1024]{1,0:T(8,128)(2,1)S(1)} %copy-done.3, bf16[512,1024]{1,0:T(8,128)(2,1)S(1)} %copy-done.6, ...), custom_call_target="tpu_custom_call" | custom-call | tf_op jit(solution)/shard_map/finish/pallas_call | solution.py:35
  125.8 0.7 collective-permute-done.21.refs_6_
  127.3 1.2 copy-done.8
  128.5 2.1 %total.1 = bf16[512,1536]{1,0:T(8,128)(2,1)} custom-call(s32[11]{0:T(128)S(1)} %stack.44.refs_0_, f32[256,1536]{1,0:T(8,128)S(1)} %get-tuple-element.58.refs_3_.refs_1_, f32[256,1536]{1,0:T(8,128)S(1)} %get-tuple-element.59.refs_2_, bf16[256,1536]{1,0:T(8,128)(2,1)S(1)} %collective-permute-done.18.refs_3_, ...), custom_call_target="tpu_custom_call" | custom-call | tf_op jit(solution)/shard_map/total/pallas_call | solution.py:35
  (54 shorter events, 6.6 us)
Async XLA Ops:
  0.6 17.1 %copy-start.1 = (bf16[512,1024]{1,0:T(8,128)(2,1)S(1)}, bf16[512,1024]{1,0:T(8,128)(2,1)}, u32[]{:S(2)}) copy-start(bf16[512,1024]{1,0:T(8,128)(2,1)} %refs_3_.14) | copy-start | bytes 3145732
  0.6 43.7 %collective-permute-start.9 = (bf16[512,1536]{1,0:T(8,128)(2,1)}, bf16[512,1536]{1,0:T(8,128)(2,1)S(1)}, u32[]{:S(2)}, u32[]{:S(2)}) collective-permute-start(bf16[512,1536]{1,0:T(8,128)(2,1)} %refs_1_.1), channel_id=1, source_target_pairs={{0,3},{1,0},{2,1},{3,2},{4,7},{5,4},{6,5},{7,6},{8,11},{9,8},{10,9... | collective-permute-start | bytes 4718600 | tf_op jit(solution)/shard_map/ppermute | solution.py:412
  3.8 40.5 %collective-permute-start.8 = (bf16[512,1536]{1,0:T(8,128)(2,1)}, bf16[512,1536]{1,0:T(8,128)(2,1)}, u32[]{:S(2)}, u32[]{:S(2)}) collective-permute-start(bf16[512,1536]{1,0:T(8,128)(2,1)} %refs_1_.1), channel_id=1, source_target_pairs={{0,1},{1,2},{2,3},{3,0},{4,5},{5,6},{6,7},{7,4},{8,9},{9,10},{10,1... | collective-permute-start | bytes 4718600 | tf_op jit(solution)/shard_map/ppermute | solution.py:411
  3.9 1.2 copy-start.2
  5.1 1.2 copy-start.4
  6.4 0.7 copy-start.9
  7.1 10.7 %copy-start.3 = (bf16[512,1024]{1,0:T(8,128)(2,1)S(1)}, bf16[512,1024]{1,0:T(8,128)(2,1)}, u32[]{:S(2)}) copy-start(bf16[512,1024]{1,0:T(8,128)(2,1)} %refs_2_.11) | copy-start | bytes 3145732
  11.2 1.4 %collective-permute-start = (bf16[528,128]{1,0:T(8,128)(2,1)S(1)}, bf16[528,128]{1,0:T(8,128)(2,1)S(1)}, u32[]{:S(2)}, u32[]{:S(2)}) collective-permute-start(bf16[528,128]{1,0:T(8,128)(2,1)S(1)} %get-tuple-element.48), channel_id=1, source_target_pairs={{0,4},{4,0},{8,12},{12,8},{16,20},{20,16},{24,28},{28,24},{32,36},... | collective-permute-start | bytes 405512 | tf_op jit(solution)/shard_map/ppermute | solution.py:202
  13.2 8.9 %collective-permute-start.3 = (bf16[528,128]{1,0:T(8,128)(2,1)S(1)}, bf16[528,128]{1,0:T(8,128)(2,1)S(1)}, u32[]{:S(2)}, u32[]{:S(2)}) collective-permute-start(bf16[528,128]{1,0:T(8,128)(2,1)S(1)} %chip_total.2.refs_6_.refs_1_), channel_id=1, source_target_pairs={{0,24},{4,28},{8,0},{12,4},{16,8},{20,12},{24,16},{28,20},{32,56},... | collective-permute-start | bytes 405512 | tf_op jit(solution)/shard_map/ppermute | solution.py:204
  16.1 8.0 %collective-permute-start.2 = (bf16[528,128]{1,0:T(8,128)(2,1)S(1)}, bf16[528,128]{1,0:T(8,128)(2,1)S(1)}, u32[]{:S(2)}, u32[]{:S(2)}) collective-permute-start(bf16[528,128]{1,0:T(8,128)(2,1)S(1)} %chip_total.2.refs_6_.refs_1_), channel_id=1, source_target_pairs={{0,16},{4,20},{8,24},{12,28},{16,0},{20,4},{24,8},{28,12},{32,48},... | collective-permute-start | bytes 405512 | tf_op jit(solution)/shard_map/ppermute | solution.py:204
  16.9 9.0 %collective-permute-start.1 = (bf16[528,128]{1,0:T(8,128)(2,1)S(1)}, bf16[528,128]{1,0:T(8,128)(2,1)S(1)}, u32[]{:S(2)}, u32[]{:S(2)}) collective-permute-start(bf16[528,128]{1,0:T(8,128)(2,1)S(1)} %chip_total.2.refs_6_.refs_1_), channel_id=1, source_target_pairs={{0,8},{4,12},{8,16},{12,20},{16,24},{20,28},{24,0},{28,4},{32,40},... | collective-permute-start | bytes 405512 | tf_op jit(solution)/shard_map/ppermute | solution.py:204
  17.7 1.2 copy-start.5
  22.0 14.6 %copy-start.7 = (bf16[512,1536]{1,0:T(8,128)(2,1)S(1)}, bf16[512,1536]{1,0:T(8,128)(2,1)}, u32[]{:S(2)}) copy-start(bf16[512,1536]{1,0:T(8,128)(2,1)} %refs_1_.1) | copy-start | bytes 4718596
  26.5 17.0 %collective-permute-start.6 = (bf16[528,128]{1,0:T(8,128)(2,1)S(1)}, bf16[528,128]{1,0:T(8,128)(2,1)S(1)}, u32[]{:S(2)}, u32[]{:S(2)}) collective-permute-start(bf16[528,128]{1,0:T(8,128)(2,1)S(1)} %get-tuple-element.49), channel_id=1, source_target_pairs={{0,96},{4,100},{8,104},{12,108},{16,112},{20,116},{24,120},{28,124... | collective-permute-start | bytes 405512 | tf_op jit(solution)/shard_map/ppermute | solution.py:214
  32.5 11.1 %collective-permute-start.5 = (bf16[528,128]{1,0:T(8,128)(2,1)S(1)}, bf16[528,128]{1,0:T(8,128)(2,1)S(1)}, u32[]{:S(2)}, u32[]{:S(2)}) collective-permute-start(bf16[528,128]{1,0:T(8,128)(2,1)S(1)} %get-tuple-element.49), channel_id=1, source_target_pairs={{0,64},{4,68},{8,72},{12,76},{16,80},{20,84},{24,88},{28,92},{32,9... | collective-permute-start | bytes 405512 | tf_op jit(solution)/shard_map/ppermute | solution.py:214
  33.8 9.8 %collective-permute-start.4 = (bf16[528,128]{1,0:T(8,128)(2,1)S(1)}, bf16[528,128]{1,0:T(8,128)(2,1)S(1)}, u32[]{:S(2)}, u32[]{:S(2)}) collective-permute-start(bf16[528,128]{1,0:T(8,128)(2,1)S(1)} %get-tuple-element.49), channel_id=1, source_target_pairs={{0,32},{4,36},{8,40},{12,44},{16,48},{20,52},{24,56},{28,60},{32,6... | collective-permute-start | bytes 405512 | tf_op jit(solution)/shard_map/ppermute | solution.py:214
  36.6 4.6 %copy-start = (bf16[1024,6144]{1,0:T(8,128)(2,1)S(1)}, bf16[1024,6144]{1,0:T(8,128)(2,1)}, u32[]{:S(2)}) copy-start(bf16[1024,6144]{1,0:T(8,128)(2,1)} %refs_3_.12) | copy-start | bytes 37748740
  41.2 11.9 %slice-start = ((s8[12582912]{0:T(1024)(128)(4,1)}), s8[4194304]{0:T(1024)(128)(4,1)S(1)}, s32[]{:S(2)}) async-start(s8[12582912]{0:T(1024)(128)(4,1)} %bitcast.11), calls=%async_computation | async-start | bytes 8388608
  41.2 11.9 %slice-start.1 = ((s8[12582912]{0:T(1024)(128)(4,1)}), s8[4194304]{0:T(1024)(128)(4,1)S(1)}, s32[]{:S(2)}) async-start(s8[12582912]{0:T(1024)(128)(4,1)} %bitcast.11), calls=%async_computation.1 | async-start | bytes 8388608
  43.6 9.5 %slice-start.2 = ((s8[12582912]{0:T(1024)(128)(4,1)}), s8[4194304]{0:T(1024)(128)(4,1)S(1)}, s32[]{:S(2)}) async-start(s8[12582912]{0:T(1024)(128)(4,1)} %bitcast.11), calls=%async_computation.2 | async-start | bytes 8388608
  46.2 23.8 %collective-permute-start.13 = (bf16[256,1536]{1,0:T(8,128)(2,1)S(1)}, bf16[256,1536]{1,0:T(8,128)(2,1)S(1)}, u32[]{:S(2)}, u32[]{:S(2)}) collective-permute-start(bf16[256,1536]{1,0:T(8,128)(2,1)S(1)} %get-tuple-element.63), channel_id=1, source_target_pairs={{0,3},{1,0},{2,1},{3,2},{4,7},{5,4},{6,5},{7,6},{8,11},{9,8},{10,9... | collective-permute-start | bytes 2359304 | tf_op jit(solution)/shard_map/ppermute | solution.py:412
  49.5 20.5 %collective-permute-start.12 = (bf16[256,1536]{1,0:T(8,128)(2,1)S(1)}, bf16[256,1536]{1,0:T(8,128)(2,1)S(1)}, u32[]{:S(2)}, u32[]{:S(2)}) collective-permute-start(bf16[256,1536]{1,0:T(8,128)(2,1)S(1)} %get-tuple-element.54.refs_6_), channel_id=1, source_target_pairs={{0,1},{1,2},{2,3},{3,0},{4,5},{5,6},{6,7},{7,4},{8,9},{9,10},{10,1... | collective-permute-start | bytes 2359304 | tf_op jit(solution)/shard_map/ppermute | solution.py:411
  49.5 1.3 %collective-permute-start.7 = (bf16[512,128]{1,0:T(8,128)(2,1)S(1)}, bf16[512,128]{1,0:T(8,128)(2,1)S(1)}, u32[]{:S(2)}, u32[]{:S(2)}) collective-permute-start(bf16[512,128]{1,0:T(8,128)(2,1)S(1)} %get-tuple-element.53), channel_id=1, source_target_pairs={{0,4},{4,0},{8,12},{12,8},{16,20},{20,16},{24,28},{28,24},{32,36},... | collective-permute-start | bytes 393224 | tf_op jit(solution)/shard_map/ppermute | solution.py:224
  66.7 27.4 %collective-permute-start.11 = (bf16[256,1536]{1,0:T(8,128)(2,1)S(1)}, bf16[256,1536]{1,0:T(8,128)(2,1)S(1)}, u32[]{:S(2)}, u32[]{:S(2)}) collective-permute-start(bf16[256,1536]{1,0:T(8,128)(2,1)S(1)} %get-tuple-element.62), channel_id=1, source_target_pairs={{0,3},{1,0},{2,1},{3,2},{4,7},{5,4},{6,5},{7,6},{8,11},{9,8},{10,9... | collective-permute-start | bytes 2359304 | tf_op jit(solution)/shard_map/ppermute | solution.py:412
  70.0 24.1 %collective-permute-start.10 = (bf16[256,1536]{1,0:T(8,128)(2,1)S(1)}, bf16[256,1536]{1,0:T(8,128)(2,1)S(1)}, u32[]{:S(2)}, u32[]{:S(2)}) collective-permute-start(bf16[256,1536]{1,0:T(8,128)(2,1)S(1)} %get-tuple-element.60.refs_9_), channel_id=1, source_target_pairs={{0,1},{1,2},{2,3},{3,0},{4,5},{5,6},{6,7},{7,4},{8,9},{9,10},{10,1... | collective-permute-start | bytes 2359304 | tf_op jit(solution)/shard_map/ppermute | solution.py:411
  78.4 1.4 %collective-permute-start.14 = (bf16[528,128]{1,0:T(8,128)(2,1)S(1)}, bf16[528,128]{1,0:T(8,128)(2,1)S(1)}, u32[]{:S(2)}, u32[]{:S(2)}) collective-permute-start(bf16[528,128]{1,0:T(8,128)(2,1)S(1)} %get-tuple-element.65), channel_id=1, source_target_pairs={{0,4},{4,0},{8,12},{12,8},{16,20},{20,16},{24,28},{28,24},{32,36},... | collective-permute-start | bytes 405512 | tf_op jit(solution)/shard_map/ppermute | solution.py:202
  80.4 9.8 %collective-permute-start.17 = (bf16[528,128]{1,0:T(8,128)(2,1)S(1)}, bf16[528,128]{1,0:T(8,128)(2,1)S(1)}, u32[]{:S(2)}, u32[]{:S(2)}) collective-permute-start(bf16[528,128]{1,0:T(8,128)(2,1)S(1)} %chip_total.3.refs_3_.refs_1_), channel_id=1, source_target_pairs={{0,8},{4,12},{8,16},{12,20},{16,24},{20,28},{24,0},{28,4},{32,40},... | collective-permute-start | bytes 405512 | tf_op jit(solution)/shard_map/ppermute | solution.py:204
  80.4 9.7 %collective-permute-start.16 = (bf16[528,128]{1,0:T(8,128)(2,1)S(1)}, bf16[528,128]{1,0:T(8,128)(2,1)S(1)}, u32[]{:S(2)}, u32[]{:S(2)}) collective-permute-start(bf16[528,128]{1,0:T(8,128)(2,1)S(1)} %chip_total.3.refs_3_.refs_1_), channel_id=1, source_target_pairs={{0,16},{4,20},{8,24},{12,28},{16,0},{20,4},{24,8},{28,12},{32,48},... | collective-permute-start | bytes 405512 | tf_op jit(solution)/shard_map/ppermute | solution.py:204
  82.5 11.0 %collective-permute-start.15 = (bf16[528,128]{1,0:T(8,128)(2,1)S(1)}, bf16[528,128]{1,0:T(8,128)(2,1)S(1)}, u32[]{:S(2)}, u32[]{:S(2)}) collective-permute-start(bf16[528,128]{1,0:T(8,128)(2,1)S(1)} %chip_total.3.refs_3_.refs_1_), channel_id=1, source_target_pairs={{0,24},{4,28},{8,0},{12,4},{16,8},{20,12},{24,16},{28,20},{32,56},... | collective-permute-start | bytes 405512 | tf_op jit(solution)/shard_map/ppermute | solution.py:204
  83.9 1.2 copy-start.6
  90.2 35.6 %collective-permute-start.20 = (bf16[256,1536]{1,0:T(8,128)(2,1)S(1)}, bf16[256,1536]{1,0:T(8,128)(2,1)S(1)}, u32[]{:S(2)}, u32[]{:S(2)}) collective-permute-start(bf16[256,1536]{1,0:T(8,128)(2,1)S(1)} %get-tuple-element.69.refs_9_), channel_id=1, source_target_pairs={{0,1},{1,2},{2,3},{3,0},{4,5},{5,6},{6,7},{7,4},{8,9},{9,10},{10,1... | collective-permute-start | bytes 2359304 | tf_op jit(solution)/shard_map/ppermute | solution.py:411
  90.2 35.6 %collective-permute-start.19 = (bf16[256,1536]{1,0:T(8,128)(2,1)S(1)}, bf16[256,1536]{1,0:T(8,128)(2,1)S(1)}, u32[]{:S(2)}, u32[]{:S(2)}) collective-permute-start(bf16[256,1536]{1,0:T(8,128)(2,1)S(1)} %get-tuple-element.73), channel_id=1, source_target_pairs={{0,3},{1,0},{2,1},{3,2},{4,7},{5,4},{6,5},{7,6},{8,11},{9,8},{10,9... | collective-permute-start | bytes 2359304 | tf_op jit(solution)/shard_map/ppermute | solution.py:412
  95.1 31.5 %collective-permute-start.21 = (bf16[256,1536]{1,0:T(8,128)(2,1)S(1)}, bf16[256,1536]{1,0:T(8,128)(2,1)S(1)}, u32[]{:S(2)}, u32[]{:S(2)}) collective-permute-start(bf16[256,1536]{1,0:T(8,128)(2,1)S(1)} %get-tuple-element.74), channel_id=1, source_target_pairs={{0,3},{1,0},{2,1},{3,2},{4,7},{5,4},{6,5},{7,6},{8,11},{9,8},{10,9... | collective-permute-start | bytes 2359304 | tf_op jit(solution)/shard_map/ppermute | solution.py:412
  97.1 30.1 %collective-permute-start.18 = (bf16[256,1536]{1,0:T(8,128)(2,1)S(1)}, bf16[256,1536]{1,0:T(8,128)(2,1)S(1)}, u32[]{:S(2)}, u32[]{:S(2)}) collective-permute-start(bf16[256,1536]{1,0:T(8,128)(2,1)S(1)} %get-tuple-element.72.refs_10_), channel_id=1, source_target_pairs={{0,1},{1,2},{2,3},{3,0},{4,5},{5,6},{6,7},{7,4},{8,9},{9,10},{10,1... | collective-permute-start | bytes 2359304 | tf_op jit(solution)/shard_map/ppermute | solution.py:411
  97.2 8.1 %collective-permute-start.24 = (bf16[528,128]{1,0:T(8,128)(2,1)S(1)}, bf16[528,128]{1,0:T(8,128)(2,1)S(1)}, u32[]{:S(2)}, u32[]{:S(2)}) collective-permute-start(bf16[528,128]{1,0:T(8,128)(2,1)S(1)} %get-tuple-element.79), channel_id=1, source_target_pairs={{96,0},{100,4},{104,8},{108,12},{112,16},{116,20},{120,24},{124,28... | collective-permute-start | bytes 405512 | tf_op jit(solution)/shard_map/ppermute | solution.py:214
  105.3 8.4 %collective-permute-start.23 = (bf16[528,128]{1,0:T(8,128)(2,1)S(1)}, bf16[528,128]{1,0:T(8,128)(2,1)S(1)}, u32[]{:S(2)}, u32[]{:S(2)}) collective-permute-start(bf16[528,128]{1,0:T(8,128)(2,1)S(1)} %get-tuple-element.79), channel_id=1, source_target_pairs={{64,0},{68,4},{72,8},{76,12},{80,16},{84,20},{88,24},{92,28},{96,3... | collective-permute-start | bytes 405512 | tf_op jit(solution)/shard_map/ppermute | solution.py:214
  113.7 6.9 %collective-permute-start.22 = (bf16[528,128]{1,0:T(8,128)(2,1)S(1)}, bf16[528,128]{1,0:T(8,128)(2,1)S(1)}, u32[]{:S(2)}, u32[]{:S(2)}) collective-permute-start(bf16[528,128]{1,0:T(8,128)(2,1)S(1)} %get-tuple-element.79), channel_id=1, source_target_pairs={{32,0},{36,4},{40,8},{44,12},{48,16},{52,20},{56,24},{60,28},{64,3... | collective-permute-start | bytes 405512 | tf_op jit(solution)/shard_map/ppermute | solution.py:214
  121.3 1.4 %collective-permute-start.25 = (bf16[512,128]{1,0:T(8,128)(2,1)S(1)}, bf16[512,128]{1,0:T(8,128)(2,1)S(1)}, u32[]{:S(2)}, u32[]{:S(2)}) collective-permute-start(bf16[512,128]{1,0:T(8,128)(2,1)S(1)} %get-tuple-element.82), channel_id=1, source_target_pairs={{0,4},{4,0},{8,12},{12,8},{16,20},{20,16},{24,28},{28,24},{32,36},... | collective-permute-start | bytes 393224 | tf_op jit(solution)/shard_map/ppermute | solution.py:224
  127.3 1.2 copy-start.8

commit v3 on v2

--- a/solution.py
+++ b/solution.py
@@ -11,6 +11,7 @@
 F32 = jnp.float32
 BF16 = jnp.bfloat16
 MIB = 1024 * 1024
+GIGA = 10**9
 
 NN = (((1,), (0,)), ((), ()))
 NT = (((1,), (1,)), ((), ()))
@@ -24,9 +25,31 @@
 VMEM = pl.BlockSpec(memory_space=pltpu.VMEM)
 SMEM = pl.BlockSpec(memory_space=pltpu.SMEM)
 ANY = pl.BlockSpec(memory_space=pl.ANY)
-
-
-def call(kernel, name, scalars, args, outs, after=(), flops=0):
+HBM = pl.BlockSpec(memory_space=pltpu.HBM)
+
+
+COST = dict(
+    own_states=4 * GIGA,
+    chip_total=GIGA // 2,
+    local=5 * GIGA,
+    row_total=GIGA // 2,
+    grad_own=2 * GIGA,
+    arrive=GIGA // 2,
+    split=GIGA // 2,
+    attend=GIGA,
+    grad_near=4 * GIGA,
+    project_far=2 * GIGA,
+    project_near=4 * GIGA,
+    project_own=2 * GIGA,
+    grad_far=6 * GIGA,
+    join=GIGA,
+    inside=8 * GIGA,
+    finish=3 * GIGA,
+    total=2 * GIGA,
+)
+
+
+def call(kernel, name, scalars, args, outs, after=(), far=(), far_outs=(), scratch=(), room=12):
     count, waits = len(args), len(after)
 
     def run(*refs):
@@ -35,10 +58,11 @@
     return pl.pallas_call(
         run,
         out_shape=[jax.ShapeDtypeStruct(shape, dtype) for shape, dtype in outs],
-        in_specs=[SMEM] + [VMEM] * count + [ANY] * waits,
-        out_specs=[VMEM] * len(outs),
-        compiler_params=pltpu.CompilerParams(vmem_limit_bytes=12 * MIB),
-        cost_estimate=pl.CostEstimate(flops=flops, bytes_accessed=0, transcendentals=0),
+        in_specs=[SMEM] + [HBM if i in far else VMEM for i in range(count)] + [ANY] * waits,
+        out_specs=[HBM if i in far_outs else VMEM for i in range(len(outs))],
+        scratch_shapes=list(scratch),
+        compiler_params=pltpu.CompilerParams(vmem_limit_bytes=room * MIB),
+        cost_estimate=pl.CostEstimate(flops=COST[name], bytes_accessed=0, transcendentals=0),
         name=name,
     )(scalars, *args, *after)
 
@@ -90,8 +114,21 @@
     send_ref[512:528, :] = pack_decays(jnp.where(swap, last[0:4], last[4:8]))
 
 
-def state_kernel(s_ref, ld_ref, k_ref, v_ref, cum_ref, cumt_ref, mine_ref, send_ref):
+def state_kernel(s_ref, ld_ref, q_hbm, k_hbm, v_hbm, cum_ref, cumt_ref, mine_ref, send_ref, q_ref, k_ref, v_ref, sems):
     core = s_ref[6]
+    loads = []
+    for part in range(4):
+        cols = slice(part * 256, part * 256 + 256)
+        pair = [
+            pltpu.make_async_copy(far.at[:, cols], near.at[:, cols], sems.at[part * 2 + i])
+            for i, (far, near) in enumerate(((k_hbm, k_ref), (v_hbm, v_ref)))
+        ]
+        for copy in pair:
+            copy.start()
+        loads.append(pair)
+    load_q = pltpu.make_async_copy(q_hbm, q_ref, sems.at[8])
+    load_q.start()
+
     rows = lax.broadcasted_iota(jnp.int32, (512, 512), 0)
     cols = lax.broadcasted_iota(jnp.int32, (512, 512), 1)
     upper = jnp.where(rows <= cols, 1.0, 0.0).astype(BF16)
@@ -105,19 +142,27 @@
     cumt_ref[...] = cum_t
     fall = jnp.exp(cum[511:512, :] - cum)
     for head in range(8):
+        if head % 2 == 0:
+            for copy in loads[head // 2]:
+                copy.wait()
         at = head_columns(head)
         faded = (k_ref[:, at].astype(F32) * fall[:, head : head + 1]).astype(BF16)
         put_state(core, head, dot(faded, v_ref[:, at], TN).astype(BF16), mine_ref, send_ref)
     put_decays(core, cum_t, mine_ref, send_ref)
-
-
-def own_states(scalars, logdecay_t, keys, values):
+    load_q.wait()
+
+
+def own_states(scalars, logdecay_t, queries, keys, values):
+    held = ((512, 1024), BF16)
     return call(
         state_kernel,
         "own_states",
         scalars,
-        (logdecay_t, keys, values),
-        [((512, 8), F32), ((8, 512), F32), MESSAGE, MESSAGE],
+        (logdecay_t, queries, keys, values),
+        [((512, 8), F32), ((8, 512), F32), MESSAGE, MESSAGE, held, held, held],
+        far=(1, 2, 3),
+        scratch=[pltpu.SemaphoreType.DMA((9,))],
+        room=50,
     )
 
 
@@ -231,19 +276,40 @@
     return jnp.exp(jnp.where(rows >= cols, diff, -1e30))
 
 
-def local_kernel(s_ref, cum_ref, cumt_ref, q_ref, k_ref, v_ref, out_ref):
+def local_kernel(s_ref, cum_ref, cumt_ref, q_ref, k_ref, v_ref, w_hbm, out_ref, scaled_ref, turned_ref, w_ref, sems):
+    loads = []
+    for part in range(4):
+        rows = slice(part * 256, part * 256 + 256)
+        loads.append(pltpu.make_async_copy(w_hbm.at[rows, :], w_ref.at[rows, :], sems.at[part]))
+        loads[-1].start()
     cum, cum_t = cum_ref[...], cumt_ref[...]
+    rise = jnp.exp(cum)
     for head in range(8):
         at = head_columns(head)
+        scaled = q_ref[:, at].astype(F32) * rise[:, head : head + 1]
+        scaled_ref[:, at] = scaled.astype(BF16)
+        turned_ref[at, :] = scaled.T.astype(BF16)
         for low in (0, 256):
             high = low + 256
             table = decay_block(cum, cum_t, head, low, high)
             probs = (dot(q_ref[low:high, at], k_ref[:high, at], NT) * table).astype(BF16)
             out_ref[low:high, at] = dot(probs, v_ref[:high, at])
-
-
-def local(scalars, cum, cum_t, q, k, v, after):
-    return call(local_kernel, "local", scalars, (cum, cum_t, q, k, v), [((512, 1024), F32)], after)
+    for copy in loads:
+        copy.wait()
+
+
+def local(scalars, cum, cum_t, q, k, v, weight, after):
+    return call(
+        local_kernel,
+        "local",
+        scalars,
+        (cum, cum_t, q, k, v, weight),
+        [((512, 1024), F32), ((512, 1024), BF16), ((1024, 512), BF16), ((1024, 6144), BF16)],
+        after,
+        far=(5,),
+        room=34,
+        scratch=[pltpu.SemaphoreType.DMA((4,))],
+    )
 
 
 def arrived(s_ref, head, keep_ref, got_ref):
@@ -251,29 +317,19 @@
     return jnp.where(s_ref[6] == head // 4, keep_ref[rows, :], got_ref[rows, :])
 
 
-def attend_kernel(s_ref, local_ref, cum_ref, q_ref, keep_ref, got_ref, normed_ref, att_ref):
-    rise = jnp.exp(cum_ref[...])
+def attend_kernel(s_ref, local_ref, scaled_ref, keep_ref, got_ref, normed_ref, unit_ref, scale_ref):
     for head in range(8):
         at = head_columns(head)
-        past = dot(q_ref[:, at], arrived(s_ref, head, keep_ref, got_ref))
-        att = local_ref[:, at] + rise[:, head : head + 1] * past
-        att_ref[:, at] = att
+        att = local_ref[:, at] + dot(scaled_ref[:, at], arrived(s_ref, head, keep_ref, got_ref))
         scale = lax.rsqrt(jnp.mean(att * att, axis=1, keepdims=True) + EPS)
-        normed_ref[:, at] = (att * scale).astype(BF16)
-
-
-def attend(scalars, local_part, cum, q, keep, got, after):
-    return call(
-        attend_kernel,
-        "attend",
-        scalars,
-        (local_part, cum, q, keep, got),
-        [((512, 1024), BF16), ((512, 1024), F32)],
-        after,
-    )
+        unit = att * scale
+        unit_ref[:, at] = unit
+        scale_ref[:, at] = jnp.broadcast_to(scale, unit.shape)
+        normed_ref[:, at] = unit.astype(BF16)
 
 
 HALF = ((256, 1536), BF16)
+WHOLE = ((512, 1536), BF16)
 WIDE_HALF = ((256, 1536), F32)
 
 
@@ -303,19 +359,25 @@
     bottom_ref[...] = b_ref[256:, :]
 
 
-def round_kernel(s_ref, a_ref, b_ref, a_out, b_out):
-    a_out[...] = a_ref[...].astype(BF16)
-    b_out[...] = b_ref[...].astype(BF16)
-
-
-def join_kernel(s_ref, right_ref, from_left, left_ref, from_right, out_right, out_left):
-    out_right[...] = (right_ref[...] + from_left[...].astype(F32)).astype(BF16)
-    out_left[...] = (left_ref[...] + from_right[...].astype(F32)).astype(BF16)
-
-
-def total_kernel(s_ref, top_ref, bottom_ref, top_a, top_b, bottom_a, bottom_b, out_ref):
-    out_ref[:256, :] = (top_ref[...] + top_a[...].astype(F32) + top_b[...].astype(F32)).astype(BF16)
-    out_ref[256:, :] = (bottom_ref[...] + bottom_a[...].astype(F32) + bottom_b[...].astype(F32)).astype(BF16)
+def join_kernel(s_ref, right_top, right_bottom, left_top, left_bottom, from_left, from_right, out_right, out_left):
+    out_right[:256, :] = (right_top[...] + from_left[...].astype(F32)).astype(BF16)
+    out_right[256:, :] = right_bottom[...]
+    out_left[:256, :] = left_top[...]
+    out_left[256:, :] = (left_bottom[...] + from_right[...].astype(F32)).astype(BF16)
+
+
+def total_kernel(s_ref, top_ref, bottom_ref, a_ref, b_ref, out_ref, out_held, sems):
+    copies = []
+    for i, own_ref in enumerate((top_ref, bottom_ref)):
+        for j in range(2):
+            rows = slice(j * 128, j * 128 + 128)
+            here = slice(i * 256 + j * 128, i * 256 + j * 128 + 128)
+            total = own_ref[rows, :] + a_ref[here, :].astype(F32) + b_ref[here, :].astype(F32)
+            out_held[here, :] = total.astype(BF16)
+            copies.append(pltpu.make_async_copy(out_held.at[here, :], out_ref.at[here, :], sems.at[i * 2 + j]))
+            copies[-1].start()
+    for copy in copies:
+        copy.wait()
 
 
 def grad_own_kernel(s_ref, x_ref, w_ref, out_ref):
@@ -334,9 +396,10 @@
         )
 
 
-def grad_far_kernel(s_ref, c_ref, d_ref, w_ref, acc_ref, att_ref, q_ref, cum_ref, cumt_ref, grad_ref, mine_ref, send_ref):
+def grad_far_kernel(
+    s_ref, c_ref, d_ref, w_ref, acc_ref, unit_ref, scale_ref, turned_ref, cumt_ref, grad_ref, mine_ref, send_ref
+):
     core = s_ref[6]
-    rise = jnp.exp(cum_ref[...])
     x = jnp.concatenate([c_ref[...], d_ref[...]], axis=0)
     for low in range(0, 1024, 256):
         rows = slice(low, low + 256)
@@ -344,26 +407,19 @@
         for i in range(2):
             head = low // 128 + i
             at = head_columns(head)
-            att, grad = att_ref[:, at], acc[:, i * 128 : i * 128 + 128]
-            scale = lax.rsqrt(jnp.mean(att * att, axis=1, keepdims=True) + EPS)
-            unit = att * scale
-            out = (scale * (grad - unit * jnp.mean(grad * unit, axis=1, keepdims=True))).astype(BF16)
+            unit, grad = unit_ref[:, at], acc[:, i * 128 : i * 128 + 128]
+            along = jnp.mean(grad * unit, axis=1, keepdims=True)
+            out = (scale_ref[:, at] * (grad - unit * along)).astype(BF16)
             grad_ref[:, at] = out
-            scaled = (q_ref[:, at].astype(F32) * rise[:, head : head + 1]).astype(BF16)
-            put_state(core, head, dot(scaled, out, TN).astype(BF16), mine_ref, send_ref)
+            put_state(core, head, dot(turned_ref[at, :], out).astype(BF16), mine_ref, send_ref)
     put_decays(core, cumt_ref[...], mine_ref, send_ref)
 
 
-def inside_kernel(heads, s_ref, cum_ref, cumt_ref, q_ref, k_ref, v_ref, g_ref, keep_ref, got_ref, *refs):
-    gq_ref, gk_ref, gv_ref = refs[-3:]
+def inside_kernel(s_ref, cum_ref, cumt_ref, q_ref, k_ref, v_ref, g_ref, keep_ref, got_ref, gq_ref, gk_ref, gv_ref):
     cum, cum_t = cum_ref[...], cumt_ref[...]
     rise = jnp.exp(cum)
-    if len(refs) > 3:
-        gq_ref[:, :512] = refs[0][...]
-    for head in heads:
+    for head in range(8):
         at = head_columns(head)
-        to = head_columns(head - heads[0])
-        to_q = at if len(refs) > 3 else to
         incoming = arrived(s_ref, head, keep_ref, got_ref)
         early_k = early_v = None
         for low in (0, 256):
@@ -374,27 +430,37 @@
             probs = (dot(q, k, NT) * table).astype(BF16)
             scores = (dot(g, v, NT) * table).astype(BF16)
             gq = dot(scores, k) + rise[low:high, head : head + 1] * dot(g, incoming, NT)
-            gq_ref[low:high, to_q] = gq.astype(BF16)
+            gq_ref[low:high, at] = gq.astype(BF16)
             part_k, part_v = dot(scores, q, TN), dot(probs, g, TN)
             if low == 0:
                 early_k, early_v = part_k, part_v
             else:
-                gk_ref[:256, to] = early_k + part_k[:256]
-                gk_ref[256:, to] = part_k[256:]
-                gv_ref[:256, to] = early_v + part_v[:256]
-                gv_ref[256:, to] = part_v[256:]
-
-
-def finish_kernel(s_ref, cum_ref, k_ref, v_ref, gk_a, gv_a, gk_b, gv_b, keep_ref, got_ref, gk_out, gv_out):
+                gk_ref[:256, at] = early_k + part_k[:256]
+                gk_ref[256:, at] = part_k[256:]
+                gv_ref[:256, at] = early_v + part_v[:256]
+                gv_ref[256:, at] = part_v[256:]
+
+
+def finish_kernel(
+    s_ref, cum_ref, k_ref, v_ref, gk_ref, gv_ref, keep_ref, got_ref, gk_out, gv_out, order_ref, gk_held, gv_held, sems
+):
     cum = cum_ref[...]
     fall = jnp.exp(cum[511:512, :] - cum)
+    copies = []
     for head in range(8):
-        at, part = head_columns(head), head_columns(head % 4)
-        gk_ref, gv_ref = ((gk_a, gv_a), (gk_b, gv_b))[head // 4]
+        at = head_columns(head)
         outgoing = arrived(s_ref, head, keep_ref, got_ref)
         factor = fall[:, head : head + 1]
-        gk_out[:, at] = (gk_ref[:, part] + factor * dot(v_ref[:, at], outgoing, NT)).astype(BF16)
-        gv_out[:, at] = (gv_ref[:, part] + factor * dot(k_ref[:, at], outgoing)).astype(BF16)
+        gk_held[:, at] = (gk_ref[:, at] + factor * dot(v_ref[:, at], outgoing, NT)).astype(BF16)
+        gv_held[:, at] = (gv_ref[:, at] + factor * dot(k_ref[:, at], outgoing)).astype(BF16)
+        if head % 2 == 1:
+            done = slice(head * 128 - 128, head * 128 + 128)
+            for i, (held, out) in enumerate(((gk_held, gk_out), (gv_held, gv_out))):
+                copies.append(pltpu.make_async_copy(held.at[:, done], out.at[:, done], sems.at[head - 1 + i]))
+                copies[-1].start()
+    order_ref[...] = jnp.zeros((8, 128), F32)
+    for copy in copies:
+        copy.wait()
 
 
 RIGHT = [(i, (i + 1) % 4) for i in range(4)]
@@ -411,85 +477,77 @@
     right = lambda a: lax.ppermute(a, "head", RIGHT)
     left = lambda a: lax.ppermute(a, "head", LEFT)
     wide, narrow = ((512, 1024), F32), ((512, 1024), BF16)
-    wide_part, narrow_part = ((512, 512), F32), ((512, 512), BF16)
 
     a, b = right(output_gradient), left(output_gradient)
 
-    cum, cum_t, mine, send = own_states(scalars, logdecay.T, keys, values)
-    keep, got, (local_part,), (acc,) = scan_blocks(
+    cum, cum_t, mine, send, q, k, v = own_states(scalars, logdecay.T, queries, keys, values)
+    keep, got, (local_part, scaled, turned, w), (acc,) = scan_blocks(
         scalars,
         mine,
         send,
         1,
         (
-            lambda after: local(scalars, cum, cum_t, queries, keys, values, after),
-            lambda after, _: call(grad_own_kernel, "grad_own", scalars, (output_gradient, weight), [wide], after),
+            lambda after: local(scalars, cum, cum_t, q, k, v, weight, after),
+            lambda after, one: call(grad_own_kernel, "grad_own", scalars, (output_gradient, one[3]), [wide], after),
         ),
     )
-    a_top, b_bottom = call(split_kernel, "split", scalars, (a, b), [HALF, HALF], (keep,))
+    a_top, b_bottom = call(
+        split_kernel,
+        "split",
+        scalars,
+        (a, b),
+        [HALF, HALF],
+        (keep,),
+    )
     c, d = right(a_top), left(b_bottom)
-    normed, att = attend(scalars, local_part, cum, queries, keep, got, (a_top,))
-
-    (acc,) = call(grad_near_kernel, "grad_near", scalars, (a, b, weight, acc), [wide], (att,))
-    near = call(project_near_kernel, "project_near", scalars, (normed, weight), [WIDE_HALF] * 4, (acc,))
-    right_top, right_bottom, left_top, left_bottom = near
-    own = call(
-        functools.partial(project_one_kernel, 3), "project_own", scalars, (normed, weight), [WIDE_HALF] * 2, near[:1]
-    )
-    far = call(functools.partial(project_one_kernel, 7), "project_far", scalars, (normed, weight), [HALF] * 2, own[:1])
+    normed, unit, scale = call(
+        attend_kernel, "attend", scalars, (local_part, scaled, keep, got), [narrow, wide, wide], (a_top,)
+    )
+
+    (acc,) = call(grad_near_kernel, "grad_near", scalars, (a, b, w, acc), [wide], (unit,))
+    far = call(functools.partial(project_one_kernel, 7), "project_far", scalars, (normed, w), [HALF] * 2, (acc,))
     from_left, from_right = right(far[0]), left(far[1])
+    near = call(
+        project_near_kernel, "project_near", scalars, (normed, w), [WIDE_HALF, HALF, HALF, WIDE_HALF], far[:1]
+    )
+    own = call(functools.partial(project_one_kernel, 3), "project_own", scalars, (normed, w), [WIDE_HALF] * 2, near[:1])
     grad, mine_g, send_g = call(
         grad_far_kernel,
         "grad_far",
         scalars,
-        (c, d, weight, acc, att, queries, cum, cum_t),
+        (c, d, w, acc, unit, scale, turned, cum_t),
         [narrow, MESSAGE, MESSAGE],
-        far[:1],
-    )
-    inputs = (cum, cum_t, queries, keys, values, grad, keep, got)
-    direct, joined = [], []
+        own[:1],
+    )
+    inputs = (cum, cum_t, q, k, v, grad, keep, got)
 
     def first(after):
-        direct.extend(call(round_kernel, "direct", scalars, (right_bottom, left_top), [HALF, HALF], after))
-        return call(
-            functools.partial(inside_kernel, range(0, 4)),
-            "inside_a",
-            scalars,
-            inputs,
-            [narrow_part, wide_part, wide_part],
-            direct[:1],
-        )
-
-    def second(after, one):
-        joined.extend(
-            call(join_kernel, "join", scalars, (right_top, from_left, left_bottom, from_right), [HALF, HALF], after)
-        )
-        return call(
-            functools.partial(inside_kernel, range(4, 8)),
-            "inside_b",
-            scalars,
-            inputs + (one[0],),
-            [narrow, wide_part, wide_part],
-            joined[:1],
-        )
-
-    keep_g, got_g, (_, gk_a, gv_a), (gq, gk_b, gv_b) = scan_blocks(scalars, mine_g, send_g, -1, (first, second))
-    direct_r, direct_l = right(direct[0]), left(direct[1])
+        parts = (*near, from_left, from_right)
+        return call(join_kernel, "join", scalars, parts, [WHOLE, WHOLE], after)
+
+    def second(after, _):
+        return call(inside_kernel, "inside", scalars, inputs, [narrow, wide, wide], after)
+
+    keep_g, got_g, joined, (gq, gk, gv) = scan_blocks(scalars, mine_g, send_g, -1, (first, second))
     joined_r, joined_l = right(joined[0]), left(joined[1])
-    gk, gv = call(
+    gk, gv, order = call(
         finish_kernel,
         "finish",
         scalars,
-        (cum, keys, values, gk_a, gv_a, gk_b, gv_b, keep_g, got_g),
-        [narrow, narrow],
+        (cum, k, v, gk, gv, keep_g, got_g),
+        [narrow, narrow, ((8, 128), F32)],
+        far_outs=(0, 1),
+        scratch=[pltpu.VMEM((512, 1024), BF16), pltpu.VMEM((512, 1024), BF16), pltpu.SemaphoreType.DMA((8,))],
     )
     (out,) = call(
         total_kernel,
         "total",
         scalars,
-        (*own, joined_r, direct_l, direct_r, joined_l),
-        [((512, 1536), BF16)],
-        (gk,),
+        (*own, joined_r, joined_l),
+        [WHOLE],
+        (order,),
+        far_outs=(0,),
+        scratch=[pltpu.VMEM((512, 1536), BF16), pltpu.SemaphoreType.DMA((4,))],
     )
     return out, gq, gk, gv
 

time: 131 us -> 116 us (0.89)
  local copies, waits for them, and re-layouts: 10.8 us -> 0.81 us
  Pallas kernels: 54.3 us -> 51 us
  waiting for transfers between devices: 27.4 us -> 25.5 us
    ppermute x6, waiting for transfers between devices: 15.1 us -> 2.05 us  [scan_blocks(): planes = [lax.ppermute(total, 'seq', shifts_z(sign * k)) for k in (1, 2, 3)]]
    ppermute x5 -> x4, waiting for transfers between devices: 0.74 us -> 12.7 us  [body(): right = lambda a: lax.ppermute(a, 'head', RIGHT)]
    unnamed x26 -> x4, local copies, waits for them, and re-layouts: 10.7 us -> 0.73 us
    ppermute x5 -> x4, starting transfers between devices: 15.1 us -> 8.97 us  [body(): left = lambda a: lax.ppermute(a, 'head', LEFT)]
    ppermute x5 -> x4, starting transfers between devices: 0.03 us -> 4.29 us  [body(): right = lambda a: lax.ppermute(a, 'head', RIGHT)]
    pallas_call x22 -> x20, Pallas kernels: 54.3 us -> 51 us  [call(): pl.pallas_call(run, out_shape=[jax.ShapeDtypeStruct(shape, dtype) for sha...]
    ppermute x6, starting transfers between devices: 8.01 us -> 9.46 us  [scan_blocks(): lax.ppermute(chip, 'seq', shifts_x(sign * k))]
    ppermute x2, waiting for transfers between devices: 2.68 us -> 1.34 us  [scan_blocks(): return (keep, lax.ppermute(send_back, 'seq', SWAP), first, second)]
  transfers between devices with their start and end apart: 26 -> 24, of which waited for: 13 -> 13; matrix products, arithmetic and copies ran while one was open for 0% -> 0% of each run, Pallas kernels for 39% -> 42%
where the time goes in v3:
time: 116 us
  Pallas kernels  51 us (44%)
  starting transfers between devices  37.7 us (33%)
  waiting for transfers between devices  25.5 us (22%)
    pallas_call x20, Pallas kernels, call(): pl.pallas_call(run, out_shape=[jax.ShapeDtypeStruct(shape, dtype) for sha...  51 us
    ppermute x6, starting transfers between devices, scan_blocks(): planes = [lax.ppermute(total, 'seq', shifts_z(sign * k)) for k in (1, 2, 3)]  14.5 us
    ppermute x4, waiting for transfers between devices, body(): right = lambda a: lax.ppermute(a, 'head', RIGHT)  12.7 us
    ppermute x6, starting transfers between devices, scan_blocks(): lax.ppermute(chip, 'seq', shifts_x(sign * k))  9.46 us
    ppermute x4, starting transfers between devices, body(): left = lambda a: lax.ppermute(a, 'head', LEFT)  8.97 us
    ppermute x6, waiting for transfers between devices, scan_blocks(): lax.ppermute(chip, 'seq', shifts_x(sign * k))  6.24 us
    ppermute x4, starting transfers between devices, body(): right = lambda a: lax.ppermute(a, 'head', RIGHT)  4.29 us
    ppermute x2, waiting for transfers between devices, scan_blocks(): got = lax.ppermute(send, 'seq', SWAP)  2.68 us
  transfers between devices with their start and end apart: 24, of which 13 were waited for; matrix products, arithmetic and copies ran while one was open for 0% of the time, Pallas kernels for 42%

profile of v3, /device:TPU:0, one launch (start us, length us, event | category | flops | bytes accessed | tf_op | source)
XLA Modules:
  0.0 116.0 jit_solution(15254528679726687605)
XLA Ops:
  0.6 1.7 %collective-permute-start.8 = (bf16[512,1536]{1,0:T(8,128)(2,1)}, bf16[512,1536]{1,0:T(8,128)(2,1)S(1)}, u32[]{:S(2)}, u32[]{:S(2)}) collective-permute-start(bf16[512,1536]{1,0:T(8,128)(2,1)} %refs_1_.1), channel_id=1, source_target_pairs={{0,1},{1,2},{2,3},{3,0},{4,5},{5,6},{6,7},{7,4},{8,9},{9,10},{10,1... | collective-permute-start | bytes 4718600 | tf_op jit(solution)/shard_map/ppermute | solution.py:477
  2.4 1.6 %collective-permute-start.9 = (bf16[512,1536]{1,0:T(8,128)(2,1)}, bf16[512,1536]{1,0:T(8,128)(2,1)S(1)}, u32[]{:S(2)}, u32[]{:S(2)}) collective-permute-start(bf16[512,1536]{1,0:T(8,128)(2,1)} %refs_1_.1), channel_id=1, source_target_pairs={{0,3},{1,0},{2,1},{3,2},{4,7},{5,4},{6,5},{7,6},{8,11},{9,8},{10,9... | collective-permute-start | bytes 4718600 | tf_op jit(solution)/shard_map/ppermute | solution.py:478
  4.0 0.7 copy-done.1
  4.7 5.0 %own_states.1 = (f32[512,8]{1,0:T(8,128)S(1)}, f32[8,512]{1,0:T(8,128)S(1)}, bf16[528,128]{1,0:T(8,128)(2,1)S(1)}, bf16[528,128]{1,0:T(8,128)(2,1)S(1)}, bf16[51...) custom-call(s32[11]{0:T(128)S(1)} %stack.44.refs_0_, f32[8,512]{1,0:T(8,128)S(1)} %bitcast.11, ...), custom_call_target="tpu_custom_call" | custom-call | flops 4000000000 | tf_op jit(solution)/shard_map/own_states/pallas_call | solution.py:58
  9.8 1.3 %collective-permute-done.refs_2_.refs_7_ = bf16[528,128]{1,0:T(8,128)(2,1)S(1)} collective-permute-done((bf16[528,128]{1,0:T(8,128)(2,1)S(1)}, bf16[528,128]{1,0:T(8,128)(2,1)S(1)}, u32[]{:S(2)}, u32[]{:S(2)}) %collective-permute-start) | collective-permute-done | bytes 135200 | tf_op jit(solution)/shard_map/ppermute | solution.py:247
  11.8 1.6 %collective-permute-start.1 = (bf16[528,128]{1,0:T(8,128)(2,1)S(1)}, bf16[528,128]{1,0:T(8,128)(2,1)S(1)}, u32[]{:S(2)}, u32[]{:S(2)}) collective-permute-start(bf16[528,128]{1,0:T(8,128)(2,1)S(1)} %chip_total.2.refs_7_.refs_1_), channel_id=1, source_target_pairs={{0,8},{4,12},{8,16},{12,20},{16,24},{20,28},{24,0},{28,4},{32,40},... | collective-permute-start | bytes 405512 | tf_op jit(solution)/shard_map/ppermute | solution.py:249
  13.4 2.7 %collective-permute-start.2 = (bf16[528,128]{1,0:T(8,128)(2,1)S(1)}, bf16[528,128]{1,0:T(8,128)(2,1)S(1)}, u32[]{:S(2)}, u32[]{:S(2)}) collective-permute-start(bf16[528,128]{1,0:T(8,128)(2,1)S(1)} %chip_total.2.refs_7_.refs_1_), channel_id=1, source_target_pairs={{0,16},{4,20},{8,24},{12,28},{16,0},{20,4},{24,8},{28,12},{32,48},... | collective-permute-start | bytes 405512 | tf_op jit(solution)/shard_map/ppermute | solution.py:249
  16.1 1.4 %collective-permute-start.3 = (bf16[528,128]{1,0:T(8,128)(2,1)S(1)}, bf16[528,128]{1,0:T(8,128)(2,1)S(1)}, u32[]{:S(2)}, u32[]{:S(2)}) collective-permute-start(bf16[528,128]{1,0:T(8,128)(2,1)S(1)} %chip_total.2.refs_7_.refs_1_), channel_id=1, source_target_pairs={{0,24},{4,28},{8,0},{12,4},{16,8},{20,12},{24,16},{28,20},{32,56},... | collective-permute-start | bytes 405512 | tf_op jit(solution)/shard_map/ppermute | solution.py:249
  17.6 5.5 %local.1 = (f32[512,1024]{1,0:T(8,128)S(1)}, bf16[512,1024]{1,0:T(8,128)(2,1)S(1)}, bf16[1024,512]{1,0:T(8,128)(2,1)S(1)}, bf16[1024,6144]{1,0:T(8,128)(2,1)S(1)}) custom-call(s32[11]{0:T(128)S(1)} %stack.44.refs_0_, f32[512,8]{1,0:T(8,128)S(1)} %get-tuple-element.49.refs_1_, f32[8,512]{1,0:T(8,128)S(1)} %get-tuple-element.50.refs_2_.refs_8_, ...), custom_call_target="tpu_custom_call" | custom-call | flops 5000000000 | tf_op jit(solution)/shard_map/local/pallas_call | solution.py:58
  23.1 0.7 row_total.2
  23.8 3.8 %collective-permute-start.4 = (bf16[528,128]{1,0:T(8,128)(2,1)S(1)}, bf16[528,128]{1,0:T(8,128)(2,1)S(1)}, u32[]{:S(2)}, u32[]{:S(2)}) collective-permute-start(bf16[528,128]{1,0:T(8,128)(2,1)S(1)} %get-tuple-element.59), channel_id=1, source_target_pairs={{0,32},{4,36},{8,40},{12,44},{16,48},{20,52},{24,56},{28,60},{32,6... | collective-permute-start | bytes 405512 | tf_op jit(solution)/shard_map/ppermute | solution.py:259
  27.6 5.5 %collective-permute-start.5 = (bf16[528,128]{1,0:T(8,128)(2,1)S(1)}, bf16[528,128]{1,0:T(8,128)(2,1)S(1)}, u32[]{:S(2)}, u32[]{:S(2)}) collective-permute-start(bf16[528,128]{1,0:T(8,128)(2,1)S(1)} %get-tuple-element.59), channel_id=1, source_target_pairs={{0,64},{4,68},{8,72},{12,76},{16,80},{20,84},{24,88},{28,92},{32,9... | collective-permute-start | bytes 405512 | tf_op jit(solution)/shard_map/ppermute | solution.py:259
  33.1 1.3 %collective-permute-start.6 = (bf16[528,128]{1,0:T(8,128)(2,1)S(1)}, bf16[528,128]{1,0:T(8,128)(2,1)S(1)}, u32[]{:S(2)}, u32[]{:S(2)}) collective-permute-start(bf16[528,128]{1,0:T(8,128)(2,1)S(1)} %get-tuple-element.59), channel_id=1, source_target_pairs={{0,96},{4,100},{8,104},{12,108},{16,112},{20,116},{24,120},{28,124... | collective-permute-start | bytes 405512 | tf_op jit(solution)/shard_map/ppermute | solution.py:259
  34.5 2.4 %grad_own.1.refs_8_.refs_4_ = f32[512,1024]{1,0:T(8,128)S(1)} custom-call(s32[11]{0:T(128)S(1)} %stack.44.refs_0_, bf16[512,1536]{1,0:T(8,128)(2,1)S(1)} %copy-done, bf16[1024,6144]{1,0:T(8,128)(2,1)S(1)} %get-tuple-element.58.refs_5_.refs_2_.refs_3_, f32[8,128]{1,0:T(8,128)S(1)} %get-tuple-element.61.refs_3_.refs_5_), custom_call_target="tpu_custom_call" | custom-call | flops 2000000000 | tf_op jit(solution)/shard_map/grad_own/pallas_call | solution.py:58
  37.0 0.7 arrive.2
  37.8 0.6 collective-permute-done.8.refs_1_
  38.4 0.6 split.1
  39.1 1.6 %collective-permute-start.12 = (bf16[256,1536]{1,0:T(8,128)(2,1)S(1)}, bf16[256,1536]{1,0:T(8,128)(2,1)S(1)}, u32[]{:S(2)}, u32[]{:S(2)}) collective-permute-start(bf16[256,1536]{1,0:T(8,128)(2,1)S(1)} %get-tuple-element.64.refs_5_), channel_id=1, source_target_pairs={{0,1},{1,2},{2,3},{3,0},{4,5},{5,6},{6,7},{7,4},{8,9},{9,10},{10,1... | collective-permute-start | bytes 2359304 | tf_op jit(solution)/shard_map/ppermute | solution.py:477
  40.7 1.7 %collective-permute-start.13 = (bf16[256,1536]{1,0:T(8,128)(2,1)S(1)}, bf16[256,1536]{1,0:T(8,128)(2,1)S(1)}, u32[]{:S(2)}, u32[]{:S(2)}) collective-permute-start(bf16[256,1536]{1,0:T(8,128)(2,1)S(1)} %get-tuple-element.75), channel_id=1, source_target_pairs={{0,3},{1,0},{2,1},{3,2},{4,7},{5,4},{6,5},{7,6},{8,11},{9,8},{10,9... | collective-permute-start | bytes 2359304 | tf_op jit(solution)/shard_map/ppermute | solution.py:478
  42.4 1.5 %attend.1 = (bf16[512,1024]{1,0:T(8,128)(2,1)S(1)}, f32[512,1024]{1,0:T(8,128)S(1)}, f32[512,1024]{1,0:T(8,128)S(1)}) custom-call(s32[11]{0:T(128)S(1)} %stack.44.refs_0_, f32[512,1024]{1,0:T(8,128)S(1)} %get-tuple-element.56.refs_1_, bf16[512,1024]{1,0:T(8,128)(2,1)S(1)} %get-tuple-element.57.refs_2_, ...), custom_call_target="tpu_custom_call" | custom-call | flops 1000000000 | tf_op jit(solution)/shard_map/attend/pallas_call | solution.py:58
  43.9 4.0 %grad_near.1.refs_3_.refs_4_ = f32[512,1024]{1,0:T(8,128)S(1)} custom-call(s32[11]{0:T(128)S(1)} %stack.44.refs_0_, bf16[512,1536]{1,0:T(8,128)(2,1)S(1)} %collective-permute-done.8.refs_1_, bf16[512,1536]{1,0:T(8,128)(2,1)S(1)} %collective-permute-done.9.refs_2_, bf16[1024,6144]{1,0:T(8,128)(2,1)S(1)} %get-tuple-element.58.refs_5_.refs_2_.refs_3_, ...), custom_call_target="tpu_custom_call" | custom-call | flops 4000000000 | tf_op jit(solution)/shard_map/grad_near/pallas_call | solution.py:58
  48.0 2.4 %project_far.1 = (bf16[256,1536]{1,0:T(8,128)(2,1)S(1)}, bf16[256,1536]{1,0:T(8,128)(2,1)S(1)}) custom-call(s32[11]{0:T(128)S(1)} %stack.44.refs_0_, bf16[512,1024]{1,0:T(8,128)(2,1)S(1)} %get-tuple-element.65.refs_1_, bf16[1024,6144]{1,0:T(8,128)(2,1)S(1)} %get-tuple-element.58.refs_5_.refs_2_.refs_3_, f32[512,1024]{1,0:T(8,128)S(1)} %grad_near.1.refs_3_.refs_4_), custom_call_target="tpu_custom_call" | custom-call | flops 2000000000 | tf_op jit(solution)/shard_map/project_far/pallas_call | solution.py:58
  50.7 2.9 %collective-permute-start.11 = (bf16[256,1536]{1,0:T(8,128)(2,1)S(1)}, bf16[256,1536]{1,0:T(8,128)(2,1)S(1)}, u32[]{:S(2)}, u32[]{:S(2)}) collective-permute-start(bf16[256,1536]{1,0:T(8,128)(2,1)S(1)} %get-tuple-element.74), channel_id=1, source_target_pairs={{0,3},{1,0},{2,1},{3,2},{4,7},{5,4},{6,5},{7,6},{8,11},{9,8},{10,9... | collective-permute-start | bytes 2359304 | tf_op jit(solution)/shard_map/ppermute | solution.py:478
  53.6 4.0 %project_near.1 = (f32[256,1536]{1,0:T(8,128)S(1)}, bf16[256,1536]{1,0:T(8,128)(2,1)S(1)}, bf16[256,1536]{1,0:T(8,128)(2,1)S(1)}, f32[256,1536]{1,0:T(8,128)S(1)}) custom-call(s32[11]{0:T(128)S(1)} %stack.44.refs_0_, bf16[512,1024]{1,0:T(8,128)(2,1)S(1)} %get-tuple-element.65.refs_1_, bf16[1024,6144]{1,0:T(8,128)(2,1)S(1)} %get-tuple-element.58.refs_5_.refs_2_.refs_3_, ...), custom_call_target="tpu_custom_call" | custom-call | flops 4000000000 | tf_op jit(solution)/shard_map/project_near/pallas_call | solution.py:58
  57.7 2.4 %project_own.1 = (f32[256,1536]{1,0:T(8,128)S(1)}, f32[256,1536]{1,0:T(8,128)S(1)}) custom-call(s32[11]{0:T(128)S(1)} %stack.44.refs_0_, bf16[512,1024]{1,0:T(8,128)(2,1)S(1)} %get-tuple-element.65.refs_1_, bf16[1024,6144]{1,0:T(8,128)(2,1)S(1)} %get-tuple-element.58.refs_5_.refs_2_.refs_3_, f32[256,1536]{1,0:T(8,128)S(1)} %get-tuple-element.68.refs_3_.refs_1_), custom_call_target="tpu_custom_call" | custom-call | flops 2000000000 | tf_op jit(solution)/shard_map/project_own/pallas_call | solution.py:58
  60.0 0.7 collective-permute-done.12.refs_1_
  61.2 6.8 %grad_far.1 = (bf16[512,1024]{1,0:T(8,128)(2,1)S(1)}, bf16[528,128]{1,0:T(8,128)(2,1)S(1)}, bf16[528,128]{1,0:T(8,128)(2,1)S(1)}) custom-call(s32[11]{0:T(128)S(1)} %stack.44.refs_0_, bf16[256,1536]{1,0:T(8,128)(2,1)S(1)} %collective-permute-done.12.refs_1_, bf16[256,1536]{1,0:T(8,128)(2,1)S(1)} %collective-permute-done.13.refs_2_, ...), custom_call_target="tpu_custom_call" | custom-call | flops 6000000000 | tf_op jit(solution)/shard_map/grad_far/pallas_call | solution.py:58
  68.3 1.3 %collective-permute-done.14.refs_2_.refs_7_ = bf16[528,128]{1,0:T(8,128)(2,1)S(1)} collective-permute-done((bf16[528,128]{1,0:T(8,128)(2,1)S(1)}, bf16[528,128]{1,0:T(8,128)(2,1)S(1)}, u32[]{:S(2)}, u32[]{:S(2)}) %collective-permute-start.14) | collective-permute-done | bytes 135200 | tf_op jit(solution)/shard_map/ppermute | solution.py:247
  70.2 6.3 %collective-permute-done.10.refs_5_ = bf16[256,1536]{1,0:T(8,128)(2,1)S(1)} collective-permute-done((bf16[256,1536]{1,0:T(8,128)(2,1)S(1)}, bf16[256,1536]{1,0:T(8,128)(2,1)S(1)}, u32[]{:S(2)}, u32[]{:S(2)}) %collective-permute-start.10) | collective-permute-done | bytes 786464 | tf_op jit(solution)/shard_map/ppermute | solution.py:477
  76.5 0.9 join.1
  77.9 2.8 %collective-permute-start.16 = (bf16[512,1536]{1,0:T(8,128)(2,1)S(1)}, bf16[512,1536]{1,0:T(8,128)(2,1)S(1)}, u32[]{:S(2)}, u32[]{:S(2)}) collective-permute-start(bf16[512,1536]{1,0:T(8,128)(2,1)S(1)} %get-tuple-element.81.refs_5_), channel_id=1, source_target_pairs={{0,3},{1,0},{2,1},{3,2},{4,7},{5,4},{6,5},{7,6},{8,11},{9,8},{10,9... | collective-permute-start | bytes 4718600 | tf_op jit(solution)/shard_map/ppermute | solution.py:478
  80.7 1.9 %collective-permute-start.17 = (bf16[528,128]{1,0:T(8,128)(2,1)S(1)}, bf16[528,128]{1,0:T(8,128)(2,1)S(1)}, u32[]{:S(2)}, u32[]{:S(2)}) collective-permute-start(bf16[528,128]{1,0:T(8,128)(2,1)S(1)} %chip_total.3.refs_7_.refs_1_), channel_id=1, source_target_pairs={{0,24},{4,28},{8,0},{12,4},{16,8},{20,12},{24,16},{28,20},{32,56},... | collective-permute-start | bytes 405512 | tf_op jit(solution)/shard_map/ppermute | solution.py:249
  82.7 1.1 collective-permute-start.18
  83.7 0.7 collective-permute-start.19
  84.4 1.7 %collective-permute-done.17.refs_2_ = bf16[528,128]{1,0:T(8,128)(2,1)S(1)} collective-permute-done((bf16[528,128]{1,0:T(8,128)(2,1)S(1)}, bf16[528,128]{1,0:T(8,128)(2,1)S(1)}, u32[]{:S(2)}, u32[]{:S(2)}) %collective-permute-start.17) | collective-permute-done | bytes 135200 | tf_op jit(solution)/shard_map/ppermute | solution.py:249
  86.1 3.1 %collective-permute-done.18.refs_3_ = bf16[528,128]{1,0:T(8,128)(2,1)S(1)} collective-permute-done((bf16[528,128]{1,0:T(8,128)(2,1)S(1)}, bf16[528,128]{1,0:T(8,128)(2,1)S(1)}, u32[]{:S(2)}, u32[]{:S(2)}) %collective-permute-start.18) | collective-permute-done | bytes 135200 | tf_op jit(solution)/shard_map/ppermute | solution.py:249
  89.2 1.4 %collective-permute-done.19.refs_4_ = bf16[528,128]{1,0:T(8,128)(2,1)S(1)} collective-permute-done((bf16[528,128]{1,0:T(8,128)(2,1)S(1)}, bf16[528,128]{1,0:T(8,128)(2,1)S(1)}, u32[]{:S(2)}, u32[]{:S(2)}) %collective-permute-start.19) | collective-permute-done | bytes 135200 | tf_op jit(solution)/shard_map/ppermute | solution.py:249
  90.6 0.7 row_total.3
  91.3 1.3 %collective-permute-start.20 = (bf16[528,128]{1,0:T(8,128)(2,1)S(1)}, bf16[528,128]{1,0:T(8,128)(2,1)S(1)}, u32[]{:S(2)}, u32[]{:S(2)}) collective-permute-start(bf16[528,128]{1,0:T(8,128)(2,1)S(1)} %get-tuple-element.86), channel_id=1, source_target_pairs={{32,0},{36,4},{40,8},{44,12},{48,16},{52,20},{56,24},{60,28},{64,3... | collective-permute-start | bytes 405512 | tf_op jit(solution)/shard_map/ppermute | solution.py:259
  92.7 1.3 %collective-permute-start.21 = (bf16[528,128]{1,0:T(8,128)(2,1)S(1)}, bf16[528,128]{1,0:T(8,128)(2,1)S(1)}, u32[]{:S(2)}, u32[]{:S(2)}) collective-permute-start(bf16[528,128]{1,0:T(8,128)(2,1)S(1)} %get-tuple-element.86), channel_id=1, source_target_pairs={{64,0},{68,4},{72,8},{76,12},{80,16},{84,20},{88,24},{92,28},{96,3... | collective-permute-start | bytes 405512 | tf_op jit(solution)/shard_map/ppermute | solution.py:259
  94.0 1.3 %collective-permute-start.22 = (bf16[528,128]{1,0:T(8,128)(2,1)S(1)}, bf16[528,128]{1,0:T(8,128)(2,1)S(1)}, u32[]{:S(2)}, u32[]{:S(2)}) collective-permute-start(bf16[528,128]{1,0:T(8,128)(2,1)S(1)} %get-tuple-element.86), channel_id=1, source_target_pairs={{96,0},{100,4},{104,8},{108,12},{112,16},{116,20},{120,24},{124,28... | collective-permute-start | bytes 405512 | tf_op jit(solution)/shard_map/ppermute | solution.py:259
  95.2 7.0 %inside.1 = (bf16[512,1024]{1,0:T(8,128)(2,1)}, f32[512,1024]{1,0:T(8,128)S(1)}, f32[512,1024]{1,0:T(8,128)S(1)}) custom-call(s32[11]{0:T(128)S(1)} %stack.44.refs_0_, f32[512,8]{1,0:T(8,128)S(1)} %get-tuple-element.49.refs_1_, f32[8,512]{1,0:T(8,128)S(1)} %get-tuple-element.50.refs_2_.refs_8_, bf16[512,1024]{1,0:T(8,128)(2,1)S(1)} %get-tuple-element.51.refs_3_, ...), custom_call_target="tpu_custom_call" | custom-call | flops 8000000000 | tf_op jit(solution)/shard_map/inside/pallas_call | solution.py:58
  102.2 1.9 %collective-permute-done.22.refs_3_ = bf16[528,128]{1,0:T(8,128)(2,1)S(1)} collective-permute-done((bf16[528,128]{1,0:T(8,128)(2,1)S(1)}, bf16[528,128]{1,0:T(8,128)(2,1)S(1)}, u32[]{:S(2)}, u32[]{:S(2)}) %collective-permute-start.22) | collective-permute-done | bytes 135200 | tf_op jit(solution)/shard_map/ppermute | solution.py:259
  104.2 0.7 arrive.3
  105.0 1.3 %collective-permute-done.23.refs_7_ = bf16[512,128]{1,0:T(8,128)(2,1)S(1)} collective-permute-done((bf16[512,128]{1,0:T(8,128)(2,1)S(1)}, bf16[512,128]{1,0:T(8,128)(2,1)S(1)}, u32[]{:S(2)}, u32[]{:S(2)}) %collective-permute-start.23) | collective-permute-done | bytes 131104 | tf_op jit(solution)/shard_map/ppermute | solution.py:269
  106.3 2.6 %finish.1 = (bf16[512,1024]{1,0:T(8,128)(2,1)}, bf16[512,1024]{1,0:T(8,128)(2,1)}, f32[8,128]{1,0:T(8,128)S(1)}) custom-call(s32[11]{0:T(128)S(1)} %stack.44.refs_0_, f32[512,8]{1,0:T(8,128)S(1)} %get-tuple-element.49.refs_1_, bf16[512,1024]{1,0:T(8,128)(2,1)S(1)} %get-tuple-element.52.refs_4_.refs_2_, ...), custom_call_target="tpu_custom_call" | custom-call | flops 3000000000 | tf_op jit(solution)/shard_map/finish/pallas_call | solution.py:58
  108.9 5.1 %collective-permute-done.15.refs_3_ = bf16[512,1536]{1,0:T(8,128)(2,1)S(1)} collective-permute-done((bf16[512,1536]{1,0:T(8,128)(2,1)S(1)}, bf16[512,1536]{1,0:T(8,128)(2,1)S(1)}, u32[]{:S(2)}, u32[]{:S(2)}) %collective-permute-start.15) | collective-permute-done | bytes 1572896 | tf_op jit(solution)/shard_map/ppermute | solution.py:477
  114.0 1.8 %total.1 = bf16[512,1536]{1,0:T(8,128)(2,1)} custom-call(s32[11]{0:T(128)S(1)} %stack.44.refs_0_, f32[256,1536]{1,0:T(8,128)S(1)} %get-tuple-element.69.refs_9_.refs_1_, f32[256,1536]{1,0:T(8,128)S(1)} %get-tuple-element.70.refs_2_, bf16[512,1536]{1,0:T(8,128)(2,1)S(1)} %collective-permute-done.15.refs_3_, ...), custom_call_target="tpu_custom_call" | custom-call | flops 2000000000 | tf_op jit(solution)/shard_map/total/pallas_call | solution.py:58
  (25 shorter events, 3.3 us)
Async XLA Ops:
  0.6 37.8 %collective-permute-start.8 = (bf16[512,1536]{1,0:T(8,128)(2,1)}, bf16[512,1536]{1,0:T(8,128)(2,1)S(1)}, u32[]{:S(2)}, u32[]{:S(2)}) collective-permute-start(bf16[512,1536]{1,0:T(8,128)(2,1)} %refs_1_.1), channel_id=1, source_target_pairs={{0,1},{1,2},{2,3},{3,0},{4,5},{5,6},{6,7},{7,4},{8,9},{9,10},{10,1... | collective-permute-start | bytes 4718600 | tf_op jit(solution)/shard_map/ppermute | solution.py:477
  2.4 36.1 %collective-permute-start.9 = (bf16[512,1536]{1,0:T(8,128)(2,1)}, bf16[512,1536]{1,0:T(8,128)(2,1)S(1)}, u32[]{:S(2)}, u32[]{:S(2)}) collective-permute-start(bf16[512,1536]{1,0:T(8,128)(2,1)} %refs_1_.1), channel_id=1, source_target_pairs={{0,3},{1,0},{2,1},{3,2},{4,7},{5,4},{6,5},{7,6},{8,11},{9,8},{10,9... | collective-permute-start | bytes 4718600 | tf_op jit(solution)/shard_map/ppermute | solution.py:478
  4.0 0.7 copy-start.1
  9.7 1.4 %collective-permute-start = (bf16[528,128]{1,0:T(8,128)(2,1)S(1)}, bf16[528,128]{1,0:T(8,128)(2,1)S(1)}, u32[]{:S(2)}, u32[]{:S(2)}) collective-permute-start(bf16[528,128]{1,0:T(8,128)(2,1)S(1)} %get-tuple-element.55), channel_id=1, source_target_pairs={{0,4},{4,0},{8,12},{12,8},{16,20},{20,16},{24,28},{28,24},{32,36},... | collective-permute-start | bytes 405512 | tf_op jit(solution)/shard_map/ppermute | solution.py:247
  11.8 11.3 %collective-permute-start.1 = (bf16[528,128]{1,0:T(8,128)(2,1)S(1)}, bf16[528,128]{1,0:T(8,128)(2,1)S(1)}, u32[]{:S(2)}, u32[]{:S(2)}) collective-permute-start(bf16[528,128]{1,0:T(8,128)(2,1)S(1)} %chip_total.2.refs_7_.refs_1_), channel_id=1, source_target_pairs={{0,8},{4,12},{8,16},{12,20},{16,24},{20,28},{24,0},{28,4},{32,40},... | collective-permute-start | bytes 405512 | tf_op jit(solution)/shard_map/ppermute | solution.py:249
  13.4 9.6 %collective-permute-start.2 = (bf16[528,128]{1,0:T(8,128)(2,1)S(1)}, bf16[528,128]{1,0:T(8,128)(2,1)S(1)}, u32[]{:S(2)}, u32[]{:S(2)}) collective-permute-start(bf16[528,128]{1,0:T(8,128)(2,1)S(1)} %chip_total.2.refs_7_.refs_1_), channel_id=1, source_target_pairs={{0,16},{4,20},{8,24},{12,28},{16,0},{20,4},{24,8},{28,12},{32,48},... | collective-permute-start | bytes 405512 | tf_op jit(solution)/shard_map/ppermute | solution.py:249
  16.1 6.9 %collective-permute-start.3 = (bf16[528,128]{1,0:T(8,128)(2,1)S(1)}, bf16[528,128]{1,0:T(8,128)(2,1)S(1)}, u32[]{:S(2)}, u32[]{:S(2)}) collective-permute-start(bf16[528,128]{1,0:T(8,128)(2,1)S(1)} %chip_total.2.refs_7_.refs_1_), channel_id=1, source_target_pairs={{0,24},{4,28},{8,0},{12,4},{16,8},{20,12},{24,16},{28,20},{32,56},... | collective-permute-start | bytes 405512 | tf_op jit(solution)/shard_map/ppermute | solution.py:249
  23.1 11.4 %copy-start = (bf16[512,1536]{1,0:T(8,128)(2,1)S(1)}, bf16[512,1536]{1,0:T(8,128)(2,1)}, u32[]{:S(2)}) copy-start(bf16[512,1536]{1,0:T(8,128)(2,1)} %refs_1_.1) | copy-start | bytes 4718596
  23.8 13.0 %collective-permute-start.4 = (bf16[528,128]{1,0:T(8,128)(2,1)S(1)}, bf16[528,128]{1,0:T(8,128)(2,1)S(1)}, u32[]{:S(2)}, u32[]{:S(2)}) collective-permute-start(bf16[528,128]{1,0:T(8,128)(2,1)S(1)} %get-tuple-element.59), channel_id=1, source_target_pairs={{0,32},{4,36},{8,40},{12,44},{16,48},{20,52},{24,56},{28,60},{32,6... | collective-permute-start | bytes 405512 | tf_op jit(solution)/shard_map/ppermute | solution.py:259
  27.6 9.2 %collective-permute-start.5 = (bf16[528,128]{1,0:T(8,128)(2,1)S(1)}, bf16[528,128]{1,0:T(8,128)(2,1)S(1)}, u32[]{:S(2)}, u32[]{:S(2)}) collective-permute-start(bf16[528,128]{1,0:T(8,128)(2,1)S(1)} %get-tuple-element.59), channel_id=1, source_target_pairs={{0,64},{4,68},{8,72},{12,76},{16,80},{20,84},{24,88},{28,92},{32,9... | collective-permute-start | bytes 405512 | tf_op jit(solution)/shard_map/ppermute | solution.py:259
  33.1 3.8 %collective-permute-start.6 = (bf16[528,128]{1,0:T(8,128)(2,1)S(1)}, bf16[528,128]{1,0:T(8,128)(2,1)S(1)}, u32[]{:S(2)}, u32[]{:S(2)}) collective-permute-start(bf16[528,128]{1,0:T(8,128)(2,1)S(1)} %get-tuple-element.59), channel_id=1, source_target_pairs={{0,96},{4,100},{8,104},{12,108},{16,112},{20,116},{24,120},{28,124... | collective-permute-start | bytes 405512 | tf_op jit(solution)/shard_map/ppermute | solution.py:259
  37.7 4.7 %collective-permute-start.7 = (bf16[512,128]{1,0:T(8,128)(2,1)S(1)}, bf16[512,128]{1,0:T(8,128)(2,1)S(1)}, u32[]{:S(2)}, u32[]{:S(2)}) collective-permute-start(bf16[512,128]{1,0:T(8,128)(2,1)S(1)} %get-tuple-element.63), channel_id=1, source_target_pairs={{0,4},{4,0},{8,12},{12,8},{16,20},{20,16},{24,28},{28,24},{32,36},... | collective-permute-start | bytes 393224 | tf_op jit(solution)/shard_map/ppermute | solution.py:269
  39.1 21.7 %collective-permute-start.12 = (bf16[256,1536]{1,0:T(8,128)(2,1)S(1)}, bf16[256,1536]{1,0:T(8,128)(2,1)S(1)}, u32[]{:S(2)}, u32[]{:S(2)}) collective-permute-start(bf16[256,1536]{1,0:T(8,128)(2,1)S(1)} %get-tuple-element.64.refs_5_), channel_id=1, source_target_pairs={{0,1},{1,2},{2,3},{3,0},{4,5},{5,6},{6,7},{7,4},{8,9},{9,10},{10,1... | collective-permute-start | bytes 2359304 | tf_op jit(solution)/shard_map/ppermute | solution.py:477
  40.7 20.5 %collective-permute-start.13 = (bf16[256,1536]{1,0:T(8,128)(2,1)S(1)}, bf16[256,1536]{1,0:T(8,128)(2,1)S(1)}, u32[]{:S(2)}, u32[]{:S(2)}) collective-permute-start(bf16[256,1536]{1,0:T(8,128)(2,1)S(1)} %get-tuple-element.75), channel_id=1, source_target_pairs={{0,3},{1,0},{2,1},{3,2},{4,7},{5,4},{6,5},{7,6},{8,11},{9,8},{10,9... | collective-permute-start | bytes 2359304 | tf_op jit(solution)/shard_map/ppermute | solution.py:478
  50.3 26.2 %collective-permute-start.10 = (bf16[256,1536]{1,0:T(8,128)(2,1)S(1)}, bf16[256,1536]{1,0:T(8,128)(2,1)S(1)}, u32[]{:S(2)}, u32[]{:S(2)}) collective-permute-start(bf16[256,1536]{1,0:T(8,128)(2,1)S(1)} %get-tuple-element.67.refs_3_), channel_id=1, source_target_pairs={{0,1},{1,2},{2,3},{3,0},{4,5},{5,6},{6,7},{7,4},{8,9},{9,10},{10,1... | collective-permute-start | bytes 2359304 | tf_op jit(solution)/shard_map/ppermute | solution.py:477
  50.7 25.8 %collective-permute-start.11 = (bf16[256,1536]{1,0:T(8,128)(2,1)S(1)}, bf16[256,1536]{1,0:T(8,128)(2,1)S(1)}, u32[]{:S(2)}, u32[]{:S(2)}) collective-permute-start(bf16[256,1536]{1,0:T(8,128)(2,1)S(1)} %get-tuple-element.74), channel_id=1, source_target_pairs={{0,3},{1,0},{2,1},{3,2},{4,7},{5,4},{6,5},{7,6},{8,11},{9,8},{10,9... | collective-permute-start | bytes 2359304 | tf_op jit(solution)/shard_map/ppermute | solution.py:478
  68.0 1.6 %collective-permute-start.14 = (bf16[528,128]{1,0:T(8,128)(2,1)S(1)}, bf16[528,128]{1,0:T(8,128)(2,1)S(1)}, u32[]{:S(2)}, u32[]{:S(2)}) collective-permute-start(bf16[528,128]{1,0:T(8,128)(2,1)S(1)} %get-tuple-element.79), channel_id=1, source_target_pairs={{0,4},{4,0},{8,12},{12,8},{16,20},{20,16},{24,28},{28,24},{32,36},... | collective-permute-start | bytes 405512 | tf_op jit(solution)/shard_map/ppermute | solution.py:247
  77.4 36.6 %collective-permute-start.15 = (bf16[512,1536]{1,0:T(8,128)(2,1)S(1)}, bf16[512,1536]{1,0:T(8,128)(2,1)S(1)}, u32[]{:S(2)}, u32[]{:S(2)}) collective-permute-start(bf16[512,1536]{1,0:T(8,128)(2,1)S(1)} %get-tuple-element.80), channel_id=1, source_target_pairs={{0,1},{1,2},{2,3},{3,0},{4,5},{5,6},{6,7},{7,4},{8,9},{9,10},{10,1... | collective-permute-start | bytes 4718600 | tf_op jit(solution)/shard_map/ppermute | solution.py:477
  77.9 36.1 %collective-permute-start.16 = (bf16[512,1536]{1,0:T(8,128)(2,1)S(1)}, bf16[512,1536]{1,0:T(8,128)(2,1)S(1)}, u32[]{:S(2)}, u32[]{:S(2)}) collective-permute-start(bf16[512,1536]{1,0:T(8,128)(2,1)S(1)} %get-tuple-element.81.refs_5_), channel_id=1, source_target_pairs={{0,3},{1,0},{2,1},{3,2},{4,7},{5,4},{6,5},{7,6},{8,11},{9,8},{10,9... | collective-permute-start | bytes 4718600 | tf_op jit(solution)/shard_map/ppermute | solution.py:478
  80.7 5.4 %collective-permute-start.17 = (bf16[528,128]{1,0:T(8,128)(2,1)S(1)}, bf16[528,128]{1,0:T(8,128)(2,1)S(1)}, u32[]{:S(2)}, u32[]{:S(2)}) collective-permute-start(bf16[528,128]{1,0:T(8,128)(2,1)S(1)} %chip_total.3.refs_7_.refs_1_), channel_id=1, source_target_pairs={{0,24},{4,28},{8,0},{12,4},{16,8},{20,12},{24,16},{28,20},{32,56},... | collective-permute-start | bytes 405512 | tf_op jit(solution)/shard_map/ppermute | solution.py:249
  82.7 6.6 %collective-permute-start.18 = (bf16[528,128]{1,0:T(8,128)(2,1)S(1)}, bf16[528,128]{1,0:T(8,128)(2,1)S(1)}, u32[]{:S(2)}, u32[]{:S(2)}) collective-permute-start(bf16[528,128]{1,0:T(8,128)(2,1)S(1)} %chip_total.3.refs_7_.refs_1_), channel_id=1, source_target_pairs={{0,16},{4,20},{8,24},{12,28},{16,0},{20,4},{24,8},{28,12},{32,48},... | collective-permute-start | bytes 405512 | tf_op jit(solution)/shard_map/ppermute | solution.py:249
  83.7 6.9 %collective-permute-start.19 = (bf16[528,128]{1,0:T(8,128)(2,1)S(1)}, bf16[528,128]{1,0:T(8,128)(2,1)S(1)}, u32[]{:S(2)}, u32[]{:S(2)}) collective-permute-start(bf16[528,128]{1,0:T(8,128)(2,1)S(1)} %chip_total.3.refs_7_.refs_1_), channel_id=1, source_target_pairs={{0,8},{4,12},{8,16},{12,20},{16,24},{20,28},{24,0},{28,4},{32,40},... | collective-permute-start | bytes 405512 | tf_op jit(solution)/shard_map/ppermute | solution.py:249
  91.3 10.9 %collective-permute-start.20 = (bf16[528,128]{1,0:T(8,128)(2,1)S(1)}, bf16[528,128]{1,0:T(8,128)(2,1)S(1)}, u32[]{:S(2)}, u32[]{:S(2)}) collective-permute-start(bf16[528,128]{1,0:T(8,128)(2,1)S(1)} %get-tuple-element.86), channel_id=1, source_target_pairs={{32,0},{36,4},{40,8},{44,12},{48,16},{52,20},{56,24},{60,28},{64,3... | collective-permute-start | bytes 405512 | tf_op jit(solution)/shard_map/ppermute | solution.py:259
  92.7 9.6 %collective-permute-start.21 = (bf16[528,128]{1,0:T(8,128)(2,1)S(1)}, bf16[528,128]{1,0:T(8,128)(2,1)S(1)}, u32[]{:S(2)}, u32[]{:S(2)}) collective-permute-start(bf16[528,128]{1,0:T(8,128)(2,1)S(1)} %get-tuple-element.86), channel_id=1, source_target_pairs={{64,0},{68,4},{72,8},{76,12},{80,16},{84,20},{88,24},{92,28},{96,3... | collective-permute-start | bytes 405512 | tf_op jit(solution)/shard_map/ppermute | solution.py:259
  94.0 10.2 %collective-permute-start.22 = (bf16[528,128]{1,0:T(8,128)(2,1)S(1)}, bf16[528,128]{1,0:T(8,128)(2,1)S(1)}, u32[]{:S(2)}, u32[]{:S(2)}) collective-permute-start(bf16[528,128]{1,0:T(8,128)(2,1)S(1)} %get-tuple-element.86), channel_id=1, source_target_pairs={{96,0},{100,4},{104,8},{108,12},{112,16},{116,20},{120,24},{124,28... | collective-permute-start | bytes 405512 | tf_op jit(solution)/shard_map/ppermute | solution.py:259
  104.9 1.4 %collective-permute-start.23 = (bf16[512,128]{1,0:T(8,128)(2,1)S(1)}, bf16[512,128]{1,0:T(8,128)(2,1)S(1)}, u32[]{:S(2)}, u32[]{:S(2)}) collective-permute-start(bf16[512,128]{1,0:T(8,128)(2,1)S(1)} %get-tuple-element.89), channel_id=1, source_target_pairs={{0,4},{4,0},{8,12},{12,8},{16,20},{20,16},{24,28},{28,24},{32,36},... | collective-permute-start | bytes 393224 | tf_op jit(solution)/shard_map/ppermute | solution.py:269

commit v4 on v3

v4 whole, which is shorter than its diff:
```python
import functools

import jax
import jax.numpy as jnp
from jax import lax
from jax.experimental import pallas as pl
from jax.experimental.pallas import tpu as pltpu
from jax.sharding import PartitionSpec as P

EPS = 1e-05
F32 = jnp.float32
BF16 = jnp.bfloat16
MIB = 1024 * 1024
GIGA = 10**9

NN = (((1,), (0,)), ((), ()))
NT = (((1,), (1,)), ((), ()))
TN = (((0,), (0,)), ((), ()))


def dot(left, right, form=NN):
    return lax.dot_general(left, right, form, preferred_element_type=F32)


VMEM = pl.BlockSpec(memory_space=pltpu.VMEM)
SMEM = pl.BlockSpec(memory_space=pltpu.SMEM)
ANY = pl.BlockSpec(memory_space=pl.ANY)
HBM = pl.BlockSpec(memory_space=pltpu.HBM)


COST = dict(
    own_states=8 * GIGA,
    chip_total=0,
    local=0,
    meet=0,
    grad_own=0,
    arrive=0,
    split=0,
    halves=0,
    attend=0,
    grad_near=0,
    project_far=0,
    project_near=0,
    project_own=0,
    grad_far=0,
    join=0,
    inside=0,
    finish=0,
    total=0,
)


def call(kernel, name, scalars, args, outs, after=(), far=(), far_outs=(), scratch=(), room=12):
    count, waits = len(args), len(after)

    def run(*refs):
        kernel(*refs[: 1 + count], *refs[1 + count + waits :])

    return pl.pallas_call(
        run,
        out_shape=[jax.ShapeDtypeStruct(shape, dtype) for shape, dtype in outs],
        in_specs=[SMEM] + [HBM if i in far else VMEM for i in range(count)] + [ANY] * waits,
        out_specs=[HBM if i in far_outs else VMEM for i in range(len(outs))],
        scratch_shapes=list(scratch),
        compiler_params=pltpu.CompilerParams(vmem_limit_bytes=room * MIB),
        cost_estimate=pl.CostEstimate(flops=COST[name], bytes_accessed=0, transcendentals=0),
        name=name,
    )(scalars, *args, *after)


def three_terms(x):
    high = x.astype(BF16)
    rest = x - high.astype(F32)
    middle = rest.astype(BF16)
    low = (rest - middle.astype(F32)).astype(BF16)
    return high, middle, low


def head_columns(head):
    return slice(head * 128, head * 128 + 128)


def pack_decays(decays):
    high, middle, low = three_terms(decays)
    rows = [t.astype(F32) for t in (high, middle, low)]
    return jnp.concatenate(rows + [jnp.zeros_like(decays)], axis=0).astype(BF16)


def message_decays(ref):
    rows = ref[512:528, :].astype(F32)
    return rows[0:4] + rows[4:8] + rows[8:12]


MESSAGE = ((528, 128), BF16)
STATES = ((512, 128), BF16)
HALF = ((256, 1536), BF16)


def put_state(core, head, state, mine_ref, send_ref):
    rows = slice(head % 4 * 128, head % 4 * 128 + 128)
    here = core == head // 4

    @pl.when(here)
    def _():
        mine_ref[rows, :] = state

    @pl.when(jnp.logical_not(here))
    def _():
        send_ref[rows, :] = state


def put_decays(core, cum_t, mine_ref, send_ref):
    last = jnp.broadcast_to(cum_t[:, 511:512], (8, 128))
    swap = core == 1
    mine_ref[512:528, :] = pack_decays(jnp.where(swap, last[4:8], last[0:4]))
    send_ref[512:528, :] = pack_decays(jnp.where(swap, last[0:4], last[4:8]))


def state_kernel(
    s_ref,
    ld_ref,
    q_hbm,
    k_hbm,
    v_hbm,
    grad_hbm,
    cum_ref,
    cumt_ref,
    mine_ref,
    send_ref,
    q_ref,
    k_ref,
    v_ref,
    top_ref,
    bottom_ref,
    sems,
):
    core = s_ref[CORE]
    loads = []
    for part in range(4):
        cols = slice(part * 256, part * 256 + 256)
        pair = [
            pltpu.make_async_copy(far.at[:, cols], near.at[:, cols], sems.at[part * 2 + i])
            for i, (far, near) in enumerate(((k_hbm, k_ref), (v_hbm, v_ref)))
        ]
        for copy in pair:
            copy.start()
        loads.append(pair)
    late = [
        pltpu.make_async_copy(q_hbm, q_ref, sems.at[8]),
        pltpu.make_async_copy(grad_hbm.at[:256, :], top_ref, sems.at[9]),
        pltpu.make_async_copy(grad_hbm.at[256:, :], bottom_ref, sems.at[10]),
    ]
    for copy in late:
        copy.start()

    rows = lax.broadcasted_iota(jnp.int32, (512, 512), 0)
    cols = lax.broadcasted_iota(jnp.int32, (512, 512), 1)
    upper = jnp.where(rows <= cols, 1.0, 0.0).astype(BF16)
    lower = jnp.where(rows >= cols, 1.0, 0.0).astype(BF16)
    cum = jnp.zeros((512, 8), F32)
    cum_t = jnp.zeros((8, 512), F32)
    for term in three_terms(ld_ref[...])[::-1]:
        cum = cum + dot(lower, term, NT)
        cum_t = cum_t + dot(term, upper)
    cum_ref[...] = cum
    cumt_ref[...] = cum_t
    fall = jnp.exp(cum[511:512, :] - cum)
    for head in range(8):
        if head % 2 == 0:
            for copy in loads[head // 2]:
                copy.wait()
        at = head_columns(head)
        faded = (k_ref[:, at].astype(F32) * fall[:, head : head + 1]).astype(BF16)
        put_state(core, head, dot(faded, v_ref[:, at], TN).astype(BF16), mine_ref, send_ref)
    put_decays(core, cum_t, mine_ref, send_ref)
    for copy in late:
        copy.wait()


def own_states(scalars, logdecay_t, queries, keys, values, grad, after):
    held = ((512, 1024), BF16)
    return call(
        state_kernel,
        "own_states",
        scalars,
        (logdecay_t, queries, keys, values, grad),
        [((512, 8), F32), ((8, 512), F32), MESSAGE, MESSAGE, held, held, held, HALF, HALF],
        after,
        far=(1, 2, 3, 4),
        scratch=[pltpu.SemaphoreType.DMA((11,))],
        room=48,
    )


def chip_kernel(base, s_ref, mine_ref, got_ref, out_ref):
    first = s_ref[base] == 0
    d_mine, d_got = message_decays(mine_ref), message_decays(got_ref)
    w_mine = jnp.where(first, jnp.exp(d_got), 1.0)
    w_got = jnp.where(first, 1.0, jnp.exp(d_mine))
    for i in range(4):
        rows = slice(i * 128, i * 128 + 128)
        out_ref[rows, :] = (
            w_mine[i : i + 1] * mine_ref[rows, :].astype(F32) + w_got[i : i + 1] * got_ref[rows, :].astype(F32)
        ).astype(BF16)
    out_ref[512:528, :] = pack_decays(d_mine + d_got)


def meet_kernel(slot, s_ref, mine_ref, got_ref, *refs):
    prefix_in = refs[0] if len(refs) > 3 else None
    before_in = refs[1] if len(refs) > 3 else None
    total_ref, prefix_ref, before_ref = refs[-3:]
    later = s_ref[slot] == 1
    d_mine, d_got = message_decays(mine_ref), message_decays(got_ref)
    w_mine = jnp.where(later, 1.0, jnp.exp(d_got))
    w_got = jnp.where(later, jnp.exp(d_mine), 1.0)
    before = jnp.zeros((4, 128), F32) if before_in is None else before_in[0:4, :]
    reach = jnp.where(later, jnp.exp(before), 0.0)
    for i in range(4):
        rows = slice(i * 128, i * 128 + 128)
        mine, got = mine_ref[rows, :].astype(F32), got_ref[rows, :].astype(F32)
        total_ref[rows, :] = (w_mine[i : i + 1] * mine + w_got[i : i + 1] * got).astype(BF16)
        prefix = reach[i : i + 1] * got
        prefix_ref[rows, :] = prefix if prefix_in is None else prefix_in[rows, :] + prefix
    total_ref[512:528, :] = pack_decays(d_mine + d_got)
    before = before + jnp.where(later, d_got, 0.0)
    before_ref[...] = jnp.concatenate([before, before], axis=0)


def arrive_kernel(base, s_ref, last_ref, prefix_ref, before_ref, mine_ref, got_ref, keep_ref, send_ref):
    first = s_ref[base] == 0
    later = s_ref[base + 4] == 1
    reach = jnp.where(later, jnp.exp(before_ref[0:4, :]), 0.0)
    d_first = jnp.where(first, message_decays(mine_ref), message_decays(got_ref))
    w_first = jnp.exp(d_first)
    for i in range(4):
        rows = slice(i * 128, i * 128 + 128)
        at_first = prefix_ref[rows, :] + reach[i : i + 1] * last_ref[rows, :].astype(F32)
        state_first = jnp.where(first, mine_ref[rows, :].astype(F32), got_ref[rows, :].astype(F32))
        at_second = w_first[i : i + 1] * at_first + state_first
        keep_ref[rows, :] = jnp.where(first, at_first, at_second).astype(BF16)
        send_ref[rows, :] = jnp.where(first, at_second, at_first).astype(BF16)


SWAP = [(i, i ^ 1) for i in range(32)]
MEETINGS = [[(i, i ^ far) for i in range(32)] for far in (2, 4, 8, 16)]


def scan_blocks(scalars, mine, send, base, beside):
    got = lax.ppermute(send, "seq", SWAP)
    (total,) = call(functools.partial(chip_kernel, base), "chip_total", scalars, (mine, got), [MESSAGE])
    held = ()
    after = (total,)
    for turn in range(3):
        met = lax.ppermute(total, "seq", MEETINGS[turn])
        after = beside[turn](after)
        held = call(
            functools.partial(meet_kernel, base + 1 + turn),
            "meet",
            scalars,
            (total, met, *held),
            [MESSAGE, ((512, 128), F32), ((8, 128), F32)],
            after,
        )
        total, held = held[0], held[1:]
        after = (held[1],)
    met = lax.ppermute(total, "seq", MEETINGS[3])
    after = beside[3](after)
    keep, send_back = call(
        functools.partial(arrive_kernel, base),
        "arrive",
        scalars,
        (met, *held, mine, got),
        [STATES, STATES],
        after,
    )
    return keep, lax.ppermute(send_back, "seq", SWAP)


def decay_block(cum, cum_t, head, low, high):
    diff = cum[low:high, head : head + 1] - cum_t[head : head + 1, :high]
    rows = lax.broadcasted_iota(jnp.int32, diff.shape, 0) + low
    cols = lax.broadcasted_iota(jnp.int32, diff.shape, 1)
    return jnp.exp(jnp.where(rows >= cols, diff, -1e30))


def local_kernel(s_ref, cum_ref, cumt_ref, q_ref, k_ref, v_ref, w_hbm, out_ref, scaled_ref, turned_ref, w_ref, sems):
    loads = []
    for part in range(4):
        rows = slice(part * 256, part * 256 + 256)
        loads.append(pltpu.make_async_copy(w_hbm.at[rows, :], w_ref.at[rows, :], sems.at[part]))
        loads[-1].start()
    cum, cum_t = cum_ref[...], cumt_ref[...]
    rise = jnp.exp(cum)
    for head in range(8):
        at = head_columns(head)
        scaled = q_ref[:, at].astype(F32) * rise[:, head : head + 1]
        scaled_ref[:, at] = scaled.astype(BF16)
        turned_ref[at, :] = scaled.T.astype(BF16)
        for low in (0, 256):
            high = low + 256
            table = decay_block(cum, cum_t, head, low, high)
            probs = (dot(q_ref[low:high, at], k_ref[:high, at], NT) * table).astype(BF16)
            out_ref[low:high, at] = dot(probs, v_ref[:high, at])
    for copy in loads:
        copy.wait()


def local(scalars, cum, cum_t, q, k, v, weight, after):
    return call(
        local_kernel,
        "local",
        scalars,
        (cum, cum_t, q, k, v, weight),
        [((512, 1024), F32), ((512, 1024), BF16), ((1024, 512), BF16), ((1024, 6144), BF16)],
        after,
        far=(5,),
        room=34,
        scratch=[pltpu.SemaphoreType.DMA((4,))],
    )


def arrived(s_ref, head, keep_ref, got_ref):
    rows = slice(head % 4 * 128, head % 4 * 128 + 128)
    return jnp.where(s_ref[CORE] == head // 4, keep_ref[rows, :], got_ref[rows, :])


def attend_kernel(s_ref, local_ref, scaled_ref, keep_ref, got_ref, normed_ref, unit_ref, scale_ref):
    for head in range(8):
        at = head_columns(head)
        att = local_ref[:, at] + dot(scaled_ref[:, at], arrived(s_ref, head, keep_ref, got_ref))
        scale = lax.rsqrt(jnp.mean(att * att, axis=1, keepdims=True) + EPS)
        unit = att * scale
        unit_ref[:, at] = unit
        scale_ref[:, at] = jnp.broadcast_to(scale, unit.shape)
        normed_ref[:, at] = unit.astype(BF16)


WHOLE = ((512, 1536), BF16)
WIDE_HALF = ((256, 1536), F32)


OWN, NEAR_LEFT, NEAR_RIGHT, FAR, CORE = 10, 11, 12, 13, 14


def block_columns(s_ref, slot, offset=0, size=1536):
    return pl.ds(pl.multiple_of(s_ref[slot] * 1536 + offset, 128), size)


def products(s_ref, x_ref, w_ref, slot, top_ref, bottom_ref):
    for offset in (0, 512, 1024):
        out = dot(x_ref[...], w_ref[:, block_columns(s_ref, slot, offset, 512)])
        at = slice(offset, offset + 512)
        top_ref[:, at] = out[:256].astype(top_ref.dtype)
        bottom_ref[:, at] = out[256:].astype(bottom_ref.dtype)


def project_near_kernel(s_ref, x_ref, w_ref, right_top, right_bottom, left_top, left_bottom):
    products(s_ref, x_ref, w_ref, NEAR_RIGHT, right_top, right_bottom)
    products(s_ref, x_ref, w_ref, NEAR_LEFT, left_top, left_bottom)


def project_one_kernel(slot, s_ref, x_ref, w_ref, top_ref, bottom_ref):
    products(s_ref, x_ref, w_ref, slot, top_ref, bottom_ref)


def halves_kernel(s_ref, grad_hbm, top_ref, bottom_ref, order_ref, sems):
    order_ref[...] = jnp.zeros((8, 128), F32)
    copies = [
        pltpu.make_async_copy(grad_hbm.at[:256, :], top_ref, sems.at[0]),
        pltpu.make_async_copy(grad_hbm.at[256:, :], bottom_ref, sems.at[1]),
    ]
    for copy in copies:
        copy.start()
    for copy in copies:
        copy.wait()


def split_kernel(s_ref, a_ref, b_ref, top_ref, bottom_ref):
    top_ref[...] = a_ref[...]
    bottom_ref[...] = b_ref[...]


def join_kernel(s_ref, right_ref, from_left, left_ref, from_right, out_right, out_left):
    out_right[...] = (right_ref[...] + from_left[...].astype(F32)).astype(BF16)
    out_left[...] = (left_ref[...] + from_right[...].astype(F32)).astype(BF16)


def total_kernel(s_ref, top_ref, bottom_ref, top_a, top_b, bottom_a, bottom_b, out_ref, out_held, sems):
    copies = []
    for i, (own_ref, a_ref, b_ref) in enumerate(((top_ref, top_a, top_b), (bottom_ref, bottom_a, bottom_b))):
        for j in range(2):
            rows = slice(j * 128, j * 128 + 128)
            here = slice(i * 256 + j * 128, i * 256 + j * 128 + 128)
            total = own_ref[rows, :] + a_ref[rows, :].astype(F32) + b_ref[rows, :].astype(F32)
            out_held[here, :] = total.astype(BF16)
            copies.append(pltpu.make_async_copy(out_held.at[here, :], out_ref.at[here, :], sems.at[i * 2 + j]))
            copies[-1].start()
    for copy in copies:
        copy.wait()


def grad_own_kernel(s_ref, x_ref, w_ref, out_ref):
    for low in range(0, 1024, 256):
        rows = slice(low, low + 256)
        out_ref[:, rows] = dot(x_ref[...], w_ref[rows, block_columns(s_ref, OWN)], NT)


def grad_near_kernel(s_ref, a_top, a_bottom, b_top, b_bottom, w_ref, acc_ref, out_ref):
    a = jnp.concatenate([a_top[...], a_bottom[...]], axis=0)
    b = jnp.concatenate([b_top[...], b_bottom[...]], axis=0)
    for low in range(0, 1024, 256):
        rows = slice(low, low + 256)
        out_ref[:, rows] = (
            acc_ref[:, rows]
            + dot(a, w_ref[rows, block_columns(s_ref, NEAR_LEFT)], NT)
            + dot(b, w_ref[rows, block_columns(s_ref, NEAR_RIGHT)], NT)
        )


def grad_far_kernel(
    s_ref, c_ref, d_ref, w_ref, acc_ref, unit_ref, scale_ref, turned_ref, cumt_ref, grad_ref, mine_ref, send_ref
):
    core = s_ref[CORE]
    x = jnp.concatenate([c_ref[...], d_ref[...]], axis=0)
    for low in range(0, 1024, 256):
        rows = slice(low, low + 256)
        acc = acc_ref[:, rows] + dot(x, w_ref[rows, block_columns(s_ref, FAR)], NT)
        for i in range(2):
            head = low // 128 + i
            at = head_columns(head)
            unit, grad = unit_ref[:, at], acc[:, i * 128 : i * 128 + 128]
            along = jnp.mean(grad * unit, axis=1, keepdims=True)
            out = (scale_ref[:, at] * (grad - unit * along)).astype(BF16)
            grad_ref[:, at] = out
            put_state(core, head, dot(turned_ref[at, :], out).astype(BF16), mine_ref, send_ref)
    put_decays(core, cumt_ref[...], mine_ref, send_ref)


def inside_kernel(heads, s_ref, cum_ref, cumt_ref, q_ref, k_ref, v_ref, g_ref, keep_ref, got_ref, *refs):
    gq_ref, gk_ref, gv_ref = refs[-3:]
    cum, cum_t = cum_ref[...], cumt_ref[...]
    rise = jnp.exp(cum)
    if len(refs) > 3:
        gq_ref[:, :512] = refs[0][...]
    for head in heads:
        at = head_columns(head)
        to = head_columns(head - heads[0])
        to_q = at if len(refs) > 3 else to
        incoming = arrived(s_ref, head, keep_ref, got_ref)
        early_k = early_v = None
        for low in (0, 256):
            high = low + 256
            q, g = q_ref[low:high, at], g_ref[low:high, at]
            k, v = k_ref[:high, at], v_ref[:high, at]
            table = decay_block(cum, cum_t, head, low, high)
            probs = (dot(q, k, NT) * table).astype(BF16)
            scores = (dot(g, v, NT) * table).astype(BF16)
            gq = dot(scores, k) + rise[low:high, head : head + 1] * dot(g, incoming, NT)
            gq_ref[low:high, to_q] = gq.astype(BF16)
            part_k, part_v = dot(scores, q, TN), dot(probs, g, TN)
            if low == 0:
                early_k, early_v = part_k, part_v
            else:
                gk_ref[:256, to] = early_k + part_k[:256]
                gk_ref[256:, to] = part_k[256:]
                gv_ref[:256, to] = early_v + part_v[:256]
                gv_ref[256:, to] = part_v[256:]


def finish_kernel(
    s_ref, cum_ref, k_ref, v_ref, gk_a, gv_a, gk_b, gv_b, keep_ref, got_ref, gk_out, gv_out, order_ref, gk_held, gv_held, sems
):
    cum = cum_ref[...]
    fall = jnp.exp(cum[511:512, :] - cum)
    copies = []
    for head in range(8):
        at, part = head_columns(head), head_columns(head % 4)
        gk_ref, gv_ref = ((gk_a, gv_a), (gk_b, gv_b))[head // 4]
        outgoing = arrived(s_ref, head, keep_ref, got_ref)
        factor = fall[:, head : head + 1]
        gk_held[:, at] = (gk_ref[:, part] + factor * dot(v_ref[:, at], outgoing, NT)).astype(BF16)
        gv_held[:, at] = (gv_ref[:, part] + factor * dot(k_ref[:, at], outgoing)).astype(BF16)
        if head % 2 == 1:
            done = slice(head * 128 - 128, head * 128 + 128)
            for i, (held, out) in enumerate(((gk_held, gk_out), (gv_held, gv_out))):
                copies.append(pltpu.make_async_copy(held.at[:, done], out.at[:, done], sems.at[head - 1 + i]))
                copies[-1].start()
    order_ref[...] = jnp.zeros((8, 128), F32)
    for copy in copies:
        copy.wait()


RIGHT = [(i, (i + 1) % 4) for i in range(4)]
LEFT = [(i, (i + 3) % 4) for i in range(4)]


def body(queries, keys, values, logdecay, weight, output_gradient):
    at = lax.axis_index("seq").astype(jnp.int32)
    h = lax.axis_index("head").astype(jnp.int32)
    core, x, z = at % 2, at // 2 % 4, at // 8
    places = [core, x % 2, x // 2, z % 2, z // 2]
    blocks = [h, (h + 3) % 4, (h + 1) % 4, (h + 2) % 4, core]
    scalars = jnp.stack(places + [1 - place for place in places] + blocks).astype(jnp.int32)

    right = lambda a: lax.ppermute(a, "head", RIGHT)
    left = lambda a: lax.ppermute(a, "head", LEFT)
    wide, narrow = ((512, 1024), F32), ((512, 1024), BF16)

    top, bottom, order = call(
        halves_kernel,
        "halves",
        scalars,
        (output_gradient,),
        [HALF, HALF, ((8, 128), F32)],
        far=(0,),
        scratch=[pltpu.SemaphoreType.DMA((2,))],
        room=52,
    )
    a_top, b_bottom = right(top), left(bottom)
    cum, cum_t, mine, send, q, k, v, top, bottom = own_states(
        scalars, logdecay.T, queries, keys, values, output_gradient, (order,)
    )
    a_bottom, b_top = right(bottom), left(top)
    made = {}

    def make_local(after):
        made["local"] = local(scalars, cum, cum_t, q, k, v, weight, after)
        return made["local"][:1]

    def make_grad_own(after):
        w = made["local"][3]
        made["acc"] = call(grad_own_kernel, "grad_own", scalars, (output_gradient, w), [wide], after)[0]
        return (made["acc"],)

    def make_split(after):
        made["split"] = call(split_kernel, "split", scalars, (a_top, b_bottom), [HALF, HALF], after)
        return made["split"][:1]

    keep, got = scan_blocks(scalars, mine, send, 0, (make_local, make_grad_own, make_split, lambda after: after))
    local_part, scaled, turned, w = made["local"]
    acc = made["acc"]
    c, d = right(made["split"][0]), left(made["split"][1])
    normed, unit, scale = call(
        attend_kernel, "attend", scalars, (local_part, scaled, keep, got), [narrow, wide, wide]
    )

    (acc,) = call(grad_near_kernel, "grad_near", scalars, (a_top, a_bottom, b_top, b_bottom, w, acc), [wide], (unit,))
    far = call(functools.partial(project_one_kernel, FAR), "project_far", scalars, (normed, w), [HALF] * 2, (acc,))
    from_left, from_right = right(far[0]), left(far[1])
    near = call(
        project_near_kernel, "project_near", scalars, (normed, w), [WIDE_HALF, HALF, HALF, WIDE_HALF], far[:1]
    )
    grad, mine_g, send_g = call(
        grad_far_kernel,
        "grad_far",
        scalars,
        (c, d, w, acc, unit, scale, turned, cum_t),
        [narrow, MESSAGE, MESSAGE],
        near[:1],
    )
    inputs = (cum, cum_t, q, k, v, grad, keep, got)
    right_top, right_bottom, left_top, left_bottom = near
    direct_r, direct_l = right(right_bottom), left(left_top)

    def inside_first(after):
        made["a"] = call(
            functools.partial(inside_kernel, range(0, 4)),
            "inside",
            scalars,
            inputs,
            [((512, 512), BF16), ((512, 512), F32), ((512, 512), F32)],
            after,
        )
        return made["a"][:1]

    def inside_second(after):
        made["b"] = call(
            functools.partial(inside_kernel, range(4, 8)),
            "inside",
            scalars,
            inputs + (made["a"][0],),
            [narrow, ((512, 512), F32), ((512, 512), F32)],
            after,
        )
        return made["b"][1:2]

    def join(after):
        parts = (right_top, from_left, left_bottom, from_right)
        made["joined"] = call(join_kernel, "join", scalars, parts, [HALF, HALF], after)
        return made["joined"][:1]

    def project_own(after):
        one = functools.partial(project_one_kernel, OWN)
        made["own"] = call(one, "project_own", scalars, (normed, w), [WIDE_HALF] * 2, after)
        return made["own"][:1]

    keep_g, got_g = scan_blocks(scalars, mine_g, send_g, 5, (inside_first, join, inside_second, project_own))
    joined_r, joined_l = right(made["joined"][0]), left(made["joined"][1])
    gq = made["b"][0]
    gk, gv, order = call(
        finish_kernel,
        "finish",
        scalars,
        (cum, k, v, *made["a"][1:], *made["b"][1:], keep_g, got_g),
        [narrow, narrow, ((8, 128), F32)],
        far_outs=(0, 1),
        scratch=[pltpu.VMEM((512, 1024), BF16), pltpu.VMEM((512, 1024), BF16), pltpu.SemaphoreType.DMA((8,))],
    )
    (out,) = call(
        total_kernel,
        "total",
        scalars,
        (*made["own"], joined_r, direct_l, direct_r, joined_l),
        [WHOLE],
        (order,),
        far_outs=(0,),
        scratch=[pltpu.VMEM((512, 1536), BF16), pltpu.SemaphoreType.DMA((4,))],
    )
    return out, gq, gk, gv


def solution(mesh):
    return jax.shard_map(
        body,
        mesh=mesh,
        in_specs=(
            P("seq", "head"),
            P("seq", "head"),
            P("seq", "head"),
            P("seq", "head"),
            P("head", None),
            P("seq", "head"),
        ),
        out_specs=(P("seq", "head"), P("seq", "head"), P("seq", "head"), P("seq", "head")),
        check_vma=False,
    )
```

time: 116 us -> 111 us (0.957)
  waiting for transfers between devices: 25.5 us -> 16.4 us
  Pallas kernels: 51 us -> 55.4 us
    ppermute x4 -> x6, waiting for transfers between devices: 12.7 us -> 1.24 us  [body(): right = lambda a: lax.ppermute(a, 'head', RIGHT)]
    pallas_call x20 -> x26, Pallas kernels: 51 us -> 55.4 us  [call(): pl.pallas_call(run, out_shape=[jax.ShapeDtypeStruct(shape, dtype) for sha...]
    ppermute x14 -> x10, starting transfers between devices: 24.1 us -> 20.2 us  [the longest x6 12.2 us: scan_blocks(): met = lax.ppermute(total, 'seq', MEETINGS[turn])]
    ppermute x4 -> x6, starting transfers between devices: 8.97 us -> 12.4 us  [body(): left = lambda a: lax.ppermute(a, 'head', LEFT)]
    ppermute x14 -> x10, waiting for transfers between devices: 9.62 us -> 11.9 us  [the longest x6 5.64 us: scan_blocks(): met = lax.ppermute(total, 'seq', MEETINGS[turn])]
    ppermute x4 -> x6, waiting for transfers between devices: 0.45 us -> 1.93 us  [body(): left = lambda a: lax.ppermute(a, 'head', LEFT)]
    ppermute x2, waiting for transfers between devices: 2.68 us -> 1.34 us  [scan_blocks(): got = lax.ppermute(send, 'seq', SWAP)]
    ppermute x4 -> x6, starting transfers between devices: 4.29 us -> 4.54 us  [body(): right = lambda a: lax.ppermute(a, 'head', RIGHT)]
  transfers between devices with their start and end apart: 24 -> 24, of which waited for: 13 -> 10; matrix products, arithmetic and copies ran while one was open for 0% -> 0% of each run, Pallas kernels for 42% -> 46%
where the time goes in v4:
time: 111 us
  Pallas kernels  55.4 us (50%)
  starting transfers between devices  37.2 us (34%)
  waiting for transfers between devices  16.4 us (15%)
  between operations  1.21 us (1%)
    pallas_call x26, Pallas kernels, call(): pl.pallas_call(run, out_shape=[jax.ShapeDtypeStruct(shape, dtype) for sha...  55.4 us
    ppermute x6, starting transfers between devices, body(): left = lambda a: lax.ppermute(a, 'head', LEFT)  12.4 us
    ppermute x6, starting transfers between devices, scan_blocks(): met = lax.ppermute(total, 'seq', MEETINGS[turn])  12.2 us
    ppermute x2, starting transfers between devices, scan_blocks(): met = lax.ppermute(total, 'seq', MEETINGS[3])  7.61 us
    ppermute x6, waiting for transfers between devices, scan_blocks(): met = lax.ppermute(total, 'seq', MEETINGS[turn])  5.64 us
    ppermute x6, starting transfers between devices, body(): right = lambda a: lax.ppermute(a, 'head', RIGHT)  4.54 us
    ppermute x2, waiting for transfers between devices, scan_blocks(): met = lax.ppermute(total, 'seq', MEETINGS[3])  3.61 us
    ppermute x2, waiting for transfers between devices, scan_blocks(): return (keep, lax.ppermute(send_back, 'seq', SWAP))  2.67 us
  transfers between devices with their start and end apart: 24, of which 10 were waited for; matrix products, arithmetic and copies ran while one was open for 0% of the time, Pallas kernels for 46%

profile of v4, /device:TPU:0, one launch (start us, length us, event | category | flops | bytes accessed | tf_op | source)
XLA Modules:
  0.0 111.1 jit_solution(10647057206725483018)
XLA Ops:
  0.9 1.9 %halves.1 = (bf16[256,1536]{1,0:T(8,128)(2,1)S(1)}, bf16[256,1536]{1,0:T(8,128)(2,1)S(1)}, f32[8,128]{1,0:T(8,128)S(1)}) custom-call(s32[15]{0:T(128)S(1)} %stack.60.refs_0_, bf16[512,1536]{1,0:T(8,128)(2,1)} %refs_1_.3), custom_call_target="tpu_custom_call" | custom-call | tf_op jit(solution)/shard_map/halves/pallas_call | solution.py:59
  2.8 1.7 %collective-permute-start.4 = (bf16[256,1536]{1,0:T(8,128)(2,1)S(1)}, bf16[256,1536]{1,0:T(8,128)(2,1)S(1)}, u32[]{:S(2)}, u32[]{:S(2)}) collective-permute-start(bf16[256,1536]{1,0:T(8,128)(2,1)S(1)} %get-tuple-element.86), channel_id=1, source_target_pairs={{0,1},{1,2},{2,3},{3,0},{4,5},{5,6},{6,7},{7,4},{8,9},{9,10},{10,1... | collective-permute-start | bytes 2359304 | tf_op jit(solution)/shard_map/ppermute | solution.py:505
  4.5 1.6 %collective-permute-start.5 = (bf16[256,1536]{1,0:T(8,128)(2,1)S(1)}, bf16[256,1536]{1,0:T(8,128)(2,1)S(1)}, u32[]{:S(2)}, u32[]{:S(2)}) collective-permute-start(bf16[256,1536]{1,0:T(8,128)(2,1)S(1)} %get-tuple-element.87), channel_id=1, source_target_pairs={{0,3},{1,0},{2,1},{3,2},{4,7},{5,4},{6,5},{7,6},{8,11},{9,8},{10,9... | collective-permute-start | bytes 2359304 | tf_op jit(solution)/shard_map/ppermute | solution.py:506
  6.1 0.7 copy-done.1
  6.8 4.4 %own_states.1 = (f32[512,8]{1,0:T(8,128)S(1)}, f32[8,512]{1,0:T(8,128)S(1)}, bf16[528,128]{1,0:T(8,128)(2,1)S(1)}, bf16[528,128]{1,0:T(8,128)(2,1)S(1)}, bf16[51...) custom-call(s32[15]{0:T(128)S(1)} %stack.60.refs_0_, ...), custom_call_target="tpu_custom_call" | custom-call | flops 8000000000 | tf_op jit(solution)/shard_map/own_states/pallas_call | solution.py:59
  11.8 2.8 %collective-permute-start.11 = (bf16[256,1536]{1,0:T(8,128)(2,1)S(1)}, bf16[256,1536]{1,0:T(8,128)(2,1)S(1)}, u32[]{:S(2)}, u32[]{:S(2)}) collective-permute-start(bf16[256,1536]{1,0:T(8,128)(2,1)S(1)} %get-tuple-element.97), channel_id=1, source_target_pairs={{0,3},{1,0},{2,1},{3,2},{4,7},{5,4},{6,5},{7,6},{8,11},{9,8},{10,9... | collective-permute-start | bytes 2359304 | tf_op jit(solution)/shard_map/ppermute | solution.py:506
  15.2 1.7 %collective-permute-start.1 = (bf16[528,128]{1,0:T(8,128)(2,1)S(1)}, bf16[528,128]{1,0:T(8,128)(2,1)S(1)}, u32[]{:S(2)}, u32[]{:S(2)}) collective-permute-start(bf16[528,128]{1,0:T(8,128)(2,1)S(1)} %chip_total.2.refs_7_.refs_1_), channel_id=1, source_target_pairs={{0,8},{4,12},{8,0},{12,4},{16,24},{20,28},{24,16},{28,20},{32,40},... | collective-permute-start | bytes 405512 | tf_op jit(solution)/shard_map/ppermute | solution.py:254
  16.9 5.5 %local.1 = (f32[512,1024]{1,0:T(8,128)S(1)}, bf16[512,1024]{1,0:T(8,128)(2,1)S(1)}, bf16[1024,512]{1,0:T(8,128)(2,1)S(1)}, bf16[1024,6144]{1,0:T(8,128)(2,1)S(1)}) custom-call(s32[15]{0:T(128)S(1)} %stack.60.refs_0_, f32[512,8]{1,0:T(8,128)S(1)} %get-tuple-element.70.refs_1_, f32[8,512]{1,0:T(8,128)S(1)} %get-tuple-element.71.refs_2_.refs_8_, ...), custom_call_target="tpu_custom_call" | custom-call | tf_op jit(solution)/shard_map/local/pallas_call | solution.py:59
  23.0 2.8 %collective-permute-start.2 = (bf16[528,128]{1,0:T(8,128)(2,1)S(1)}, bf16[528,128]{1,0:T(8,128)(2,1)S(1)}, u32[]{:S(2)}, u32[]{:S(2)}) collective-permute-start(bf16[528,128]{1,0:T(8,128)(2,1)S(1)} %get-tuple-element.79.refs_1_), channel_id=1, source_target_pairs={{0,16},{4,20},{8,24},{12,28},{16,0},{20,4},{24,8},{28,12},{32,48},... | collective-permute-start | bytes 405512 | tf_op jit(solution)/shard_map/ppermute | solution.py:254
  25.8 2.4 %grad_own.1.refs_5_.refs_6_ = f32[512,1024]{1,0:T(8,128)S(1)} custom-call(s32[15]{0:T(128)S(1)} %stack.60.refs_0_, bf16[512,1536]{1,0:T(8,128)(2,1)S(1)} %copy-done, bf16[1024,6144]{1,0:T(8,128)(2,1)S(1)} %get-tuple-element.82.refs_2_.refs_5_.refs_3_, f32[8,128]{1,0:T(8,128)S(1)} %get-tuple-element.81.refs_3_.refs_4_), custom_call_target="tpu_custom_call" | custom-call | tf_op jit(solution)/shard_map/grad_own/pallas_call | solution.py:59
  28.1 1.5 %collective-permute-done.2.refs_2_ = bf16[528,128]{1,0:T(8,128)(2,1)S(1)} collective-permute-done((bf16[528,128]{1,0:T(8,128)(2,1)S(1)}, bf16[528,128]{1,0:T(8,128)(2,1)S(1)}, u32[]{:S(2)}, u32[]{:S(2)}) %collective-permute-start.2) | collective-permute-done | bytes 135200 | tf_op jit(solution)/shard_map/ppermute | solution.py:254
  29.6 0.6 meet.7
  30.3 2.0 %collective-permute-start.3 = (bf16[528,128]{1,0:T(8,128)(2,1)S(1)}, bf16[528,128]{1,0:T(8,128)(2,1)S(1)}, u32[]{:S(2)}, u32[]{:S(2)}) collective-permute-start(bf16[528,128]{1,0:T(8,128)(2,1)S(1)} %get-tuple-element.83.refs_1_), channel_id=1, source_target_pairs={{0,32},{4,36},{8,40},{12,44},{16,48},{20,52},{24,56},{28,60},{32,0... | collective-permute-start | bytes 405512 | tf_op jit(solution)/shard_map/ppermute | solution.py:254
  32.3 0.6 split.1
  32.9 0.7 collective-permute-start.9
  33.6 1.4 %collective-permute-start.8 = (bf16[256,1536]{1,0:T(8,128)(2,1)S(1)}, bf16[256,1536]{1,0:T(8,128)(2,1)S(1)}, u32[]{:S(2)}, u32[]{:S(2)}) collective-permute-start(bf16[256,1536]{1,0:T(8,128)(2,1)S(1)} %get-tuple-element.88.refs_5_), channel_id=1, source_target_pairs={{0,1},{1,2},{2,3},{3,0},{4,5},{5,6},{6,7},{7,4},{8,9},{9,10},{10,1... | collective-permute-start | bytes 2359304 | tf_op jit(solution)/shard_map/ppermute | solution.py:505
  35.4 0.6 meet.8
  36.0 4.0 %collective-permute-start.6 = (bf16[528,128]{1,0:T(8,128)(2,1)S(1)}, bf16[528,128]{1,0:T(8,128)(2,1)S(1)}, u32[]{:S(2)}, u32[]{:S(2)}) collective-permute-start(bf16[528,128]{1,0:T(8,128)(2,1)S(1)} %get-tuple-element.89), channel_id=1, source_target_pairs={{0,64},{4,68},{8,72},{12,76},{16,80},{20,84},{24,88},{28,92},{32,9... | collective-permute-start | bytes 405512 | tf_op jit(solution)/shard_map/ppermute | solution.py:266
  40.0 3.0 %collective-permute-done.6.refs_1_ = bf16[528,128]{1,0:T(8,128)(2,1)S(1)} collective-permute-done((bf16[528,128]{1,0:T(8,128)(2,1)S(1)}, bf16[528,128]{1,0:T(8,128)(2,1)S(1)}, u32[]{:S(2)}, u32[]{:S(2)}) %collective-permute-start.6) | collective-permute-done | bytes 135200 | tf_op jit(solution)/shard_map/ppermute | solution.py:266
  42.9 0.6 arrive.2
  43.9 1.3 %collective-permute-done.7.refs_4_.refs_8_ = bf16[512,128]{1,0:T(8,128)(2,1)S(1)} collective-permute-done((bf16[512,128]{1,0:T(8,128)(2,1)S(1)}, bf16[512,128]{1,0:T(8,128)(2,1)S(1)}, u32[]{:S(2)}, u32[]{:S(2)}) %collective-permute-start.7) | collective-permute-done | bytes 131104 | tf_op jit(solution)/shard_map/ppermute | solution.py:276
  45.2 1.5 %attend.1 = (bf16[512,1024]{1,0:T(8,128)(2,1)S(1)}, f32[512,1024]{1,0:T(8,128)S(1)}, f32[512,1024]{1,0:T(8,128)S(1)}) custom-call(s32[15]{0:T(128)S(1)} %stack.60.refs_0_, f32[512,1024]{1,0:T(8,128)S(1)} %get-tuple-element.77.refs_3_.refs_1_, bf16[512,1024]{1,0:T(8,128)(2,1)S(1)} %get-tuple-element.78.refs_2_, ...), custom_call_target="tpu_custom_call" | custom-call | tf_op jit(solution)/shard_map/attend/pallas_call | solution.py:59
  46.7 4.0 %grad_near.1.refs_3_.refs_4_ = f32[512,1024]{1,0:T(8,128)S(1)} custom-call(s32[15]{0:T(128)S(1)} %stack.60.refs_0_, bf16[256,1536]{1,0:T(8,128)(2,1)S(1)} %collective-permute-done.4.refs_1_, bf16[256,1536]{1,0:T(8,128)(2,1)S(1)} %collective-permute-done.10.refs_2_, bf16[256,1536]{1,0:T(8,128)(2,1)S(1)} %collective-permute-done.11.refs_3_, ...), custom_call_target="tpu_custom_call" | custom-call | tf_op jit(solution)/shard_map/grad_near/pallas_call | solution.py:59
  50.7 2.4 %project_far.1 = (bf16[256,1536]{1,0:T(8,128)(2,1)S(1)}, bf16[256,1536]{1,0:T(8,128)(2,1)S(1)}) custom-call(s32[15]{0:T(128)S(1)} %stack.60.refs_0_, bf16[512,1024]{1,0:T(8,128)(2,1)S(1)} %get-tuple-element.94.refs_1_, bf16[1024,6144]{1,0:T(8,128)(2,1)S(1)} %get-tuple-element.82.refs_2_.refs_5_.refs_3_, f32[512,1024]{1,0:T(8,128)S(1)} %grad_near.1.refs_3_.refs_4_), custom_call_target="tpu_custom_call" | custom-call | tf_op jit(solution)/shard_map/project_far/pallas_call | solution.py:59
  53.1 1.2 %collective-permute-start.16 = (bf16[256,1536]{1,0:T(8,128)(2,1)S(1)}, bf16[256,1536]{1,0:T(8,128)(2,1)S(1)}, u32[]{:S(2)}, u32[]{:S(2)}) collective-permute-start(bf16[256,1536]{1,0:T(8,128)(2,1)S(1)} %get-tuple-element.111), channel_id=1, source_target_pairs={{0,3},{1,0},{2,1},{3,2},{4,7},{5,4},{6,5},{7,6},{8,11},{9,8},{10,9... | collective-permute-start | bytes 2359304 | tf_op jit(solution)/shard_map/ppermute | solution.py:506
  54.3 0.9 collective-permute-start.15
  55.2 4.0 %project_near.1 = (f32[256,1536]{1,0:T(8,128)S(1)}, bf16[256,1536]{1,0:T(8,128)(2,1)S(1)}, bf16[256,1536]{1,0:T(8,128)(2,1)S(1)}, f32[256,1536]{1,0:T(8,128)S(1)}) custom-call(s32[15]{0:T(128)S(1)} %stack.60.refs_0_, bf16[512,1024]{1,0:T(8,128)(2,1)S(1)} %get-tuple-element.94.refs_1_, bf16[1024,6144]{1,0:T(8,128)(2,1)S(1)} %get-tuple-element.82.refs_2_.refs_5_.refs_3_, ...), custom_call_target="tpu_custom_call" | custom-call | tf_op jit(solution)/shard_map/project_near/pallas_call | solution.py:59
  59.2 6.8 %grad_far.1 = (bf16[512,1024]{1,0:T(8,128)(2,1)S(1)}, bf16[528,128]{1,0:T(8,128)(2,1)S(1)}, bf16[528,128]{1,0:T(8,128)(2,1)S(1)}) custom-call(s32[15]{0:T(128)S(1)} %stack.60.refs_0_, bf16[256,1536]{1,0:T(8,128)(2,1)S(1)} %collective-permute-done.8.refs_1_, bf16[256,1536]{1,0:T(8,128)(2,1)S(1)} %collective-permute-done.9.refs_2_, ...), custom_call_target="tpu_custom_call" | custom-call | tf_op jit(solution)/shard_map/grad_far/pallas_call | solution.py:59
  66.1 1.3 %collective-permute-done.12.refs_2_.refs_5_ = bf16[528,128]{1,0:T(8,128)(2,1)S(1)} collective-permute-done((bf16[528,128]{1,0:T(8,128)(2,1)S(1)}, bf16[528,128]{1,0:T(8,128)(2,1)S(1)}, u32[]{:S(2)}, u32[]{:S(2)}) %collective-permute-start.12) | collective-permute-done | bytes 135200 | tf_op jit(solution)/shard_map/ppermute | solution.py:249
  68.0 1.0 collective-permute-start.13
  69.1 2.8 %collective-permute-start.19 = (bf16[256,1536]{1,0:T(8,128)(2,1)S(1)}, bf16[256,1536]{1,0:T(8,128)(2,1)S(1)}, u32[]{:S(2)}, u32[]{:S(2)}) collective-permute-start(bf16[256,1536]{1,0:T(8,128)(2,1)S(1)} %get-tuple-element.120), channel_id=1, source_target_pairs={{0,3},{1,0},{2,1},{3,2},{4,7},{5,4},{6,5},{7,6},{8,11},{9,8},{10,9... | collective-permute-start | bytes 2359304 | tf_op jit(solution)/shard_map/ppermute | solution.py:506
  71.9 3.4 %inside.2 = (bf16[512,512]{1,0:T(8,128)(2,1)S(1)}, f32[512,512]{1,0:T(8,128)S(1)}, f32[512,512]{1,0:T(8,128)S(1)}) custom-call(s32[15]{0:T(128)S(1)} %stack.60.refs_0_, f32[512,8]{1,0:T(8,128)S(1)} %get-tuple-element.70.refs_1_, f32[8,512]{1,0:T(8,128)S(1)} %get-tuple-element.71.refs_2_.refs_8_, bf16[512,1024]{1,0:T(8,128)(2,1)S(1)} %get-tuple-element.72.refs_3_, ...), custom_call_target="tpu_custom_call" | custom-call | tf_op jit(solution)/shard_map/inside/pallas_call | solution.py:59
  76.0 0.9 join.1
  76.9 3.3 %collective-permute-start.21 = (bf16[256,1536]{1,0:T(8,128)(2,1)S(1)}, bf16[256,1536]{1,0:T(8,128)(2,1)S(1)}, u32[]{:S(2)}, u32[]{:S(2)}) collective-permute-start(bf16[256,1536]{1,0:T(8,128)(2,1)S(1)} %get-tuple-element.122), channel_id=1, source_target_pairs={{0,3},{1,0},{2,1},{3,2},{4,7},{5,4},{6,5},{7,6},{8,11},{9,8},{10,9... | collective-permute-start | bytes 2359304 | tf_op jit(solution)/shard_map/ppermute | solution.py:506
  80.2 2.7 %collective-permute-start.14 = (bf16[528,128]{1,0:T(8,128)(2,1)S(1)}, bf16[528,128]{1,0:T(8,128)(2,1)S(1)}, u32[]{:S(2)}, u32[]{:S(2)}) collective-permute-start(bf16[528,128]{1,0:T(8,128)(2,1)S(1)} %get-tuple-element.107.refs_1_), channel_id=1, source_target_pairs={{0,16},{4,20},{8,24},{12,28},{16,0},{20,4},{24,8},{28,12},{32,48},... | collective-permute-start | bytes 405512 | tf_op jit(solution)/shard_map/ppermute | solution.py:254
  82.9 3.8 %collective-permute-done.14.refs_2_ = bf16[528,128]{1,0:T(8,128)(2,1)S(1)} collective-permute-done((bf16[528,128]{1,0:T(8,128)(2,1)S(1)}, bf16[528,128]{1,0:T(8,128)(2,1)S(1)}, u32[]{:S(2)}, u32[]{:S(2)}) %collective-permute-start.14) | collective-permute-done | bytes 135200 | tf_op jit(solution)/shard_map/ppermute | solution.py:254
  86.7 0.6 meet.10
  87.4 2.0 %collective-permute-start.17 = (bf16[528,128]{1,0:T(8,128)(2,1)S(1)}, bf16[528,128]{1,0:T(8,128)(2,1)S(1)}, u32[]{:S(2)}, u32[]{:S(2)}) collective-permute-start(bf16[528,128]{1,0:T(8,128)(2,1)S(1)} %get-tuple-element.113.refs_1_), channel_id=1, source_target_pairs={{0,32},{4,36},{8,40},{12,44},{16,48},{20,52},{24,56},{28,60},{32,0... | collective-permute-start | bytes 405512 | tf_op jit(solution)/shard_map/ppermute | solution.py:254
  89.4 4.4 %inside.3 = (bf16[512,1024]{1,0:T(8,128)(2,1)}, f32[512,512]{1,0:T(8,128)S(1)}, f32[512,512]{1,0:T(8,128)S(1)}) custom-call(s32[15]{0:T(128)S(1)} %stack.60.refs_0_, f32[512,8]{1,0:T(8,128)S(1)} %get-tuple-element.70.refs_1_, f32[8,512]{1,0:T(8,128)S(1)} %get-tuple-element.71.refs_2_.refs_8_, bf16[512,1024]{1,0:T(8,128)(2,1)S(1)} %get-tuple-element.72.refs_3_, ...), custom_call_target="tpu_custom_call" | custom-call | tf_op jit(solution)/shard_map/inside/pallas_call | solution.py:59
  93.8 0.6 meet.11
  94.4 3.7 %collective-permute-start.22 = (bf16[528,128]{1,0:T(8,128)(2,1)S(1)}, bf16[528,128]{1,0:T(8,128)(2,1)S(1)}, u32[]{:S(2)}, u32[]{:S(2)}) collective-permute-start(bf16[528,128]{1,0:T(8,128)(2,1)S(1)} %get-tuple-element.126), channel_id=1, source_target_pairs={{0,64},{4,68},{8,72},{12,76},{16,80},{20,84},{24,88},{28,92},{32,9... | collective-permute-start | bytes 405512 | tf_op jit(solution)/shard_map/ppermute | solution.py:266
  98.1 2.4 %project_own.1 = (f32[256,1536]{1,0:T(8,128)S(1)}, f32[256,1536]{1,0:T(8,128)S(1)}) custom-call(s32[15]{0:T(128)S(1)} %stack.60.refs_0_, bf16[512,1024]{1,0:T(8,128)(2,1)S(1)} %get-tuple-element.94.refs_1_, bf16[1024,6144]{1,0:T(8,128)(2,1)S(1)} %get-tuple-element.82.refs_2_.refs_5_.refs_3_, f32[8,128]{1,0:T(8,128)S(1)} %get-tuple-element.117.refs_3_), custom_call_target="tpu_custom_call" | custom-call | tf_op jit(solution)/shard_map/project_own/pallas_call | solution.py:59
  101.1 0.6 arrive.3
  101.8 1.3 %collective-permute-done.23.refs_9_ = bf16[512,128]{1,0:T(8,128)(2,1)S(1)} collective-permute-done((bf16[512,128]{1,0:T(8,128)(2,1)S(1)}, bf16[512,128]{1,0:T(8,128)(2,1)S(1)}, u32[]{:S(2)}, u32[]{:S(2)}) %collective-permute-start.23) | collective-permute-done | bytes 131104 | tf_op jit(solution)/shard_map/ppermute | solution.py:276
  103.1 2.7 %finish.1 = (bf16[512,1024]{1,0:T(8,128)(2,1)}, bf16[512,1024]{1,0:T(8,128)(2,1)}, f32[8,128]{1,0:T(8,128)S(1)}) custom-call(s32[15]{0:T(128)S(1)} %stack.60.refs_0_, f32[512,8]{1,0:T(8,128)S(1)} %get-tuple-element.70.refs_1_, bf16[512,1024]{1,0:T(8,128)(2,1)S(1)} %get-tuple-element.73.refs_4_.refs_2_, ...), custom_call_target="tpu_custom_call" | custom-call | tf_op jit(solution)/shard_map/finish/pallas_call | solution.py:59
  105.9 1.9 %collective-permute-done.21.refs_6_ = bf16[256,1536]{1,0:T(8,128)(2,1)S(1)} collective-permute-done((bf16[256,1536]{1,0:T(8,128)(2,1)S(1)}, bf16[256,1536]{1,0:T(8,128)(2,1)S(1)}, u32[]{:S(2)}, u32[]{:S(2)}) %collective-permute-start.21) | collective-permute-done | bytes 786464 | tf_op jit(solution)/shard_map/ppermute | solution.py:506
  107.8 1.2 %collective-permute-done.18.refs_3_ = bf16[256,1536]{1,0:T(8,128)(2,1)S(1)} collective-permute-done((bf16[256,1536]{1,0:T(8,128)(2,1)S(1)}, bf16[256,1536]{1,0:T(8,128)(2,1)S(1)}, u32[]{:S(2)}, u32[]{:S(2)}) %collective-permute-start.18) | collective-permute-done | bytes 786464 | tf_op jit(solution)/shard_map/ppermute | solution.py:505
  109.0 1.9 %total.1 = bf16[512,1536]{1,0:T(8,128)(2,1)} custom-call(s32[15]{0:T(128)S(1)} %stack.60.refs_0_, f32[256,1536]{1,0:T(8,128)S(1)} %get-tuple-element.118.refs_6_.refs_1_, f32[256,1536]{1,0:T(8,128)S(1)} %get-tuple-element.119.refs_2_, bf16[256,1536]{1,0:T(8,128)(2,1)S(1)} %collective-permute-done.18.refs_3_, ...), custom_call_target="tpu_custom_call" | custom-call | tf_op jit(solution)/shard_map/total/pallas_call | solution.py:59
  (31 shorter events, 4.6 us)
Async XLA Ops:
  2.8 29.5 %collective-permute-start.4 = (bf16[256,1536]{1,0:T(8,128)(2,1)S(1)}, bf16[256,1536]{1,0:T(8,128)(2,1)S(1)}, u32[]{:S(2)}, u32[]{:S(2)}) collective-permute-start(bf16[256,1536]{1,0:T(8,128)(2,1)S(1)} %get-tuple-element.86), channel_id=1, source_target_pairs={{0,1},{1,2},{2,3},{3,0},{4,5},{5,6},{6,7},{7,4},{8,9},{9,10},{10,1... | collective-permute-start | bytes 2359304 | tf_op jit(solution)/shard_map/ppermute | solution.py:505
  4.5 27.8 %collective-permute-start.5 = (bf16[256,1536]{1,0:T(8,128)(2,1)S(1)}, bf16[256,1536]{1,0:T(8,128)(2,1)S(1)}, u32[]{:S(2)}, u32[]{:S(2)}) collective-permute-start(bf16[256,1536]{1,0:T(8,128)(2,1)S(1)} %get-tuple-element.87), channel_id=1, source_target_pairs={{0,3},{1,0},{2,1},{3,2},{4,7},{5,4},{6,5},{7,6},{8,11},{9,8},{10,9... | collective-permute-start | bytes 2359304 | tf_op jit(solution)/shard_map/ppermute | solution.py:506
  6.1 0.7 copy-start.1
  11.2 3.4 %collective-permute-start = (bf16[528,128]{1,0:T(8,128)(2,1)S(1)}, bf16[528,128]{1,0:T(8,128)(2,1)S(1)}, u32[]{:S(2)}, u32[]{:S(2)}) collective-permute-start(bf16[528,128]{1,0:T(8,128)(2,1)S(1)} %get-tuple-element.76), channel_id=1, source_target_pairs={{0,4},{4,0},{8,12},{12,8},{16,20},{20,16},{24,28},{28,24},{32,36},... | collective-permute-start | bytes 405512 | tf_op jit(solution)/shard_map/ppermute | solution.py:249
  11.3 35.4 %collective-permute-start.10 = (bf16[256,1536]{1,0:T(8,128)(2,1)S(1)}, bf16[256,1536]{1,0:T(8,128)(2,1)S(1)}, u32[]{:S(2)}, u32[]{:S(2)}) collective-permute-start(bf16[256,1536]{1,0:T(8,128)(2,1)S(1)} %get-tuple-element.96), channel_id=1, source_target_pairs={{0,1},{1,2},{2,3},{3,0},{4,5},{5,6},{6,7},{7,4},{8,9},{9,10},{10,1... | collective-permute-start | bytes 2359304 | tf_op jit(solution)/shard_map/ppermute | solution.py:505
  11.8 34.9 %collective-permute-start.11 = (bf16[256,1536]{1,0:T(8,128)(2,1)S(1)}, bf16[256,1536]{1,0:T(8,128)(2,1)S(1)}, u32[]{:S(2)}, u32[]{:S(2)}) collective-permute-start(bf16[256,1536]{1,0:T(8,128)(2,1)S(1)} %get-tuple-element.97), channel_id=1, source_target_pairs={{0,3},{1,0},{2,1},{3,2},{4,7},{5,4},{6,5},{7,6},{8,11},{9,8},{10,9... | collective-permute-start | bytes 2359304 | tf_op jit(solution)/shard_map/ppermute | solution.py:506
  15.2 7.1 %collective-permute-start.1 = (bf16[528,128]{1,0:T(8,128)(2,1)S(1)}, bf16[528,128]{1,0:T(8,128)(2,1)S(1)}, u32[]{:S(2)}, u32[]{:S(2)}) collective-permute-start(bf16[528,128]{1,0:T(8,128)(2,1)S(1)} %chip_total.2.refs_7_.refs_1_), channel_id=1, source_target_pairs={{0,8},{4,12},{8,0},{12,4},{16,24},{20,28},{24,16},{28,20},{32,40},... | collective-permute-start | bytes 405512 | tf_op jit(solution)/shard_map/ppermute | solution.py:254
  22.3 3.5 %copy-start = (bf16[512,1536]{1,0:T(8,128)(2,1)S(1)}, bf16[512,1536]{1,0:T(8,128)(2,1)}, u32[]{:S(2)}) copy-start(bf16[512,1536]{1,0:T(8,128)(2,1)} %refs_1_.3) | copy-start | bytes 4718596
  23.0 6.7 %collective-permute-start.2 = (bf16[528,128]{1,0:T(8,128)(2,1)S(1)}, bf16[528,128]{1,0:T(8,128)(2,1)S(1)}, u32[]{:S(2)}, u32[]{:S(2)}) collective-permute-start(bf16[528,128]{1,0:T(8,128)(2,1)S(1)} %get-tuple-element.79.refs_1_), channel_id=1, source_target_pairs={{0,16},{4,20},{8,24},{12,28},{16,0},{20,4},{24,8},{28,12},{32,48},... | collective-permute-start | bytes 405512 | tf_op jit(solution)/shard_map/ppermute | solution.py:254
  30.3 5.1 %collective-permute-start.3 = (bf16[528,128]{1,0:T(8,128)(2,1)S(1)}, bf16[528,128]{1,0:T(8,128)(2,1)S(1)}, u32[]{:S(2)}, u32[]{:S(2)}) collective-permute-start(bf16[528,128]{1,0:T(8,128)(2,1)S(1)} %get-tuple-element.83.refs_1_), channel_id=1, source_target_pairs={{0,32},{4,36},{8,40},{12,44},{16,48},{20,52},{24,56},{28,60},{32,0... | collective-permute-start | bytes 405512 | tf_op jit(solution)/shard_map/ppermute | solution.py:254
  32.9 26.3 %collective-permute-start.9 = (bf16[256,1536]{1,0:T(8,128)(2,1)S(1)}, bf16[256,1536]{1,0:T(8,128)(2,1)S(1)}, u32[]{:S(2)}, u32[]{:S(2)}) collective-permute-start(bf16[256,1536]{1,0:T(8,128)(2,1)S(1)} %get-tuple-element.95), channel_id=1, source_target_pairs={{0,3},{1,0},{2,1},{3,2},{4,7},{5,4},{6,5},{7,6},{8,11},{9,8},{10,9... | collective-permute-start | bytes 2359304 | tf_op jit(solution)/shard_map/ppermute | solution.py:506
  33.6 25.6 %collective-permute-start.8 = (bf16[256,1536]{1,0:T(8,128)(2,1)S(1)}, bf16[256,1536]{1,0:T(8,128)(2,1)S(1)}, u32[]{:S(2)}, u32[]{:S(2)}) collective-permute-start(bf16[256,1536]{1,0:T(8,128)(2,1)S(1)} %get-tuple-element.88.refs_5_), channel_id=1, source_target_pairs={{0,1},{1,2},{2,3},{3,0},{4,5},{5,6},{6,7},{7,4},{8,9},{9,10},{10,1... | collective-permute-start | bytes 2359304 | tf_op jit(solution)/shard_map/ppermute | solution.py:505
  36.0 6.9 %collective-permute-start.6 = (bf16[528,128]{1,0:T(8,128)(2,1)S(1)}, bf16[528,128]{1,0:T(8,128)(2,1)S(1)}, u32[]{:S(2)}, u32[]{:S(2)}) collective-permute-start(bf16[528,128]{1,0:T(8,128)(2,1)S(1)} %get-tuple-element.89), channel_id=1, source_target_pairs={{0,64},{4,68},{8,72},{12,76},{16,80},{20,84},{24,88},{28,92},{32,9... | collective-permute-start | bytes 405512 | tf_op jit(solution)/shard_map/ppermute | solution.py:266
  43.6 1.6 %collective-permute-start.7 = (bf16[512,128]{1,0:T(8,128)(2,1)S(1)}, bf16[512,128]{1,0:T(8,128)(2,1)S(1)}, u32[]{:S(2)}, u32[]{:S(2)}) collective-permute-start(bf16[512,128]{1,0:T(8,128)(2,1)S(1)} %get-tuple-element.93), channel_id=1, source_target_pairs={{0,4},{4,0},{8,12},{12,8},{16,20},{20,16},{24,28},{28,24},{32,36},... | collective-permute-start | bytes 393224 | tf_op jit(solution)/shard_map/ppermute | solution.py:276
  53.1 22.9 %collective-permute-start.16 = (bf16[256,1536]{1,0:T(8,128)(2,1)S(1)}, bf16[256,1536]{1,0:T(8,128)(2,1)S(1)}, u32[]{:S(2)}, u32[]{:S(2)}) collective-permute-start(bf16[256,1536]{1,0:T(8,128)(2,1)S(1)} %get-tuple-element.111), channel_id=1, source_target_pairs={{0,3},{1,0},{2,1},{3,2},{4,7},{5,4},{6,5},{7,6},{8,11},{9,8},{10,9... | collective-permute-start | bytes 2359304 | tf_op jit(solution)/shard_map/ppermute | solution.py:506
  54.3 21.7 %collective-permute-start.15 = (bf16[256,1536]{1,0:T(8,128)(2,1)S(1)}, bf16[256,1536]{1,0:T(8,128)(2,1)S(1)}, u32[]{:S(2)}, u32[]{:S(2)}) collective-permute-start(bf16[256,1536]{1,0:T(8,128)(2,1)S(1)} %get-tuple-element.101.refs_3_), channel_id=1, source_target_pairs={{0,1},{1,2},{2,3},{3,0},{4,5},{5,6},{6,7},{7,4},{8,9},{9,10},{10,1... | collective-permute-start | bytes 2359304 | tf_op jit(solution)/shard_map/ppermute | solution.py:505
  66.0 1.4 %collective-permute-start.12 = (bf16[528,128]{1,0:T(8,128)(2,1)S(1)}, bf16[528,128]{1,0:T(8,128)(2,1)S(1)}, u32[]{:S(2)}, u32[]{:S(2)}) collective-permute-start(bf16[528,128]{1,0:T(8,128)(2,1)S(1)} %get-tuple-element.104), channel_id=1, source_target_pairs={{0,4},{4,0},{8,12},{12,8},{16,20},{20,16},{24,28},{28,24},{32,36},... | collective-permute-start | bytes 405512 | tf_op jit(solution)/shard_map/ppermute | solution.py:249
  68.0 7.3 %collective-permute-start.13 = (bf16[528,128]{1,0:T(8,128)(2,1)S(1)}, bf16[528,128]{1,0:T(8,128)(2,1)S(1)}, u32[]{:S(2)}, u32[]{:S(2)}) collective-permute-start(bf16[528,128]{1,0:T(8,128)(2,1)S(1)} %chip_total.3.refs_9_.refs_1_), channel_id=1, source_target_pairs={{0,8},{4,12},{8,0},{12,4},{16,24},{20,28},{24,16},{28,20},{32,40},... | collective-permute-start | bytes 405512 | tf_op jit(solution)/shard_map/ppermute | solution.py:254
  69.1 36.8 %collective-permute-start.19 = (bf16[256,1536]{1,0:T(8,128)(2,1)S(1)}, bf16[256,1536]{1,0:T(8,128)(2,1)S(1)}, u32[]{:S(2)}, u32[]{:S(2)}) collective-permute-start(bf16[256,1536]{1,0:T(8,128)(2,1)S(1)} %get-tuple-element.120), channel_id=1, source_target_pairs={{0,3},{1,0},{2,1},{3,2},{4,7},{5,4},{6,5},{7,6},{8,11},{9,8},{10,9... | collective-permute-start | bytes 2359304 | tf_op jit(solution)/shard_map/ppermute | solution.py:506
  71.9 33.9 %collective-permute-start.20 = (bf16[256,1536]{1,0:T(8,128)(2,1)S(1)}, bf16[256,1536]{1,0:T(8,128)(2,1)S(1)}, u32[]{:S(2)}, u32[]{:S(2)}) collective-permute-start(bf16[256,1536]{1,0:T(8,128)(2,1)S(1)} %get-tuple-element.121), channel_id=1, source_target_pairs={{0,1},{1,2},{2,3},{3,0},{4,5},{5,6},{6,7},{7,4},{8,9},{9,10},{10,1... | collective-permute-start | bytes 2359304 | tf_op jit(solution)/shard_map/ppermute | solution.py:505
  76.9 30.9 %collective-permute-start.21 = (bf16[256,1536]{1,0:T(8,128)(2,1)S(1)}, bf16[256,1536]{1,0:T(8,128)(2,1)S(1)}, u32[]{:S(2)}, u32[]{:S(2)}) collective-permute-start(bf16[256,1536]{1,0:T(8,128)(2,1)S(1)} %get-tuple-element.122), channel_id=1, source_target_pairs={{0,3},{1,0},{2,1},{3,2},{4,7},{5,4},{6,5},{7,6},{8,11},{9,8},{10,9... | collective-permute-start | bytes 2359304 | tf_op jit(solution)/shard_map/ppermute | solution.py:506
  80.2 28.8 %collective-permute-start.18 = (bf16[256,1536]{1,0:T(8,128)(2,1)S(1)}, bf16[256,1536]{1,0:T(8,128)(2,1)S(1)}, u32[]{:S(2)}, u32[]{:S(2)}) collective-permute-start(bf16[256,1536]{1,0:T(8,128)(2,1)S(1)} %get-tuple-element.112.refs_5_), channel_id=1, source_target_pairs={{0,1},{1,2},{2,3},{3,0},{4,5},{5,6},{6,7},{7,4},{8,9},{9,10},{10,1... | collective-permute-start | bytes 2359304 | tf_op jit(solution)/shard_map/ppermute | solution.py:505
  80.2 6.5 %collective-permute-start.14 = (bf16[528,128]{1,0:T(8,128)(2,1)S(1)}, bf16[528,128]{1,0:T(8,128)(2,1)S(1)}, u32[]{:S(2)}, u32[]{:S(2)}) collective-permute-start(bf16[528,128]{1,0:T(8,128)(2,1)S(1)} %get-tuple-element.107.refs_1_), channel_id=1, source_target_pairs={{0,16},{4,20},{8,24},{12,28},{16,0},{20,4},{24,8},{28,12},{32,48},... | collective-permute-start | bytes 405512 | tf_op jit(solution)/shard_map/ppermute | solution.py:254
  87.4 6.4 %collective-permute-start.17 = (bf16[528,128]{1,0:T(8,128)(2,1)S(1)}, bf16[528,128]{1,0:T(8,128)(2,1)S(1)}, u32[]{:S(2)}, u32[]{:S(2)}) collective-permute-start(bf16[528,128]{1,0:T(8,128)(2,1)S(1)} %get-tuple-element.113.refs_1_), channel_id=1, source_target_pairs={{0,32},{4,36},{8,40},{12,44},{16,48},{20,52},{24,56},{28,60},{32,0... | collective-permute-start | bytes 405512 | tf_op jit(solution)/shard_map/ppermute | solution.py:254
  94.4 6.6 %collective-permute-start.22 = (bf16[528,128]{1,0:T(8,128)(2,1)S(1)}, bf16[528,128]{1,0:T(8,128)(2,1)S(1)}, u32[]{:S(2)}, u32[]{:S(2)}) collective-permute-start(bf16[528,128]{1,0:T(8,128)(2,1)S(1)} %get-tuple-element.126), channel_id=1, source_target_pairs={{0,64},{4,68},{8,72},{12,76},{16,80},{20,84},{24,88},{28,92},{32,9... | collective-permute-start | bytes 405512 | tf_op jit(solution)/shard_map/ppermute | solution.py:266
  101.7 1.4 %collective-permute-start.23 = (bf16[512,128]{1,0:T(8,128)(2,1)S(1)}, bf16[512,128]{1,0:T(8,128)(2,1)S(1)}, u32[]{:S(2)}, u32[]{:S(2)}) collective-permute-start(bf16[512,128]{1,0:T(8,128)(2,1)S(1)} %get-tuple-element.129), channel_id=1, source_target_pairs={{0,4},{4,0},{8,12},{12,8},{16,20},{20,16},{24,28},{28,24},{32,36},... | collective-permute-start | bytes 393224 | tf_op jit(solution)/shard_map/ppermute | solution.py:276

commit v5 on v4

--- a/solution.py
+++ b/solution.py
@@ -44,6 +44,7 @@
     project_own=0,
     grad_far=0,
     join=0,
+    add_direct=0,
     inside=0,
     finish=0,
     total=0,
@@ -385,13 +386,18 @@
     out_left[...] = (left_ref[...] + from_right[...].astype(F32)).astype(BF16)
 
 
-def total_kernel(s_ref, top_ref, bottom_ref, top_a, top_b, bottom_a, bottom_b, out_ref, out_held, sems):
+def add_direct_kernel(s_ref, top_ref, bottom_ref, from_right, from_left, top_out, bottom_out):
+    top_out[...] = top_ref[...] + from_right[...].astype(F32)
+    bottom_out[...] = bottom_ref[...] + from_left[...].astype(F32)
+
+
+def total_kernel(s_ref, top_ref, bottom_ref, from_left, from_right, out_ref, out_held, sems):
     copies = []
-    for i, (own_ref, a_ref, b_ref) in enumerate(((top_ref, top_a, top_b), (bottom_ref, bottom_a, bottom_b))):
+    for i, (own_ref, a_ref) in enumerate(((top_ref, from_left), (bottom_ref, from_right))):
         for j in range(2):
             rows = slice(j * 128, j * 128 + 128)
             here = slice(i * 256 + j * 128, i * 256 + j * 128 + 128)
-            total = own_ref[rows, :] + a_ref[rows, :].astype(F32) + b_ref[rows, :].astype(F32)
+            total = own_ref[rows, :] + a_ref[rows, :].astype(F32)
             out_held[here, :] = total.astype(BF16)
             copies.append(pltpu.make_async_copy(out_held.at[here, :], out_ref.at[here, :], sems.at[i * 2 + j]))
             copies[-1].start()
@@ -594,7 +600,18 @@
         made["own"] = call(one, "project_own", scalars, (normed, w), [WIDE_HALF] * 2, after)
         return made["own"][:1]
 
-    keep_g, got_g = scan_blocks(scalars, mine_g, send_g, 5, (inside_first, join, inside_second, project_own))
+    def add_direct(after):
+        parts = (*made["own"], direct_l, direct_r)
+        made["own"] = call(add_direct_kernel, "add_direct", scalars, parts, [WIDE_HALF] * 2, after)
+        return made["own"][:1]
+
+    turns = (
+        inside_first,
+        lambda after: project_own(join(after)),
+        lambda after: add_direct(inside_second(after)),
+        lambda after: after,
+    )
+    keep_g, got_g = scan_blocks(scalars, mine_g, send_g, 5, turns)
     joined_r, joined_l = right(made["joined"][0]), left(made["joined"][1])
     gq = made["b"][0]
     gk, gv, order = call(
@@ -610,7 +627,7 @@
         total_kernel,
         "total",
         scalars,
-        (*made["own"], joined_r, direct_l, direct_r, joined_l),
+        (*made["own"], joined_r, joined_l),
         [WHOLE],
         (order,),
         far_outs=(0,),

time: 111 us -> 110 us (level)
  waiting for transfers between devices: 16.4 us -> 14 us
    ppermute x2, waiting for transfers between devices: 3.61 us -> 5.98 us  [scan_blocks(): met = lax.ppermute(total, 'seq', MEETINGS[3])]
    ppermute x6, waiting for transfers between devices: 5.64 us -> 3.49 us  [scan_blocks(): met = lax.ppermute(total, 'seq', MEETINGS[turn])]
    ppermute x6, starting transfers between devices: 12.2 us -> 13.6 us  [scan_blocks(): met = lax.ppermute(total, 'seq', MEETINGS[turn])]
    ppermute x2, waiting for transfers between devices: 1.34 us -> 0.01 us  [scan_blocks(): got = lax.ppermute(send, 'seq', SWAP)]
    ppermute x6, waiting for transfers between devices: 1.24 us -> 0.08 us  [body(): right = lambda a: lax.ppermute(a, 'head', RIGHT)]
    pallas_call x26 -> x27, Pallas kernels: 55.4 us -> 56.2 us  [call(): pl.pallas_call(run, out_shape=[jax.ShapeDtypeStruct(shape, dtype) for sha...]
  transfers between devices with their start and end apart: 24 -> 24, of which waited for: 10 -> 11; matrix products, arithmetic and copies ran while one was open for 0% -> 0% of each run, Pallas kernels for 46% -> 48%
where the time goes in v5:
time: 110 us
  Pallas kernels  56.2 us (51%)
  starting transfers between devices  38.3 us (35%)
  waiting for transfers between devices  14 us (13%)
  between operations  1.19 us (1%)
    pallas_call x27, Pallas kernels, call(): pl.pallas_call(run, out_shape=[jax.ShapeDtypeStruct(shape, dtype) for sha...  56.2 us
    ppermute x6, starting transfers between devices, scan_blocks(): met = lax.ppermute(total, 'seq', MEETINGS[turn])  13.6 us
    ppermute x6, starting transfers between devices, body(): left = lambda a: lax.ppermute(a, 'head', LEFT)  12.1 us
    ppermute x2, starting transfers between devices, scan_blocks(): met = lax.ppermute(total, 'seq', MEETINGS[3])  7.62 us
    ppermute x2, waiting for transfers between devices, scan_blocks(): met = lax.ppermute(total, 'seq', MEETINGS[3])  5.98 us
    ppermute x6, starting transfers between devices, body(): right = lambda a: lax.ppermute(a, 'head', RIGHT)  4.54 us
    ppermute x6, waiting for transfers between devices, scan_blocks(): met = lax.ppermute(total, 'seq', MEETINGS[turn])  3.49 us
    ppermute x2, waiting for transfers between devices, scan_blocks(): return (keep, lax.ppermute(send_back, 'seq', SWAP))  2.67 us
  transfers between devices with their start and end apart: 24, of which 11 were waited for; matrix products, arithmetic and copies ran while one was open for 0% of the time, Pallas kernels for 48%

profile of v5, /device:TPU:0, one launch (start us, length us, event | category | flops | bytes accessed | tf_op | source)
XLA Modules:
  0.0 109.8 jit_solution(10619078937715415950)
XLA Ops:
  0.9 1.9 %halves.1 = (bf16[256,1536]{1,0:T(8,128)(2,1)S(1)}, bf16[256,1536]{1,0:T(8,128)(2,1)S(1)}, f32[8,128]{1,0:T(8,128)S(1)}) custom-call(s32[15]{0:T(128)S(1)} %stack.60.refs_0_, bf16[512,1536]{1,0:T(8,128)(2,1)} %refs_1_.3), custom_call_target="tpu_custom_call" | custom-call | tf_op jit(solution)/shard_map/halves/pallas_call | solution.py:60
  2.8 1.7 %collective-permute-start.4 = (bf16[256,1536]{1,0:T(8,128)(2,1)S(1)}, bf16[256,1536]{1,0:T(8,128)(2,1)S(1)}, u32[]{:S(2)}, u32[]{:S(2)}) collective-permute-start(bf16[256,1536]{1,0:T(8,128)(2,1)S(1)} %get-tuple-element.88), channel_id=1, source_target_pairs={{0,1},{1,2},{2,3},{3,0},{4,5},{5,6},{6,7},{7,4},{8,9},{9,10},{10,1... | collective-permute-start | bytes 2359304 | tf_op jit(solution)/shard_map/ppermute | solution.py:511
  4.5 1.6 %collective-permute-start.5 = (bf16[256,1536]{1,0:T(8,128)(2,1)S(1)}, bf16[256,1536]{1,0:T(8,128)(2,1)S(1)}, u32[]{:S(2)}, u32[]{:S(2)}) collective-permute-start(bf16[256,1536]{1,0:T(8,128)(2,1)S(1)} %get-tuple-element.89), channel_id=1, source_target_pairs={{0,3},{1,0},{2,1},{3,2},{4,7},{5,4},{6,5},{7,6},{8,11},{9,8},{10,9... | collective-permute-start | bytes 2359304 | tf_op jit(solution)/shard_map/ppermute | solution.py:512
  6.1 4.4 %own_states.1 = (f32[512,8]{1,0:T(8,128)S(1)}, f32[8,512]{1,0:T(8,128)S(1)}, bf16[528,128]{1,0:T(8,128)(2,1)S(1)}, bf16[528,128]{1,0:T(8,128)(2,1)S(1)}, bf16[51...) custom-call(s32[15]{0:T(128)S(1)} %stack.60.refs_0_, ...), custom_call_target="tpu_custom_call" | custom-call | flops 8000000000 | tf_op jit(solution)/shard_map/own_states/pallas_call | solution.py:60
  11.1 2.8 %collective-permute-start.9 = (bf16[256,1536]{1,0:T(8,128)(2,1)S(1)}, bf16[256,1536]{1,0:T(8,128)(2,1)S(1)}, u32[]{:S(2)}, u32[]{:S(2)}) collective-permute-start(bf16[256,1536]{1,0:T(8,128)(2,1)S(1)} %get-tuple-element.98), channel_id=1, source_target_pairs={{0,3},{1,0},{2,1},{3,2},{4,7},{5,4},{6,5},{7,6},{8,11},{9,8},{10,9... | collective-permute-start | bytes 2359304 | tf_op jit(solution)/shard_map/ppermute | solution.py:512
  14.5 1.7 %collective-permute-start.1 = (bf16[528,128]{1,0:T(8,128)(2,1)S(1)}, bf16[528,128]{1,0:T(8,128)(2,1)S(1)}, u32[]{:S(2)}, u32[]{:S(2)}) collective-permute-start(bf16[528,128]{1,0:T(8,128)(2,1)S(1)} %chip_total.2.refs_7_.refs_1_), channel_id=1, source_target_pairs={{0,8},{4,12},{8,0},{12,4},{16,24},{20,28},{24,16},{28,20},{32,40},... | collective-permute-start | bytes 405512 | tf_op jit(solution)/shard_map/ppermute | solution.py:255
  16.1 5.5 %local.1 = (f32[512,1024]{1,0:T(8,128)S(1)}, bf16[512,1024]{1,0:T(8,128)(2,1)S(1)}, bf16[1024,512]{1,0:T(8,128)(2,1)S(1)}, bf16[1024,6144]{1,0:T(8,128)(2,1)S(1)}) custom-call(s32[15]{0:T(128)S(1)} %stack.60.refs_0_, f32[512,8]{1,0:T(8,128)S(1)} %get-tuple-element.72.refs_1_, f32[8,512]{1,0:T(8,128)S(1)} %get-tuple-element.73.refs_2_.refs_8_, ...), custom_call_target="tpu_custom_call" | custom-call | tf_op jit(solution)/shard_map/local/pallas_call | solution.py:60
  22.3 2.8 %collective-permute-start.2 = (bf16[528,128]{1,0:T(8,128)(2,1)S(1)}, bf16[528,128]{1,0:T(8,128)(2,1)S(1)}, u32[]{:S(2)}, u32[]{:S(2)}) collective-permute-start(bf16[528,128]{1,0:T(8,128)(2,1)S(1)} %get-tuple-element.81.refs_1_), channel_id=1, source_target_pairs={{0,16},{4,20},{8,24},{12,28},{16,0},{20,4},{24,8},{28,12},{32,48},... | collective-permute-start | bytes 405512 | tf_op jit(solution)/shard_map/ppermute | solution.py:255
  25.1 2.4 %grad_own.1.refs_5_.refs_6_ = f32[512,1024]{1,0:T(8,128)S(1)} custom-call(s32[15]{0:T(128)S(1)} %stack.60.refs_0_, bf16[512,1536]{1,0:T(8,128)(2,1)S(1)} %copy-done, bf16[1024,6144]{1,0:T(8,128)(2,1)S(1)} %get-tuple-element.84.refs_2_.refs_5_.refs_3_, f32[8,128]{1,0:T(8,128)S(1)} %get-tuple-element.83.refs_3_.refs_4_), custom_call_target="tpu_custom_call" | custom-call | tf_op jit(solution)/shard_map/grad_own/pallas_call | solution.py:60
  27.4 1.5 %collective-permute-done.2.refs_2_ = bf16[528,128]{1,0:T(8,128)(2,1)S(1)} collective-permute-done((bf16[528,128]{1,0:T(8,128)(2,1)S(1)}, bf16[528,128]{1,0:T(8,128)(2,1)S(1)}, u32[]{:S(2)}, u32[]{:S(2)}) %collective-permute-start.2) | collective-permute-done | bytes 135200 | tf_op jit(solution)/shard_map/ppermute | solution.py:255
  28.9 0.6 meet.7
  29.6 2.0 %collective-permute-start.3 = (bf16[528,128]{1,0:T(8,128)(2,1)S(1)}, bf16[528,128]{1,0:T(8,128)(2,1)S(1)}, u32[]{:S(2)}, u32[]{:S(2)}) collective-permute-start(bf16[528,128]{1,0:T(8,128)(2,1)S(1)} %get-tuple-element.85.refs_1_), channel_id=1, source_target_pairs={{0,32},{4,36},{8,40},{12,44},{16,48},{20,52},{24,56},{28,60},{32,0... | collective-permute-start | bytes 405512 | tf_op jit(solution)/shard_map/ppermute | solution.py:255
  31.6 0.6 split.1
  32.2 0.7 collective-permute-start.13
  32.9 1.4 %collective-permute-start.12 = (bf16[256,1536]{1,0:T(8,128)(2,1)S(1)}, bf16[256,1536]{1,0:T(8,128)(2,1)S(1)}, u32[]{:S(2)}, u32[]{:S(2)}) collective-permute-start(bf16[256,1536]{1,0:T(8,128)(2,1)S(1)} %get-tuple-element.90.refs_5_), channel_id=1, source_target_pairs={{0,1},{1,2},{2,3},{3,0},{4,5},{5,6},{6,7},{7,4},{8,9},{9,10},{10,1... | collective-permute-start | bytes 2359304 | tf_op jit(solution)/shard_map/ppermute | solution.py:511
  34.7 0.6 meet.8
  35.3 4.0 %collective-permute-start.6 = (bf16[528,128]{1,0:T(8,128)(2,1)S(1)}, bf16[528,128]{1,0:T(8,128)(2,1)S(1)}, u32[]{:S(2)}, u32[]{:S(2)}) collective-permute-start(bf16[528,128]{1,0:T(8,128)(2,1)S(1)} %get-tuple-element.91), channel_id=1, source_target_pairs={{0,64},{4,68},{8,72},{12,76},{16,80},{20,84},{24,88},{28,92},{32,9... | collective-permute-start | bytes 405512 | tf_op jit(solution)/shard_map/ppermute | solution.py:267
  39.2 3.0 %collective-permute-done.6.refs_1_ = bf16[528,128]{1,0:T(8,128)(2,1)S(1)} collective-permute-done((bf16[528,128]{1,0:T(8,128)(2,1)S(1)}, bf16[528,128]{1,0:T(8,128)(2,1)S(1)}, u32[]{:S(2)}, u32[]{:S(2)}) %collective-permute-start.6) | collective-permute-done | bytes 135200 | tf_op jit(solution)/shard_map/ppermute | solution.py:267
  42.2 0.6 arrive.2
  43.2 1.3 %collective-permute-done.7.refs_4_.refs_8_ = bf16[512,128]{1,0:T(8,128)(2,1)S(1)} collective-permute-done((bf16[512,128]{1,0:T(8,128)(2,1)S(1)}, bf16[512,128]{1,0:T(8,128)(2,1)S(1)}, u32[]{:S(2)}, u32[]{:S(2)}) %collective-permute-start.7) | collective-permute-done | bytes 131104 | tf_op jit(solution)/shard_map/ppermute | solution.py:277
  44.5 1.5 %attend.1 = (bf16[512,1024]{1,0:T(8,128)(2,1)S(1)}, f32[512,1024]{1,0:T(8,128)S(1)}, f32[512,1024]{1,0:T(8,128)S(1)}) custom-call(s32[15]{0:T(128)S(1)} %stack.60.refs_0_, f32[512,1024]{1,0:T(8,128)S(1)} %get-tuple-element.79.refs_3_.refs_1_, bf16[512,1024]{1,0:T(8,128)(2,1)S(1)} %get-tuple-element.80.refs_2_, ...), custom_call_target="tpu_custom_call" | custom-call | tf_op jit(solution)/shard_map/attend/pallas_call | solution.py:60
  46.0 4.0 %grad_near.1.refs_3_.refs_4_ = f32[512,1024]{1,0:T(8,128)S(1)} custom-call(s32[15]{0:T(128)S(1)} %stack.60.refs_0_, bf16[256,1536]{1,0:T(8,128)(2,1)S(1)} %collective-permute-done.4.refs_1_, bf16[256,1536]{1,0:T(8,128)(2,1)S(1)} %collective-permute-done.8.refs_2_, bf16[256,1536]{1,0:T(8,128)(2,1)S(1)} %collective-permute-done.9.refs_3_, ...), custom_call_target="tpu_custom_call" | custom-call | tf_op jit(solution)/shard_map/grad_near/pallas_call | solution.py:60
  50.0 2.4 %project_far.1 = (bf16[256,1536]{1,0:T(8,128)(2,1)S(1)}, bf16[256,1536]{1,0:T(8,128)(2,1)S(1)}) custom-call(s32[15]{0:T(128)S(1)} %stack.60.refs_0_, bf16[512,1024]{1,0:T(8,128)(2,1)S(1)} %get-tuple-element.96.refs_1_, bf16[1024,6144]{1,0:T(8,128)(2,1)S(1)} %get-tuple-element.84.refs_2_.refs_5_.refs_3_, f32[512,1024]{1,0:T(8,128)S(1)} %grad_near.1.refs_3_.refs_4_), custom_call_target="tpu_custom_call" | custom-call | tf_op jit(solution)/shard_map/project_far/pallas_call | solution.py:60
  52.4 1.2 %collective-permute-start.11 = (bf16[256,1536]{1,0:T(8,128)(2,1)S(1)}, bf16[256,1536]{1,0:T(8,128)(2,1)S(1)}, u32[]{:S(2)}, u32[]{:S(2)}) collective-permute-start(bf16[256,1536]{1,0:T(8,128)(2,1)S(1)} %get-tuple-element.103), channel_id=1, source_target_pairs={{0,3},{1,0},{2,1},{3,2},{4,7},{5,4},{6,5},{7,6},{8,11},{9,8},{10,9... | collective-permute-start | bytes 2359304 | tf_op jit(solution)/shard_map/ppermute | solution.py:512
  53.6 0.9 collective-permute-start.10
  54.5 4.0 %project_near.1 = (f32[256,1536]{1,0:T(8,128)S(1)}, bf16[256,1536]{1,0:T(8,128)(2,1)S(1)}, bf16[256,1536]{1,0:T(8,128)(2,1)S(1)}, f32[256,1536]{1,0:T(8,128)S(1)}) custom-call(s32[15]{0:T(128)S(1)} %stack.60.refs_0_, bf16[512,1024]{1,0:T(8,128)(2,1)S(1)} %get-tuple-element.96.refs_1_, bf16[1024,6144]{1,0:T(8,128)(2,1)S(1)} %get-tuple-element.84.refs_2_.refs_5_.refs_3_, ...), custom_call_target="tpu_custom_call" | custom-call | tf_op jit(solution)/shard_map/project_near/pallas_call | solution.py:60
  58.7 6.8 %grad_far.1 = (bf16[512,1024]{1,0:T(8,128)(2,1)S(1)}, bf16[528,128]{1,0:T(8,128)(2,1)S(1)}, bf16[528,128]{1,0:T(8,128)(2,1)S(1)}) custom-call(s32[15]{0:T(128)S(1)} %stack.60.refs_0_, bf16[256,1536]{1,0:T(8,128)(2,1)S(1)} %collective-permute-done.12.refs_1_, bf16[256,1536]{1,0:T(8,128)(2,1)S(1)} %collective-permute-done.13.refs_2_, ...), custom_call_target="tpu_custom_call" | custom-call | tf_op jit(solution)/shard_map/grad_far/pallas_call | solution.py:60
  65.6 2.8 %collective-permute-start.16 = (bf16[256,1536]{1,0:T(8,128)(2,1)S(1)}, bf16[256,1536]{1,0:T(8,128)(2,1)S(1)}, u32[]{:S(2)}, u32[]{:S(2)}) collective-permute-start(bf16[256,1536]{1,0:T(8,128)(2,1)S(1)} %get-tuple-element.115), channel_id=1, source_target_pairs={{0,3},{1,0},{2,1},{3,2},{4,7},{5,4},{6,5},{7,6},{8,11},{9,8},{10,9... | collective-permute-start | bytes 2359304 | tf_op jit(solution)/shard_map/ppermute | solution.py:512
  69.0 1.9 %collective-permute-start.15 = (bf16[528,128]{1,0:T(8,128)(2,1)S(1)}, bf16[528,128]{1,0:T(8,128)(2,1)S(1)}, u32[]{:S(2)}, u32[]{:S(2)}) collective-permute-start(bf16[528,128]{1,0:T(8,128)(2,1)S(1)} %chip_total.3.refs_9_.refs_1_), channel_id=1, source_target_pairs={{0,8},{4,12},{8,0},{12,4},{16,24},{20,28},{24,16},{28,20},{32,40},... | collective-permute-start | bytes 405512 | tf_op jit(solution)/shard_map/ppermute | solution.py:255
  70.9 3.4 %inside.2 = (bf16[512,512]{1,0:T(8,128)(2,1)S(1)}, f32[512,512]{1,0:T(8,128)S(1)}, f32[512,512]{1,0:T(8,128)S(1)}) custom-call(s32[15]{0:T(128)S(1)} %stack.60.refs_0_, f32[512,8]{1,0:T(8,128)S(1)} %get-tuple-element.72.refs_1_, f32[8,512]{1,0:T(8,128)S(1)} %get-tuple-element.73.refs_2_.refs_8_, bf16[512,1024]{1,0:T(8,128)(2,1)S(1)} %get-tuple-element.74.refs_3_, ...), custom_call_target="tpu_custom_call" | custom-call | tf_op jit(solution)/shard_map/inside/pallas_call | solution.py:60
  74.3 0.6 collective-permute-done.15.refs_2_
  75.6 1.0 join.1
  76.6 3.0 %collective-permute-start.20 = (bf16[256,1536]{1,0:T(8,128)(2,1)S(1)}, bf16[256,1536]{1,0:T(8,128)(2,1)S(1)}, u32[]{:S(2)}, u32[]{:S(2)}) collective-permute-start(bf16[256,1536]{1,0:T(8,128)(2,1)S(1)} %get-tuple-element.123), channel_id=1, source_target_pairs={{0,3},{1,0},{2,1},{3,2},{4,7},{5,4},{6,5},{7,6},{8,11},{9,8},{10,9... | collective-permute-start | bytes 2359304 | tf_op jit(solution)/shard_map/ppermute | solution.py:512
  79.6 3.1 %collective-permute-start.18 = (bf16[528,128]{1,0:T(8,128)(2,1)S(1)}, bf16[528,128]{1,0:T(8,128)(2,1)S(1)}, u32[]{:S(2)}, u32[]{:S(2)}) collective-permute-start(bf16[528,128]{1,0:T(8,128)(2,1)S(1)} %get-tuple-element.117.refs_1_), channel_id=1, source_target_pairs={{0,16},{4,20},{8,24},{12,28},{16,0},{20,4},{24,8},{28,12},{32,48},... | collective-permute-start | bytes 405512 | tf_op jit(solution)/shard_map/ppermute | solution.py:255
  82.7 2.4 %project_own.1 = (f32[256,1536]{1,0:T(8,128)S(1)}, f32[256,1536]{1,0:T(8,128)S(1)}) custom-call(s32[15]{0:T(128)S(1)} %stack.60.refs_0_, bf16[512,1024]{1,0:T(8,128)(2,1)S(1)} %get-tuple-element.96.refs_1_, bf16[1024,6144]{1,0:T(8,128)(2,1)S(1)} %get-tuple-element.84.refs_2_.refs_5_.refs_3_, bf16[256,1536]{1,0:T(8,128)(2,1)S(1)} %get-tuple-element.112.refs_3_), custom_call_target="tpu_custom_call" | custom-call | tf_op jit(solution)/shard_map/project_own/pallas_call | solution.py:60
  85.1 1.0 collective-permute-done.18.refs_2_
  86.1 0.6 meet.10
  86.7 2.1 %collective-permute-start.21 = (bf16[528,128]{1,0:T(8,128)(2,1)S(1)}, bf16[528,128]{1,0:T(8,128)(2,1)S(1)}, u32[]{:S(2)}, u32[]{:S(2)}) collective-permute-start(bf16[528,128]{1,0:T(8,128)(2,1)S(1)} %get-tuple-element.127.refs_1_), channel_id=1, source_target_pairs={{0,32},{4,36},{8,40},{12,44},{16,48},{20,52},{24,56},{28,60},{32,0... | collective-permute-start | bytes 405512 | tf_op jit(solution)/shard_map/ppermute | solution.py:255
  88.8 4.4 %inside.3 = (bf16[512,1024]{1,0:T(8,128)(2,1)}, f32[512,512]{1,0:T(8,128)S(1)}, f32[512,512]{1,0:T(8,128)S(1)}) custom-call(s32[15]{0:T(128)S(1)} %stack.60.refs_0_, f32[512,8]{1,0:T(8,128)S(1)} %get-tuple-element.72.refs_1_, f32[8,512]{1,0:T(8,128)S(1)} %get-tuple-element.73.refs_2_.refs_8_, bf16[512,1024]{1,0:T(8,128)(2,1)S(1)} %get-tuple-element.74.refs_3_, ...), custom_call_target="tpu_custom_call" | custom-call | tf_op jit(solution)/shard_map/inside/pallas_call | solution.py:60
  93.3 0.9 add_direct.1
  94.2 0.6 meet.11
  94.8 3.7 %collective-permute-start.22 = (bf16[528,128]{1,0:T(8,128)(2,1)S(1)}, bf16[528,128]{1,0:T(8,128)(2,1)S(1)}, u32[]{:S(2)}, u32[]{:S(2)}) collective-permute-start(bf16[528,128]{1,0:T(8,128)(2,1)S(1)} %get-tuple-element.129), channel_id=1, source_target_pairs={{0,64},{4,68},{8,72},{12,76},{16,80},{20,84},{24,88},{28,92},{32,9... | collective-permute-start | bytes 405512 | tf_op jit(solution)/shard_map/ppermute | solution.py:267
  98.5 3.0 %collective-permute-done.22.refs_1_ = bf16[528,128]{1,0:T(8,128)(2,1)S(1)} collective-permute-done((bf16[528,128]{1,0:T(8,128)(2,1)S(1)}, bf16[528,128]{1,0:T(8,128)(2,1)S(1)}, u32[]{:S(2)}, u32[]{:S(2)}) %collective-permute-start.22) | collective-permute-done | bytes 135200 | tf_op jit(solution)/shard_map/ppermute | solution.py:267
  101.5 0.6 arrive.3
  102.2 1.3 %collective-permute-done.23.refs_9_ = bf16[512,128]{1,0:T(8,128)(2,1)S(1)} collective-permute-done((bf16[512,128]{1,0:T(8,128)(2,1)S(1)}, bf16[512,128]{1,0:T(8,128)(2,1)S(1)}, u32[]{:S(2)}, u32[]{:S(2)}) %collective-permute-start.23) | collective-permute-done | bytes 131104 | tf_op jit(solution)/shard_map/ppermute | solution.py:277
  103.5 2.7 %finish.1 = (bf16[512,1024]{1,0:T(8,128)(2,1)}, bf16[512,1024]{1,0:T(8,128)(2,1)}, f32[8,128]{1,0:T(8,128)S(1)}) custom-call(s32[15]{0:T(128)S(1)} %stack.60.refs_0_, f32[512,8]{1,0:T(8,128)S(1)} %get-tuple-element.72.refs_1_, bf16[512,1024]{1,0:T(8,128)(2,1)S(1)} %get-tuple-element.75.refs_4_.refs_2_, ...), custom_call_target="tpu_custom_call" | custom-call | tf_op jit(solution)/shard_map/finish/pallas_call | solution.py:60
  106.2 1.5 %collective-permute-done.20.refs_4_ = bf16[256,1536]{1,0:T(8,128)(2,1)S(1)} collective-permute-done((bf16[256,1536]{1,0:T(8,128)(2,1)S(1)}, bf16[256,1536]{1,0:T(8,128)(2,1)S(1)}, u32[]{:S(2)}, u32[]{:S(2)}) %collective-permute-start.20) | collective-permute-done | bytes 786464 | tf_op jit(solution)/shard_map/ppermute | solution.py:512
  107.9 1.8 %total.1 = bf16[512,1536]{1,0:T(8,128)(2,1)} custom-call(s32[15]{0:T(128)S(1)} %stack.60.refs_0_, f32[256,1536]{1,0:T(8,128)S(1)} %get-tuple-element.121.refs_5_.refs_1_, f32[256,1536]{1,0:T(8,128)S(1)} %get-tuple-element.122.refs_2_, bf16[256,1536]{1,0:T(8,128)(2,1)S(1)} %collective-permute-done.19.refs_3_, ...), custom_call_target="tpu_custom_call" | custom-call | tf_op jit(solution)/shard_map/total/pallas_call | solution.py:60
  (32 shorter events, 4.2 us)
Async XLA Ops:
  0.6 5.5 %copy-start.1 = (f32[512,8]{0,1:T(8,128)S(1)}, f32[512,8]{0,1:T(8,128)}, u32[]{:S(2)}) copy-start(f32[512,8]{0,1:T(8,128)} %param.9) | copy-start | bytes 49156
  2.8 28.8 %collective-permute-start.4 = (bf16[256,1536]{1,0:T(8,128)(2,1)S(1)}, bf16[256,1536]{1,0:T(8,128)(2,1)S(1)}, u32[]{:S(2)}, u32[]{:S(2)}) collective-permute-start(bf16[256,1536]{1,0:T(8,128)(2,1)S(1)} %get-tuple-element.88), channel_id=1, source_target_pairs={{0,1},{1,2},{2,3},{3,0},{4,5},{5,6},{6,7},{7,4},{8,9},{9,10},{10,1... | collective-permute-start | bytes 2359304 | tf_op jit(solution)/shard_map/ppermute | solution.py:511
  4.5 27.0 %collective-permute-start.5 = (bf16[256,1536]{1,0:T(8,128)(2,1)S(1)}, bf16[256,1536]{1,0:T(8,128)(2,1)S(1)}, u32[]{:S(2)}, u32[]{:S(2)}) collective-permute-start(bf16[256,1536]{1,0:T(8,128)(2,1)S(1)} %get-tuple-element.89), channel_id=1, source_target_pairs={{0,3},{1,0},{2,1},{3,2},{4,7},{5,4},{6,5},{7,6},{8,11},{9,8},{10,9... | collective-permute-start | bytes 2359304 | tf_op jit(solution)/shard_map/ppermute | solution.py:512
  10.5 3.4 %collective-permute-start = (bf16[528,128]{1,0:T(8,128)(2,1)S(1)}, bf16[528,128]{1,0:T(8,128)(2,1)S(1)}, u32[]{:S(2)}, u32[]{:S(2)}) collective-permute-start(bf16[528,128]{1,0:T(8,128)(2,1)S(1)} %get-tuple-element.78), channel_id=1, source_target_pairs={{0,4},{4,0},{8,12},{12,8},{16,20},{20,16},{24,28},{28,24},{32,36},... | collective-permute-start | bytes 405512 | tf_op jit(solution)/shard_map/ppermute | solution.py:250
  10.6 35.4 %collective-permute-start.8 = (bf16[256,1536]{1,0:T(8,128)(2,1)S(1)}, bf16[256,1536]{1,0:T(8,128)(2,1)S(1)}, u32[]{:S(2)}, u32[]{:S(2)}) collective-permute-start(bf16[256,1536]{1,0:T(8,128)(2,1)S(1)} %get-tuple-element.97), channel_id=1, source_target_pairs={{0,1},{1,2},{2,3},{3,0},{4,5},{5,6},{6,7},{7,4},{8,9},{9,10},{10,1... | collective-permute-start | bytes 2359304 | tf_op jit(solution)/shard_map/ppermute | solution.py:511
  11.1 34.9 %collective-permute-start.9 = (bf16[256,1536]{1,0:T(8,128)(2,1)S(1)}, bf16[256,1536]{1,0:T(8,128)(2,1)S(1)}, u32[]{:S(2)}, u32[]{:S(2)}) collective-permute-start(bf16[256,1536]{1,0:T(8,128)(2,1)S(1)} %get-tuple-element.98), channel_id=1, source_target_pairs={{0,3},{1,0},{2,1},{3,2},{4,7},{5,4},{6,5},{7,6},{8,11},{9,8},{10,9... | collective-permute-start | bytes 2359304 | tf_op jit(solution)/shard_map/ppermute | solution.py:512
  14.5 7.1 %collective-permute-start.1 = (bf16[528,128]{1,0:T(8,128)(2,1)S(1)}, bf16[528,128]{1,0:T(8,128)(2,1)S(1)}, u32[]{:S(2)}, u32[]{:S(2)}) collective-permute-start(bf16[528,128]{1,0:T(8,128)(2,1)S(1)} %chip_total.2.refs_7_.refs_1_), channel_id=1, source_target_pairs={{0,8},{4,12},{8,0},{12,4},{16,24},{20,28},{24,16},{28,20},{32,40},... | collective-permute-start | bytes 405512 | tf_op jit(solution)/shard_map/ppermute | solution.py:255
  21.6 3.5 %copy-start = (bf16[512,1536]{1,0:T(8,128)(2,1)S(1)}, bf16[512,1536]{1,0:T(8,128)(2,1)}, u32[]{:S(2)}) copy-start(bf16[512,1536]{1,0:T(8,128)(2,1)} %refs_1_.3) | copy-start | bytes 4718596
  22.3 6.7 %collective-permute-start.2 = (bf16[528,128]{1,0:T(8,128)(2,1)S(1)}, bf16[528,128]{1,0:T(8,128)(2,1)S(1)}, u32[]{:S(2)}, u32[]{:S(2)}) collective-permute-start(bf16[528,128]{1,0:T(8,128)(2,1)S(1)} %get-tuple-element.81.refs_1_), channel_id=1, source_target_pairs={{0,16},{4,20},{8,24},{12,28},{16,0},{20,4},{24,8},{28,12},{32,48},... | collective-permute-start | bytes 405512 | tf_op jit(solution)/shard_map/ppermute | solution.py:255
  29.6 5.1 %collective-permute-start.3 = (bf16[528,128]{1,0:T(8,128)(2,1)S(1)}, bf16[528,128]{1,0:T(8,128)(2,1)S(1)}, u32[]{:S(2)}, u32[]{:S(2)}) collective-permute-start(bf16[528,128]{1,0:T(8,128)(2,1)S(1)} %get-tuple-element.85.refs_1_), channel_id=1, source_target_pairs={{0,32},{4,36},{8,40},{12,44},{16,48},{20,52},{24,56},{28,60},{32,0... | collective-permute-start | bytes 405512 | tf_op jit(solution)/shard_map/ppermute | solution.py:255
  32.2 26.5 %collective-permute-start.13 = (bf16[256,1536]{1,0:T(8,128)(2,1)S(1)}, bf16[256,1536]{1,0:T(8,128)(2,1)S(1)}, u32[]{:S(2)}, u32[]{:S(2)}) collective-permute-start(bf16[256,1536]{1,0:T(8,128)(2,1)S(1)} %get-tuple-element.104), channel_id=1, source_target_pairs={{0,3},{1,0},{2,1},{3,2},{4,7},{5,4},{6,5},{7,6},{8,11},{9,8},{10,9... | collective-permute-start | bytes 2359304 | tf_op jit(solution)/shard_map/ppermute | solution.py:512
  32.9 25.8 %collective-permute-start.12 = (bf16[256,1536]{1,0:T(8,128)(2,1)S(1)}, bf16[256,1536]{1,0:T(8,128)(2,1)S(1)}, u32[]{:S(2)}, u32[]{:S(2)}) collective-permute-start(bf16[256,1536]{1,0:T(8,128)(2,1)S(1)} %get-tuple-element.90.refs_5_), channel_id=1, source_target_pairs={{0,1},{1,2},{2,3},{3,0},{4,5},{5,6},{6,7},{7,4},{8,9},{9,10},{10,1... | collective-permute-start | bytes 2359304 | tf_op jit(solution)/shard_map/ppermute | solution.py:511
  35.3 7.0 %collective-permute-start.6 = (bf16[528,128]{1,0:T(8,128)(2,1)S(1)}, bf16[528,128]{1,0:T(8,128)(2,1)S(1)}, u32[]{:S(2)}, u32[]{:S(2)}) collective-permute-start(bf16[528,128]{1,0:T(8,128)(2,1)S(1)} %get-tuple-element.91), channel_id=1, source_target_pairs={{0,64},{4,68},{8,72},{12,76},{16,80},{20,84},{24,88},{28,92},{32,9... | collective-permute-start | bytes 405512 | tf_op jit(solution)/shard_map/ppermute | solution.py:267
  42.9 1.6 %collective-permute-start.7 = (bf16[512,128]{1,0:T(8,128)(2,1)S(1)}, bf16[512,128]{1,0:T(8,128)(2,1)S(1)}, u32[]{:S(2)}, u32[]{:S(2)}) collective-permute-start(bf16[512,128]{1,0:T(8,128)(2,1)S(1)} %get-tuple-element.95), channel_id=1, source_target_pairs={{0,4},{4,0},{8,12},{12,8},{16,20},{20,16},{24,28},{28,24},{32,36},... | collective-permute-start | bytes 393224 | tf_op jit(solution)/shard_map/ppermute | solution.py:277
  52.4 23.2 %collective-permute-start.11 = (bf16[256,1536]{1,0:T(8,128)(2,1)S(1)}, bf16[256,1536]{1,0:T(8,128)(2,1)S(1)}, u32[]{:S(2)}, u32[]{:S(2)}) collective-permute-start(bf16[256,1536]{1,0:T(8,128)(2,1)S(1)} %get-tuple-element.103), channel_id=1, source_target_pairs={{0,3},{1,0},{2,1},{3,2},{4,7},{5,4},{6,5},{7,6},{8,11},{9,8},{10,9... | collective-permute-start | bytes 2359304 | tf_op jit(solution)/shard_map/ppermute | solution.py:512
  53.6 21.9 %collective-permute-start.10 = (bf16[256,1536]{1,0:T(8,128)(2,1)S(1)}, bf16[256,1536]{1,0:T(8,128)(2,1)S(1)}, u32[]{:S(2)}, u32[]{:S(2)}) collective-permute-start(bf16[256,1536]{1,0:T(8,128)(2,1)S(1)} %get-tuple-element.100.refs_3_), channel_id=1, source_target_pairs={{0,1},{1,2},{2,3},{3,0},{4,5},{5,6},{6,7},{7,4},{8,9},{9,10},{10,1... | collective-permute-start | bytes 2359304 | tf_op jit(solution)/shard_map/ppermute | solution.py:511
  65.5 2.9 %collective-permute-start.14 = (bf16[528,128]{1,0:T(8,128)(2,1)S(1)}, bf16[528,128]{1,0:T(8,128)(2,1)S(1)}, u32[]{:S(2)}, u32[]{:S(2)}) collective-permute-start(bf16[528,128]{1,0:T(8,128)(2,1)S(1)} %get-tuple-element.108), channel_id=1, source_target_pairs={{0,4},{4,0},{8,12},{12,8},{16,20},{20,16},{24,28},{28,24},{32,36},... | collective-permute-start | bytes 405512 | tf_op jit(solution)/shard_map/ppermute | solution.py:250
  65.6 27.7 %collective-permute-start.16 = (bf16[256,1536]{1,0:T(8,128)(2,1)S(1)}, bf16[256,1536]{1,0:T(8,128)(2,1)S(1)}, u32[]{:S(2)}, u32[]{:S(2)}) collective-permute-start(bf16[256,1536]{1,0:T(8,128)(2,1)S(1)} %get-tuple-element.115), channel_id=1, source_target_pairs={{0,3},{1,0},{2,1},{3,2},{4,7},{5,4},{6,5},{7,6},{8,11},{9,8},{10,9... | collective-permute-start | bytes 2359304 | tf_op jit(solution)/shard_map/ppermute | solution.py:512
  68.4 24.9 %collective-permute-start.17 = (bf16[256,1536]{1,0:T(8,128)(2,1)S(1)}, bf16[256,1536]{1,0:T(8,128)(2,1)S(1)}, u32[]{:S(2)}, u32[]{:S(2)}) collective-permute-start(bf16[256,1536]{1,0:T(8,128)(2,1)S(1)} %get-tuple-element.116), channel_id=1, source_target_pairs={{0,1},{1,2},{2,3},{3,0},{4,5},{5,6},{6,7},{7,4},{8,9},{9,10},{10,1... | collective-permute-start | bytes 2359304 | tf_op jit(solution)/shard_map/ppermute | solution.py:511
  69.0 6.0 %collective-permute-start.15 = (bf16[528,128]{1,0:T(8,128)(2,1)S(1)}, bf16[528,128]{1,0:T(8,128)(2,1)S(1)}, u32[]{:S(2)}, u32[]{:S(2)}) collective-permute-start(bf16[528,128]{1,0:T(8,128)(2,1)S(1)} %chip_total.3.refs_9_.refs_1_), channel_id=1, source_target_pairs={{0,8},{4,12},{8,0},{12,4},{16,24},{20,28},{24,16},{28,20},{32,40},... | collective-permute-start | bytes 405512 | tf_op jit(solution)/shard_map/ppermute | solution.py:255
  76.6 31.2 %collective-permute-start.20 = (bf16[256,1536]{1,0:T(8,128)(2,1)S(1)}, bf16[256,1536]{1,0:T(8,128)(2,1)S(1)}, u32[]{:S(2)}, u32[]{:S(2)}) collective-permute-start(bf16[256,1536]{1,0:T(8,128)(2,1)S(1)} %get-tuple-element.123), channel_id=1, source_target_pairs={{0,3},{1,0},{2,1},{3,2},{4,7},{5,4},{6,5},{7,6},{8,11},{9,8},{10,9... | collective-permute-start | bytes 2359304 | tf_op jit(solution)/shard_map/ppermute | solution.py:512
  79.6 28.3 %collective-permute-start.19 = (bf16[256,1536]{1,0:T(8,128)(2,1)S(1)}, bf16[256,1536]{1,0:T(8,128)(2,1)S(1)}, u32[]{:S(2)}, u32[]{:S(2)}) collective-permute-start(bf16[256,1536]{1,0:T(8,128)(2,1)S(1)} %get-tuple-element.112.refs_3_), channel_id=1, source_target_pairs={{0,1},{1,2},{2,3},{3,0},{4,5},{5,6},{6,7},{7,4},{8,9},{9,10},{10,1... | collective-permute-start | bytes 2359304 | tf_op jit(solution)/shard_map/ppermute | solution.py:511
  79.6 6.5 %collective-permute-start.18 = (bf16[528,128]{1,0:T(8,128)(2,1)S(1)}, bf16[528,128]{1,0:T(8,128)(2,1)S(1)}, u32[]{:S(2)}, u32[]{:S(2)}) collective-permute-start(bf16[528,128]{1,0:T(8,128)(2,1)S(1)} %get-tuple-element.117.refs_1_), channel_id=1, source_target_pairs={{0,16},{4,20},{8,24},{12,28},{16,0},{20,4},{24,8},{28,12},{32,48},... | collective-permute-start | bytes 405512 | tf_op jit(solution)/shard_map/ppermute | solution.py:255
  86.7 7.4 %collective-permute-start.21 = (bf16[528,128]{1,0:T(8,128)(2,1)S(1)}, bf16[528,128]{1,0:T(8,128)(2,1)S(1)}, u32[]{:S(2)}, u32[]{:S(2)}) collective-permute-start(bf16[528,128]{1,0:T(8,128)(2,1)S(1)} %get-tuple-element.127.refs_1_), channel_id=1, source_target_pairs={{0,32},{4,36},{8,40},{12,44},{16,48},{20,52},{24,56},{28,60},{32,0... | collective-permute-start | bytes 405512 | tf_op jit(solution)/shard_map/ppermute | solution.py:255
  94.8 6.7 %collective-permute-start.22 = (bf16[528,128]{1,0:T(8,128)(2,1)S(1)}, bf16[528,128]{1,0:T(8,128)(2,1)S(1)}, u32[]{:S(2)}, u32[]{:S(2)}) collective-permute-start(bf16[528,128]{1,0:T(8,128)(2,1)S(1)} %get-tuple-element.129), channel_id=1, source_target_pairs={{0,64},{4,68},{8,72},{12,76},{16,80},{20,84},{24,88},{28,92},{32,9... | collective-permute-start | bytes 405512 | tf_op jit(solution)/shard_map/ppermute | solution.py:267
  102.1 1.4 %collective-permute-start.23 = (bf16[512,128]{1,0:T(8,128)(2,1)S(1)}, bf16[512,128]{1,0:T(8,128)(2,1)S(1)}, u32[]{:S(2)}, u32[]{:S(2)}) collective-permute-start(bf16[512,128]{1,0:T(8,128)(2,1)S(1)} %get-tuple-element.133), channel_id=1, source_target_pairs={{0,4},{4,0},{8,12},{12,8},{16,20},{20,16},{24,28},{28,24},{32,36},... | collective-permute-start | bytes 393224 | tf_op jit(solution)/shard_map/ppermute | solution.py:277

commit v6 on v5

--- a/solution.py
+++ b/solution.py
@@ -53,20 +53,22 @@
 
 def call(kernel, name, scalars, args, outs, after=(), far=(), far_outs=(), scratch=(), room=12):
     count, waits = len(args), len(after)
+    lead = () if scalars is None else (scalars,)
 
     def run(*refs):
+        refs = refs if lead else (None, *refs)
         kernel(*refs[: 1 + count], *refs[1 + count + waits :])
 
     return pl.pallas_call(
         run,
         out_shape=[jax.ShapeDtypeStruct(shape, dtype) for shape, dtype in outs],
-        in_specs=[SMEM] + [HBM if i in far else VMEM for i in range(count)] + [ANY] * waits,
+        in_specs=[SMEM] * len(lead) + [HBM if i in far else VMEM for i in range(count)] + [ANY] * waits,
         out_specs=[HBM if i in far_outs else VMEM for i in range(len(outs))],
         scratch_shapes=list(scratch),
         compiler_params=pltpu.CompilerParams(vmem_limit_bytes=room * MIB),
         cost_estimate=pl.CostEstimate(flops=COST[name], bytes_accessed=0, transcendentals=0),
         name=name,
-    )(scalars, *args, *after)
+    )(*lead, *args, *after)
 
 
 def three_terms(x):
@@ -515,7 +517,7 @@
     top, bottom, order = call(
         halves_kernel,
         "halves",
-        scalars,
+        None,
         (output_gradient,),
         [HALF, HALF, ((8, 128), F32)],
         far=(0,),
@@ -539,7 +541,7 @@
         return (made["acc"],)
 
     def make_split(after):
-        made["split"] = call(split_kernel, "split", scalars, (a_top, b_bottom), [HALF, HALF], after)
+        made["split"] = call(split_kernel, "split", None, (a_top, b_bottom), [HALF, HALF], after)
         return made["split"][:1]
 
     keep, got = scan_blocks(scalars, mine, send, 0, (make_local, make_grad_own, make_split, lambda after: after))
@@ -592,7 +594,7 @@
 
     def join(after):
         parts = (right_top, from_left, left_bottom, from_right)
-        made["joined"] = call(join_kernel, "join", scalars, parts, [HALF, HALF], after)
+        made["joined"] = call(join_kernel, "join", None, parts, [HALF, HALF], after)
         return made["joined"][:1]
 
     def project_own(after):
@@ -602,7 +604,7 @@
 
     def add_direct(after):
         parts = (*made["own"], direct_l, direct_r)
-        made["own"] = call(add_direct_kernel, "add_direct", scalars, parts, [WIDE_HALF] * 2, after)
+        made["own"] = call(add_direct_kernel, "add_direct", None, parts, [WIDE_HALF] * 2, after)
         return made["own"][:1]
 
     turns = (
@@ -626,7 +628,7 @@
     (out,) = call(
         total_kernel,
         "total",
-        scalars,
+        None,
         (*made["own"], joined_r, joined_l),
         [WHOLE],
         (order,),

time: 110 us -> 109 us (level)
  waiting for transfers between devices: 14 us -> 16.8 us
  Pallas kernels: 56.2 us -> 54.6 us
  starting transfers between devices: 38.3 us -> 36.7 us
    ppermute x6, starting transfers between devices: 12.1 us -> 10.4 us  [body(): left = lambda a: lax.ppermute(a, 'head', LEFT)]
    pallas_call x27, Pallas kernels: 56.2 us -> 54.6 us  [call(): pl.pallas_call(run, out_shape=[jax.ShapeDtypeStruct(shape, dtype) for sha...]
  transfers between devices with their start and end apart: 24 -> 24, of which waited for: 11 -> 12; matrix products, arithmetic and copies ran while one was open for 0% -> 0% of each run, Pallas kernels for 48% -> 48%
where the time goes in v6:
time: 109 us
  Pallas kernels  54.6 us (50%)
  starting transfers between devices  36.7 us (34%)
  waiting for transfers between devices  16.8 us (15%)
    pallas_call x27, Pallas kernels, call(): pl.pallas_call(run, out_shape=[jax.ShapeDtypeStruct(shape, dtype) for sha...  54.6 us
    ppermute x6, starting transfers between devices, scan_blocks(): met = lax.ppermute(total, 'seq', MEETINGS[turn])  13 us
    ppermute x6, starting transfers between devices, body(): left = lambda a: lax.ppermute(a, 'head', LEFT)  10.4 us
    ppermute x2, starting transfers between devices, scan_blocks(): met = lax.ppermute(total, 'seq', MEETINGS[3])  7.56 us
    ppermute x2, waiting for transfers between devices, scan_blocks(): met = lax.ppermute(total, 'seq', MEETINGS[3])  5.98 us
    ppermute x6, starting transfers between devices, body(): right = lambda a: lax.ppermute(a, 'head', RIGHT)  5.28 us
    ppermute x6, waiting for transfers between devices, scan_blocks(): met = lax.ppermute(total, 'seq', MEETINGS[turn])  4.32 us
    ppermute x2, waiting for transfers between devices, scan_blocks(): return (keep, lax.ppermute(send_back, 'seq', SWAP))  2.67 us
  transfers between devices with their start and end apart: 24, of which 12 were waited for; matrix products, arithmetic and copies ran while one was open for 0% of the time, Pallas kernels for 48%

profile of v6, /device:TPU:0, one launch (start us, length us, event | category | flops | bytes accessed | tf_op | source)
XLA Modules:
  0.0 109.2 jit_solution(721692672588833270)
XLA Ops:
  0.6 1.4 %halves.1 = (bf16[256,1536]{1,0:T(8,128)(2,1)S(1)}, bf16[256,1536]{1,0:T(8,128)(2,1)S(1)}, f32[8,128]{1,0:T(8,128)S(1)}) custom-call(bf16[512,1536]{1,0:T(8,128)(2,1)} %refs_1_.1), custom_call_target="tpu_custom_call" | custom-call | tf_op jit(solution)/shard_map/halves/pallas_call | solution.py:62
  2.0 1.7 %collective-permute-start.4 = (bf16[256,1536]{1,0:T(8,128)(2,1)S(1)}, bf16[256,1536]{1,0:T(8,128)(2,1)S(1)}, u32[]{:S(2)}, u32[]{:S(2)}) collective-permute-start(bf16[256,1536]{1,0:T(8,128)(2,1)S(1)} %get-tuple-element.88), channel_id=1, source_target_pairs={{0,1},{1,2},{2,3},{3,0},{4,5},{5,6},{6,7},{7,4},{8,9},{9,10},{10,1... | collective-permute-start | bytes 2359304 | tf_op jit(solution)/shard_map/ppermute | solution.py:513
  3.8 1.6 %collective-permute-start.5 = (bf16[256,1536]{1,0:T(8,128)(2,1)S(1)}, bf16[256,1536]{1,0:T(8,128)(2,1)S(1)}, u32[]{:S(2)}, u32[]{:S(2)}) collective-permute-start(bf16[256,1536]{1,0:T(8,128)(2,1)S(1)} %get-tuple-element.89), channel_id=1, source_target_pairs={{0,3},{1,0},{2,1},{3,2},{4,7},{5,4},{6,5},{7,6},{8,11},{9,8},{10,9... | collective-permute-start | bytes 2359304 | tf_op jit(solution)/shard_map/ppermute | solution.py:514
  5.4 5.5 %own_states.1 = (f32[512,8]{1,0:T(8,128)S(1)}, f32[8,512]{1,0:T(8,128)S(1)}, bf16[528,128]{1,0:T(8,128)(2,1)S(1)}, bf16[528,128]{1,0:T(8,128)(2,1)S(1)}, bf16[51...) custom-call(s32[15]{0:T(128)S(1)} %stack.60.refs_0_, ...), custom_call_target="tpu_custom_call" | custom-call | flops 8000000000 | tf_op jit(solution)/shard_map/own_states/pallas_call | solution.py:62
  11.6 2.8 %collective-permute-start.9 = (bf16[256,1536]{1,0:T(8,128)(2,1)}, bf16[256,1536]{1,0:T(8,128)(2,1)S(1)}, u32[]{:S(2)}, u32[]{:S(2)}) collective-permute-start(bf16[256,1536]{1,0:T(8,128)(2,1)} %get-tuple-element.98), channel_id=1, source_target_pairs={{0,3},{1,0},{2,1},{3,2},{4,7},{5,4},{6,5},{7,6},{8,11},{9,8},{10,9... | collective-permute-start | bytes 2359304 | tf_op jit(solution)/shard_map/ppermute | solution.py:514
  15.0 1.7 %collective-permute-start.1 = (bf16[528,128]{1,0:T(8,128)(2,1)S(1)}, bf16[528,128]{1,0:T(8,128)(2,1)S(1)}, u32[]{:S(2)}, u32[]{:S(2)}) collective-permute-start(bf16[528,128]{1,0:T(8,128)(2,1)S(1)} %chip_total.2.refs_7_.refs_1_), channel_id=1, source_target_pairs={{0,8},{4,12},{8,0},{12,4},{16,24},{20,28},{24,16},{28,20},{32,40},... | collective-permute-start | bytes 405512 | tf_op jit(solution)/shard_map/ppermute | solution.py:257
  16.6 5.5 %local.1 = (f32[512,1024]{1,0:T(8,128)S(1)}, bf16[512,1024]{1,0:T(8,128)(2,1)S(1)}, bf16[1024,512]{1,0:T(8,128)(2,1)S(1)}, bf16[1024,6144]{1,0:T(8,128)(2,1)S(1)}) custom-call(s32[15]{0:T(128)S(1)} %stack.60.refs_0_, f32[512,8]{1,0:T(8,128)S(1)} %get-tuple-element.72.refs_1_, f32[8,512]{1,0:T(8,128)S(1)} %get-tuple-element.73.refs_2_.refs_8_, ...), custom_call_target="tpu_custom_call" | custom-call | tf_op jit(solution)/shard_map/local/pallas_call | solution.py:62
  22.1 0.6 meet.6
  22.7 2.8 %collective-permute-start.2 = (bf16[528,128]{1,0:T(8,128)(2,1)S(1)}, bf16[528,128]{1,0:T(8,128)(2,1)S(1)}, u32[]{:S(2)}, u32[]{:S(2)}) collective-permute-start(bf16[528,128]{1,0:T(8,128)(2,1)S(1)} %get-tuple-element.81.refs_1_), channel_id=1, source_target_pairs={{0,16},{4,20},{8,24},{12,28},{16,0},{20,4},{24,8},{28,12},{32,48},... | collective-permute-start | bytes 405512 | tf_op jit(solution)/shard_map/ppermute | solution.py:257
  25.6 2.4 %grad_own.1.refs_5_.refs_6_ = f32[512,1024]{1,0:T(8,128)S(1)} custom-call(s32[15]{0:T(128)S(1)} %stack.60.refs_0_, bf16[512,1536]{1,0:T(8,128)(2,1)S(1)} %copy-done, bf16[1024,6144]{1,0:T(8,128)(2,1)S(1)} %get-tuple-element.84.refs_2_.refs_5_.refs_3_, f32[8,128]{1,0:T(8,128)S(1)} %get-tuple-element.83.refs_3_.refs_4_), custom_call_target="tpu_custom_call" | custom-call | tf_op jit(solution)/shard_map/grad_own/pallas_call | solution.py:62
  27.9 1.5 %collective-permute-done.2.refs_2_ = bf16[528,128]{1,0:T(8,128)(2,1)S(1)} collective-permute-done((bf16[528,128]{1,0:T(8,128)(2,1)S(1)}, bf16[528,128]{1,0:T(8,128)(2,1)S(1)}, u32[]{:S(2)}, u32[]{:S(2)}) %collective-permute-start.2) | collective-permute-done | bytes 135200 | tf_op jit(solution)/shard_map/ppermute | solution.py:257
  29.4 0.6 meet.7
  30.1 2.0 %collective-permute-start.3 = (bf16[528,128]{1,0:T(8,128)(2,1)S(1)}, bf16[528,128]{1,0:T(8,128)(2,1)S(1)}, u32[]{:S(2)}, u32[]{:S(2)}) collective-permute-start(bf16[528,128]{1,0:T(8,128)(2,1)S(1)} %get-tuple-element.85.refs_1_), channel_id=1, source_target_pairs={{0,32},{4,36},{8,40},{12,44},{16,48},{20,52},{24,56},{28,60},{32,0... | collective-permute-start | bytes 405512 | tf_op jit(solution)/shard_map/ppermute | solution.py:257
  32.2 0.7 collective-permute-start.13
  32.8 1.4 %collective-permute-start.12 = (bf16[256,1536]{1,0:T(8,128)(2,1)S(1)}, bf16[256,1536]{1,0:T(8,128)(2,1)S(1)}, u32[]{:S(2)}, u32[]{:S(2)}) collective-permute-start(bf16[256,1536]{1,0:T(8,128)(2,1)S(1)} %get-tuple-element.90.refs_5_), channel_id=1, source_target_pairs={{0,1},{1,2},{2,3},{3,0},{4,5},{5,6},{6,7},{7,4},{8,9},{9,10},{10,1... | collective-permute-start | bytes 2359304 | tf_op jit(solution)/shard_map/ppermute | solution.py:513
  34.3 0.9 collective-permute-done.3.refs_2_
  35.1 0.6 meet.8
  35.8 4.0 %collective-permute-start.6 = (bf16[528,128]{1,0:T(8,128)(2,1)S(1)}, bf16[528,128]{1,0:T(8,128)(2,1)S(1)}, u32[]{:S(2)}, u32[]{:S(2)}) collective-permute-start(bf16[528,128]{1,0:T(8,128)(2,1)S(1)} %get-tuple-element.91), channel_id=1, source_target_pairs={{0,64},{4,68},{8,72},{12,76},{16,80},{20,84},{24,88},{28,92},{32,9... | collective-permute-start | bytes 405512 | tf_op jit(solution)/shard_map/ppermute | solution.py:269
  39.7 3.0 %collective-permute-done.6.refs_1_ = bf16[528,128]{1,0:T(8,128)(2,1)S(1)} collective-permute-done((bf16[528,128]{1,0:T(8,128)(2,1)S(1)}, bf16[528,128]{1,0:T(8,128)(2,1)S(1)}, u32[]{:S(2)}, u32[]{:S(2)}) %collective-permute-start.6) | collective-permute-done | bytes 135200 | tf_op jit(solution)/shard_map/ppermute | solution.py:269
  42.7 0.6 arrive.2
  43.6 1.3 %collective-permute-done.7.refs_4_.refs_8_ = bf16[512,128]{1,0:T(8,128)(2,1)S(1)} collective-permute-done((bf16[512,128]{1,0:T(8,128)(2,1)S(1)}, bf16[512,128]{1,0:T(8,128)(2,1)S(1)}, u32[]{:S(2)}, u32[]{:S(2)}) %collective-permute-start.7) | collective-permute-done | bytes 131104 | tf_op jit(solution)/shard_map/ppermute | solution.py:279
  45.0 1.5 %attend.1 = (bf16[512,1024]{1,0:T(8,128)(2,1)S(1)}, f32[512,1024]{1,0:T(8,128)S(1)}, f32[512,1024]{1,0:T(8,128)S(1)}) custom-call(s32[15]{0:T(128)S(1)} %stack.60.refs_0_, f32[512,1024]{1,0:T(8,128)S(1)} %get-tuple-element.79.refs_3_.refs_1_, bf16[512,1024]{1,0:T(8,128)(2,1)S(1)} %get-tuple-element.80.refs_2_, ...), custom_call_target="tpu_custom_call" | custom-call | tf_op jit(solution)/shard_map/attend/pallas_call | solution.py:62
  46.5 4.0 %grad_near.1.refs_3_.refs_4_ = f32[512,1024]{1,0:T(8,128)S(1)} custom-call(s32[15]{0:T(128)S(1)} %stack.60.refs_0_, bf16[256,1536]{1,0:T(8,128)(2,1)S(1)} %collective-permute-done.4.refs_0_.refs_1_, bf16[256,1536]{1,0:T(8,128)(2,1)S(1)} %collective-permute-done.8.refs_2_, bf16[256,1536]{1,0:T(8,128)(2,1)S(1)} %collective-permute-done.9.refs_3_, ...), custom_call_target="tpu_custom_call" | custom-call | tf_op jit(solution)/shard_map/grad_near/pallas_call | solution.py:62
  50.5 2.4 %project_far.1 = (bf16[256,1536]{1,0:T(8,128)(2,1)S(1)}, bf16[256,1536]{1,0:T(8,128)(2,1)S(1)}) custom-call(s32[15]{0:T(128)S(1)} %stack.60.refs_0_, bf16[512,1024]{1,0:T(8,128)(2,1)S(1)} %get-tuple-element.96.refs_1_, bf16[1024,6144]{1,0:T(8,128)(2,1)S(1)} %get-tuple-element.84.refs_2_.refs_5_.refs_3_, f32[512,1024]{1,0:T(8,128)S(1)} %grad_near.1.refs_3_.refs_4_), custom_call_target="tpu_custom_call" | custom-call | tf_op jit(solution)/shard_map/project_far/pallas_call | solution.py:62
  52.9 0.7 collective-permute-start.11
  53.6 1.4 %collective-permute-start.10 = (bf16[256,1536]{1,0:T(8,128)(2,1)S(1)}, bf16[256,1536]{1,0:T(8,128)(2,1)S(1)}, u32[]{:S(2)}, u32[]{:S(2)}) collective-permute-start(bf16[256,1536]{1,0:T(8,128)(2,1)S(1)} %get-tuple-element.100.refs_3_), channel_id=1, source_target_pairs={{0,1},{1,2},{2,3},{3,0},{4,5},{5,6},{6,7},{7,4},{8,9},{9,10},{10,1... | collective-permute-start | bytes 2359304 | tf_op jit(solution)/shard_map/ppermute | solution.py:513
  55.0 4.0 %project_near.1 = (f32[256,1536]{1,0:T(8,128)S(1)}, bf16[256,1536]{1,0:T(8,128)(2,1)S(1)}, bf16[256,1536]{1,0:T(8,128)(2,1)S(1)}, f32[256,1536]{1,0:T(8,128)S(1)}) custom-call(s32[15]{0:T(128)S(1)} %stack.60.refs_0_, bf16[512,1024]{1,0:T(8,128)(2,1)S(1)} %get-tuple-element.96.refs_1_, bf16[1024,6144]{1,0:T(8,128)(2,1)S(1)} %get-tuple-element.84.refs_2_.refs_5_.refs_3_, ...), custom_call_target="tpu_custom_call" | custom-call | tf_op jit(solution)/shard_map/project_near/pallas_call | solution.py:62
  59.0 6.8 %grad_far.1 = (bf16[512,1024]{1,0:T(8,128)(2,1)S(1)}, bf16[528,128]{1,0:T(8,128)(2,1)S(1)}, bf16[528,128]{1,0:T(8,128)(2,1)S(1)}) custom-call(s32[15]{0:T(128)S(1)} %stack.60.refs_0_, bf16[256,1536]{1,0:T(8,128)(2,1)S(1)} %collective-permute-done.12.refs_1_, bf16[256,1536]{1,0:T(8,128)(2,1)S(1)} %collective-permute-done.13.refs_2_, ...), custom_call_target="tpu_custom_call" | custom-call | tf_op jit(solution)/shard_map/grad_far/pallas_call | solution.py:62
  65.9 1.9 %collective-permute-start.16 = (bf16[256,1536]{1,0:T(8,128)(2,1)S(1)}, bf16[256,1536]{1,0:T(8,128)(2,1)S(1)}, u32[]{:S(2)}, u32[]{:S(2)}) collective-permute-start(bf16[256,1536]{1,0:T(8,128)(2,1)S(1)} %get-tuple-element.115), channel_id=1, source_target_pairs={{0,3},{1,0},{2,1},{3,2},{4,7},{5,4},{6,5},{7,6},{8,11},{9,8},{10,9... | collective-permute-start | bytes 2359304 | tf_op jit(solution)/shard_map/ppermute | solution.py:514
  68.6 1.6 %collective-permute-start.15 = (bf16[528,128]{1,0:T(8,128)(2,1)S(1)}, bf16[528,128]{1,0:T(8,128)(2,1)S(1)}, u32[]{:S(2)}, u32[]{:S(2)}) collective-permute-start(bf16[528,128]{1,0:T(8,128)(2,1)S(1)} %chip_total.3.refs_9_.refs_1_), channel_id=1, source_target_pairs={{0,8},{4,12},{8,0},{12,4},{16,24},{20,28},{24,16},{28,20},{32,40},... | collective-permute-start | bytes 405512 | tf_op jit(solution)/shard_map/ppermute | solution.py:257
  70.1 3.4 %inside.2 = (bf16[512,512]{1,0:T(8,128)(2,1)S(1)}, f32[512,512]{1,0:T(8,128)S(1)}, f32[512,512]{1,0:T(8,128)S(1)}) custom-call(s32[15]{0:T(128)S(1)} %stack.60.refs_0_, f32[512,8]{1,0:T(8,128)S(1)} %get-tuple-element.72.refs_1_, f32[8,512]{1,0:T(8,128)S(1)} %get-tuple-element.73.refs_2_.refs_8_, bf16[512,1024]{1,0:T(8,128)(2,1)S(1)} %get-tuple-element.74.refs_3_, ...), custom_call_target="tpu_custom_call" | custom-call | tf_op jit(solution)/shard_map/inside/pallas_call | solution.py:62
  73.5 0.8 collective-permute-done.15.refs_2_
  75.5 2.8 %collective-permute-start.20 = (bf16[256,1536]{1,0:T(8,128)(2,1)S(1)}, bf16[256,1536]{1,0:T(8,128)(2,1)S(1)}, u32[]{:S(2)}, u32[]{:S(2)}) collective-permute-start(bf16[256,1536]{1,0:T(8,128)(2,1)S(1)} %get-tuple-element.123), channel_id=1, source_target_pairs={{0,3},{1,0},{2,1},{3,2},{4,7},{5,4},{6,5},{7,6},{8,11},{9,8},{10,9... | collective-permute-start | bytes 2359304 | tf_op jit(solution)/shard_map/ppermute | solution.py:514
  78.3 3.0 %collective-permute-start.18 = (bf16[528,128]{1,0:T(8,128)(2,1)S(1)}, bf16[528,128]{1,0:T(8,128)(2,1)S(1)}, u32[]{:S(2)}, u32[]{:S(2)}) collective-permute-start(bf16[528,128]{1,0:T(8,128)(2,1)S(1)} %get-tuple-element.117.refs_1_), channel_id=1, source_target_pairs={{0,16},{4,20},{8,24},{12,28},{16,0},{20,4},{24,8},{28,12},{32,48},... | collective-permute-start | bytes 405512 | tf_op jit(solution)/shard_map/ppermute | solution.py:257
  81.3 2.4 %project_own.1 = (f32[256,1536]{1,0:T(8,128)S(1)}, f32[256,1536]{1,0:T(8,128)S(1)}) custom-call(s32[15]{0:T(128)S(1)} %stack.60.refs_0_, bf16[512,1024]{1,0:T(8,128)(2,1)S(1)} %get-tuple-element.96.refs_1_, bf16[1024,6144]{1,0:T(8,128)(2,1)S(1)} %get-tuple-element.84.refs_2_.refs_5_.refs_3_, bf16[256,1536]{1,0:T(8,128)(2,1)S(1)} %get-tuple-element.112.refs_3_), custom_call_target="tpu_custom_call" | custom-call | tf_op jit(solution)/shard_map/project_own/pallas_call | solution.py:62
  83.7 1.2 %collective-permute-done.18.refs_2_ = bf16[528,128]{1,0:T(8,128)(2,1)S(1)} collective-permute-done((bf16[528,128]{1,0:T(8,128)(2,1)S(1)}, bf16[528,128]{1,0:T(8,128)(2,1)S(1)}, u32[]{:S(2)}, u32[]{:S(2)}) %collective-permute-start.18) | collective-permute-done | bytes 135200 | tf_op jit(solution)/shard_map/ppermute | solution.py:257
  84.9 0.6 meet.10
  85.5 2.0 %collective-permute-start.21 = (bf16[528,128]{1,0:T(8,128)(2,1)S(1)}, bf16[528,128]{1,0:T(8,128)(2,1)S(1)}, u32[]{:S(2)}, u32[]{:S(2)}) collective-permute-start(bf16[528,128]{1,0:T(8,128)(2,1)S(1)} %get-tuple-element.127.refs_1_), channel_id=1, source_target_pairs={{0,32},{4,36},{8,40},{12,44},{16,48},{20,52},{24,56},{28,60},{32,0... | collective-permute-start | bytes 405512 | tf_op jit(solution)/shard_map/ppermute | solution.py:257
  87.4 4.4 %inside.3 = (bf16[512,1024]{1,0:T(8,128)(2,1)}, f32[512,512]{1,0:T(8,128)S(1)}, f32[512,512]{1,0:T(8,128)S(1)}) custom-call(s32[15]{0:T(128)S(1)} %stack.60.refs_0_, f32[512,8]{1,0:T(8,128)S(1)} %get-tuple-element.72.refs_1_, f32[8,512]{1,0:T(8,128)S(1)} %get-tuple-element.73.refs_2_.refs_8_, bf16[512,1024]{1,0:T(8,128)(2,1)S(1)} %get-tuple-element.74.refs_3_, ...), custom_call_target="tpu_custom_call" | custom-call | tf_op jit(solution)/shard_map/inside/pallas_call | solution.py:62
  92.4 0.6 meet.11
  93.0 3.6 %collective-permute-start.22 = (bf16[528,128]{1,0:T(8,128)(2,1)S(1)}, bf16[528,128]{1,0:T(8,128)(2,1)S(1)}, u32[]{:S(2)}, u32[]{:S(2)}) collective-permute-start(bf16[528,128]{1,0:T(8,128)(2,1)S(1)} %get-tuple-element.129), channel_id=1, source_target_pairs={{0,64},{4,68},{8,72},{12,76},{16,80},{20,84},{24,88},{28,92},{32,9... | collective-permute-start | bytes 405512 | tf_op jit(solution)/shard_map/ppermute | solution.py:269
  96.6 3.0 %collective-permute-done.22.refs_1_ = bf16[528,128]{1,0:T(8,128)(2,1)S(1)} collective-permute-done((bf16[528,128]{1,0:T(8,128)(2,1)S(1)}, bf16[528,128]{1,0:T(8,128)(2,1)S(1)}, u32[]{:S(2)}, u32[]{:S(2)}) %collective-permute-start.22) | collective-permute-done | bytes 135200 | tf_op jit(solution)/shard_map/ppermute | solution.py:269
  99.6 0.6 arrive.3
  100.4 1.3 %collective-permute-done.23.refs_9_ = bf16[512,128]{1,0:T(8,128)(2,1)S(1)} collective-permute-done((bf16[512,128]{1,0:T(8,128)(2,1)S(1)}, bf16[512,128]{1,0:T(8,128)(2,1)S(1)}, u32[]{:S(2)}, u32[]{:S(2)}) %collective-permute-start.23) | collective-permute-done | bytes 131104 | tf_op jit(solution)/shard_map/ppermute | solution.py:279
  101.7 2.7 %finish.1 = (bf16[512,1024]{1,0:T(8,128)(2,1)}, bf16[512,1024]{1,0:T(8,128)(2,1)}, f32[8,128]{1,0:T(8,128)S(1)}) custom-call(s32[15]{0:T(128)S(1)} %stack.60.refs_0_, f32[512,8]{1,0:T(8,128)S(1)} %get-tuple-element.72.refs_1_, bf16[512,1024]{1,0:T(8,128)(2,1)S(1)} %get-tuple-element.75.refs_4_.refs_2_, ...), custom_call_target="tpu_custom_call" | custom-call | tf_op jit(solution)/shard_map/finish/pallas_call | solution.py:62
  104.4 2.6 %collective-permute-done.20.refs_3_ = bf16[256,1536]{1,0:T(8,128)(2,1)S(1)} collective-permute-done((bf16[256,1536]{1,0:T(8,128)(2,1)S(1)}, bf16[256,1536]{1,0:T(8,128)(2,1)S(1)}, u32[]{:S(2)}, u32[]{:S(2)}) %collective-permute-start.20) | collective-permute-done | bytes 786464 | tf_op jit(solution)/shard_map/ppermute | solution.py:514
  107.0 0.8 collective-permute-done.19.refs_2_
  107.8 1.2 %total.1 = bf16[512,1536]{1,0:T(8,128)(2,1)} custom-call(f32[256,1536]{1,0:T(8,128)S(1)} %get-tuple-element.121.refs_5_.refs_0_, f32[256,1536]{1,0:T(8,128)S(1)} %get-tuple-element.122.refs_1_, bf16[256,1536]{1,0:T(8,128)(2,1)S(1)} %collective-permute-done.19.refs_2_, bf16[256,1536]{1,0:T(8,128)(2,1)S(1)} %collective-permute-done.20.refs_3_, ...), custom_call_target="tpu_custom_call" | custom-call | tf_op jit(solution)/shard_map/total/pallas_call | solution.py:62
  (32 shorter events, 4.3 us)
Async XLA Ops:
  0.6 4.8 %copy-start.1 = (f32[512,8]{0,1:T(8,128)S(1)}, f32[512,8]{0,1:T(8,128)}, u32[]{:S(2)}) copy-start(f32[512,8]{0,1:T(8,128)} %param.9) | copy-start | bytes 49156
  2.0 30.0 %collective-permute-start.4 = (bf16[256,1536]{1,0:T(8,128)(2,1)S(1)}, bf16[256,1536]{1,0:T(8,128)(2,1)S(1)}, u32[]{:S(2)}, u32[]{:S(2)}) collective-permute-start(bf16[256,1536]{1,0:T(8,128)(2,1)S(1)} %get-tuple-element.88), channel_id=1, source_target_pairs={{0,1},{1,2},{2,3},{3,0},{4,5},{5,6},{6,7},{7,4},{8,9},{9,10},{10,1... | collective-permute-start | bytes 2359304 | tf_op jit(solution)/shard_map/ppermute | solution.py:513
  3.8 28.3 %collective-permute-start.5 = (bf16[256,1536]{1,0:T(8,128)(2,1)S(1)}, bf16[256,1536]{1,0:T(8,128)(2,1)S(1)}, u32[]{:S(2)}, u32[]{:S(2)}) collective-permute-start(bf16[256,1536]{1,0:T(8,128)(2,1)S(1)} %get-tuple-element.89), channel_id=1, source_target_pairs={{0,3},{1,0},{2,1},{3,2},{4,7},{5,4},{6,5},{7,6},{8,11},{9,8},{10,9... | collective-permute-start | bytes 2359304 | tf_op jit(solution)/shard_map/ppermute | solution.py:514
  11.0 3.4 %collective-permute-start = (bf16[528,128]{1,0:T(8,128)(2,1)S(1)}, bf16[528,128]{1,0:T(8,128)(2,1)S(1)}, u32[]{:S(2)}, u32[]{:S(2)}) collective-permute-start(bf16[528,128]{1,0:T(8,128)(2,1)S(1)} %get-tuple-element.78), channel_id=1, source_target_pairs={{0,4},{4,0},{8,12},{12,8},{16,20},{20,16},{24,28},{28,24},{32,36},... | collective-permute-start | bytes 405512 | tf_op jit(solution)/shard_map/ppermute | solution.py:252
  11.1 35.4 %collective-permute-start.8 = (bf16[256,1536]{1,0:T(8,128)(2,1)}, bf16[256,1536]{1,0:T(8,128)(2,1)S(1)}, u32[]{:S(2)}, u32[]{:S(2)}) collective-permute-start(bf16[256,1536]{1,0:T(8,128)(2,1)} %get-tuple-element.97), channel_id=1, source_target_pairs={{0,1},{1,2},{2,3},{3,0},{4,5},{5,6},{6,7},{7,4},{8,9},{9,10},{10,1... | collective-permute-start | bytes 2359304 | tf_op jit(solution)/shard_map/ppermute | solution.py:513
  11.6 34.9 %collective-permute-start.9 = (bf16[256,1536]{1,0:T(8,128)(2,1)}, bf16[256,1536]{1,0:T(8,128)(2,1)S(1)}, u32[]{:S(2)}, u32[]{:S(2)}) collective-permute-start(bf16[256,1536]{1,0:T(8,128)(2,1)} %get-tuple-element.98), channel_id=1, source_target_pairs={{0,3},{1,0},{2,1},{3,2},{4,7},{5,4},{6,5},{7,6},{8,11},{9,8},{10,9... | collective-permute-start | bytes 2359304 | tf_op jit(solution)/shard_map/ppermute | solution.py:514
  15.0 7.1 %collective-permute-start.1 = (bf16[528,128]{1,0:T(8,128)(2,1)S(1)}, bf16[528,128]{1,0:T(8,128)(2,1)S(1)}, u32[]{:S(2)}, u32[]{:S(2)}) collective-permute-start(bf16[528,128]{1,0:T(8,128)(2,1)S(1)} %chip_total.2.refs_7_.refs_1_), channel_id=1, source_target_pairs={{0,8},{4,12},{8,0},{12,4},{16,24},{20,28},{24,16},{28,20},{32,40},... | collective-permute-start | bytes 405512 | tf_op jit(solution)/shard_map/ppermute | solution.py:257
  22.1 3.5 %copy-start = (bf16[512,1536]{1,0:T(8,128)(2,1)S(1)}, bf16[512,1536]{1,0:T(8,128)(2,1)}, u32[]{:S(2)}) copy-start(bf16[512,1536]{1,0:T(8,128)(2,1)} %refs_1_.1) | copy-start | bytes 4718596
  22.7 6.7 %collective-permute-start.2 = (bf16[528,128]{1,0:T(8,128)(2,1)S(1)}, bf16[528,128]{1,0:T(8,128)(2,1)S(1)}, u32[]{:S(2)}, u32[]{:S(2)}) collective-permute-start(bf16[528,128]{1,0:T(8,128)(2,1)S(1)} %get-tuple-element.81.refs_1_), channel_id=1, source_target_pairs={{0,16},{4,20},{8,24},{12,28},{16,0},{20,4},{24,8},{28,12},{32,48},... | collective-permute-start | bytes 405512 | tf_op jit(solution)/shard_map/ppermute | solution.py:257
  30.1 5.1 %collective-permute-start.3 = (bf16[528,128]{1,0:T(8,128)(2,1)S(1)}, bf16[528,128]{1,0:T(8,128)(2,1)S(1)}, u32[]{:S(2)}, u32[]{:S(2)}) collective-permute-start(bf16[528,128]{1,0:T(8,128)(2,1)S(1)} %get-tuple-element.85.refs_1_), channel_id=1, source_target_pairs={{0,32},{4,36},{8,40},{12,44},{16,48},{20,52},{24,56},{28,60},{32,0... | collective-permute-start | bytes 405512 | tf_op jit(solution)/shard_map/ppermute | solution.py:257
  32.2 26.8 %collective-permute-start.13 = (bf16[256,1536]{1,0:T(8,128)(2,1)S(1)}, bf16[256,1536]{1,0:T(8,128)(2,1)S(1)}, u32[]{:S(2)}, u32[]{:S(2)}) collective-permute-start(bf16[256,1536]{1,0:T(8,128)(2,1)S(1)} %get-tuple-element.104), channel_id=1, source_target_pairs={{0,3},{1,0},{2,1},{3,2},{4,7},{5,4},{6,5},{7,6},{8,11},{9,8},{10,9... | collective-permute-start | bytes 2359304 | tf_op jit(solution)/shard_map/ppermute | solution.py:514
  32.8 26.2 %collective-permute-start.12 = (bf16[256,1536]{1,0:T(8,128)(2,1)S(1)}, bf16[256,1536]{1,0:T(8,128)(2,1)S(1)}, u32[]{:S(2)}, u32[]{:S(2)}) collective-permute-start(bf16[256,1536]{1,0:T(8,128)(2,1)S(1)} %get-tuple-element.90.refs_5_), channel_id=1, source_target_pairs={{0,1},{1,2},{2,3},{3,0},{4,5},{5,6},{6,7},{7,4},{8,9},{9,10},{10,1... | collective-permute-start | bytes 2359304 | tf_op jit(solution)/shard_map/ppermute | solution.py:513
  35.8 7.0 %collective-permute-start.6 = (bf16[528,128]{1,0:T(8,128)(2,1)S(1)}, bf16[528,128]{1,0:T(8,128)(2,1)S(1)}, u32[]{:S(2)}, u32[]{:S(2)}) collective-permute-start(bf16[528,128]{1,0:T(8,128)(2,1)S(1)} %get-tuple-element.91), channel_id=1, source_target_pairs={{0,64},{4,68},{8,72},{12,76},{16,80},{20,84},{24,88},{28,92},{32,9... | collective-permute-start | bytes 405512 | tf_op jit(solution)/shard_map/ppermute | solution.py:269
  43.4 1.6 %collective-permute-start.7 = (bf16[512,128]{1,0:T(8,128)(2,1)S(1)}, bf16[512,128]{1,0:T(8,128)(2,1)S(1)}, u32[]{:S(2)}, u32[]{:S(2)}) collective-permute-start(bf16[512,128]{1,0:T(8,128)(2,1)S(1)} %get-tuple-element.95), channel_id=1, source_target_pairs={{0,4},{4,0},{8,12},{12,8},{16,20},{20,16},{24,28},{28,24},{32,36},... | collective-permute-start | bytes 393224 | tf_op jit(solution)/shard_map/ppermute | solution.py:279
  52.9 22.1 %collective-permute-start.11 = (bf16[256,1536]{1,0:T(8,128)(2,1)S(1)}, bf16[256,1536]{1,0:T(8,128)(2,1)S(1)}, u32[]{:S(2)}, u32[]{:S(2)}) collective-permute-start(bf16[256,1536]{1,0:T(8,128)(2,1)S(1)} %get-tuple-element.103), channel_id=1, source_target_pairs={{0,3},{1,0},{2,1},{3,2},{4,7},{5,4},{6,5},{7,6},{8,11},{9,8},{10,9... | collective-permute-start | bytes 2359304 | tf_op jit(solution)/shard_map/ppermute | solution.py:514
  53.6 21.6 %collective-permute-start.10 = (bf16[256,1536]{1,0:T(8,128)(2,1)S(1)}, bf16[256,1536]{1,0:T(8,128)(2,1)S(1)}, u32[]{:S(2)}, u32[]{:S(2)}) collective-permute-start(bf16[256,1536]{1,0:T(8,128)(2,1)S(1)} %get-tuple-element.100.refs_3_), channel_id=1, source_target_pairs={{0,1},{1,2},{2,3},{3,0},{4,5},{5,6},{6,7},{7,4},{8,9},{9,10},{10,1... | collective-permute-start | bytes 2359304 | tf_op jit(solution)/shard_map/ppermute | solution.py:513
  65.8 2.1 %collective-permute-start.14 = (bf16[528,128]{1,0:T(8,128)(2,1)S(1)}, bf16[528,128]{1,0:T(8,128)(2,1)S(1)}, u32[]{:S(2)}, u32[]{:S(2)}) collective-permute-start(bf16[528,128]{1,0:T(8,128)(2,1)S(1)} %get-tuple-element.108), channel_id=1, source_target_pairs={{0,4},{4,0},{8,12},{12,8},{16,20},{20,16},{24,28},{28,24},{32,36},... | collective-permute-start | bytes 405512 | tf_op jit(solution)/shard_map/ppermute | solution.py:252
  65.9 26.0 %collective-permute-start.16 = (bf16[256,1536]{1,0:T(8,128)(2,1)S(1)}, bf16[256,1536]{1,0:T(8,128)(2,1)S(1)}, u32[]{:S(2)}, u32[]{:S(2)}) collective-permute-start(bf16[256,1536]{1,0:T(8,128)(2,1)S(1)} %get-tuple-element.115), channel_id=1, source_target_pairs={{0,3},{1,0},{2,1},{3,2},{4,7},{5,4},{6,5},{7,6},{8,11},{9,8},{10,9... | collective-permute-start | bytes 2359304 | tf_op jit(solution)/shard_map/ppermute | solution.py:514
  67.8 24.3 %collective-permute-start.17 = (bf16[256,1536]{1,0:T(8,128)(2,1)S(1)}, bf16[256,1536]{1,0:T(8,128)(2,1)S(1)}, u32[]{:S(2)}, u32[]{:S(2)}) collective-permute-start(bf16[256,1536]{1,0:T(8,128)(2,1)S(1)} %get-tuple-element.116), channel_id=1, source_target_pairs={{0,1},{1,2},{2,3},{3,0},{4,5},{5,6},{6,7},{7,4},{8,9},{9,10},{10,1... | collective-permute-start | bytes 2359304 | tf_op jit(solution)/shard_map/ppermute | solution.py:513
  68.6 5.8 %collective-permute-start.15 = (bf16[528,128]{1,0:T(8,128)(2,1)S(1)}, bf16[528,128]{1,0:T(8,128)(2,1)S(1)}, u32[]{:S(2)}, u32[]{:S(2)}) collective-permute-start(bf16[528,128]{1,0:T(8,128)(2,1)S(1)} %chip_total.3.refs_9_.refs_1_), channel_id=1, source_target_pairs={{0,8},{4,12},{8,0},{12,4},{16,24},{20,28},{24,16},{28,20},{32,40},... | collective-permute-start | bytes 405512 | tf_op jit(solution)/shard_map/ppermute | solution.py:257
  75.5 31.5 %collective-permute-start.20 = (bf16[256,1536]{1,0:T(8,128)(2,1)S(1)}, bf16[256,1536]{1,0:T(8,128)(2,1)S(1)}, u32[]{:S(2)}, u32[]{:S(2)}) collective-permute-start(bf16[256,1536]{1,0:T(8,128)(2,1)S(1)} %get-tuple-element.123), channel_id=1, source_target_pairs={{0,3},{1,0},{2,1},{3,2},{4,7},{5,4},{6,5},{7,6},{8,11},{9,8},{10,9... | collective-permute-start | bytes 2359304 | tf_op jit(solution)/shard_map/ppermute | solution.py:514
  78.3 29.4 %collective-permute-start.19 = (bf16[256,1536]{1,0:T(8,128)(2,1)S(1)}, bf16[256,1536]{1,0:T(8,128)(2,1)S(1)}, u32[]{:S(2)}, u32[]{:S(2)}) collective-permute-start(bf16[256,1536]{1,0:T(8,128)(2,1)S(1)} %get-tuple-element.112.refs_3_), channel_id=1, source_target_pairs={{0,1},{1,2},{2,3},{3,0},{4,5},{5,6},{6,7},{7,4},{8,9},{9,10},{10,1... | collective-permute-start | bytes 2359304 | tf_op jit(solution)/shard_map/ppermute | solution.py:513
  78.3 6.5 %collective-permute-start.18 = (bf16[528,128]{1,0:T(8,128)(2,1)S(1)}, bf16[528,128]{1,0:T(8,128)(2,1)S(1)}, u32[]{:S(2)}, u32[]{:S(2)}) collective-permute-start(bf16[528,128]{1,0:T(8,128)(2,1)S(1)} %get-tuple-element.117.refs_1_), channel_id=1, source_target_pairs={{0,16},{4,20},{8,24},{12,28},{16,0},{20,4},{24,8},{28,12},{32,48},... | collective-permute-start | bytes 405512 | tf_op jit(solution)/shard_map/ppermute | solution.py:257
  85.5 6.9 %collective-permute-start.21 = (bf16[528,128]{1,0:T(8,128)(2,1)S(1)}, bf16[528,128]{1,0:T(8,128)(2,1)S(1)}, u32[]{:S(2)}, u32[]{:S(2)}) collective-permute-start(bf16[528,128]{1,0:T(8,128)(2,1)S(1)} %get-tuple-element.127.refs_1_), channel_id=1, source_target_pairs={{0,32},{4,36},{8,40},{12,44},{16,48},{20,52},{24,56},{28,60},{32,0... | collective-permute-start | bytes 405512 | tf_op jit(solution)/shard_map/ppermute | solution.py:257
  93.0 6.6 %collective-permute-start.22 = (bf16[528,128]{1,0:T(8,128)(2,1)S(1)}, bf16[528,128]{1,0:T(8,128)(2,1)S(1)}, u32[]{:S(2)}, u32[]{:S(2)}) collective-permute-start(bf16[528,128]{1,0:T(8,128)(2,1)S(1)} %get-tuple-element.129), channel_id=1, source_target_pairs={{0,64},{4,68},{8,72},{12,76},{16,80},{20,84},{24,88},{28,92},{32,9... | collective-permute-start | bytes 405512 | tf_op jit(solution)/shard_map/ppermute | solution.py:269
  100.3 1.4 %collective-permute-start.23 = (bf16[512,128]{1,0:T(8,128)(2,1)S(1)}, bf16[512,128]{1,0:T(8,128)(2,1)S(1)}, u32[]{:S(2)}, u32[]{:S(2)}) collective-permute-start(bf16[512,128]{1,0:T(8,128)(2,1)S(1)} %get-tuple-element.133), channel_id=1, source_target_pairs={{0,4},{4,0},{8,12},{12,8},{16,20},{20,16},{24,28},{28,24},{32,36},... | collective-permute-start | bytes 393224 | tf_op jit(solution)/shard_map/ppermute | solution.py:279

commit v7 on v6

--- a/solution.py
+++ b/solution.py
@@ -610,8 +610,8 @@
     turns = (
         inside_first,
         lambda after: project_own(join(after)),
-        lambda after: add_direct(inside_second(after)),
-        lambda after: after,
+        lambda after: (*inside_second(after), direct_l, direct_r),
+        add_direct,
     )
     keep_g, got_g = scan_blocks(scalars, mine_g, send_g, 5, turns)
     joined_r, joined_l = right(made["joined"][0]), left(made["joined"][1])

time: 109 us -> 109 us (level)
  transfers between devices with their start and end apart: 24 -> 24, of which waited for: 12 -> 12; matrix products, arithmetic and copies ran while one was open for 0% -> 0% of each run, Pallas kernels for 48% -> 47%
where the time goes in v7:
time: 109 us
  Pallas kernels  54.5 us (50%)
  starting transfers between devices  36.7 us (34%)
  waiting for transfers between devices  16.9 us (16%)
    pallas_call x27, Pallas kernels, call(): pl.pallas_call(run, out_shape=[jax.ShapeDtypeStruct(shape, dtype) for sha...  54.5 us
    ppermute x6, starting transfers between devices, scan_blocks(): met = lax.ppermute(total, 'seq', MEETINGS[turn])  13 us
    ppermute x6, starting transfers between devices, body(): left = lambda a: lax.ppermute(a, 'head', LEFT)  10.4 us
    ppermute x2, starting transfers between devices, scan_blocks(): met = lax.ppermute(total, 'seq', MEETINGS[3])  7.56 us
    ppermute x2, waiting for transfers between devices, scan_blocks(): met = lax.ppermute(total, 'seq', MEETINGS[3])  5.72 us
    ppermute x6, starting transfers between devices, body(): right = lambda a: lax.ppermute(a, 'head', RIGHT)  5.28 us
    ppermute x6, waiting for transfers between devices, scan_blocks(): met = lax.ppermute(total, 'seq', MEETINGS[turn])  4.32 us
    ppermute x6, waiting for transfers between devices, body(): left = lambda a: lax.ppermute(a, 'head', LEFT)  2.99 us
  transfers between devices with their start and end apart: 24, of which 12 were waited for; matrix products, arithmetic and copies ran while one was open for 0% of the time, Pallas kernels for 47%

profile of v7, /device:TPU:0, one launch (start us, length us, event | category | flops | bytes accessed | tf_op | source)
XLA Modules:
  0.0 109.2 jit_solution(11149474449850743609)
XLA Ops:
  0.6 1.4 %halves.1 = (bf16[256,1536]{1,0:T(8,128)(2,1)S(1)}, bf16[256,1536]{1,0:T(8,128)(2,1)S(1)}, f32[8,128]{1,0:T(8,128)S(1)}) custom-call(bf16[512,1536]{1,0:T(8,128)(2,1)} %refs_1_.1), custom_call_target="tpu_custom_call" | custom-call | tf_op jit(solution)/shard_map/halves/pallas_call | solution.py:62
  2.0 1.7 %collective-permute-start.4 = (bf16[256,1536]{1,0:T(8,128)(2,1)S(1)}, bf16[256,1536]{1,0:T(8,128)(2,1)S(1)}, u32[]{:S(2)}, u32[]{:S(2)}) collective-permute-start(bf16[256,1536]{1,0:T(8,128)(2,1)S(1)} %get-tuple-element.88), channel_id=1, source_target_pairs={{0,1},{1,2},{2,3},{3,0},{4,5},{5,6},{6,7},{7,4},{8,9},{9,10},{10,1... | collective-permute-start | bytes 2359304 | tf_op jit(solution)/shard_map/ppermute | solution.py:513
  3.8 1.6 %collective-permute-start.5 = (bf16[256,1536]{1,0:T(8,128)(2,1)S(1)}, bf16[256,1536]{1,0:T(8,128)(2,1)S(1)}, u32[]{:S(2)}, u32[]{:S(2)}) collective-permute-start(bf16[256,1536]{1,0:T(8,128)(2,1)S(1)} %get-tuple-element.89), channel_id=1, source_target_pairs={{0,3},{1,0},{2,1},{3,2},{4,7},{5,4},{6,5},{7,6},{8,11},{9,8},{10,9... | collective-permute-start | bytes 2359304 | tf_op jit(solution)/shard_map/ppermute | solution.py:514
  5.4 5.5 %own_states.1 = (f32[512,8]{1,0:T(8,128)S(1)}, f32[8,512]{1,0:T(8,128)S(1)}, bf16[528,128]{1,0:T(8,128)(2,1)S(1)}, bf16[528,128]{1,0:T(8,128)(2,1)S(1)}, bf16[51...) custom-call(s32[15]{0:T(128)S(1)} %stack.60.refs_0_, ...), custom_call_target="tpu_custom_call" | custom-call | flops 8000000000 | tf_op jit(solution)/shard_map/own_states/pallas_call | solution.py:62
  11.6 2.8 %collective-permute-start.9 = (bf16[256,1536]{1,0:T(8,128)(2,1)}, bf16[256,1536]{1,0:T(8,128)(2,1)S(1)}, u32[]{:S(2)}, u32[]{:S(2)}) collective-permute-start(bf16[256,1536]{1,0:T(8,128)(2,1)} %get-tuple-element.98), channel_id=1, source_target_pairs={{0,3},{1,0},{2,1},{3,2},{4,7},{5,4},{6,5},{7,6},{8,11},{9,8},{10,9... | collective-permute-start | bytes 2359304 | tf_op jit(solution)/shard_map/ppermute | solution.py:514
  15.0 1.7 %collective-permute-start.1 = (bf16[528,128]{1,0:T(8,128)(2,1)S(1)}, bf16[528,128]{1,0:T(8,128)(2,1)S(1)}, u32[]{:S(2)}, u32[]{:S(2)}) collective-permute-start(bf16[528,128]{1,0:T(8,128)(2,1)S(1)} %chip_total.2.refs_7_.refs_1_), channel_id=1, source_target_pairs={{0,8},{4,12},{8,0},{12,4},{16,24},{20,28},{24,16},{28,20},{32,40},... | collective-permute-start | bytes 405512 | tf_op jit(solution)/shard_map/ppermute | solution.py:257
  16.6 5.5 %local.1 = (f32[512,1024]{1,0:T(8,128)S(1)}, bf16[512,1024]{1,0:T(8,128)(2,1)S(1)}, bf16[1024,512]{1,0:T(8,128)(2,1)S(1)}, bf16[1024,6144]{1,0:T(8,128)(2,1)S(1)}) custom-call(s32[15]{0:T(128)S(1)} %stack.60.refs_0_, f32[512,8]{1,0:T(8,128)S(1)} %get-tuple-element.72.refs_1_, f32[8,512]{1,0:T(8,128)S(1)} %get-tuple-element.73.refs_2_.refs_8_, ...), custom_call_target="tpu_custom_call" | custom-call | tf_op jit(solution)/shard_map/local/pallas_call | solution.py:62
  22.1 0.6 meet.6
  22.7 2.8 %collective-permute-start.2 = (bf16[528,128]{1,0:T(8,128)(2,1)S(1)}, bf16[528,128]{1,0:T(8,128)(2,1)S(1)}, u32[]{:S(2)}, u32[]{:S(2)}) collective-permute-start(bf16[528,128]{1,0:T(8,128)(2,1)S(1)} %get-tuple-element.81.refs_1_), channel_id=1, source_target_pairs={{0,16},{4,20},{8,24},{12,28},{16,0},{20,4},{24,8},{28,12},{32,48},... | collective-permute-start | bytes 405512 | tf_op jit(solution)/shard_map/ppermute | solution.py:257
  25.6 2.4 %grad_own.1.refs_5_.refs_6_ = f32[512,1024]{1,0:T(8,128)S(1)} custom-call(s32[15]{0:T(128)S(1)} %stack.60.refs_0_, bf16[512,1536]{1,0:T(8,128)(2,1)S(1)} %copy-done, bf16[1024,6144]{1,0:T(8,128)(2,1)S(1)} %get-tuple-element.84.refs_2_.refs_5_.refs_3_, f32[8,128]{1,0:T(8,128)S(1)} %get-tuple-element.83.refs_3_.refs_4_), custom_call_target="tpu_custom_call" | custom-call | tf_op jit(solution)/shard_map/grad_own/pallas_call | solution.py:62
  27.9 1.5 %collective-permute-done.2.refs_2_ = bf16[528,128]{1,0:T(8,128)(2,1)S(1)} collective-permute-done((bf16[528,128]{1,0:T(8,128)(2,1)S(1)}, bf16[528,128]{1,0:T(8,128)(2,1)S(1)}, u32[]{:S(2)}, u32[]{:S(2)}) %collective-permute-start.2) | collective-permute-done | bytes 135200 | tf_op jit(solution)/shard_map/ppermute | solution.py:257
  29.4 0.6 meet.7
  30.1 2.0 %collective-permute-start.3 = (bf16[528,128]{1,0:T(8,128)(2,1)S(1)}, bf16[528,128]{1,0:T(8,128)(2,1)S(1)}, u32[]{:S(2)}, u32[]{:S(2)}) collective-permute-start(bf16[528,128]{1,0:T(8,128)(2,1)S(1)} %get-tuple-element.85.refs_1_), channel_id=1, source_target_pairs={{0,32},{4,36},{8,40},{12,44},{16,48},{20,52},{24,56},{28,60},{32,0... | collective-permute-start | bytes 405512 | tf_op jit(solution)/shard_map/ppermute | solution.py:257
  32.2 0.7 collective-permute-start.13
  32.8 1.4 %collective-permute-start.12 = (bf16[256,1536]{1,0:T(8,128)(2,1)S(1)}, bf16[256,1536]{1,0:T(8,128)(2,1)S(1)}, u32[]{:S(2)}, u32[]{:S(2)}) collective-permute-start(bf16[256,1536]{1,0:T(8,128)(2,1)S(1)} %get-tuple-element.90.refs_5_), channel_id=1, source_target_pairs={{0,1},{1,2},{2,3},{3,0},{4,5},{5,6},{6,7},{7,4},{8,9},{9,10},{10,1... | collective-permute-start | bytes 2359304 | tf_op jit(solution)/shard_map/ppermute | solution.py:513
  34.3 0.9 collective-permute-done.3.refs_2_
  35.1 0.6 meet.8
  35.8 4.0 %collective-permute-start.6 = (bf16[528,128]{1,0:T(8,128)(2,1)S(1)}, bf16[528,128]{1,0:T(8,128)(2,1)S(1)}, u32[]{:S(2)}, u32[]{:S(2)}) collective-permute-start(bf16[528,128]{1,0:T(8,128)(2,1)S(1)} %get-tuple-element.91), channel_id=1, source_target_pairs={{0,64},{4,68},{8,72},{12,76},{16,80},{20,84},{24,88},{28,92},{32,9... | collective-permute-start | bytes 405512 | tf_op jit(solution)/shard_map/ppermute | solution.py:269
  39.7 3.0 %collective-permute-done.6.refs_1_ = bf16[528,128]{1,0:T(8,128)(2,1)S(1)} collective-permute-done((bf16[528,128]{1,0:T(8,128)(2,1)S(1)}, bf16[528,128]{1,0:T(8,128)(2,1)S(1)}, u32[]{:S(2)}, u32[]{:S(2)}) %collective-permute-start.6) | collective-permute-done | bytes 135200 | tf_op jit(solution)/shard_map/ppermute | solution.py:269
  42.7 0.6 arrive.2
  43.6 1.3 %collective-permute-done.7.refs_4_.refs_8_ = bf16[512,128]{1,0:T(8,128)(2,1)S(1)} collective-permute-done((bf16[512,128]{1,0:T(8,128)(2,1)S(1)}, bf16[512,128]{1,0:T(8,128)(2,1)S(1)}, u32[]{:S(2)}, u32[]{:S(2)}) %collective-permute-start.7) | collective-permute-done | bytes 131104 | tf_op jit(solution)/shard_map/ppermute | solution.py:279
  45.0 1.5 %attend.1 = (bf16[512,1024]{1,0:T(8,128)(2,1)S(1)}, f32[512,1024]{1,0:T(8,128)S(1)}, f32[512,1024]{1,0:T(8,128)S(1)}) custom-call(s32[15]{0:T(128)S(1)} %stack.60.refs_0_, f32[512,1024]{1,0:T(8,128)S(1)} %get-tuple-element.79.refs_3_.refs_1_, bf16[512,1024]{1,0:T(8,128)(2,1)S(1)} %get-tuple-element.80.refs_2_, ...), custom_call_target="tpu_custom_call" | custom-call | tf_op jit(solution)/shard_map/attend/pallas_call | solution.py:62
  46.5 4.0 %grad_near.1.refs_3_.refs_4_ = f32[512,1024]{1,0:T(8,128)S(1)} custom-call(s32[15]{0:T(128)S(1)} %stack.60.refs_0_, bf16[256,1536]{1,0:T(8,128)(2,1)S(1)} %collective-permute-done.4.refs_0_.refs_1_, bf16[256,1536]{1,0:T(8,128)(2,1)S(1)} %collective-permute-done.8.refs_2_, bf16[256,1536]{1,0:T(8,128)(2,1)S(1)} %collective-permute-done.9.refs_3_, ...), custom_call_target="tpu_custom_call" | custom-call | tf_op jit(solution)/shard_map/grad_near/pallas_call | solution.py:62
  50.5 2.4 %project_far.1 = (bf16[256,1536]{1,0:T(8,128)(2,1)S(1)}, bf16[256,1536]{1,0:T(8,128)(2,1)S(1)}) custom-call(s32[15]{0:T(128)S(1)} %stack.60.refs_0_, bf16[512,1024]{1,0:T(8,128)(2,1)S(1)} %get-tuple-element.96.refs_1_, bf16[1024,6144]{1,0:T(8,128)(2,1)S(1)} %get-tuple-element.84.refs_2_.refs_5_.refs_3_, f32[512,1024]{1,0:T(8,128)S(1)} %grad_near.1.refs_3_.refs_4_), custom_call_target="tpu_custom_call" | custom-call | tf_op jit(solution)/shard_map/project_far/pallas_call | solution.py:62
  52.9 0.7 collective-permute-start.11
  53.6 1.4 %collective-permute-start.10 = (bf16[256,1536]{1,0:T(8,128)(2,1)S(1)}, bf16[256,1536]{1,0:T(8,128)(2,1)S(1)}, u32[]{:S(2)}, u32[]{:S(2)}) collective-permute-start(bf16[256,1536]{1,0:T(8,128)(2,1)S(1)} %get-tuple-element.100.refs_3_), channel_id=1, source_target_pairs={{0,1},{1,2},{2,3},{3,0},{4,5},{5,6},{6,7},{7,4},{8,9},{9,10},{10,1... | collective-permute-start | bytes 2359304 | tf_op jit(solution)/shard_map/ppermute | solution.py:513
  55.0 4.0 %project_near.1 = (f32[256,1536]{1,0:T(8,128)S(1)}, bf16[256,1536]{1,0:T(8,128)(2,1)S(1)}, bf16[256,1536]{1,0:T(8,128)(2,1)S(1)}, f32[256,1536]{1,0:T(8,128)S(1)}) custom-call(s32[15]{0:T(128)S(1)} %stack.60.refs_0_, bf16[512,1024]{1,0:T(8,128)(2,1)S(1)} %get-tuple-element.96.refs_1_, bf16[1024,6144]{1,0:T(8,128)(2,1)S(1)} %get-tuple-element.84.refs_2_.refs_5_.refs_3_, ...), custom_call_target="tpu_custom_call" | custom-call | tf_op jit(solution)/shard_map/project_near/pallas_call | solution.py:62
  59.0 6.8 %grad_far.1 = (bf16[512,1024]{1,0:T(8,128)(2,1)S(1)}, bf16[528,128]{1,0:T(8,128)(2,1)S(1)}, bf16[528,128]{1,0:T(8,128)(2,1)S(1)}) custom-call(s32[15]{0:T(128)S(1)} %stack.60.refs_0_, bf16[256,1536]{1,0:T(8,128)(2,1)S(1)} %collective-permute-done.12.refs_1_, bf16[256,1536]{1,0:T(8,128)(2,1)S(1)} %collective-permute-done.13.refs_2_, ...), custom_call_target="tpu_custom_call" | custom-call | tf_op jit(solution)/shard_map/grad_far/pallas_call | solution.py:62
  65.9 1.9 %collective-permute-start.16 = (bf16[256,1536]{1,0:T(8,128)(2,1)S(1)}, bf16[256,1536]{1,0:T(8,128)(2,1)S(1)}, u32[]{:S(2)}, u32[]{:S(2)}) collective-permute-start(bf16[256,1536]{1,0:T(8,128)(2,1)S(1)} %get-tuple-element.115), channel_id=1, source_target_pairs={{0,3},{1,0},{2,1},{3,2},{4,7},{5,4},{6,5},{7,6},{8,11},{9,8},{10,9... | collective-permute-start | bytes 2359304 | tf_op jit(solution)/shard_map/ppermute | solution.py:514
  68.6 1.6 %collective-permute-start.15 = (bf16[528,128]{1,0:T(8,128)(2,1)S(1)}, bf16[528,128]{1,0:T(8,128)(2,1)S(1)}, u32[]{:S(2)}, u32[]{:S(2)}) collective-permute-start(bf16[528,128]{1,0:T(8,128)(2,1)S(1)} %chip_total.3.refs_9_.refs_1_), channel_id=1, source_target_pairs={{0,8},{4,12},{8,0},{12,4},{16,24},{20,28},{24,16},{28,20},{32,40},... | collective-permute-start | bytes 405512 | tf_op jit(solution)/shard_map/ppermute | solution.py:257
  70.1 3.4 %inside.2 = (bf16[512,512]{1,0:T(8,128)(2,1)S(1)}, f32[512,512]{1,0:T(8,128)S(1)}, f32[512,512]{1,0:T(8,128)S(1)}) custom-call(s32[15]{0:T(128)S(1)} %stack.60.refs_0_, f32[512,8]{1,0:T(8,128)S(1)} %get-tuple-element.72.refs_1_, f32[8,512]{1,0:T(8,128)S(1)} %get-tuple-element.73.refs_2_.refs_8_, bf16[512,1024]{1,0:T(8,128)(2,1)S(1)} %get-tuple-element.74.refs_3_, ...), custom_call_target="tpu_custom_call" | custom-call | tf_op jit(solution)/shard_map/inside/pallas_call | solution.py:62
  73.5 0.8 collective-permute-done.15.refs_2_
  75.5 2.8 %collective-permute-start.21 = (bf16[256,1536]{1,0:T(8,128)(2,1)S(1)}, bf16[256,1536]{1,0:T(8,128)(2,1)S(1)}, u32[]{:S(2)}, u32[]{:S(2)}) collective-permute-start(bf16[256,1536]{1,0:T(8,128)(2,1)S(1)} %get-tuple-element.126), channel_id=1, source_target_pairs={{0,3},{1,0},{2,1},{3,2},{4,7},{5,4},{6,5},{7,6},{8,11},{9,8},{10,9... | collective-permute-start | bytes 2359304 | tf_op jit(solution)/shard_map/ppermute | solution.py:514
  78.3 3.0 %collective-permute-start.18 = (bf16[528,128]{1,0:T(8,128)(2,1)S(1)}, bf16[528,128]{1,0:T(8,128)(2,1)S(1)}, u32[]{:S(2)}, u32[]{:S(2)}) collective-permute-start(bf16[528,128]{1,0:T(8,128)(2,1)S(1)} %get-tuple-element.117.refs_1_), channel_id=1, source_target_pairs={{0,16},{4,20},{8,24},{12,28},{16,0},{20,4},{24,8},{28,12},{32,48},... | collective-permute-start | bytes 405512 | tf_op jit(solution)/shard_map/ppermute | solution.py:257
  81.3 2.4 %project_own.1 = (f32[256,1536]{1,0:T(8,128)S(1)}, f32[256,1536]{1,0:T(8,128)S(1)}) custom-call(s32[15]{0:T(128)S(1)} %stack.60.refs_0_, bf16[512,1024]{1,0:T(8,128)(2,1)S(1)} %get-tuple-element.96.refs_1_, bf16[1024,6144]{1,0:T(8,128)(2,1)S(1)} %get-tuple-element.84.refs_2_.refs_5_.refs_3_, bf16[256,1536]{1,0:T(8,128)(2,1)S(1)} %get-tuple-element.112.refs_3_), custom_call_target="tpu_custom_call" | custom-call | tf_op jit(solution)/shard_map/project_own/pallas_call | solution.py:62
  83.7 1.2 %collective-permute-done.18.refs_2_ = bf16[528,128]{1,0:T(8,128)(2,1)S(1)} collective-permute-done((bf16[528,128]{1,0:T(8,128)(2,1)S(1)}, bf16[528,128]{1,0:T(8,128)(2,1)S(1)}, u32[]{:S(2)}, u32[]{:S(2)}) %collective-permute-start.18) | collective-permute-done | bytes 135200 | tf_op jit(solution)/shard_map/ppermute | solution.py:257
  84.9 0.6 meet.10
  85.5 2.0 %collective-permute-start.19 = (bf16[528,128]{1,0:T(8,128)(2,1)S(1)}, bf16[528,128]{1,0:T(8,128)(2,1)S(1)}, u32[]{:S(2)}, u32[]{:S(2)}) collective-permute-start(bf16[528,128]{1,0:T(8,128)(2,1)S(1)} %get-tuple-element.119.refs_1_), channel_id=1, source_target_pairs={{0,32},{4,36},{8,40},{12,44},{16,48},{20,52},{24,56},{28,60},{32,0... | collective-permute-start | bytes 405512 | tf_op jit(solution)/shard_map/ppermute | solution.py:257
  87.4 4.4 %inside.3 = (bf16[512,1024]{1,0:T(8,128)(2,1)}, f32[512,512]{1,0:T(8,128)S(1)}, f32[512,512]{1,0:T(8,128)S(1)}) custom-call(s32[15]{0:T(128)S(1)} %stack.60.refs_0_, f32[512,8]{1,0:T(8,128)S(1)} %get-tuple-element.72.refs_1_, f32[8,512]{1,0:T(8,128)S(1)} %get-tuple-element.73.refs_2_.refs_8_, bf16[512,1024]{1,0:T(8,128)(2,1)S(1)} %get-tuple-element.74.refs_3_, ...), custom_call_target="tpu_custom_call" | custom-call | tf_op jit(solution)/shard_map/inside/pallas_call | solution.py:62
  92.0 0.6 meet.11
  92.7 3.6 %collective-permute-start.22 = (bf16[528,128]{1,0:T(8,128)(2,1)S(1)}, bf16[528,128]{1,0:T(8,128)(2,1)S(1)}, u32[]{:S(2)}, u32[]{:S(2)}) collective-permute-start(bf16[528,128]{1,0:T(8,128)(2,1)S(1)} %get-tuple-element.130), channel_id=1, source_target_pairs={{0,64},{4,68},{8,72},{12,76},{16,80},{20,84},{24,88},{28,92},{32,9... | collective-permute-start | bytes 405512 | tf_op jit(solution)/shard_map/ppermute | solution.py:269
  96.5 2.7 %collective-permute-done.22.refs_1_ = bf16[528,128]{1,0:T(8,128)(2,1)S(1)} collective-permute-done((bf16[528,128]{1,0:T(8,128)(2,1)S(1)}, bf16[528,128]{1,0:T(8,128)(2,1)S(1)}, u32[]{:S(2)}, u32[]{:S(2)}) %collective-permute-start.22) | collective-permute-done | bytes 135200 | tf_op jit(solution)/shard_map/ppermute | solution.py:269
  99.3 0.6 arrive.3
  100.0 1.3 %collective-permute-done.23.refs_9_ = bf16[512,128]{1,0:T(8,128)(2,1)S(1)} collective-permute-done((bf16[512,128]{1,0:T(8,128)(2,1)S(1)}, bf16[512,128]{1,0:T(8,128)(2,1)S(1)}, u32[]{:S(2)}, u32[]{:S(2)}) %collective-permute-start.23) | collective-permute-done | bytes 131104 | tf_op jit(solution)/shard_map/ppermute | solution.py:279
  101.4 2.7 %finish.1 = (bf16[512,1024]{1,0:T(8,128)(2,1)}, bf16[512,1024]{1,0:T(8,128)(2,1)}, f32[8,128]{1,0:T(8,128)S(1)}) custom-call(s32[15]{0:T(128)S(1)} %stack.60.refs_0_, f32[512,8]{1,0:T(8,128)S(1)} %get-tuple-element.72.refs_1_, bf16[512,1024]{1,0:T(8,128)(2,1)S(1)} %get-tuple-element.75.refs_4_.refs_2_, ...), custom_call_target="tpu_custom_call" | custom-call | tf_op jit(solution)/shard_map/finish/pallas_call | solution.py:62
  104.1 3.0 %collective-permute-done.21.refs_3_ = bf16[256,1536]{1,0:T(8,128)(2,1)S(1)} collective-permute-done((bf16[256,1536]{1,0:T(8,128)(2,1)S(1)}, bf16[256,1536]{1,0:T(8,128)(2,1)S(1)}, u32[]{:S(2)}, u32[]{:S(2)}) %collective-permute-start.21) | collective-permute-done | bytes 786464 | tf_op jit(solution)/shard_map/ppermute | solution.py:514
  107.0 0.8 collective-permute-done.20.refs_2_
  107.8 1.2 %total.1 = bf16[512,1536]{1,0:T(8,128)(2,1)} custom-call(f32[256,1536]{1,0:T(8,128)S(1)} %get-tuple-element.124.refs_6_.refs_0_, f32[256,1536]{1,0:T(8,128)S(1)} %get-tuple-element.125.refs_1_, bf16[256,1536]{1,0:T(8,128)(2,1)S(1)} %collective-permute-done.20.refs_2_, bf16[256,1536]{1,0:T(8,128)(2,1)S(1)} %collective-permute-done.21.refs_3_, ...), custom_call_target="tpu_custom_call" | custom-call | tf_op jit(solution)/shard_map/total/pallas_call | solution.py:62
  (32 shorter events, 4.2 us)
Async XLA Ops:
  0.6 4.8 %copy-start.1 = (f32[512,8]{0,1:T(8,128)S(1)}, f32[512,8]{0,1:T(8,128)}, u32[]{:S(2)}) copy-start(f32[512,8]{0,1:T(8,128)} %param.9) | copy-start | bytes 49156
  2.0 30.0 %collective-permute-start.4 = (bf16[256,1536]{1,0:T(8,128)(2,1)S(1)}, bf16[256,1536]{1,0:T(8,128)(2,1)S(1)}, u32[]{:S(2)}, u32[]{:S(2)}) collective-permute-start(bf16[256,1536]{1,0:T(8,128)(2,1)S(1)} %get-tuple-element.88), channel_id=1, source_target_pairs={{0,1},{1,2},{2,3},{3,0},{4,5},{5,6},{6,7},{7,4},{8,9},{9,10},{10,1... | collective-permute-start | bytes 2359304 | tf_op jit(solution)/shard_map/ppermute | solution.py:513
  3.8 28.3 %collective-permute-start.5 = (bf16[256,1536]{1,0:T(8,128)(2,1)S(1)}, bf16[256,1536]{1,0:T(8,128)(2,1)S(1)}, u32[]{:S(2)}, u32[]{:S(2)}) collective-permute-start(bf16[256,1536]{1,0:T(8,128)(2,1)S(1)} %get-tuple-element.89), channel_id=1, source_target_pairs={{0,3},{1,0},{2,1},{3,2},{4,7},{5,4},{6,5},{7,6},{8,11},{9,8},{10,9... | collective-permute-start | bytes 2359304 | tf_op jit(solution)/shard_map/ppermute | solution.py:514
  11.0 3.4 %collective-permute-start = (bf16[528,128]{1,0:T(8,128)(2,1)S(1)}, bf16[528,128]{1,0:T(8,128)(2,1)S(1)}, u32[]{:S(2)}, u32[]{:S(2)}) collective-permute-start(bf16[528,128]{1,0:T(8,128)(2,1)S(1)} %get-tuple-element.78), channel_id=1, source_target_pairs={{0,4},{4,0},{8,12},{12,8},{16,20},{20,16},{24,28},{28,24},{32,36},... | collective-permute-start | bytes 405512 | tf_op jit(solution)/shard_map/ppermute | solution.py:252
  11.1 35.4 %collective-permute-start.8 = (bf16[256,1536]{1,0:T(8,128)(2,1)}, bf16[256,1536]{1,0:T(8,128)(2,1)S(1)}, u32[]{:S(2)}, u32[]{:S(2)}) collective-permute-start(bf16[256,1536]{1,0:T(8,128)(2,1)} %get-tuple-element.97), channel_id=1, source_target_pairs={{0,1},{1,2},{2,3},{3,0},{4,5},{5,6},{6,7},{7,4},{8,9},{9,10},{10,1... | collective-permute-start | bytes 2359304 | tf_op jit(solution)/shard_map/ppermute | solution.py:513
  11.6 34.9 %collective-permute-start.9 = (bf16[256,1536]{1,0:T(8,128)(2,1)}, bf16[256,1536]{1,0:T(8,128)(2,1)S(1)}, u32[]{:S(2)}, u32[]{:S(2)}) collective-permute-start(bf16[256,1536]{1,0:T(8,128)(2,1)} %get-tuple-element.98), channel_id=1, source_target_pairs={{0,3},{1,0},{2,1},{3,2},{4,7},{5,4},{6,5},{7,6},{8,11},{9,8},{10,9... | collective-permute-start | bytes 2359304 | tf_op jit(solution)/shard_map/ppermute | solution.py:514
  15.0 7.1 %collective-permute-start.1 = (bf16[528,128]{1,0:T(8,128)(2,1)S(1)}, bf16[528,128]{1,0:T(8,128)(2,1)S(1)}, u32[]{:S(2)}, u32[]{:S(2)}) collective-permute-start(bf16[528,128]{1,0:T(8,128)(2,1)S(1)} %chip_total.2.refs_7_.refs_1_), channel_id=1, source_target_pairs={{0,8},{4,12},{8,0},{12,4},{16,24},{20,28},{24,16},{28,20},{32,40},... | collective-permute-start | bytes 405512 | tf_op jit(solution)/shard_map/ppermute | solution.py:257
  22.1 3.5 %copy-start = (bf16[512,1536]{1,0:T(8,128)(2,1)S(1)}, bf16[512,1536]{1,0:T(8,128)(2,1)}, u32[]{:S(2)}) copy-start(bf16[512,1536]{1,0:T(8,128)(2,1)} %refs_1_.1) | copy-start | bytes 4718596
  22.7 6.7 %collective-permute-start.2 = (bf16[528,128]{1,0:T(8,128)(2,1)S(1)}, bf16[528,128]{1,0:T(8,128)(2,1)S(1)}, u32[]{:S(2)}, u32[]{:S(2)}) collective-permute-start(bf16[528,128]{1,0:T(8,128)(2,1)S(1)} %get-tuple-element.81.refs_1_), channel_id=1, source_target_pairs={{0,16},{4,20},{8,24},{12,28},{16,0},{20,4},{24,8},{28,12},{32,48},... | collective-permute-start | bytes 405512 | tf_op jit(solution)/shard_map/ppermute | solution.py:257
  30.1 5.1 %collective-permute-start.3 = (bf16[528,128]{1,0:T(8,128)(2,1)S(1)}, bf16[528,128]{1,0:T(8,128)(2,1)S(1)}, u32[]{:S(2)}, u32[]{:S(2)}) collective-permute-start(bf16[528,128]{1,0:T(8,128)(2,1)S(1)} %get-tuple-element.85.refs_1_), channel_id=1, source_target_pairs={{0,32},{4,36},{8,40},{12,44},{16,48},{20,52},{24,56},{28,60},{32,0... | collective-permute-start | bytes 405512 | tf_op jit(solution)/shard_map/ppermute | solution.py:257
  32.2 26.8 %collective-permute-start.13 = (bf16[256,1536]{1,0:T(8,128)(2,1)S(1)}, bf16[256,1536]{1,0:T(8,128)(2,1)S(1)}, u32[]{:S(2)}, u32[]{:S(2)}) collective-permute-start(bf16[256,1536]{1,0:T(8,128)(2,1)S(1)} %get-tuple-element.104), channel_id=1, source_target_pairs={{0,3},{1,0},{2,1},{3,2},{4,7},{5,4},{6,5},{7,6},{8,11},{9,8},{10,9... | collective-permute-start | bytes 2359304 | tf_op jit(solution)/shard_map/ppermute | solution.py:514
  32.8 26.2 %collective-permute-start.12 = (bf16[256,1536]{1,0:T(8,128)(2,1)S(1)}, bf16[256,1536]{1,0:T(8,128)(2,1)S(1)}, u32[]{:S(2)}, u32[]{:S(2)}) collective-permute-start(bf16[256,1536]{1,0:T(8,128)(2,1)S(1)} %get-tuple-element.90.refs_5_), channel_id=1, source_target_pairs={{0,1},{1,2},{2,3},{3,0},{4,5},{5,6},{6,7},{7,4},{8,9},{9,10},{10,1... | collective-permute-start | bytes 2359304 | tf_op jit(solution)/shard_map/ppermute | solution.py:513
  35.8 7.0 %collective-permute-start.6 = (bf16[528,128]{1,0:T(8,128)(2,1)S(1)}, bf16[528,128]{1,0:T(8,128)(2,1)S(1)}, u32[]{:S(2)}, u32[]{:S(2)}) collective-permute-start(bf16[528,128]{1,0:T(8,128)(2,1)S(1)} %get-tuple-element.91), channel_id=1, source_target_pairs={{0,64},{4,68},{8,72},{12,76},{16,80},{20,84},{24,88},{28,92},{32,9... | collective-permute-start | bytes 405512 | tf_op jit(solution)/shard_map/ppermute | solution.py:269
  43.4 1.6 %collective-permute-start.7 = (bf16[512,128]{1,0:T(8,128)(2,1)S(1)}, bf16[512,128]{1,0:T(8,128)(2,1)S(1)}, u32[]{:S(2)}, u32[]{:S(2)}) collective-permute-start(bf16[512,128]{1,0:T(8,128)(2,1)S(1)} %get-tuple-element.95), channel_id=1, source_target_pairs={{0,4},{4,0},{8,12},{12,8},{16,20},{20,16},{24,28},{28,24},{32,36},... | collective-permute-start | bytes 393224 | tf_op jit(solution)/shard_map/ppermute | solution.py:279
  52.9 22.1 %collective-permute-start.11 = (bf16[256,1536]{1,0:T(8,128)(2,1)S(1)}, bf16[256,1536]{1,0:T(8,128)(2,1)S(1)}, u32[]{:S(2)}, u32[]{:S(2)}) collective-permute-start(bf16[256,1536]{1,0:T(8,128)(2,1)S(1)} %get-tuple-element.103), channel_id=1, source_target_pairs={{0,3},{1,0},{2,1},{3,2},{4,7},{5,4},{6,5},{7,6},{8,11},{9,8},{10,9... | collective-permute-start | bytes 2359304 | tf_op jit(solution)/shard_map/ppermute | solution.py:514
  53.6 21.6 %collective-permute-start.10 = (bf16[256,1536]{1,0:T(8,128)(2,1)S(1)}, bf16[256,1536]{1,0:T(8,128)(2,1)S(1)}, u32[]{:S(2)}, u32[]{:S(2)}) collective-permute-start(bf16[256,1536]{1,0:T(8,128)(2,1)S(1)} %get-tuple-element.100.refs_3_), channel_id=1, source_target_pairs={{0,1},{1,2},{2,3},{3,0},{4,5},{5,6},{6,7},{7,4},{8,9},{9,10},{10,1... | collective-permute-start | bytes 2359304 | tf_op jit(solution)/shard_map/ppermute | solution.py:513
  65.8 2.1 %collective-permute-start.14 = (bf16[528,128]{1,0:T(8,128)(2,1)S(1)}, bf16[528,128]{1,0:T(8,128)(2,1)S(1)}, u32[]{:S(2)}, u32[]{:S(2)}) collective-permute-start(bf16[528,128]{1,0:T(8,128)(2,1)S(1)} %get-tuple-element.108), channel_id=1, source_target_pairs={{0,4},{4,0},{8,12},{12,8},{16,20},{20,16},{24,28},{28,24},{32,36},... | collective-permute-start | bytes 405512 | tf_op jit(solution)/shard_map/ppermute | solution.py:252
  65.9 26.0 %collective-permute-start.16 = (bf16[256,1536]{1,0:T(8,128)(2,1)S(1)}, bf16[256,1536]{1,0:T(8,128)(2,1)S(1)}, u32[]{:S(2)}, u32[]{:S(2)}) collective-permute-start(bf16[256,1536]{1,0:T(8,128)(2,1)S(1)} %get-tuple-element.115), channel_id=1, source_target_pairs={{0,3},{1,0},{2,1},{3,2},{4,7},{5,4},{6,5},{7,6},{8,11},{9,8},{10,9... | collective-permute-start | bytes 2359304 | tf_op jit(solution)/shard_map/ppermute | solution.py:514
  67.8 24.3 %collective-permute-start.17 = (bf16[256,1536]{1,0:T(8,128)(2,1)S(1)}, bf16[256,1536]{1,0:T(8,128)(2,1)S(1)}, u32[]{:S(2)}, u32[]{:S(2)}) collective-permute-start(bf16[256,1536]{1,0:T(8,128)(2,1)S(1)} %get-tuple-element.116), channel_id=1, source_target_pairs={{0,1},{1,2},{2,3},{3,0},{4,5},{5,6},{6,7},{7,4},{8,9},{9,10},{10,1... | collective-permute-start | bytes 2359304 | tf_op jit(solution)/shard_map/ppermute | solution.py:513
  68.6 5.8 %collective-permute-start.15 = (bf16[528,128]{1,0:T(8,128)(2,1)S(1)}, bf16[528,128]{1,0:T(8,128)(2,1)S(1)}, u32[]{:S(2)}, u32[]{:S(2)}) collective-permute-start(bf16[528,128]{1,0:T(8,128)(2,1)S(1)} %chip_total.3.refs_9_.refs_1_), channel_id=1, source_target_pairs={{0,8},{4,12},{8,0},{12,4},{16,24},{20,28},{24,16},{28,20},{32,40},... | collective-permute-start | bytes 405512 | tf_op jit(solution)/shard_map/ppermute | solution.py:257
  75.5 31.5 %collective-permute-start.21 = (bf16[256,1536]{1,0:T(8,128)(2,1)S(1)}, bf16[256,1536]{1,0:T(8,128)(2,1)S(1)}, u32[]{:S(2)}, u32[]{:S(2)}) collective-permute-start(bf16[256,1536]{1,0:T(8,128)(2,1)S(1)} %get-tuple-element.126), channel_id=1, source_target_pairs={{0,3},{1,0},{2,1},{3,2},{4,7},{5,4},{6,5},{7,6},{8,11},{9,8},{10,9... | collective-permute-start | bytes 2359304 | tf_op jit(solution)/shard_map/ppermute | solution.py:514
  78.3 29.4 %collective-permute-start.20 = (bf16[256,1536]{1,0:T(8,128)(2,1)S(1)}, bf16[256,1536]{1,0:T(8,128)(2,1)S(1)}, u32[]{:S(2)}, u32[]{:S(2)}) collective-permute-start(bf16[256,1536]{1,0:T(8,128)(2,1)S(1)} %get-tuple-element.112.refs_3_), channel_id=1, source_target_pairs={{0,1},{1,2},{2,3},{3,0},{4,5},{5,6},{6,7},{7,4},{8,9},{9,10},{10,1... | collective-permute-start | bytes 2359304 | tf_op jit(solution)/shard_map/ppermute | solution.py:513
  78.3 6.5 %collective-permute-start.18 = (bf16[528,128]{1,0:T(8,128)(2,1)S(1)}, bf16[528,128]{1,0:T(8,128)(2,1)S(1)}, u32[]{:S(2)}, u32[]{:S(2)}) collective-permute-start(bf16[528,128]{1,0:T(8,128)(2,1)S(1)} %get-tuple-element.117.refs_1_), channel_id=1, source_target_pairs={{0,16},{4,20},{8,24},{12,28},{16,0},{20,4},{24,8},{28,12},{32,48},... | collective-permute-start | bytes 405512 | tf_op jit(solution)/shard_map/ppermute | solution.py:257
  85.5 6.6 %collective-permute-start.19 = (bf16[528,128]{1,0:T(8,128)(2,1)S(1)}, bf16[528,128]{1,0:T(8,128)(2,1)S(1)}, u32[]{:S(2)}, u32[]{:S(2)}) collective-permute-start(bf16[528,128]{1,0:T(8,128)(2,1)S(1)} %get-tuple-element.119.refs_1_), channel_id=1, source_target_pairs={{0,32},{4,36},{8,40},{12,44},{16,48},{20,52},{24,56},{28,60},{32,0... | collective-permute-start | bytes 405512 | tf_op jit(solution)/shard_map/ppermute | solution.py:257
  92.7 6.6 %collective-permute-start.22 = (bf16[528,128]{1,0:T(8,128)(2,1)S(1)}, bf16[528,128]{1,0:T(8,128)(2,1)S(1)}, u32[]{:S(2)}, u32[]{:S(2)}) collective-permute-start(bf16[528,128]{1,0:T(8,128)(2,1)S(1)} %get-tuple-element.130), channel_id=1, source_target_pairs={{0,64},{4,68},{8,72},{12,76},{16,80},{20,84},{24,88},{28,92},{32,9... | collective-permute-start | bytes 405512 | tf_op jit(solution)/shard_map/ppermute | solution.py:269
  99.9 1.4 %collective-permute-start.23 = (bf16[512,128]{1,0:T(8,128)(2,1)S(1)}, bf16[512,128]{1,0:T(8,128)(2,1)S(1)}, u32[]{:S(2)}, u32[]{:S(2)}) collective-permute-start(bf16[512,128]{1,0:T(8,128)(2,1)S(1)} %get-tuple-element.133), channel_id=1, source_target_pairs={{0,4},{4,0},{8,12},{12,8},{16,20},{20,16},{24,28},{28,24},{32,36},... | collective-permute-start | bytes 393224 | tf_op jit(solution)/shard_map/ppermute | solution.py:279
